TPU v7x, 32 devices: a whole 2x2x4 slice. The times are simulated.
32 devices in a mesh: tm: 4 (over z), tok: 2 (over y), rep: 4 (over x, core).
Axes of the slice: x: 2, y: 2, z: 4, core: 2. Of those that a mesh axis runs over, the one named last changes fastest.
Arguments:
- x_branch: bfloat16 [8, 1024, 1024], P(('tok', 'rep'), 'tm'), may hold values from -6 to 6
- z_gate: bfloat16 [8, 1024, 1024], P(('tok', 'rep'), 'tm'), may hold values from -6 to 6
- b_input: bfloat16 [8, 1024, 128], P(('tok', 'rep'), 'tm'), may hold values from -6 to 6
- c_input: bfloat16 [8, 1024, 128], P(('tok', 'rep'), 'tm'), may hold values from -0.59765625 to 0.59765625
- step_raw: float32 [8, 16, 1024], P(('tok', 'rep'), None, 'tm'), may hold values from -4 to 4
- rate_log: float32 [16], replicated, may hold values from -3.5 to 1
- step_bias: float32 [16], replicated, may hold values from -4.5 to -3
- skip_gain: float32 [16], replicated, may hold values from 0.5 to 2
- norm_gain: float32 [1024], replicated, may hold values from 0.5 to 1.5
- out_weight: bfloat16 [1024, 1024], P(('tok', 'rep')), may hold values from -0.1875 to 0.1875
- out_grad: bfloat16 [8, 1024, 1024], P(('tok', 'rep'), 'tm'), may hold values from -6 to 6
Outputs:
- mixed_out: bfloat16 [8, 1024, 1024], P(('tok', 'rep'), 'tm')
- x_grad: bfloat16 [8, 1024, 1024], P(('tok', 'rep'), 'tm')
- z_grad: bfloat16 [8, 1024, 1024], P(('tok', 'rep'), 'tm')
- b_grad: bfloat16 [8, 1024, 128], P(('tok', 'rep'), 'tm')
- c_grad: bfloat16 [8, 1024, 128], P(('tok', 'rep'), 'tm')
- step_grad: float32 [8, 16, 1024], P(('tok', 'rep'), None, 'tm')
- rate_grad: float32 [16], replicated
- bias_grad: float32 [16], replicated
- skip_grad: float32 [16], replicated
- gain_grad: float32 [1024], replicated
- weight_grad: bfloat16 [1024, 1024], P(('tok', 'rep'))
All inputs are finite; a program needn't handle non-finite values.
Results may differ from a plain program's by a relative error of at most 0.0085.
Values may be sent and summed in bfloat16 or wider, within the bound.
No kernel may reach another device: no remote copies, remote signals or barrier semaphores. Data moves between devices by JAX's collectives and lax.ppermute only.
A program may use at most 128 MiB of HBM per device.

v0:
```python
import jax
import jax.numpy as jnp
from jax import lax
from jax.sharding import PartitionSpec as P


def carried_in(value, axis, combine, identity, reverse):
    count, position = (lax.axis_size(axis), lax.axis_index(axis))
    everything = jax.tree.map(lambda part: lax.all_gather(part, axis), value)
    start = jax.tree.map(
        lambda part, zero: jnp.broadcast_to(jnp.asarray(zero, part.dtype), part.shape),
        value,
        identity,
    )

    def lap(k, before):
        at = count - 1 - k if reverse else k
        reached = at > position if reverse else at < position
        new = combine(before, jax.tree.map(lambda part: part[at], everything))
        return jax.tree.map(lambda a, b: jnp.where(reached, a, b), new, before)

    return lax.fori_loop(0, count, lap, start)


def decay_terms(step_raw, rate_log, step_bias):
    delta = jax.nn.softplus(step_raw + step_bias[None, :, None])
    cumlog = jnp.cumsum(delta * (-jnp.exp(rate_log))[None, :, None], axis=2)
    return (delta, cumlog)


def block_parts(x_feat, b_feat, step_raw, rate_log, step_bias):
    delta, cumlog = decay_terms(step_raw, rate_log, step_bias)
    seqs, length, width = x_feat.shape
    heads = rate_log.shape[0]
    x_heads = x_feat.reshape(seqs, length, heads, width // heads)
    tailing = jnp.exp(cumlog[:, :, -1:] - cumlog) * delta
    weighted = x_heads * tailing.transpose(0, 2, 1)[..., None]
    state = jnp.einsum("sqhp,sqn->shpn", weighted, b_feat, precision=lax.Precision.HIGHEST)
    return (state, jnp.exp(cumlog[:, :, -1]))


def block_output(
    x_feat, z_feat, b_feat, c_feat, step_raw, rate_log, step_bias, skip_gain, norm_gain, incoming
):
    delta, cumlog = decay_terms(step_raw, rate_log, step_bias)
    seqs, length, width = x_feat.shape
    heads = rate_log.shape[0]
    x_heads = x_feat.reshape(seqs, length, heads, width // heads)
    scores = jnp.einsum(
        "sqn,skn->sqk",
        c_feat.astype(jnp.bfloat16),
        b_feat.astype(jnp.bfloat16),
        preferred_element_type=jnp.float32,
    )
    positions = jnp.arange(length)
    later = positions[:, None] >= positions[None, :]
    gaps = cumlog[:, :, :, None] - cumlog[:, :, None, :]
    mixing = jnp.where(later, jnp.exp(jnp.where(later, gaps, 0.0)), 0.0)
    mixing = mixing * scores[:, None] * delta[:, :, None, :]
    within = jnp.einsum("shqk,skhp->sqhp", mixing, x_heads, precision=lax.Precision.HIGHEST)
    carried = jnp.einsum("sqn,shpn->sqhp", c_feat, incoming, precision=lax.Precision.HIGHEST)
    carried = carried * jnp.exp(cumlog).transpose(0, 2, 1)[..., None]
    inner = (within + carried + skip_gain[None, None, :, None] * x_heads).reshape(
        seqs, length, width
    )
    gated = inner * jax.nn.silu(z_feat)
    factor = lax.rsqrt(jnp.mean(gated * gated, axis=-1, keepdims=True) + 1e-05)
    return gated * factor * norm_gain


def link(earlier, later_one):
    return (earlier[0] * later_one[0], later_one[0][:, :, None, None] * earlier[1] + later_one[1])


def shards(
    x_branch,
    z_gate,
    b_input,
    c_input,
    step_raw,
    rate_log,
    step_bias,
    skip_gain,
    norm_gain,
    out_weight,
    out_grad,
):
    x_feat = x_branch.astype(jnp.float32)
    z_feat = z_gate.astype(jnp.float32)
    b_feat = b_input.astype(jnp.float32)
    c_feat = c_input.astype(jnp.float32)
    seqs, length, width = x_branch.shape
    state, total = block_parts(x_feat, b_feat, step_raw, rate_log, step_bias)
    neutral = (jnp.ones_like(total), jnp.zeros_like(state))
    incoming = carried_in((total, state), "tm", link, neutral, False)[1]
    normed_f, pull_out = jax.vjp(
        block_output,
        x_feat,
        z_feat,
        b_feat,
        c_feat,
        step_raw,
        rate_log,
        step_bias,
        skip_gain,
        norm_gain,
        incoming,
    )
    normed = normed_f.astype(jnp.bfloat16)
    flat = normed.reshape(seqs * length, width)
    grad_flat = out_grad.reshape(seqs * length, out_grad.shape[2])
    columns = flat
    mixed = jnp.dot(
        columns,
        lax.all_gather(out_weight, ("tok", "rep"), axis=0, tiled=True),
        preferred_element_type=jnp.float32,
    )
    backward = lax.dot_general(
        grad_flat,
        lax.all_gather(out_weight, ("tok", "rep"), axis=0, tiled=True),
        (((1,), (1,)), ((), ())),
        preferred_element_type=jnp.float32,
    )
    mixed_out = mixed.astype(jnp.bfloat16).reshape(seqs, length, out_weight.shape[1])
    normed_grad = backward.astype(jnp.bfloat16)
    grads_out = pull_out(normed_grad.astype(jnp.float32).reshape(seqs, length, width))
    local_carry = grads_out[9]
    later_grad = carried_in((total, local_carry), "tm", link, neutral, True)[1]
    total_grad = jnp.sum(later_grad * incoming, axis=(2, 3))
    _, pull_parts = jax.vjp(block_parts, x_feat, b_feat, step_raw, rate_log, step_bias)
    grads_parts = pull_parts((later_grad, total_grad))
    x_grad = (grads_out[0] + grads_parts[0]).astype(jnp.bfloat16)
    z_grad = grads_out[1].astype(jnp.bfloat16)
    b_grad = (grads_out[2] + grads_parts[1]).astype(jnp.bfloat16)
    c_grad = grads_out[3].astype(jnp.bfloat16)
    step_grad = grads_out[4] + grads_parts[2]
    rate_grad, bias_grad, skip_grad, gain_grad = lax.psum(
        (grads_out[5] + grads_parts[3], grads_out[6] + grads_parts[4], grads_out[7], grads_out[8]),
        ("tm", "tok", "rep"),
    )
    columns = flat
    share = lax.psum_scatter(
        lax.dot_general(
            columns, grad_flat, (((0,), (0,)), ((), ())), preferred_element_type=jnp.float32
        ),
        ("tok", "rep"),
        scatter_dimension=0,
        tiled=True,
    )
    weight_sum = lax.psum(share, "tm")
    weight_grad = weight_sum.astype(jnp.bfloat16)
    return (
        mixed_out,
        x_grad,
        z_grad,
        b_grad,
        c_grad,
        step_grad,
        rate_grad,
        bias_grad,
        skip_grad,
        gain_grad,
        weight_grad,
    )


def solution(mesh):
    placed = (
        P(("tok", "rep"), "tm", None),
        P(("tok", "rep"), "tm", None),
        P(("tok", "rep"), "tm", None),
        P(("tok", "rep"), "tm", None),
        P(("tok", "rep"), None, "tm"),
        P(),
        P(),
        P(),
        P(),
        P(("tok", "rep"), None),
        P(("tok", "rep"), "tm", None),
    )
    return jax.shard_map(
        shards,
        mesh=mesh,
        in_specs=placed,
        out_specs=(
            P(("tok", "rep"), "tm", None),
            P(("tok", "rep"), "tm", None),
            P(("tok", "rep"), "tm", None),
            P(("tok", "rep"), "tm", None),
            P(("tok", "rep"), "tm", None),
            P(("tok", "rep"), None, "tm"),
            P(),
            P(),
            P(),
            P(),
            P(("tok", "rep"), None),
        ),
        check_vma=False,
    )
```

profile of v0, /device:TPU:0, one launch (start us, length us, event | category | flops | bytes accessed | tf_op | source)
XLA Modules:
  0.0 258.3 jit_solution(362924654458052213)
XLA Ops:
  7.2 0.8 exponential_negate_fusion
  8.0 0.8 copy.233
  8.8 0.7 broadcast_multiply_fusion
  10.6 0.8 multiply_bitcast_fusion
  11.5 1.1 mul.417
  12.6 1.6 copy.243
  14.1 1.1 convert_multiply_fusion.3
  15.3 1.6 copy.244
  16.9 1.4 fusion.88
  18.3 0.7 all-gather.7.cloned.1.call-update
  19.1 1.0 copy.238
  20.1 1.2 copy.250
  21.4 0.7 copy.237
  22.2 1.3 copy.253
  23.5 12.7 %all-gather = f32[4,16,1]{1,2,0:T(1,128)S(1)} all-gather(f32[1,16,1]{1,2,0:T(1,128)S(1)} %get-tuple-element.479), channel_id=2, replica_groups=mesh['tm'=4,'tok'=2,'rep'=4] {'tm'}, dimensions={0}, use_global_device_ids=true | all-gather | bytes 320 | tf_op jit(solution)/shard_map/all_gather | solution.py:9
  36.2 0.7 iota_compare_fusion
  37.5 0.9 fusion.91
  38.4 28.7 %all-gather.9.cloned.1.call-done = f32[64,64,128]{2,1,0:T(8,128)} async-done(((f32[16,64,128]{2,1,0:T(8,128)}), f32[64,64,128]{2,1,0:T(8,128)}) %all-gather.9.cloned.1.call-update) | async-done | bytes 2097168 | tf_op jit(solution)/shard_map/all_gather | solution.py:9
  67.1 4.9 %while.30 = (s32[]{:T(128)}, f32[1,16,64,128]{3,2,1,0:T(8,128)S(1)}, s32[]{:T(128)}, f32[4,1,16]{2,1,0:T(1,128)S(1)}, f32[4,1,16,64,128]{4,3,2,1,0:T(8,128)}, /*index=5*/s32[]{:T(128)}, s32[]{:T(128)}) while((s32[]{:T(128)}, f32[1,16,64,128]{3,2,1,0:T(8,128)S(1)}, s32[]{:T(128)}, f32[4,1,16]{2,1,0:T(1,128)S(1)}, ...), condition=%wide.region_5.7_spmd.clone, body=%wide.region_4.6_spmd.clone.sunk | while | flops 524292 | bytes 1573169 | solution.py:22
  67.1 1.3 fusion.123
  68.4 1.2 fusion.123
  69.6 1.2 fusion.123
  70.8 1.2 fusion.123
  72.7 5.9 %fusion.32 = f32[1,256,16,64]{1,3,2,0:T(8,128)} fusion(bf16[256,16,64]{0,2,1:T(8,128)(2,1)} %bitcast.284, f32[16,256]{1,0:T(8,128)} %copy.237, f32[256,256]{1,0:T(8,128)} %fusion.91, f32[16,256]{1,0:T(8,128)} %bitcast_add_fusion.6, pred[256,256]{1,0:T(8,128)(4,1)} %iota_compare_fusion, f32[1,256,16,64]{1,3,2,0:T(8,128)S(1)} %bitcast.278, ...), kind=kOutput, calls=%fused_computation.39 | convolution fusion | flops 811597824 | bytes 4046912 | tf_op jit(solution)/shard_map/jvp(shqk,skhp->sqhp)/dot_general | solution.py:60
  78.6 2.6 copy.251
  81.2 1.6 multiply_reduce_fusion.5
  83.9 11.7 %all-gather.7.cloned.1.call-done = bf16[1024,1024]{1,0:T(8,128)(2,1)} async-done(((bf16[128,1024]{1,0:T(8,128)(2,1)}), bf16[1024,1024]{1,0:T(8,128)(2,1)}) %all-gather.7.cloned.1.call-update) | async-done | bytes 2097168 | tf_op jit(solution)/shard_map/all_gather | solution.py:115
  95.6 3.3 %fusion.59 = (f32[1024]{0:T(1024)}, f32[256]{0:T(256)S(1)}, bf16[256,1024]{1,0:T(8,128)(2,1)S(1)}) fusion(f32[1,256,1024]{2,1,0:T(8,128)S(1)} %get-tuple-element.467, f32[256]{0:T(256)} %fusion.95, f32[1024]{0:T(1024)} %param.24, bf16[1024,1024]{1,0:T(8,128)(2,1)} %all-gather.7.cloned.1.call-done, bf16[1,256,1024]{2,1,0:T(8,128)(2,1)S(1)} %copy-done), kind=kOutput, calls=%fused_computation.66 | convolution fusion | flops 538966784 | bytes 4204544 | tf_op jit(solution)/shard_map/dot_general | solution.py:118
  99.0 2.4 multiply_reduce_fusion.2
  101.4 1.0 copy-done.1
  102.4 1.1 mul.448
  103.5 2.6 %copy.254 = f32[1,256,1024]{1,2,0:T(8,128)} copy(f32[1,256,1024]{2,1,0:T(8,128)} %mul.448) | data formatting | bytes 2097152 | tf_op jit(solution)/shard_map/transpose(jvp())/mul | solution.py:62
  106.1 2.6 %fusion.84 = f32[16,64,128]{2,1,0:T(8,128)} fusion(f32[256,16,64]{0,2,1:T(8,128)} %bitcast.270, bf16[1,256,128]{2,1,0:T(8,128)(2,1)S(1)} %copy-done.11), kind=kOutput, calls=%fused_computation.115 | convolution fusion | flops 402653184 | bytes 1638400 | tf_op jit(solution)/shard_map/transpose(jvp(sqn,shpn->sqhp))/dot_general | solution.py:61
  109.0 2.8 %fusion.69 = f32[1024,1024]{1,0:T(8,128)} fusion(bf16[1,256,1024]{2,1,0:T(8,128)(2,1)S(1)} %copy-done, f32[1,256,1024]{2,1,0:T(8,128)S(1)} %get-tuple-element.467, f32[1024]{0:T(1024)S(1)} %copy-done.17, f32[256]{0:T(256)S(1)} %copy-done.19), kind=kOutput, calls=%fused_computation.81 | convolution fusion | flops 537657344 | bytes 5772288 | tf_op jit(solution)/shard_map/dot_general | solution.py:143
  111.8 2.6 copy.252
  114.4 0.6 reduce_sum.190
  115.1 1.8 multiply_reduce_fusion.4
  117.0 6.9 %fusion.10 = (f32[16,256]{1,0:T(8,128)}, f32[16,256]{1,0:T(8,128)S(1)}, f32[16,256]{1,0:T(8,128)S(1)}, bf16[256,256]{1,0:T(8,128)(2,1)S(1)}) fusion(f32[16,256]{1,0:T(8,128)S(1)} %copy-done.21, f32[256,256]{1,0:T(8,128)} %fusion.91, f32[16,256]{1,0:T(8,128)S(1)} %copy-done.23, pred[256,256]{1,0:T(8,128)(4,1)S(1)} %copy-done.15, ...), kind=kOutput, calls=%fused_computation.16 | convolution fusion | flops 820957184 | bytes 2113536 | tf_op jit(solution)/shard_map/transpose(jvp(shqk,skhp->sqhp))/dot_general | solution.py:60
  123.9 0.8 copy.266
  124.7 0.8 copy.267
  125.5 0.7 copy.263
  126.4 3.7 %fusion.54 = bf16[1,256,128]{2,1,0:T(8,128)(2,1)} fusion(f32[256,128]{1,0:T(8,128)S(1)} %fusion.51, f32[256,16,64]{0,2,1:T(8,128)} %bitcast.271, f32[1,16,64,128]{3,2,1,0:T(8,128)S(1)} %get-tuple-element.240), kind=kOutput, calls=%fused_computation.61 | convolution fusion | flops 402718720 | bytes 1769472 | tf_op jit(solution)/shard_map/transpose(jvp(sqn,shpn->sqhp))/dot_general | solution.py:61
  130.1 1.1 fusion.53
  131.2 3.2 %fusion.46 = bf16[1,256,1024]{2,1,0:T(8,128)(2,1)} fusion(bf16[1024,1024]{1,0:T(8,128)(2,1)} %all-gather.7.cloned.1.call-done, f32[1,256,1024]{2,1,0:T(8,128)S(1)} %get-tuple-element.467, f32[1024]{0:T(1024)} %param.24, f32[256]{0:T(256)} %fusion.95), kind=kOutput, calls=%fused_computation.49 | convolution fusion | flops 537919488 | bytes 3675136 | tf_op jit(solution)/shard_map/dot_general | solution.py:113
  134.4 20.5 %all-gather.11.cloned.1.call-done = f32[64,64,128]{2,1,0:T(8,128)} async-done(((f32[16,64,128]{2,1,0:T(8,128)}), f32[64,64,128]{2,1,0:T(8,128)}) %all-gather.11.cloned.1.call-update) | async-done | bytes 2097168 | tf_op jit(solution)/shard_map/all_gather | solution.py:9
  154.9 7.3 %while.31 = (s32[]{:T(128)}, f32[1,16,64,128]{3,2,1,0:T(8,128)S(1)}, s32[]{:T(128)}, f32[4,1,16]{2,1,0:T(1,128)}, f32[4,1,16,64,128]{4,3,2,1,0:T(8,128)}, /*index=5*/s32[]{:T(128)}, s32[]{:T(128)}, s32[]{:T(128)}, s32[]{:T(128)}) while((s32[]{:T(128)}, f32[1,16,64,128]{3,2,1,0:T(8,128)S(1)}, s32[]{:T(128)}, ...), condition=%wide.region_9.11_spmd.clone, body=%wide.region_8.10_spmd.clone.sunk | while | flops 524296 | bytes 1573231 | solution.py:22
  154.9 0.6 dynamic-slice_bitcast_fusion.5
  155.6 1.2 fusion.124
  157.4 1.2 fusion.124
  159.1 1.2 fusion.124
  160.3 0.7 dynamic-slice_bitcast_fusion.5
  161.0 1.2 fusion.124
  162.2 1.6 multiply_reduce_fusion.3
  164.1 1.1 fusion.106
  165.3 2.5 reduce-window.36
  168.0 2.5 reduce-window.34
  170.8 1.2 multiply_reduce_fusion.8
  172.0 0.7 add_multiply_fusion
  172.7 39.7 %all-reduce.2 = (f32[16]{0:T(128)}, f32[16]{0:T(128)}, f32[16]{0:T(128)}, f32[1024]{0:T(1024)}) all-reduce(f32[16]{0:T(128)S(1)} %add_multiply_fusion, f32[16]{0:T(128)S(1)} %add.169, f32[16]{0:T(128)} %reduce_sum.190, f32[1024]{0:T(1024)} %get-tuple-element.430), channel_id=1, replica_groups=mesh['tm'=4,'tok'=2,'rep'=4] {'tm','tok','rep'}, use_global_device_ids=true, to_apply=%region_24.26 | all-reduce | flops 1072 | bytes 8576 | tf_op jit(solution)/shard_map/psum | solution.py:137
  212.4 5.8 %fusion.41 = bf16[1,256,16,64]{1,3,2,0:T(8,128)(2,1)S(1)} fusion(f32[16,64,256]{2,1,0:T(8,128)} %bitcast.274, f32[16,256]{1,0:T(8,128)S(1)} %copy-done.22, f32[256,256]{1,0:T(8,128)} %fusion.91, f32[16,256]{1,0:T(8,128)S(1)} %copy-done.24, pred[256,256]{1,0:T(8,128)(4,1)} %iota_compare_fusion, f32[1,256,16,64]{1,3,2,0:T(8,128)} %get-tuple-element.482, ...), kind=kOutput, calls=%fused_computation.44 | convolution fusion | flops 811859968 | bytes 4046912 | tf_op jit(solution)/shard_map/transpose(jvp(shqk,skhp->sqhp))/dot_general | solution.py:60
  218.2 1.0 copy.275
  219.3 0.7 copy.276
  219.9 2.4 fusion.50
  222.4 29.4 %all-reduce.4 = bf16[128,1024]{1,0:T(8,128)(2,1)} all-reduce(f32[128,1024]{1,0:T(8,128)} %reduce-scatter.2.cloned.1.call-done), channel_id=1, replica_groups=mesh['tm'=4,'tok'=2,'rep'=4] {'tm'}, use_global_device_ids=true, to_apply=%region_34.36 | all-reduce | flops 131072 | bytes 786432 | tf_op jit(solution)/shard_map/psum | solution.py:150
  (118 shorter events, 6.6 us)
Async XLA Ops:
  7.2 88.5 %copy-start = (bf16[1,256,1024]{2,1,0:T(8,128)(2,1)S(1)}, bf16[1,256,1024]{2,1,0:T(8,128)(2,1)}, u32[]{:S(2)}) copy-start(bf16[1,256,1024]{2,1,0:T(8,128)(2,1)} %param.26) | copy-start | bytes 1572868
  7.2 6.9 %copy-start.5 = (bf16[1,256,1024]{2,1,0:T(8,128)(2,1)S(1)}, bf16[1,256,1024]{2,1,0:T(8,128)(2,1)}, u32[]{:S(2)}) copy-start(bf16[1,256,1024]{2,1,0:T(8,128)(2,1)} %param.16) | copy-start | bytes 1572868
  7.2 59.9 %all-gather.9.cloned.1.call-start = ((), (), s32[]{:S(2)}) async-start(), calls=%async_computation.3 | async-start | bytes 2621440 | tf_op jit(solution)/shard_map/all_gather | solution.py:9
  8.0 1.6 copy-start.30
  10.6 6.2 %copy-start.28 = (f32[16]{0:T(128)}, f32[16]{0:T(128)S(1)}, u32[]{:S(2)}) copy-start(f32[16]{0:T(128)S(1)} %get-tuple-element.478) | copy-start | bytes 196
  10.6 6.2 %copy-start.12 = (bf16[1,256,128]{2,1,0:T(8,128)(2,1)S(1)}, bf16[1,256,128]{2,1,0:T(8,128)(2,1)}, u32[]{:S(2)}) copy-start(bf16[1,256,128]{2,1,0:T(8,128)(2,1)} %param.18) | copy-start | bytes 196612
  16.8 2.3 copy-start.3
  16.8 20.6 %copy-start.11 = (bf16[1,256,128]{2,1,0:T(8,128)(2,1)S(1)}, bf16[1,256,128]{2,1,0:T(8,128)(2,1)}, u32[]{:S(2)}) copy-start(bf16[1,256,128]{2,1,0:T(8,128)(2,1)} %param.19) | copy-start | bytes 196612
  18.3 77.3 %all-gather.7.cloned.1.call-start = ((), (), s32[]{:S(2)}) async-start(), calls=%async_computation.1 | async-start | bytes 2359296 | tf_op jit(solution)/shard_map/all_gather | solution.py:115
  19.0 135.9 %all-gather.11.cloned.1.call-start = ((), (), s32[]{:S(2)}) async-start(), calls=%async_computation.4 | async-start | bytes 2621440 | tf_op jit(solution)/shard_map/all_gather | solution.py:9
  21.4 45.7 %copy-start.14 = (f32[256,16]{0,1:T(8,128)}, f32[256,16]{0,1:T(8,128)S(1)}, u32[]{:S(2)}) copy-start(f32[256,16]{0,1:T(8,128)S(1)} %copy.249) | copy-start | bytes 49156
  67.1 5.6 %copy-start.8 = (f32[1,256,1024]{1,2,0:T(8,128)S(1)}, f32[1,256,1024]{1,2,0:T(8,128)}, u32[]{:S(2)}) copy-start(f32[1,256,1024]{1,2,0:T(8,128)} %copy.250) | copy-start | bytes 3145732
  72.0 0.6 copy-start.31
  72.6 6.0 %copy-start.7 = (f32[256,16,64]{0,2,1:T(8,128)}, f32[256,16,64]{0,2,1:T(8,128)S(1)}, u32[]{:S(2)}) copy-start(f32[256,16,64]{0,2,1:T(8,128)S(1)} %convolution_bitcast_fusion.1) | copy-start | bytes 3145732
  72.6 8.5 %copy-start.10 = (bf16[1,256,1024]{2,1,0:T(8,128)(2,1)S(1)}, bf16[1,256,1024]{2,1,0:T(8,128)(2,1)}, u32[]{:S(2)}) copy-start(bf16[1,256,1024]{2,1,0:T(8,128)(2,1)} %param.17) | copy-start | bytes 1572868
  82.8 0.6 copy-start.25
  95.6 3.3 %copy-start.26 = (f32[256]{0:T(256)S(1)}, f32[256]{0:T(256)}, u32[]{:S(2)}) copy-start(f32[256]{0:T(256)} %copy-done.25) | copy-start | bytes 3076
  95.6 3.3 %copy-start.2 = (f32[1,256,1024]{2,1,0:T(8,128)S(1)}, f32[1,256,1024]{2,1,0:T(8,128)}, u32[]{:S(2)}) copy-start(f32[1,256,1024]{2,1,0:T(8,128)} %copy.251) | copy-start | bytes 3145732
  95.6 3.3 %copy-start.16 = (f32[1024]{0:T(1024)S(1)}, f32[1024]{0:T(1024)}, u32[]{:S(2)}) copy-start(f32[1024]{0:T(1024)} %param.24) | copy-start | bytes 12292
  95.6 3.3 %copy-start.18 = (f32[256]{0:T(256)S(1)}, f32[256]{0:T(256)}, u32[]{:S(2)}) copy-start(f32[256]{0:T(256)} %fusion.95) | copy-start | bytes 3076
  95.6 6.7 %copy-start.6 = (f32[1,256,1024]{2,1,0:T(8,128)S(1)}, f32[1,256,1024]{2,1,0:T(8,128)}, u32[]{:S(2)}) copy-start(f32[1,256,1024]{2,1,0:T(8,128)} %copy.253) | copy-start | bytes 3145732
  101.4 1.0 copy-start.1
  101.4 7.6 %copy-start.17 = (f32[1024]{0:T(1024)S(1)}, f32[1024]{0:T(1024)}, u32[]{:S(2)}) copy-start(f32[1024]{0:T(1024)} %param.24) | copy-start | bytes 12292
  101.4 7.6 %copy-start.19 = (f32[256]{0:T(256)S(1)}, f32[256]{0:T(256)}, u32[]{:S(2)}) copy-start(f32[256]{0:T(256)} %fusion.95) | copy-start | bytes 3076
  108.8 113.6 %reduce-scatter.2.cloned.1.call-start = ((), (), s32[]{:S(2)}) async-start(), calls=%async_computation.2 | async-start | bytes 4718592 | tf_op jit(solution)/shard_map/reduce_scatter | solution.py:142
  111.8 2.6 %copy-start.20 = (f32[1024]{0:T(1024)S(1)}, f32[1024]{0:T(1024)}, u32[]{:S(2)}) copy-start(f32[1024]{0:T(1024)} %get-tuple-element.458) | copy-start | bytes 12292
  111.8 5.3 %copy-start.15 = (pred[256,256]{1,0:T(8,128)(4,1)S(1)}, pred[256,256]{1,0:T(8,128)(4,1)}, u32[]{:S(2)}) copy-start(pred[256,256]{1,0:T(8,128)(4,1)} %iota_compare_fusion) | copy-start | bytes 196612
  111.8 5.3 %copy-start.21 = (f32[16,256]{1,0:T(8,128)S(1)}, f32[16,256]{1,0:T(8,128)}, u32[]{:S(2)}) copy-start(f32[16,256]{1,0:T(8,128)} %copy.237) | copy-start | bytes 49156
  111.8 5.3 %copy-start.23 = (f32[16,256]{1,0:T(8,128)S(1)}, f32[16,256]{1,0:T(8,128)}, u32[]{:S(2)}) copy-start(f32[16,256]{1,0:T(8,128)} %bitcast_add_fusion.6) | copy-start | bytes 49156
  123.9 2.5 copy-start.13
  134.4 27.8 %copy-start.9 = (f32[1,256,1024]{1,2,0:T(8,128)S(1)}, f32[1,256,1024]{1,2,0:T(8,128)}, u32[]{:S(2)}) copy-start(f32[1,256,1024]{1,2,0:T(8,128)} %copy.250) | copy-start | bytes 3145732
  154.9 9.2 %copy-start.27 = (f32[16]{0:T(128)S(1)}, f32[16]{0:T(128)}, u32[]{:S(2)}) copy-start(f32[16]{0:T(128)} %param.22) | copy-start | bytes 196
  154.9 9.2 %copy-start.29 = (f32[16]{0:T(128)S(1)}, f32[16]{0:T(128)}, u32[]{:S(2)}) copy-start(f32[16]{0:T(128)} %copy-done.28) | copy-start | bytes 196
  162.2 50.2 %copy-start.22 = (f32[16,256]{1,0:T(8,128)S(1)}, f32[16,256]{1,0:T(8,128)}, u32[]{:S(2)}) copy-start(f32[16,256]{1,0:T(8,128)} %copy.237) | copy-start | bytes 49156
  162.2 50.2 %copy-start.24 = (f32[16,256]{1,0:T(8,128)S(1)}, f32[16,256]{1,0:T(8,128)}, u32[]{:S(2)}) copy-start(f32[16,256]{1,0:T(8,128)} %bitcast_add_fusion.6) | copy-start | bytes 49156
  212.4 7.5 %copy-start.4 = (f32[1,256,1024]{1,2,0:T(8,128)S(1)}, f32[1,256,1024]{1,2,0:T(8,128)}, u32[]{:S(2)}) copy-start(f32[1,256,1024]{1,2,0:T(8,128)} %copy-done.3) | copy-start | bytes 3145732
Sparse Core Ops, SparseCore 0:
  18.4 48.6 all-gather.8
  69.0 26.6 all-gather.6
  108.9 45.9 all-gather.10
  158.1 50.3 reduce-scatter.1
where the time goes:
time: 260 us; the launch traced here: 258 us
  blocking collectives  81.8 us (31%)
  waiting for transfers between devices  61.7 us (24%)
  matrix products  42.3 us (16%)
  other arithmetic  31.2 us (12%)
  local copies, waits for them, and re-layouts  26.5 us (10%)
  between operations  14.2 us (5%)
    all_gather x2, waiting for transfers between devices, carried_in(): everything = jax.tree.map(lambda part: lax.all_gather(part, axis), value)  49.3 us
    psum x1, blocking collectives, shards(): lax.psum((grads_out[5] + grads_parts[3], grads_out[6] + grads_parts[4], g...  39.7 us
    psum x1, blocking collectives, shards(): weight_sum = lax.psum(share, 'tm')  29.4 us
    dot_general x3, matrix products, block_output(): jnp.einsum('shqk,skhp->sqhp', mixing, x_heads, precision=lax.Precision.HI...  18.6 us
    all_gather x1, blocking collectives, carried_in(): everything = jax.tree.map(lambda part: lax.all_gather(part, axis), value)  12.7 us
    all_gather x1, waiting for transfers between devices, shards(): lax.all_gather(out_weight, ('tok', 'rep'), axis=0, tiled=True)  11.7 us
    select_n x8, other arithmetic, lap(): return jax.tree.map(lambda a, b: jnp.where(reached, a, b), new, before)  9.47 us
    dot_general x3, matrix products, block_output(): jnp.einsum('sqn,shpn->sqhp', c_feat, incoming, precision=lax.Precision.HI...  6.89 us
  transfers between devices with their start and end apart: 4, of which 3 were waited for; matrix products, arithmetic and copies ran while one was open for 29% of the time, Pallas kernels for 0%

commit v1 on v0

v1 whole, which is shorter than its diff:
```python
import functools

import jax
import jax.numpy as jnp
from jax import lax
from jax.experimental import pallas as pl
from jax.experimental.pallas import tpu as pltpu
from jax.sharding import PartitionSpec as P

BF = jnp.bfloat16
F32 = jnp.float32
ROWS = ((0,), (0,))
LAST = ((1,), (1,))
VMEM_LIMIT = 56 * 1024 * 1024


def mm(a, b):
    return jnp.dot(a, b, preferred_element_type=F32)


def mm_tn(a, b):
    return lax.dot_general(a, b, (ROWS, ((), ())), preferred_element_type=F32)


def mm_nt(a, b):
    return lax.dot_general(a, b, (LAST, ((), ())), preferred_element_type=F32)


def split(v, parts):
    pieces = []
    for _ in range(parts):
        piece = v.astype(BF)
        pieces.append(piece)
        v = v - piece.astype(F32)
    return pieces


def column(ref):
    row = ref[...].reshape(1, -1)
    heads = row.shape[1]
    i = lax.broadcasted_iota(jnp.int32, (heads, heads), 0)
    j = lax.broadcasted_iota(jnp.int32, (heads, heads), 1)
    return jnp.sum(jnp.where(i == j, row, 0.0), axis=1, keepdims=True)


def head_map(heads, width):
    i = lax.broadcasted_iota(jnp.int32, (heads, width), 0)
    j = lax.broadcasted_iota(jnp.int32, (heads, width), 1)
    wide = width // heads
    return jnp.where((j >= i * wide) & (j < (i + 1) * wide), 1.0, 0.0).astype(F32)


def triangle(length, keep):
    i = lax.broadcasted_iota(jnp.int32, (length, length), 0)
    j = lax.broadcasted_iota(jnp.int32, (length, length), 1)
    return jnp.where(keep(i, j), 1.0, 0.0).astype(BF)


def along_frames(v, tri):
    heads = v.shape[0]
    out = mm(jnp.concatenate(split(v, 3), axis=0), tri)
    return out[:heads] + out[heads : 2 * heads] + out[2 * heads :]


def expand(v, hmap):
    return mm_tn(jnp.concatenate(split(v, 2), axis=0), jnp.concatenate([hmap, hmap], axis=0).astype(BF))


def expand_row(col, hmap):
    return jnp.sum(col * hmap, axis=0, keepdims=True)


def head_sums(y, hmap):
    hb = hmap.astype(BF)
    hi, lo = split(y, 2)
    return mm_nt(hb, hi) + mm_nt(hb, lo)


def decay(s_ref, rate_ref, bias_ref):
    v = s_ref[...] + column(bias_ref)
    e = jnp.exp(-jnp.abs(v))
    u = 1.0 + e
    d = u - 1.0
    log1p = jnp.where(d == 0.0, e, jnp.log(u) * (e / jnp.where(d == 0.0, 1.0, d)))
    delta = jnp.maximum(v, 0.0) + log1p
    a = -jnp.exp(column(rate_ref))
    ld = delta * a
    cum = along_frames(ld, triangle(ld.shape[1], lambda i, j: i <= j))
    return v, delta, a, ld, cum


def call(kernel, outs, *args, smem=(), name=None, scratch=()):
    specs = [
        pl.BlockSpec(memory_space=pltpu.SMEM if k in smem else pltpu.VMEM) for k in range(len(args))
    ]
    return pl.pallas_call(
        kernel,
        out_shape=[jax.ShapeDtypeStruct(s, t) for s, t in outs],
        in_specs=specs,
        out_specs=[pl.BlockSpec(memory_space=pltpu.VMEM)] * len(outs),
        scratch_shapes=list(scratch),
        compiler_params=pltpu.CompilerParams(vmem_limit_bytes=VMEM_LIMIT),
        name=name,
    )(*args)


def state_kernel(x_ref, b_ref, s_ref, rate_ref, bias_ref, state_ref, total_ref):
    _, delta, _, _, cum = decay(s_ref, rate_ref, bias_ref)
    hmap = head_map(cum.shape[0], x_ref.shape[1])
    last = cum[:, -1:]
    tail = expand(jnp.exp(last - cum) * delta, hmap)
    weighted = (x_ref[...].astype(F32) * tail).astype(BF)
    state_ref[...] = mm_tn(b_ref[...], weighted).astype(BF)
    total_ref[...] = expand_row(jnp.exp(last), hmap)


def inner_kernel(x_ref, b_ref, c_ref, s_ref, rate_ref, bias_ref, skip_ref, inner_ref):
    _, delta, _, _, cum = decay(s_ref, rate_ref, bias_ref)
    heads, length = cum.shape
    width = x_ref.shape[1]
    hmap = head_map(heads, width)
    cum_t = cum.T
    x = x_ref[...].astype(F32)
    xd = (x * expand(delta, hmap)).astype(BF)
    skip = expand_row(column(skip_ref), hmap)
    half = length // 2
    scores = mm_nt(c_ref[...], b_ref[...])
    i = lax.broadcasted_iota(jnp.int32, (half, half), 0)
    j = lax.broadcasted_iota(jnp.int32, (half, half), 1)
    diag = i >= j
    s00 = jnp.where(diag, scores[:half, :half], 0.0)
    s10 = scores[half:, :half]
    s11 = jnp.where(diag, scores[half:, half:], 0.0)
    pair = 2 * (width // heads)
    first = lax.broadcasted_iota(jnp.int32, (half, pair), 1) < pair // 2
    for p in range(heads // 2):
        cols = slice(p * pair, (p + 1) * pair)
        upper, lower = [], []
        for h in (2 * p, 2 * p + 1):
            q0, q1 = cum_t[:half, h : h + 1], cum_t[half:, h : h + 1]
            k0, k1 = cum[h : h + 1, :half], cum[h : h + 1, half:]
            m00 = jnp.exp(jnp.minimum(q0 - k0, 0.0)) * s00
            m10 = jnp.exp(jnp.minimum(q1 - k0, 0.0)) * s10
            m11 = jnp.exp(jnp.minimum(q1 - k1, 0.0)) * s11
            upper.append(m00.astype(BF))
            lower.append(jnp.concatenate([m10.astype(BF), m11.astype(BF)], axis=1))
        y0 = mm(jnp.concatenate(upper, axis=0), xd[:half, cols])
        y1 = mm(jnp.concatenate(lower, axis=0), xd[:, cols])
        inner_ref[:half, cols] = jnp.where(first, y0[:half], y0[half:]) + skip[:, cols] * x[:half, cols]
        inner_ref[half:, cols] = jnp.where(first, y1[:half], y1[half:]) + skip[:, cols] * x[half:, cols]


def weight_kernel(idx_ref, g_ref, *refs):
    pieces, (full_ref, ng_ref) = refs[:-2], refs[-2:]
    me = idx_ref[0]
    rows, half = pieces[0].shape[0], pieces[0].shape[1] // 2

    def place(k):
        return pl.ds(pl.multiple_of((me ^ k) * rows, rows), rows)

    w, wc, wx, wxc, wy, wyc, d1, d2, d1c, d2c = pieces
    for k, piece in ((0, w), (1, wc), (2, wx), (3, wxc), (4, wy), (5, wyc)):
        full_ref[place(k), :] = piece[...]
    full_ref[place(6), :half] = d1[...]
    full_ref[place(6), half:] = d2[...]
    full_ref[place(7), :half] = d1c[...]
    full_ref[place(7), half:] = d2c[...]
    ng_ref[...] = mm_nt(g_ref[...], full_ref[...]).astype(BF)


def grad_kernel(g_ref, full_ref, ng_ref):
    ng_ref[...] = mm_nt(g_ref[...], full_ref[...]).astype(BF)


def norm_kernel(
    local_ref, inc_ref, c_ref, z_ref, x_ref, s_ref, rate_ref, bias_ref, skip_ref, gain_ref, ng_ref,
    normed_ref, dy_ref, carry_ref, zg_ref, rows_ref, gains_ref, skips_ref,
):
    _, _, _, _, cum = decay(s_ref, rate_ref, bias_ref)
    heads = cum.shape[0]
    width = x_ref.shape[1]
    hmap = head_map(heads, width)
    ec = expand(jnp.exp(cum), hmap)
    inner = local_ref[...] + mm(c_ref[...], inc_ref[...]) * ec
    z = z_ref[...].astype(F32)
    sig = 1.0 / (1.0 + jnp.exp(-z))
    silu = z * sig
    gated = inner * silu
    gain = gain_ref[...].reshape(1, -1)
    r = lax.rsqrt(jnp.mean(gated * gated, axis=1, keepdims=True) + 1e-05)
    nhat = gated * r
    normed_ref[...] = (nhat * gain).astype(BF)
    ng = ng_ref[...].astype(F32)
    prod = ng * nhat
    gains_ref[...] = jnp.sum(prod, axis=0, keepdims=True)
    m = jnp.mean(prod * gain, axis=1, keepdims=True)
    dgated = r * (ng * gain - nhat * m)
    dinner = dgated * silu
    dy = dinner.astype(BF)
    dy_ref[...] = dy
    carry_ref[...] = mm_tn(c_ref[...], (dinner * ec).astype(BF)).astype(BF)
    zg_ref[...] = (dgated * inner * (sig + silu * (1.0 - sig))).astype(BF)
    x = x_ref[...].astype(F32)
    dyf = dy.astype(F32)
    skip = expand_row(column(skip_ref), hmap)
    rows_ref[...] = head_sums(dyf * (inner - skip * x), hmap)
    skips_ref[...] = jnp.sum(jnp.sum(dinner * x, axis=0, keepdims=True) * hmap, axis=1, keepdims=True)


def outer_kernel(idx_ref, normed_ref, g_ref, mine_ref, other_ref):
    me = idx_ref[0]
    rows = mine_ref.shape[1]
    for k in range(8):
        cols = pl.ds(pl.multiple_of((me ^ k) * rows, rows), rows)
        part = mm_tn(normed_ref[:, cols], g_ref[...]).astype(BF)
        if k % 2 == 0:
            mine_ref[k // 2] = part
        else:
            other_ref[k // 2] = part


def outer_full_kernel(normed_ref, g_ref, out_ref):
    out_ref[...] = mm_tn(normed_ref[...], g_ref[...])


def add_pair_kernel(mine_ref, got_ref, a_keep, a_send, b_keep, b_send):
    half = mine_ref.shape[2] // 2

    def total(k, cols):
        return mine_ref[k, :, cols].astype(F32) + got_ref[k, :, cols].astype(F32)

    left, right = slice(0, half), slice(half, 2 * half)
    a_keep[0], a_keep[1] = total(0, left), total(2, left)
    a_send[0], a_send[1] = total(1, left).astype(BF), total(3, left).astype(BF)
    b_keep[0], b_keep[1] = total(0, right), total(1, right)
    b_send[0], b_send[1] = total(2, right).astype(BF), total(3, right).astype(BF)


def add_second_kernel(a_ref, ga_ref, b_ref, gb_ref, a_keep, a_send, b_keep, b_send):
    a_keep[...] = a_ref[0] + ga_ref[0].astype(F32)
    a_send[...] = (a_ref[1] + ga_ref[1].astype(F32)).astype(BF)
    b_keep[...] = b_ref[0] + gb_ref[0].astype(F32)
    b_send[...] = (b_ref[1] + gb_ref[1].astype(F32)).astype(BF)


def add_third_kernel(pos_ref, a_ref, ga_ref, b_ref, gb_ref, keep_ref, *refs):
    sends, scratch = refs[:-1], refs[-1]
    half = a_ref.shape[1]
    count = len(sends) + 1
    rows = a_ref.shape[0] // count
    scratch[:, :half] = a_ref[...] + ga_ref[...].astype(F32)
    scratch[:, half:] = b_ref[...] + gb_ref[...].astype(F32)
    z = pos_ref[1]

    def quarter(k):
        return scratch[pl.ds(pl.multiple_of(lax.rem(z + k, count) * rows, rows), rows), :]

    keep_ref[...] = quarter(0)
    for k, send in enumerate(sends):
        send[...] = quarter(k + 1).astype(BF)


def add_quarter_kernel(*refs):
    keep_ref, gots, out_ref = refs[0], refs[1:-1], refs[-1]
    total = keep_ref[...]
    for got in gots:
        total = total + got[...].astype(F32)
    out_ref[...] = total.astype(BF)


def join_kernel(pos_ref, *refs):
    pieces, out_ref = refs[:-1], refs[-1]
    count = len(pieces)
    rows = pieces[0].shape[0]
    z = pos_ref[1]
    for k, piece in enumerate(pieces):
        at = lax.rem(z + count - k, count) * rows
        out_ref[pl.ds(pl.multiple_of(at, rows), rows), :] = piece[...]


def back_kernel(
    x_ref, b_ref, c_ref, s_ref, rate_ref, bias_ref, skip_ref, dy_ref, inc_ref, normed_ref, full_ref,
    mixed_ref, cg_ref, xg_ref, bg_ref, cols_ref, dxw_ref,
):
    _, delta, _, _, cum = decay(s_ref, rate_ref, bias_ref)
    heads, length = cum.shape
    width = x_ref.shape[1]
    hmap = head_map(heads, width)
    cum_t = cum.T
    delta_e = expand(delta, hmap)
    xd = (x_ref[...].astype(F32) * delta_e).astype(BF)
    dy = dy_ref[...]
    half = length // 2
    scores = mm_nt(b_ref[...], c_ref[...])
    i = lax.broadcasted_iota(jnp.int32, (half, half), 0)
    j = lax.broadcasted_iota(jnp.int32, (half, half), 1)
    diag = j >= i
    s00 = jnp.where(diag, scores[:half, :half], 0.0)
    s01 = scores[:half, half:]
    s11 = jnp.where(diag, scores[half:, half:], 0.0)
    pair = 2 * (width // heads)
    first = lax.broadcasted_iota(jnp.int32, (half, pair), 1) < pair // 2
    whole_first = lax.broadcasted_iota(jnp.int32, (length, pair), 1) < pair // 2
    d00 = jnp.zeros((half, half), F32)
    d01 = jnp.zeros((half, half), F32)
    d11 = jnp.zeros((half, half), F32)
    none = jnp.zeros((length, pair), BF)
    for p in range(heads // 2):
        cols = slice(p * pair, (p + 1) * pair)
        xp, dp = xd[:, cols], dy[:, cols]
        stacked = jnp.concatenate([jnp.where(whole_first, xp, none), jnp.where(whole_first, none, xp)], axis=0)
        dm = mm_nt(stacked, dp)
        upper, lower = [], []
        for n, h in enumerate((2 * p, 2 * p + 1)):
            k0, k1 = cum_t[:half, h : h + 1], cum_t[half:, h : h + 1]
            q0, q1 = cum[h : h + 1, :half], cum[h : h + 1, half:]
            l00 = jnp.exp(jnp.minimum(q0 - k0, 0.0))
            l01 = jnp.exp(jnp.minimum(q1 - k0, 0.0))
            l11 = jnp.exp(jnp.minimum(q1 - k1, 0.0))
            at = n * length
            d00 = d00 + l00 * dm[at : at + half, :half]
            d01 = d01 + l01 * dm[at : at + half, half:]
            d11 = d11 + l11 * dm[at + half : at + length, half:]
            upper.append(jnp.concatenate([(l00 * s00).astype(BF), (l01 * s01).astype(BF)], axis=1))
            lower.append((l11 * s11).astype(BF))
        y0 = mm(jnp.concatenate(upper, axis=0), dp)
        y1 = mm(jnp.concatenate(lower, axis=0), dp[half:])
        dxw_ref[:half, cols] = jnp.where(first, y0[:half], y0[half:])
        dxw_ref[half:, cols] = jnp.where(first, y1[:half], y1[half:])
    d00 = jnp.where(diag, d00, 0.0).astype(BF)
    d01 = d01.astype(BF)
    d11 = jnp.where(diag, d11, 0.0).astype(BF)
    c0, c1 = c_ref[:half, :], c_ref[half:, :]
    b0, b1 = b_ref[:half, :], b_ref[half:, :]
    bg_ref[:half, :] = (mm(d00, c0) + mm(d01, c1)).astype(BF)
    bg_ref[half:, :] = mm(d11, c1).astype(BF)
    ec = expand(jnp.exp(cum), hmap)
    carried = mm_nt((dy.astype(F32) * ec).astype(BF), inc_ref[...])
    cg_ref[:half, :] = (carried[:half] + mm_tn(d00, b0).astype(BF).astype(F32)).astype(BF)
    cg_ref[half:, :] = (carried[half:] + (mm_tn(d01, b0) + mm_tn(d11, b1)).astype(BF).astype(F32)).astype(BF)
    dxw = dxw_ref[...]
    cols_ref[...] = head_sums(xd.astype(F32) * dxw, hmap)
    skip = expand_row(column(skip_ref), hmap)
    xg_ref[...] = delta_e * dxw + skip * dy.astype(F32)
    mixed_ref[...] = mm(normed_ref[...], full_ref[...]).astype(BF)


def last_kernel(
    x_ref, b_ref, s_ref, rate_ref, bias_ref, later_ref, inc_ref, xg_ref, bg_ref, rows_ref, cols_ref, gains_ref, skips_ref,
    x_out, b_out, step_out, sums_out,
):
    v, delta, a, ld, cum = decay(s_ref, rate_ref, bias_ref)
    heads, length = cum.shape
    width = x_ref.shape[1]
    hmap = head_map(heads, width)
    last = cum[:, -1:]
    tailing = jnp.exp(last - cum)
    tail = tailing * delta
    tail_e = expand(tail, hmap)
    x = x_ref[...].astype(F32)
    later = later_ref[...]
    dweighted = mm(b_ref[...], later)
    x_out[...] = (xg_ref[...] + tail_e * dweighted).astype(BF)
    weighted = (x * tail_e).astype(BF)
    b_out[...] = (bg_ref[...].astype(F32) + mm_nt(weighted, later)).astype(BF)
    dtail = head_sums(x * dweighted, hmap)
    cross = jnp.sum(later.astype(F32) * inc_ref[...].astype(F32), axis=0, keepdims=True)
    dtotal = jnp.sum(cross * hmap, axis=1, keepdims=True) * jnp.exp(last)
    cols = cols_ref[...]
    dld = along_frames(rows_ref[...] - cols, triangle(length, lambda i, j: i >= j))
    dld = dld + along_frames(dtail * tail, triangle(length, lambda i, j: i < j)) + dtotal
    ddelta = cols / delta + dtail * tailing + a * dld
    dstep = ddelta / (1.0 + jnp.exp(-v))
    step_out[...] = dstep
    drate = jnp.sum(dld * ld, axis=1, keepdims=True)
    dbias = jnp.sum(dstep, axis=1, keepdims=True)
    i = lax.broadcasted_iota(jnp.int32, (heads, 128), 0)
    j = lax.broadcasted_iota(jnp.int32, (heads, 128), 1)

    def lay(col, at):
        return jnp.sum(jnp.where(j == i + at, col, 0.0), axis=0, keepdims=True)

    small = lay(drate, 0) + lay(dbias, heads) + lay(skips_ref[...], 2 * heads)
    sums_out[:, :width] = jnp.broadcast_to(gains_ref[...], (sums_out.shape[0], width))
    sums_out[:, width:] = jnp.broadcast_to(small, (sums_out.shape[0], 128))


def sums_kernel(all_ref, out_ref):
    out_ref[...] = jnp.sum(all_ref[...], axis=0, keepdims=True)


def chain(value, total, axis, reverse):
    count = lax.axis_size(axis)
    incoming = jnp.zeros(value.shape, BF)
    for hop in range(count - 1):
        at = count - 1 - hop if reverse else hop
        to = at - 1 if reverse else at + 1
        send = (incoming.astype(F32) * total + value.astype(F32)).astype(BF)
        incoming = incoming + lax.ppermute(send, axis, [(at, to)])
    return incoming


def scan_far(value, total, axis, reverse):
    count = lax.axis_size(axis)
    position = lax.axis_index(axis)
    decayed, state = total, value.astype(F32)
    step = 1
    while step < count:
        pairs = [(k, k - step) for k in range(step, count)] if reverse else [(k, k + step) for k in range(count - step)]
        inside = position + step < count if reverse else position >= step
        got_state = lax.ppermute(state.astype(BF), axis, pairs).astype(F32)
        got_total = lax.ppermute(decayed, axis, pairs)
        state = jnp.where(inside, decayed * got_state + state, state)
        decayed = jnp.where(inside, decayed * got_total, decayed)
        step *= 2
    pairs = [(k, k - 1) for k in range(1, count)] if reverse else [(k, k + 1) for k in range(count - 1)]
    return lax.ppermute(state.astype(BF), axis, pairs)


def shards(x_branch, z_gate, b_input, c_input, step_raw, rate_log, step_bias, skip_gain, norm_gain, out_weight, out_grad):
    seqs, length, width = x_branch.shape
    model = out_grad.shape[2]
    heads = rate_log.shape[0]
    state_size = b_input.shape[2]
    x, z, b, c, s, g = x_branch[0], z_gate[0], b_input[0], c_input[0], step_raw[0], out_grad[0]
    n_tm, n_tok, n_rep = lax.axis_size("tm"), lax.axis_size("tok"), lax.axis_size("rep")
    rep, tok, tm = lax.axis_index("rep"), lax.axis_index("tok"), lax.axis_index("tm")
    near = (n_tok, n_rep) == (2, 4)
    rows = out_weight.shape[0]
    full = (width, model)
    wide = (length, width)
    place = jnp.stack([tok * n_rep + rep, tm]).astype(jnp.int32)
    core = [(k, k ^ 1) for k in range(4)]
    side = [(k, k ^ 2) for k in range(4)]
    front = [(0, 1), (1, 0)]
    scan = chain if n_tm <= 4 else scan_far

    state, total = call(
        state_kernel, [((state_size, width), BF), ((1, width), F32)], x, b, s, rate_log, step_bias, name="state"
    )
    if near:
        half = model // 2
        wx = lax.ppermute(out_weight, "rep", side)
        wy = lax.ppermute(out_weight, "tok", front)
        wc = lax.ppermute(out_weight, "rep", core)
        d1 = lax.ppermute(wx[:, :half], "tok", front)
        d2 = lax.ppermute(wy[:, half:], "rep", side)
        wxc = lax.ppermute(wx, "rep", core)
        wyc = lax.ppermute(wy, "rep", core)
        d1c = lax.ppermute(d1, "rep", core)
        d2c = lax.ppermute(d2, "rep", core)
    incoming = scan(state, total, "tm", False)
    (local,) = call(inner_kernel, [(wide, F32)], x, b, c, s, rate_log, step_bias, skip_gain, name="inner")
    if near:
        weight, ng = call(
            weight_kernel, [(full, BF), (wide, BF)], place, g, out_weight, wc, wx, wxc, wy, wyc, d1, d2, d1c, d2c,
            smem=(0,), name="normed_grad",
        )
    else:
        weight = lax.all_gather(out_weight, ("tok", "rep"), axis=0, tiled=True)
        (ng,) = call(grad_kernel, [(wide, BF)], g, weight, name="normed_grad")
    normed, dy, carry, zg, row_sums, gains, skips = call(
        norm_kernel,
        [(wide, BF), (wide, BF), ((state_size, width), BF), (wide, BF), ((heads, length), F32), ((1, width), F32), ((heads, 1), F32)],
        local, incoming, c, z, x, s, rate_log, step_bias, skip_gain, norm_gain, ng, name="norm",
    )
    later = scan(carry, total, "tm", True)
    if near:
        block = (4, rows, model)
        mine, other = call(outer_kernel, [(block, BF), (block, BF)], place, normed, g, smem=(0,), name="outer")
        got = lax.ppermute(other, "rep", core)
        cut = (2, rows, half)
        a_keep, a_send, b_keep, b_send = call(
            add_pair_kernel, [(cut, F32), (cut, BF), (cut, F32), (cut, BF)], mine, got, name="add_pair"
        )
        ga = lax.ppermute(a_send, "rep", side)
        gb = lax.ppermute(b_send, "tok", front)
        cut = (rows, half)
        a_keep, a_send, b_keep, b_send = call(
            add_second_kernel, [(cut, F32), (cut, BF), (cut, F32), (cut, BF)], a_keep, ga, b_keep, gb, name="add_second"
        )
        ga = lax.ppermute(a_send, "tok", front)
        gb = lax.ppermute(b_send, "rep", side)
        part = (rows // n_tm, model)
        keep, *sends = call(
            add_third_kernel, [(part, F32)] + [(part, BF)] * (n_tm - 1), place, a_keep, ga, b_keep, gb,
            smem=(0,), name="add_third", scratch=[pltpu.VMEM((rows, model), F32)],
        )
        ahead = [[(i, (i + k) % n_tm) for i in range(n_tm)] for k in range(1, n_tm)]
        gots = [lax.ppermute(v, "tm", pairs) for v, pairs in zip(sends, ahead)]
        (quarter,) = call(add_quarter_kernel, [(part, BF)], keep, *gots, name="add_quarter")
        pieces = [quarter] + [lax.ppermute(quarter, "tm", pairs) for pairs in ahead]
        (weight_grad,) = call(join_kernel, [((rows, model), BF)], place, *pieces, smem=(0,), name="join")
    else:
        (outer,) = call(outer_full_kernel, [(full, F32)], normed, g, name="outer")
        share = lax.psum_scatter(outer, ("tok", "rep"), scatter_dimension=0, tiled=True)
        weight_grad = lax.psum(share, "tm").astype(BF)
    mixed, c_grad, xg, bg, col_sums = call(
        back_kernel,
        [(wide, BF), ((length, state_size), BF), (wide, F32), ((length, state_size), BF), ((heads, length), F32)],
        x, b, c, s, rate_log, step_bias, skip_gain, dy, incoming, normed, weight,
        name="back", scratch=[pltpu.VMEM(wide, F32)],
    )
    devices = n_tm * n_tok * n_rep
    copies = devices if near else 1
    x_grad, b_grad, step_grad, sums = call(
        last_kernel,
        [(wide, BF), ((length, state_size), BF), ((heads, length), F32), ((copies, width + 128), F32)],
        x, b, s, rate_log, step_bias, later, incoming, xg, bg, row_sums, col_sums, gains, skips, name="last",
    )
    everywhere = ("tm", "tok", "rep")
    if near:
        sums = lax.all_to_all(sums, everywhere, 0, 0, tiled=True)
        (sums,) = call(sums_kernel, [((1, width + 128), F32)], sums, name="sums")
    else:
        sums = lax.psum(sums, everywhere)
    sums = sums[0]
    gain_grad = sums[:width]
    rate_grad = sums[width : width + heads]
    bias_grad = sums[width + heads : width + 2 * heads]
    skip_grad = sums[width + 2 * heads : width + 3 * heads]
    return (
        mixed[None], x_grad[None], zg[None], b_grad[None], c_grad[None], step_grad[None],
        rate_grad, bias_grad, skip_grad, gain_grad, weight_grad,
    )


def solution(mesh):
    tokens = P(("tok", "rep"), "tm", None)
    frames = P(("tok", "rep"), None, "tm")
    weight = P(("tok", "rep"), None)
    return jax.shard_map(
        shards,
        mesh=mesh,
        in_specs=(tokens, tokens, tokens, tokens, frames, P(), P(), P(), P(), weight, tokens),
        out_specs=(tokens, tokens, tokens, tokens, tokens, frames, P(), P(), P(), P(), weight),
        check_vma=False,
    )
```

time: 260 us -> 123 us (0.47)
  blocking collectives: 81.8 us -> 0 us
  matrix products: 42.3 us -> 0 us
  Pallas kernels: 0 us -> 40 us
  starting transfers between devices: 0.34 us -> 38.5 us
  waiting for transfers between devices: 61.7 us -> 24.9 us
  other arithmetic: 31.2 us -> 8.21 us
  local copies, waits for them, and re-layouts: 26.5 us -> 9.4 us
  between operations: 14.2 us -> 0.99 us
    psum x2 -> x0, blocking collectives: 69.1 us -> none  [the longest x1 39.7 us: shards(): lax.psum((grads_out[5] + grads_parts[3], grads_out[6] + grads_parts[4], g...]
    all_gather x3 -> x0, waiting for transfers between devices: 61 us -> none  [the longest x2 49.3 us: carried_in(): everything = jax.tree.map(lambda part: lax.all_gather(part, axis), value)]
    dot_general x15 -> x0, matrix products: 42.3 us -> none  [the longest x3 18.6 us: block_output(): jnp.einsum('shqk,skhp->sqhp', mixing, x_heads, precision=lax.Precision.HI...]
    pallas_call x0 -> x13, Pallas kernels: none -> 40 us  [call(): pl.pallas_call(kernel, out_shape=[jax.ShapeDtypeStruct(s, t) for s, t in...]
    ppermute x0 -> x26, starting transfers between devices: none -> 30.2 us  [the longest x6 9.13 us: chain(): incoming = incoming + lax.ppermute(send, axis, [(at, to)])]
    ppermute x0 -> x26, waiting for transfers between devices: none -> 24.9 us  [the longest x6 14.6 us: chain(): incoming = incoming + lax.ppermute(send, axis, [(at, to)])]
    mul x18 -> x0, local copies, waits for them, and re-layouts: 14.1 us -> none  [the longest x4 4.25 us: block_parts(): weighted = x_heads * tailing.transpose(0, 2, 1)[..., None]]
    all_gather x1 -> x0, blocking collectives: 12.7 us -> none  [carried_in(): everything = jax.tree.map(lambda part: lax.all_gather(part, axis), value)]
  transfers between devices with their start and end apart: 4 -> 27, of which waited for: 3 -> 10; matrix products, arithmetic and copies ran while one was open for 29% -> 8% of each run, Pallas kernels for 0% -> 24%
where the time goes in v1:
time: 123 us; the launch traced here: 122 us
  Pallas kernels  40 us (33%)
  starting transfers between devices  38.5 us (31%)
  waiting for transfers between devices  24.9 us (20%)
  local copies, waits for them, and re-layouts  9.4 us (8%)
  other arithmetic  8.21 us (7%)
    pallas_call x13, Pallas kernels, call(): pl.pallas_call(kernel, out_shape=[jax.ShapeDtypeStruct(s, t) for s, t in...  40 us
    ppermute x6, waiting for transfers between devices, chain(): incoming = incoming + lax.ppermute(send, axis, [(at, to)])  14.6 us
    ppermute x6, starting transfers between devices, chain(): incoming = incoming + lax.ppermute(send, axis, [(at, to)])  9.13 us
    all_to_all x1, starting transfers between devices, shards(): sums = lax.all_to_all(sums, everywhere, 0, 0, tiled=True)  8.24 us
    convert_element_type x6, other arithmetic, chain(): send = (incoming.astype(F32) * total + value.astype(F32)).astype(BF)  5.39 us
    ppermute x3, starting transfers between devices, shards(): gots = [lax.ppermute(v, 'tm', pairs) for v, pairs in zip(sends, ahead)]  5.26 us
    unnamed x45, local copies, waits for them, and re-layouts  5.1 us
    ppermute x3, starting transfers between devices, shards(): pieces = [quarter] + [lax.ppermute(quarter, 'tm', pairs) for pairs in ahead]  3.27 us
  transfers between devices with their start and end apart: 27, of which 10 were waited for; matrix products, arithmetic and copies ran while one was open for 8% of the time, Pallas kernels for 24%

profile of v1, /device:TPU:0, one launch (start us, length us, event | category | flops | bytes accessed | tf_op | source)
XLA Modules:
  0.0 122.0 jit_solution(9679343117663408922)
XLA Ops:
  0.6 2.6 %state.1 = (bf16[128,1024]{1,0:T(8,128)(2,1)}, f32[1,1024]{1,0:T(1,128)}) custom-call(bf16[256,1024]{1,0:T(8,128)(2,1)} %bitcast.26, bf16[256,128]{1,0:T(8,128)(2,1)} %bitcast.33, f32[16,256]{1,0:T(8,128)} %bitcast.42, f32[16]{0:T(128)} %rate_ref.9, f32[16]{0:T(128)} %bias_ref.9), custom_call_target="tpu_custom_call" | custom-call | tf_op jit(solution)/shard_map/state/pallas_call | solution.py:96
  3.2 0.7 broadcast_multiply_fusion
  3.9 1.0 fusion
  4.9 4.9 %collective-permute-start = (bf16[128,1024]{1,0:T(8,128)(2,1)S(1)}, bf16[128,1024]{1,0:T(8,128)(2,1)S(1)}, u32[]{:S(2)}, u32[]{:S(2)}) collective-permute-start(bf16[128,1024]{1,0:T(8,128)(2,1)S(1)} %fusion), channel_id=1, source_target_pairs={{0,8},{1,9},{2,10},{3,11},{4,12},{5,13},{6,14},{7,15}} | collective-permute-start | bytes 786440 | tf_op jit(solution)/shard_map/ppermute | solution.py:399
  9.9 1.6 %collective-permute-start.4 = (bf16[128,1024]{1,0:T(8,128)(2,1)}, bf16[128,1024]{1,0:T(8,128)(2,1)S(1)}, u32[]{:S(2)}, u32[]{:S(2)}) collective-permute-start(bf16[128,1024]{1,0:T(8,128)(2,1)} %refs_0_.1), channel_id=1, source_target_pairs={{0,2},{1,3},{2,0},{3,1},{4,6},{5,7},{6,4},{7,5},{8,10},{9,11},{10,... | collective-permute-start | bytes 786440 | tf_op jit(solution)/shard_map/ppermute | solution.py:443
  11.4 1.5 %collective-permute-start.6 = (bf16[128,1024]{1,0:T(8,128)(2,1)}, bf16[128,1024]{1,0:T(8,128)(2,1)S(1)}, u32[]{:S(2)}, u32[]{:S(2)}) collective-permute-start(bf16[128,1024]{1,0:T(8,128)(2,1)} %refs_0_.1), channel_id=1, source_target_pairs={{0,4},{4,0},{1,5},{5,1},{2,6},{6,2},{3,7},{7,3},{8,12},{12,8},{9,1... | collective-permute-start | bytes 786440 | tf_op jit(solution)/shard_map/ppermute | solution.py:444
  13.0 2.5 %collective-permute-done = bf16[128,1024]{1,0:T(8,128)(2,1)S(1)} collective-permute-done((bf16[128,1024]{1,0:T(8,128)(2,1)S(1)}, bf16[128,1024]{1,0:T(8,128)(2,1)S(1)}, u32[]{:S(2)}, u32[]{:S(2)}) %collective-permute-start) | collective-permute-done | bytes 262176 | tf_op jit(solution)/shard_map/ppermute | solution.py:399
  15.4 1.0 fusion.1
  16.5 0.7 collective-permute-start.1
  17.2 0.7 collective-permute-done.4.refs_2_
  18.0 1.6 %collective-permute-start.8 = (bf16[128,512]{1,0:T(8,128)(2,1)S(1)}, bf16[128,512]{1,0:T(8,128)(2,1)S(1)}, u32[]{:S(2)}, u32[]{:S(2)}) collective-permute-start(bf16[128,512]{1,0:T(8,128)(2,1)S(1)} %slice.40), channel_id=1, source_target_pairs={{0,4},{4,0},{1,5},{5,1},{2,6},{6,2},{3,7},{7,3},{8,12},{12,8},{9,1... | collective-permute-start | bytes 393224 | tf_op jit(solution)/shard_map/ppermute | solution.py:446
  19.6 1.6 %collective-permute-start.9 = (bf16[128,512]{1,0:T(8,128)(2,1)S(1)}, bf16[128,512]{1,0:T(8,128)(2,1)S(1)}, u32[]{:S(2)}, u32[]{:S(2)}) collective-permute-start(bf16[128,512]{1,0:T(8,128)(2,1)S(1)} %slice.41), channel_id=1, source_target_pairs={{0,2},{1,3},{2,0},{3,1},{4,6},{5,7},{6,4},{7,5},{8,10},{9,11},{10,... | collective-permute-start | bytes 393224 | tf_op jit(solution)/shard_map/ppermute | solution.py:447
  21.1 0.5 collective-permute-start.7
  21.6 1.1 fusion.2
  22.8 0.7 collective-permute-start.2
  23.5 1.0 collective-permute-done.9.refs_7_
  24.6 3.6 %inner.1.local_ref = f32[256,1024]{1,0:T(8,128)} custom-call(bf16[256,1024]{1,0:T(8,128)(2,1)} %bitcast.27, bf16[256,128]{1,0:T(8,128)(2,1)} %bitcast.34, bf16[256,128]{1,0:T(8,128)(2,1)} %bitcast.37, f32[16,256]{1,0:T(8,128)} %bitcast.43, f32[16]{0:T(128)} %rate_ref.9, f32[16]{0:T(128)} %bias_ref.9, f32[16]{0:T(128)} %skip_ref.5), custom_call_target="tpu_custom_call" | custom-call | tf_op jit(solution)/shard_map/inner/pallas_call | solution.py:96
  28.2 0.6 pad_add_fusion.idx_ref.pos_ref
  28.9 0.5 copy-done.11
  29.7 3.3 %normed_grad.1 = (bf16[1024,1024]{1,0:T(8,128)(2,1)}, bf16[256,1024]{1,0:T(8,128)(2,1)}) custom-call(s32[2]{0:T(128)} %pad_add_fusion.idx_ref.pos_ref, bf16[256,1024]{1,0:T(8,128)(2,1)} %bitcast.31, bf16[128,1024]{1,0:T(8,128)(2,1)} %refs_0_.1, bf16[128,1024]{1,0:T(8,128)(2,1)} %copy-done.6, bf16[128,1024]{1,0:T(8,128)(2,1)} %copy-done.2, ...), custom_call_target="tpu_custom_call" | custom-call | tf_op jit(solution)/shard_map/normed_grad/pallas_call | solution.py:96
  33.0 0.8 add.37.inc_ref
  33.8 5.1 %norm.1 = (bf16[256,1024]{1,0:T(8,128)(2,1)}, bf16[256,1024]{1,0:T(8,128)(2,1)}, bf16[128,1024]{1,0:T(8,128)(2,1)}, bf16[256,1024]{1,0:T(8,128)(2,1)}, f32[16,25...) custom-call(f32[256,1024]{1,0:T(8,128)} %inner.1.local_ref, bf16[128,1024]{1,0:T(8,128)(2,1)} %add.37.inc_ref, ...), custom_call_target="tpu_custom_call" | custom-call | tf_op jit(solution)/shard_map/norm/pallas_call | solution.py:96
  38.8 1.1 fusion.3
  39.9 0.7 collective-permute-start.12
  40.6 3.3 %outer.1 = (bf16[4,128,1024]{2,1,0:T(8,128)(2,1)}, bf16[4,128,1024]{2,1,0:T(8,128)(2,1)}) custom-call(s32[2]{0:T(128)} %pad_add_fusion.idx_ref.pos_ref, bf16[256,1024]{1,0:T(8,128)(2,1)} %get-tuple-element.49.normed_ref, bf16[256,1024]{1,0:T(8,128)(2,1)} %bitcast.32), custom_call_target="tpu_custom_call" | custom-call | tf_op jit(solution)/shard_map/outer/pallas_call | solution.py:96
  43.9 0.5 collective-permute-start.15
  44.3 1.0 fusion.4
  45.4 0.7 collective-permute-start.13
  46.3 1.5 %collective-permute-start.14 = (bf16[128,1024]{1,0:T(8,128)(2,1)S(1)}, bf16[128,1024]{1,0:T(8,128)(2,1)S(1)}, u32[]{:S(2)}, u32[]{:S(2)}) collective-permute-start(bf16[128,1024]{1,0:T(8,128)(2,1)S(1)} %get-tuple-element.79), channel_id=1, source_target_pairs={{8,0},{9,1},{10,2},{11,3},{12,4},{13,5},{14,6},{15,7}} | collective-permute-start | bytes 786440 | tf_op jit(solution)/shard_map/ppermute | solution.py:399
  47.8 1.0 copy-done.1
  48.7 2.8 %add_pair.1 = (f32[2,128,512]{2,1,0:T(8,128)}, bf16[2,128,512]{2,1,0:T(8,128)(2,1)}, f32[2,128,512]{2,1,0:T(8,128)}, bf16[2,128,512]{2,1,0:T(8,128)(2,1)}) custom-call(bf16[4,128,1024]{2,1,0:T(8,128)(2,1)} %get-tuple-element.65.mine_ref, bf16[4,128,1024]{2,1,0:T(8,128)(2,1)} %copy-done.1), custom_call_target="tpu_custom_call" | custom-call | tf_op jit(solution)/shard_map/add_pair/pallas_call | solution.py:96
  51.5 1.5 %collective-permute-start.16 = (bf16[2,128,512]{2,1,0:T(8,128)(2,1)}, bf16[2,128,512]{2,1,0:T(8,128)(2,1)S(1)}, u32[]{:S(2)}, u32[]{:S(2)}) collective-permute-start(bf16[2,128,512]{2,1,0:T(8,128)(2,1)} %get-tuple-element.68), channel_id=1, source_target_pairs={{0,2},{1,3},{2,0},{3,1},{4,6},{5,7},{6,4},{7,5},{8,10},{9,11},{10,... | collective-permute-start | bytes 786440 | tf_op jit(solution)/shard_map/ppermute | solution.py:476
  53.0 0.5 collective-permute-start.17
  53.5 6.4 %back.1 = (bf16[256,1024]{1,0:T(8,128)(2,1)}, bf16[256,128]{1,0:T(8,128)(2,1)}, f32[256,1024]{1,0:T(8,128)}, bf16[256,128]{1,0:T(8,128)(2,1)}, f32[16,256]{1,0:T(8,128)}) custom-call(bf16[256,1024]{1,0:T(8,128)(2,1)} %bitcast.29, bf16[256,128]{1,0:T(8,128)(2,1)} %bitcast.35, bf16[256,128]{1,0:T(8,128)(2,1)} %bitcast.39, f32[16,256]{1,0:T(8,128)} %bitcast.45, ...), custom_call_target="tpu_custom_call" | custom-call | tf_op jit(solution)/shard_map/back/pallas_call | solution.py:96
  59.9 12.1 %collective-permute-done.14 = bf16[128,1024]{1,0:T(8,128)(2,1)S(1)} collective-permute-done((bf16[128,1024]{1,0:T(8,128)(2,1)S(1)}, bf16[128,1024]{1,0:T(8,128)(2,1)S(1)}, u32[]{:S(2)}, u32[]{:S(2)}) %collective-permute-start.14) | collective-permute-done | bytes 262176 | tf_op jit(solution)/shard_map/ppermute | solution.py:399
  72.0 0.8 add.43.later_ref
  72.8 3.9 %last.1 = (bf16[256,1024]{1,0:T(8,128)(2,1)}, bf16[256,128]{1,0:T(8,128)(2,1)}, f32[16,256]{1,0:T(8,128)}, f32[32,1152]{1,0:T(8,128)}) custom-call(bf16[256,1024]{1,0:T(8,128)(2,1)} %bitcast.30, bf16[256,128]{1,0:T(8,128)(2,1)} %bitcast.36, f32[16,256]{1,0:T(8,128)} %bitcast.46, f32[16]{0:T(128)} %rate_ref.9, f32[16]{0:T(128)} %bias_ref.9, ...), custom_call_target="tpu_custom_call" | custom-call | tf_op jit(solution)/shard_map/last/pallas_call | solution.py:96
  76.7 1.7 %copy.22 = f32[32,1,1152]{2,1,0:T(1,128)} copy(f32[32,1,1152]{2,0,1:T(8,128)} %bitcast.47) | data formatting | bytes 294912 | tf_op jit(solution)/shard_map/all_to_all | solution.py:513
  78.4 8.2 %all-to-all-start = ((f32[32,1,1152]{2,1,0:T(1,128)}), f32[32,1,1152]{2,1,0:T(1,128)S(1)}, u32[]{:S(2)}, u32[]{:S(2)}) async-start(f32[32,1,1152]{2,1,0:T(1,128)} %copy.22), calls=%async_computation | async-start | bytes 294912 | tf_op jit(solution)/shard_map/all_to_all | solution.py:513
  86.7 0.7 copy-done.4
  87.5 2.3 %add_second.1 = (f32[128,512]{1,0:T(8,128)}, bf16[128,512]{1,0:T(8,128)(2,1)}, f32[128,512]{1,0:T(8,128)}, bf16[128,512]{1,0:T(8,128)(2,1)}) custom-call(f32[2,128,512]{2,1,0:T(8,128)} %get-tuple-element.67.a_ref, bf16[2,128,512]{2,1,0:T(8,128)(2,1)} %copy-done.4, f32[2,128,512]{2,1,0:T(8,128)} %get-tuple-element.69.b_ref, bf16[2,128,512]{2,1,0:T(8,128)(2,1)} %copy-done.5), custom_call_target="tpu_custom_call" | custom-call | tf_op jit(solution)/shard_map/add_second/pallas_call | solution.py:96
  89.8 1.8 %collective-permute-start.18 = (bf16[128,512]{1,0:T(8,128)(2,1)}, bf16[128,512]{1,0:T(8,128)(2,1)S(1)}, u32[]{:S(2)}, u32[]{:S(2)}) collective-permute-start(bf16[128,512]{1,0:T(8,128)(2,1)} %get-tuple-element.72), channel_id=1, source_target_pairs={{0,4},{4,0},{1,5},{5,1},{2,6},{6,2},{3,7},{7,3},{8,12},{12,8},{9,1... | collective-permute-start | bytes 393224 | tf_op jit(solution)/shard_map/ppermute | solution.py:482
  91.5 1.5 %collective-permute-start.19 = (bf16[128,512]{1,0:T(8,128)(2,1)}, bf16[128,512]{1,0:T(8,128)(2,1)S(1)}, u32[]{:S(2)}, u32[]{:S(2)}) collective-permute-start(bf16[128,512]{1,0:T(8,128)(2,1)} %get-tuple-element.74), channel_id=1, source_target_pairs={{0,2},{1,3},{2,0},{3,1},{4,6},{5,7},{6,4},{7,5},{8,10},{9,11},{10,... | collective-permute-start | bytes 393224 | tf_op jit(solution)/shard_map/ppermute | solution.py:483
  93.0 3.1 %collective-permute-done.18.ga_ref = bf16[128,512]{1,0:T(8,128)(2,1)S(1)} collective-permute-done((bf16[128,512]{1,0:T(8,128)(2,1)}, bf16[128,512]{1,0:T(8,128)(2,1)S(1)}, u32[]{:S(2)}, u32[]{:S(2)}) %collective-permute-start.18) | collective-permute-done | bytes 131104 | tf_op jit(solution)/shard_map/ppermute | solution.py:482
  96.1 0.9 collective-permute-done.19.gb_ref
  97.1 0.6 copy-done.14
  97.7 1.9 %add_third.1 = (f32[32,1024]{1,0:T(8,128)}, bf16[32,1024]{1,0:T(8,128)(2,1)}, bf16[32,1024]{1,0:T(8,128)(2,1)}, bf16[32,1024]{1,0:T(8,128)(2,1)}) custom-call(s32[2]{0:T(128)} %pad_add_fusion.idx_ref.pos_ref, f32[128,512]{1,0:T(8,128)} %get-tuple-element.71.a_ref, bf16[128,512]{1,0:T(8,128)(2,1)} %copy-done.13, f32[128,512]{1,0:T(8,128)} %get-tuple-element.73.b_ref, ...), custom_call_target="tpu_custom_call" | custom-call | tf_op jit(solution)/shard_map/add_third/pallas_call | solution.py:96
  99.7 1.4 %collective-permute-start.20 = (bf16[32,1024]{1,0:T(8,128)(2,1)}, bf16[32,1024]{1,0:T(8,128)(2,1)S(1)}, u32[]{:S(2)}, u32[]{:S(2)}) collective-permute-start(bf16[32,1024]{1,0:T(8,128)(2,1)} %get-tuple-element.76), channel_id=1, source_target_pairs={{0,8},{8,16},{16,24},{24,0},{1,9},{9,17},{17,25},{25,1},{2,10},{10... | collective-permute-start | bytes 196616 | tf_op jit(solution)/shard_map/ppermute | solution.py:490
  101.1 2.4 %collective-permute-start.21 = (bf16[32,1024]{1,0:T(8,128)(2,1)}, bf16[32,1024]{1,0:T(8,128)(2,1)S(1)}, u32[]{:S(2)}, u32[]{:S(2)}) collective-permute-start(bf16[32,1024]{1,0:T(8,128)(2,1)} %get-tuple-element.77), channel_id=1, source_target_pairs={{0,16},{8,24},{16,0},{24,8},{1,17},{9,25},{17,1},{25,9},{2,18},{10... | collective-permute-start | bytes 196616 | tf_op jit(solution)/shard_map/ppermute | solution.py:490
  103.5 1.4 %collective-permute-start.22 = (bf16[32,1024]{1,0:T(8,128)(2,1)}, bf16[32,1024]{1,0:T(8,128)(2,1)S(1)}, u32[]{:S(2)}, u32[]{:S(2)}) collective-permute-start(bf16[32,1024]{1,0:T(8,128)(2,1)} %get-tuple-element.78), channel_id=1, source_target_pairs={{0,24},{8,0},{16,8},{24,16},{1,25},{9,1},{17,9},{25,17},{2,26},{10... | collective-permute-start | bytes 196616 | tf_op jit(solution)/shard_map/ppermute | solution.py:490
  104.9 0.7 copy.25
  105.6 1.5 %sums.1 = f32[1,1152]{1,0:T(1,128)} custom-call(f32[32,1152]{1,0:T(8,128)} %bitcast.40), custom_call_target="tpu_custom_call" | custom-call | tf_op jit(solution)/shard_map/sums/pallas_call | solution.py:96
  107.1 1.2 collective-permute-done.21.refs_2_
  108.5 0.5 copy-done.20
  109.0 0.2 copy-done.21
  109.1 1.6 %add_quarter.1.refs_0_ = bf16[32,1024]{1,0:T(8,128)(2,1)} custom-call(f32[32,1024]{1,0:T(8,128)} %get-tuple-element.75.refs_0_, bf16[32,1024]{1,0:T(8,128)(2,1)} %copy-done.19, bf16[32,1024]{1,0:T(8,128)(2,1)} %copy-done.20, bf16[32,1024]{1,0:T(8,128)(2,1)} %copy-done.21), custom_call_target="tpu_custom_call" | custom-call | tf_op jit(solution)/shard_map/add_quarter/pallas_call | solution.py:96
  110.7 2.7 %collective-permute-start.25 = (bf16[32,1024]{1,0:T(8,128)(2,1)}, bf16[32,1024]{1,0:T(8,128)(2,1)S(1)}, u32[]{:S(2)}, u32[]{:S(2)}) collective-permute-start(bf16[32,1024]{1,0:T(8,128)(2,1)} %add_quarter.1.refs_0_), channel_id=1, source_target_pairs={{0,24},{8,0},{16,8},{24,16},{1,25},{9,1},{17,9},{25,17},{2,26},{10... | collective-permute-start | bytes 196616 | tf_op jit(solution)/shard_map/ppermute | solution.py:492
  113.4 0.6 collective-permute-start.23
  114.0 1.3 %slice_bitcast_fusion = (f32[16]{0:T(128)}, f32[16]{0:T(128)}, f32[16]{0:T(128)}) fusion(f32[1,1152]{1,0:T(1,128)} %sums.1), kind=kLoop, calls=%fused_computation.14 | loop fusion | bytes 384 | tf_op jit(solution)/shard_map/slice | solution.py:521
  115.3 1.3 %slice.45 = f32[1,1024]{1,0:T(1,128)} slice(f32[1,1152]{1,0:T(1,128)} %sums.1), slice={[0:1], [0:1024]} | slice | bytes 8192 | tf_op jit(solution)/shard_map/slice | solution.py:518
  116.6 2.2 %collective-permute-done.24.refs_2_ = bf16[32,1024]{1,0:T(8,128)(2,1)S(1)} collective-permute-done((bf16[32,1024]{1,0:T(8,128)(2,1)}, bf16[32,1024]{1,0:T(8,128)(2,1)S(1)}, u32[]{:S(2)}, u32[]{:S(2)}) %collective-permute-start.24) | collective-permute-done | bytes 65568 | tf_op jit(solution)/shard_map/ppermute | solution.py:492
  118.8 0.9 collective-permute-done.23.refs_1_
  119.7 0.6 copy-done.18
  120.3 1.7 %join.1 = bf16[128,1024]{1,0:T(8,128)(2,1)} custom-call(s32[2]{0:T(128)} %pad_add_fusion.idx_ref.pos_ref, bf16[32,1024]{1,0:T(8,128)(2,1)} %add_quarter.1.refs_0_, bf16[32,1024]{1,0:T(8,128)(2,1)} %copy-done.18, bf16[32,1024]{1,0:T(8,128)(2,1)} %copy-done.17, bf16[32,1024]{1,0:T(8,128)(2,1)} %copy-done.16), custom_call_target="tpu_custom_call" | custom-call | tf_op jit(solution)/shard_map/join/pallas_call | solution.py:96
  (63 shorter events, 0.9 us)
Async XLA Ops:
  4.9 10.5 %collective-permute-start = (bf16[128,1024]{1,0:T(8,128)(2,1)S(1)}, bf16[128,1024]{1,0:T(8,128)(2,1)S(1)}, u32[]{:S(2)}, u32[]{:S(2)}) collective-permute-start(bf16[128,1024]{1,0:T(8,128)(2,1)S(1)} %fusion), channel_id=1, source_target_pairs={{0,8},{1,9},{2,10},{3,11},{4,12},{5,13},{6,14},{7,15}} | collective-permute-start | bytes 786440 | tf_op jit(solution)/shard_map/ppermute | solution.py:399
  9.9 8.0 %collective-permute-start.4 = (bf16[128,1024]{1,0:T(8,128)(2,1)}, bf16[128,1024]{1,0:T(8,128)(2,1)S(1)}, u32[]{:S(2)}, u32[]{:S(2)}) collective-permute-start(bf16[128,1024]{1,0:T(8,128)(2,1)} %refs_0_.1), channel_id=1, source_target_pairs={{0,2},{1,3},{2,0},{3,1},{4,6},{5,7},{6,4},{7,5},{8,10},{9,11},{10,... | collective-permute-start | bytes 786440 | tf_op jit(solution)/shard_map/ppermute | solution.py:443
  11.4 8.1 %collective-permute-start.6 = (bf16[128,1024]{1,0:T(8,128)(2,1)}, bf16[128,1024]{1,0:T(8,128)(2,1)S(1)}, u32[]{:S(2)}, u32[]{:S(2)}) collective-permute-start(bf16[128,1024]{1,0:T(8,128)(2,1)} %refs_0_.1), channel_id=1, source_target_pairs={{0,4},{4,0},{1,5},{5,1},{2,6},{6,2},{3,7},{7,3},{8,12},{12,8},{9,1... | collective-permute-start | bytes 786440 | tf_op jit(solution)/shard_map/ppermute | solution.py:444
  16.5 4.7 %collective-permute-start.1 = (bf16[128,1024]{1,0:T(8,128)(2,1)S(1)}, bf16[128,1024]{1,0:T(8,128)(2,1)S(1)}, u32[]{:S(2)}, u32[]{:S(2)}) collective-permute-start(bf16[128,1024]{1,0:T(8,128)(2,1)S(1)} %fusion.1), channel_id=1, source_target_pairs={{8,16},{9,17},{10,18},{11,19},{12,20},{13,21},{14,22},{15,23}} | collective-permute-start | bytes 786440 | tf_op jit(solution)/shard_map/ppermute | solution.py:399
  17.2 5.6 %collective-permute-start.3 = (bf16[128,1024]{1,0:T(8,128)(2,1)}, bf16[128,1024]{1,0:T(8,128)(2,1)S(1)}, u32[]{:S(2)}, u32[]{:S(2)}) collective-permute-start(bf16[128,1024]{1,0:T(8,128)(2,1)} %refs_0_.1), channel_id=1, source_target_pairs={{0,1},{1,0},{2,3},{3,2},{4,5},{5,4},{6,7},{7,6},{8,9},{9,8},{10,11... | collective-permute-start | bytes 786440 | tf_op jit(solution)/shard_map/ppermute | solution.py:445
  17.9 10.9 %copy-start.2 = (bf16[128,1024]{1,0:T(8,128)(2,1)}, bf16[128,1024]{1,0:T(8,128)(2,1)S(1)}, u32[]{:S(2)}) copy-start(bf16[128,1024]{1,0:T(8,128)(2,1)S(1)} %collective-permute-done.4.refs_2_) | copy-start | bytes 786436
  18.0 5.5 %collective-permute-start.8 = (bf16[128,512]{1,0:T(8,128)(2,1)S(1)}, bf16[128,512]{1,0:T(8,128)(2,1)S(1)}, u32[]{:S(2)}, u32[]{:S(2)}) collective-permute-start(bf16[128,512]{1,0:T(8,128)(2,1)S(1)} %slice.40), channel_id=1, source_target_pairs={{0,4},{4,0},{1,5},{5,1},{2,6},{6,2},{3,7},{7,3},{8,12},{12,8},{9,1... | collective-permute-start | bytes 393224 | tf_op jit(solution)/shard_map/ppermute | solution.py:446
  19.5 9.3 %copy-start.3 = (bf16[128,1024]{1,0:T(8,128)(2,1)}, bf16[128,1024]{1,0:T(8,128)(2,1)S(1)}, u32[]{:S(2)}) copy-start(bf16[128,1024]{1,0:T(8,128)(2,1)S(1)} %collective-permute-done.6.refs_4_) | copy-start | bytes 786436
  19.6 5.0 %collective-permute-start.9 = (bf16[128,512]{1,0:T(8,128)(2,1)S(1)}, bf16[128,512]{1,0:T(8,128)(2,1)S(1)}, u32[]{:S(2)}, u32[]{:S(2)}) collective-permute-start(bf16[128,512]{1,0:T(8,128)(2,1)S(1)} %slice.41), channel_id=1, source_target_pairs={{0,2},{1,3},{2,0},{3,1},{4,6},{5,7},{6,4},{7,5},{8,10},{9,11},{10,... | collective-permute-start | bytes 393224 | tf_op jit(solution)/shard_map/ppermute | solution.py:447
  21.1 7.7 %collective-permute-start.5 = (bf16[128,1024]{1,0:T(8,128)(2,1)S(1)}, bf16[128,1024]{1,0:T(8,128)(2,1)S(1)}, u32[]{:S(2)}, u32[]{:S(2)}) collective-permute-start(bf16[128,1024]{1,0:T(8,128)(2,1)S(1)} %collective-permute-done.4.refs_2_), channel_id=1, source_target_pairs={{0,1},{1,0},{2,3},{3,2},{4,5},{5,4},{6,7},{7,6},{8,9},{9,8},{10,11... | collective-permute-start | bytes 786440 | tf_op jit(solution)/shard_map/ppermute | solution.py:448
  21.1 7.7 %collective-permute-start.7 = (bf16[128,1024]{1,0:T(8,128)(2,1)S(1)}, bf16[128,1024]{1,0:T(8,128)(2,1)S(1)}, u32[]{:S(2)}, u32[]{:S(2)}) collective-permute-start(bf16[128,1024]{1,0:T(8,128)(2,1)S(1)} %collective-permute-done.6.refs_4_), channel_id=1, source_target_pairs={{0,1},{1,0},{2,3},{3,2},{4,5},{5,4},{6,7},{7,6},{8,9},{9,8},{10,11... | collective-permute-start | bytes 786440 | tf_op jit(solution)/shard_map/ppermute | solution.py:449
  22.7 6.1 %copy-start.6 = (bf16[128,1024]{1,0:T(8,128)(2,1)}, bf16[128,1024]{1,0:T(8,128)(2,1)S(1)}, u32[]{:S(2)}) copy-start(bf16[128,1024]{1,0:T(8,128)(2,1)S(1)} %collective-permute-done.3.refs_1_) | copy-start | bytes 786436
  22.8 10.2 %collective-permute-start.2 = (bf16[128,1024]{1,0:T(8,128)(2,1)S(1)}, bf16[128,1024]{1,0:T(8,128)(2,1)S(1)}, u32[]{:S(2)}, u32[]{:S(2)}) collective-permute-start(bf16[128,1024]{1,0:T(8,128)(2,1)S(1)} %get-tuple-element.81), channel_id=1, source_target_pairs={{16,24},{17,25},{18,26},{19,27},{20,28},{21,29},{22,30},{23,31}} | collective-permute-start | bytes 786440 | tf_op jit(solution)/shard_map/ppermute | solution.py:399
  23.5 5.4 %copy-start.9 = (bf16[128,512]{1,0:T(8,128)(2,1)}, bf16[128,512]{1,0:T(8,128)(2,1)S(1)}, u32[]{:S(2)}) copy-start(bf16[128,512]{1,0:T(8,128)(2,1)S(1)} %collective-permute-done.8.refs_6_) | copy-start | bytes 393220
  23.5 5.3 %collective-permute-start.10 = (bf16[128,512]{1,0:T(8,128)(2,1)S(1)}, bf16[128,512]{1,0:T(8,128)(2,1)S(1)}, u32[]{:S(2)}, u32[]{:S(2)}) collective-permute-start(bf16[128,512]{1,0:T(8,128)(2,1)S(1)} %collective-permute-done.8.refs_6_), channel_id=1, source_target_pairs={{0,1},{1,0},{2,3},{3,2},{4,5},{5,4},{6,7},{7,6},{8,9},{9,8},{10,11... | collective-permute-start | bytes 393224 | tf_op jit(solution)/shard_map/ppermute | solution.py:450
  24.6 4.3 %copy-start.10 = (bf16[128,512]{1,0:T(8,128)(2,1)}, bf16[128,512]{1,0:T(8,128)(2,1)S(1)}, u32[]{:S(2)}) copy-start(bf16[128,512]{1,0:T(8,128)(2,1)S(1)} %collective-permute-done.9.refs_7_) | copy-start | bytes 393220
  24.6 4.2 %collective-permute-start.11 = (bf16[128,512]{1,0:T(8,128)(2,1)S(1)}, bf16[128,512]{1,0:T(8,128)(2,1)S(1)}, u32[]{:S(2)}, u32[]{:S(2)}) collective-permute-start(bf16[128,512]{1,0:T(8,128)(2,1)S(1)} %collective-permute-done.9.refs_7_), channel_id=1, source_target_pairs={{0,1},{1,0},{2,3},{3,2},{4,5},{5,4},{6,7},{7,6},{8,9},{9,8},{10,11... | collective-permute-start | bytes 393224 | tf_op jit(solution)/shard_map/ppermute | solution.py:451
  28.8 0.7 copy-start.11
  28.8 0.7 copy-start.7
  28.8 0.7 copy-start.12
  28.8 0.8 copy-start.8
  33.8 10.6 %copy-start.15 = (f32[1,1024]{1,0:T(1,128)S(1)}, f32[1,1024]{1,0:T(1,128)}, u32[]{:S(2)}) copy-start(f32[1,1024]{1,0:T(1,128)} %get-tuple-element.45) | copy-start | bytes 12292
  38.8 7.3 %copy-start = (bf16[128,1024]{1,0:T(8,128)(2,1)S(1)}, bf16[128,1024]{1,0:T(8,128)(2,1)}, u32[]{:S(2)}) copy-start(bf16[128,1024]{1,0:T(8,128)(2,1)} %get-tuple-element.52) | copy-start | bytes 786436
  39.9 4.4 %collective-permute-start.12 = (bf16[128,1024]{1,0:T(8,128)(2,1)S(1)}, bf16[128,1024]{1,0:T(8,128)(2,1)S(1)}, u32[]{:S(2)}, u32[]{:S(2)}) collective-permute-start(bf16[128,1024]{1,0:T(8,128)(2,1)S(1)} %fusion.3), channel_id=1, source_target_pairs={{24,16},{25,17},{26,18},{27,19},{28,20},{29,21},{30,22},{31,23}} | collective-permute-start | bytes 786440 | tf_op jit(solution)/shard_map/ppermute | solution.py:399
  43.9 3.9 %collective-permute-start.15 = (bf16[4,128,1024]{2,1,0:T(8,128)(2,1)}, bf16[4,128,1024]{2,1,0:T(8,128)(2,1)S(1)}, u32[]{:S(2)}, u32[]{:S(2)}) collective-permute-start(bf16[4,128,1024]{2,1,0:T(8,128)(2,1)} %get-tuple-element.66), channel_id=1, source_target_pairs={{0,1},{1,0},{2,3},{3,2},{4,5},{5,4},{6,7},{7,6},{8,9},{9,8},{10,11... | collective-permute-start | bytes 3145736 | tf_op jit(solution)/shard_map/ppermute | solution.py:471
  45.4 0.7 collective-permute-start.13
  46.3 25.8 %collective-permute-start.14 = (bf16[128,1024]{1,0:T(8,128)(2,1)S(1)}, bf16[128,1024]{1,0:T(8,128)(2,1)S(1)}, u32[]{:S(2)}, u32[]{:S(2)}) collective-permute-start(bf16[128,1024]{1,0:T(8,128)(2,1)S(1)} %get-tuple-element.79), channel_id=1, source_target_pairs={{8,0},{9,1},{10,2},{11,3},{12,4},{13,5},{14,6},{15,7}} | collective-permute-start | bytes 786440 | tf_op jit(solution)/shard_map/ppermute | solution.py:399
  47.7 1.0 copy-start.1
  51.5 35.2 %collective-permute-start.16 = (bf16[2,128,512]{2,1,0:T(8,128)(2,1)}, bf16[2,128,512]{2,1,0:T(8,128)(2,1)S(1)}, u32[]{:S(2)}, u32[]{:S(2)}) collective-permute-start(bf16[2,128,512]{2,1,0:T(8,128)(2,1)} %get-tuple-element.68), channel_id=1, source_target_pairs={{0,2},{1,3},{2,0},{3,1},{4,6},{5,7},{6,4},{7,5},{8,10},{9,11},{10,... | collective-permute-start | bytes 786440 | tf_op jit(solution)/shard_map/ppermute | solution.py:476
  53.0 33.7 %collective-permute-start.17 = (bf16[2,128,512]{2,1,0:T(8,128)(2,1)}, bf16[2,128,512]{2,1,0:T(8,128)(2,1)S(1)}, u32[]{:S(2)}, u32[]{:S(2)}) collective-permute-start(bf16[2,128,512]{2,1,0:T(8,128)(2,1)} %get-tuple-element.70), channel_id=1, source_target_pairs={{0,4},{4,0},{1,5},{5,1},{2,6},{6,2},{3,7},{7,3},{8,12},{12,8},{9,1... | collective-permute-start | bytes 786440 | tf_op jit(solution)/shard_map/ppermute | solution.py:477
  78.4 26.5 %all-to-all-start = ((f32[32,1,1152]{2,1,0:T(1,128)}), f32[32,1,1152]{2,1,0:T(1,128)S(1)}, u32[]{:S(2)}, u32[]{:S(2)}) async-start(f32[32,1,1152]{2,1,0:T(1,128)} %copy.22), calls=%async_computation | async-start | bytes 294912 | tf_op jit(solution)/shard_map/all_to_all | solution.py:513
  86.7 0.7 copy-start.4
  86.7 0.8 copy-start.5
  89.8 6.4 %collective-permute-start.18 = (bf16[128,512]{1,0:T(8,128)(2,1)}, bf16[128,512]{1,0:T(8,128)(2,1)S(1)}, u32[]{:S(2)}, u32[]{:S(2)}) collective-permute-start(bf16[128,512]{1,0:T(8,128)(2,1)} %get-tuple-element.72), channel_id=1, source_target_pairs={{0,4},{4,0},{1,5},{5,1},{2,6},{6,2},{3,7},{7,3},{8,12},{12,8},{9,1... | collective-permute-start | bytes 393224 | tf_op jit(solution)/shard_map/ppermute | solution.py:482
  91.5 5.5 %collective-permute-start.19 = (bf16[128,512]{1,0:T(8,128)(2,1)}, bf16[128,512]{1,0:T(8,128)(2,1)S(1)}, u32[]{:S(2)}, u32[]{:S(2)}) collective-permute-start(bf16[128,512]{1,0:T(8,128)(2,1)} %get-tuple-element.74), channel_id=1, source_target_pairs={{0,2},{1,3},{2,0},{3,1},{4,6},{5,7},{6,4},{7,5},{8,10},{9,11},{10,... | collective-permute-start | bytes 393224 | tf_op jit(solution)/shard_map/ppermute | solution.py:483
  96.1 0.9 copy-start.13
  97.1 0.6 copy-start.14
  99.7 7.5 %collective-permute-start.20 = (bf16[32,1024]{1,0:T(8,128)(2,1)}, bf16[32,1024]{1,0:T(8,128)(2,1)S(1)}, u32[]{:S(2)}, u32[]{:S(2)}) collective-permute-start(bf16[32,1024]{1,0:T(8,128)(2,1)} %get-tuple-element.76), channel_id=1, source_target_pairs={{0,8},{8,16},{16,24},{24,0},{1,9},{9,17},{17,25},{25,1},{2,10},{10... | collective-permute-start | bytes 196616 | tf_op jit(solution)/shard_map/ppermute | solution.py:490
  101.1 7.3 %collective-permute-start.21 = (bf16[32,1024]{1,0:T(8,128)(2,1)}, bf16[32,1024]{1,0:T(8,128)(2,1)S(1)}, u32[]{:S(2)}, u32[]{:S(2)}) collective-permute-start(bf16[32,1024]{1,0:T(8,128)(2,1)} %get-tuple-element.77), channel_id=1, source_target_pairs={{0,16},{8,24},{16,0},{24,8},{1,17},{9,25},{17,1},{25,9},{2,18},{10... | collective-permute-start | bytes 196616 | tf_op jit(solution)/shard_map/ppermute | solution.py:490
  103.5 5.0 %collective-permute-start.22 = (bf16[32,1024]{1,0:T(8,128)(2,1)}, bf16[32,1024]{1,0:T(8,128)(2,1)S(1)}, u32[]{:S(2)}, u32[]{:S(2)}) collective-permute-start(bf16[32,1024]{1,0:T(8,128)(2,1)} %get-tuple-element.78), channel_id=1, source_target_pairs={{0,24},{8,0},{16,8},{24,16},{1,25},{9,1},{17,9},{25,17},{2,26},{10... | collective-permute-start | bytes 196616 | tf_op jit(solution)/shard_map/ppermute | solution.py:490
  107.1 1.4 %copy-start.19 = (bf16[32,1024]{1,0:T(8,128)(2,1)}, bf16[32,1024]{1,0:T(8,128)(2,1)S(1)}, u32[]{:S(2)}) copy-start(bf16[32,1024]{1,0:T(8,128)(2,1)S(1)} %collective-permute-done.20.refs_1_) | copy-start | bytes 196612
  108.3 0.6 copy-start.20
  108.5 0.6 copy-start.21
  110.7 5.8 %collective-permute-start.25 = (bf16[32,1024]{1,0:T(8,128)(2,1)}, bf16[32,1024]{1,0:T(8,128)(2,1)S(1)}, u32[]{:S(2)}, u32[]{:S(2)}) collective-permute-start(bf16[32,1024]{1,0:T(8,128)(2,1)} %add_quarter.1.refs_0_), channel_id=1, source_target_pairs={{0,24},{8,0},{16,8},{24,16},{1,25},{9,1},{17,9},{25,17},{2,26},{10... | collective-permute-start | bytes 196616 | tf_op jit(solution)/shard_map/ppermute | solution.py:492
  113.4 5.4 %collective-permute-start.24 = (bf16[32,1024]{1,0:T(8,128)(2,1)}, bf16[32,1024]{1,0:T(8,128)(2,1)S(1)}, u32[]{:S(2)}, u32[]{:S(2)}) collective-permute-start(bf16[32,1024]{1,0:T(8,128)(2,1)} %add_quarter.1.refs_0_), channel_id=1, source_target_pairs={{0,16},{8,24},{16,0},{24,8},{1,17},{9,25},{17,1},{25,9},{2,18},{10... | collective-permute-start | bytes 196616 | tf_op jit(solution)/shard_map/ppermute | solution.py:492
  113.4 6.3 %collective-permute-start.23 = (bf16[32,1024]{1,0:T(8,128)(2,1)}, bf16[32,1024]{1,0:T(8,128)(2,1)S(1)}, u32[]{:S(2)}, u32[]{:S(2)}) collective-permute-start(bf16[32,1024]{1,0:T(8,128)(2,1)} %add_quarter.1.refs_0_), channel_id=1, source_target_pairs={{0,8},{8,16},{16,24},{24,0},{1,9},{9,17},{17,25},{25,1},{2,10},{10... | collective-permute-start | bytes 196616 | tf_op jit(solution)/shard_map/ppermute | solution.py:492
  116.6 3.1 %copy-start.16 = (bf16[32,1024]{1,0:T(8,128)(2,1)}, bf16[32,1024]{1,0:T(8,128)(2,1)S(1)}, u32[]{:S(2)}) copy-start(bf16[32,1024]{1,0:T(8,128)(2,1)S(1)} %collective-permute-done.25.refs_3_) | copy-start | bytes 196612
  118.8 0.9 copy-start.17
  119.7 0.6 copy-start.18

commit v2 on v1

v2 whole, which is shorter than its diff:
```python
import functools

import jax
import jax.numpy as jnp
from jax import lax
from jax.experimental import pallas as pl
from jax.experimental.pallas import tpu as pltpu
from jax.sharding import PartitionSpec as P

BF = jnp.bfloat16
F32 = jnp.float32
ROWS = ((0,), (0,))
LAST = ((1,), (1,))
CHUNKS = 8
HBM_BYTES_PER_US = 3.69e6
TM = 4
VMEM_LIMIT = 24 * 1024 * 1024


def mm(a, b):
    return jnp.dot(a, b, preferred_element_type=F32)


def mm_tn(a, b):
    return lax.dot_general(a, b, (ROWS, ((), ())), preferred_element_type=F32)


def mm_nt(a, b):
    return lax.dot_general(a, b, (LAST, ((), ())), preferred_element_type=F32)


def split(v, parts):
    pieces = []
    for _ in range(parts):
        piece = v.astype(BF)
        pieces.append(piece)
        v = v - piece.astype(F32)
    return pieces


def column(ref):
    row = ref[...].reshape(1, -1)
    heads = row.shape[1]
    i = lax.broadcasted_iota(jnp.int32, (heads, heads), 0)
    j = lax.broadcasted_iota(jnp.int32, (heads, heads), 1)
    return jnp.sum(jnp.where(i == j, row, 0.0), axis=1, keepdims=True)


def head_map(heads, width):
    i = lax.broadcasted_iota(jnp.int32, (heads, width), 0)
    j = lax.broadcasted_iota(jnp.int32, (heads, width), 1)
    wide = width // heads
    return jnp.where((j >= i * wide) & (j < (i + 1) * wide), 1.0, 0.0).astype(F32)


def triangle(length, keep):
    i = lax.broadcasted_iota(jnp.int32, (length, length), 0)
    j = lax.broadcasted_iota(jnp.int32, (length, length), 1)
    return jnp.where(keep(i, j), 1.0, 0.0).astype(BF)


def along_frames(v, tri):
    heads = v.shape[0]
    out = mm(jnp.concatenate(split(v, 3), axis=0), tri)
    return out[:heads] + out[heads : 2 * heads] + out[2 * heads :]


def expand(v, hmap):
    return mm_tn(jnp.concatenate(split(v, 2), axis=0), jnp.concatenate([hmap, hmap], axis=0).astype(BF))


def expand_row(col, hmap):
    return jnp.sum(col * hmap, axis=0, keepdims=True)


def head_sums(y, hmap):
    hb = hmap.astype(BF)
    hi, lo = split(y, 2)
    return mm_nt(hb, hi) + mm_nt(hb, lo)


def decay(s_ref, rate_ref, bias_ref):
    v = s_ref[...] + column(bias_ref)
    e = jnp.exp(-jnp.abs(v))
    u = 1.0 + e
    d = u - 1.0
    log1p = jnp.where(d == 0.0, e, jnp.log(u) * (e / jnp.where(d == 0.0, 1.0, d)))
    delta = jnp.maximum(v, 0.0) + log1p
    a = -jnp.exp(column(rate_ref))
    ld = delta * a
    cum = along_frames(ld, triangle(ld.shape[1], lambda i, j: i <= j))
    return v, delta, a, ld, cum


class Coming:
    def __init__(self, source, target, semaphore):
        self.copy = pltpu.make_async_copy(source, target, semaphore)
        self.copy.start()
        self.target, self.waited = target, False

    def ready(self):
        if not self.waited:
            self.copy.wait()
            self.waited = True
        return self.target


def near_by(shape, dtype):
    return pltpu.VMEM(shape, dtype)


def away(shape, dtype):
    return pltpu.HBM(shape, dtype)


def free(shape, dtype):
    return jax.ShapeDtypeStruct(shape, dtype)


def call(kernel, outs, far, *args, smem=(), name=None, scratch=(), after=(), beside=(), us=3):
    waits = len(after) + len(beside)
    specs = [pl.BlockSpec(memory_space=pl.ANY)] * len(far)
    specs += [
        pl.BlockSpec(memory_space=pltpu.SMEM if k in smem else pltpu.VMEM) for k in range(len(args))
    ]
    specs += [pl.BlockSpec(memory_space=pl.ANY)] * waits
    first, used = len(far), len(far) + len(args)
    landing = [pltpu.VMEM(v.shape, v.dtype) for v in far]
    semaphores = [pltpu.SemaphoreType.DMA((len(far),))] if far else []

    def body(*refs):
        refs, own = list(refs), len(far)
        coming = []
        if far:
            refs, targets, semaphore = refs[: -own - 1], refs[-own - 1 : -1], refs[-1]
            coming = [Coming(refs[k], targets[k], semaphore.at[k]) for k in range(own)]
        kernel(*coming, *refs[first:used], *refs[used + waits :])
        for one in coming:
            one.ready()

    return pl.pallas_call(
        body,
        out_shape=[where(shape, dtype) for shape, dtype, where in outs],
        in_specs=specs,
        out_specs=[pl.BlockSpec(memory_space=pltpu.VMEM)] * len(outs),
        scratch_shapes=list(scratch) + landing + semaphores,
        compiler_params=pltpu.CompilerParams(vmem_limit_bytes=VMEM_LIMIT),
        cost_estimate=pl.CostEstimate(flops=0, bytes_accessed=int(us * HBM_BYTES_PER_US), transcendentals=0),
        name=name,
    )(*[pltpu.with_memory_space_constraint(v, pltpu.HBM) for v in far], *args, *[pltpu.with_memory_space_constraint(v, pltpu.HBM) for v in after], *beside)


def store_decay(aux_ref, rows_ref, v, delta, a, ld, cum, skip, gain):
    heads = cum.shape[0]
    for k, value in enumerate((v, delta, ld, cum, jnp.broadcast_to(a, cum.shape))):
        aux_ref[k * heads : (k + 1) * heads, :] = value
    rows_ref[0:1, :] = skip
    rows_ref[1:2, :] = gain


def load_decay(aux_ref):
    heads = aux_ref.shape[0] // 5
    return [aux_ref[k * heads : (k + 1) * heads, :] for k in range(5)]


def store_parts(out_ref, state, row):
    count, blocks = out_ref.shape[0], row.shape[1] // 128
    rows = state.shape[0] // count
    tail = [v[:, n * 128 : (n + 1) * 128].astype(F32) for v in split(row, 2) for n in range(blocks)]
    tail = jnp.concatenate(tail, axis=0).astype(BF)
    for k in range(count):
        for n in range(blocks):
            out_ref[k, n * rows : (n + 1) * rows, :] = state[k * rows : (k + 1) * rows, n * 128 : (n + 1) * 128]
        out_ref[k, blocks * rows :, :] = tail


def payload_kernel(s_in, rate_in, bias_in, b_in, x_in, skip_in, gain_in, aux_ref, rows_ref, *outs):
    v, delta, a, ld, cum = decay(s_in.ready(), rate_in.ready(), bias_in.ready())
    x_ref, b_ref = x_in.ready(), b_in.ready()
    width = x_ref.shape[1]
    hmap = head_map(cum.shape[0], width)
    skip = expand_row(column(skip_in.ready()), hmap)
    store_decay(aux_ref, rows_ref, v, delta, a, ld, cum, skip, gain_in.ready()[...].reshape(1, -1))
    last = cum[:, -1:]
    tail = expand(jnp.exp(last - cum) * delta, hmap)
    weighted = (x_ref[...].astype(F32) * tail).astype(BF)
    state = mm_tn(b_ref[...], weighted).astype(BF)
    total = expand_row(jnp.exp(last), hmap)
    if len(outs) == 2:
        outs[0][...] = state
        outs[1][...] = total
        return
    (out_ref,) = outs
    store_parts(out_ref, state, total)


def part_decay(all_ref, k, n, rows, blocks):
    pair = all_ref[k, blocks * rows :, :].astype(F32)
    return pair[n : n + 1] + pair[blocks + n : blocks + n + 1]


def prefix_kernel(all_ref, out_ref):
    count, rows, width = out_ref.shape
    blocks = width // 128
    for n in range(blocks):
        cols = slice(n * 128, (n + 1) * 128)
        carried = jnp.zeros((rows, 128), F32)
        for k in range(count):
            out_ref[k, :, cols] = carried.astype(BF)
            if k + 1 < count:
                state = all_ref[k, n * rows : (n + 1) * rows, :].astype(F32)
                carried = state + part_decay(all_ref, k, n, rows, blocks) * carried


def suffix_kernel(grads_ref, all_ref, out_ref, gains_ref):
    count, rows, width = out_ref.shape
    blocks = width // 128
    for n in range(blocks):
        cols = slice(n * 128, (n + 1) * 128)
        carried = jnp.zeros((rows, 128), F32)
        for k in reversed(range(count)):
            out_ref[k, :, cols] = carried.astype(BF)
            if k > 0:
                grad = grads_ref[k, n * rows : (n + 1) * rows, :].astype(F32)
                carried = grad + part_decay(all_ref, k, n, rows, blocks) * carried
    gains = sum(grads_ref[k, blocks * rows :, :].astype(F32) for k in range(count))
    gains_ref[...] = gains[:blocks] + gains[blocks:]


def inner_kernel(b_in, c_in, x_in, aux_ref, rows_ref, inner_ref):
    _, delta, _, cum, _ = load_decay(aux_ref)
    x_ref, b_ref, c_ref = x_in.ready(), b_in.ready(), c_in.ready()
    heads, length = cum.shape
    width = x_ref.shape[1]
    hmap = head_map(heads, width)
    cum_t = cum.T
    x = x_ref[...].astype(F32)
    xd = (x * expand(delta, hmap)).astype(BF)
    skip = rows_ref[0:1, :]
    half = length // 2
    scores = mm_nt(c_ref[...], b_ref[...])
    i = lax.broadcasted_iota(jnp.int32, (half, half), 0)
    j = lax.broadcasted_iota(jnp.int32, (half, half), 1)
    diag = i >= j
    s00 = jnp.where(diag, scores[:half, :half], 0.0)
    s10 = scores[half:, :half]
    s11 = jnp.where(diag, scores[half:, half:], 0.0)
    pair = 2 * (width // heads)
    first = lax.broadcasted_iota(jnp.int32, (half, pair), 1) < pair // 2
    for p in range(heads // 2):
        cols = slice(p * pair, (p + 1) * pair)
        upper, lower = [], []
        for h in (2 * p, 2 * p + 1):
            q0, q1 = cum_t[:half, h : h + 1], cum_t[half:, h : h + 1]
            k0, k1 = cum[h : h + 1, :half], cum[h : h + 1, half:]
            m00 = jnp.exp(jnp.minimum(q0 - k0, 0.0)) * s00
            m10 = jnp.exp(jnp.minimum(q1 - k0, 0.0)) * s10
            m11 = jnp.exp(jnp.minimum(q1 - k1, 0.0)) * s11
            upper.append(m00.astype(BF))
            lower.append(jnp.concatenate([m10.astype(BF), m11.astype(BF)], axis=1))
        y0 = mm(jnp.concatenate(upper, axis=0), xd[:half, cols])
        y1 = mm(jnp.concatenate(lower, axis=0), xd[:, cols])
        inner_ref[:half, cols] = jnp.where(first, y0[:half], y0[half:]) + skip[:, cols] * x[:half, cols]
        inner_ref[half:, cols] = jnp.where(first, y1[:half], y1[half:]) + skip[:, cols] * x[half:, cols]


def weight_kernel(*refs):
    pieces, g_in, idx_ref, full_ref, ng_ref = [v.ready() for v in refs[:8]], *refs[8:]
    me = idx_ref[0]
    rows = pieces[0].shape[0]
    for k, piece in enumerate(pieces):
        full_ref[pl.ds(pl.multiple_of((me ^ k) * rows, rows), rows), :] = piece[...]
    ng_ref[...] = mm_nt(g_in.ready()[...], full_ref[...]).astype(BF)


def grad_kernel(g_ref, full_ref, ng_ref):
    ng_ref[...] = mm_nt(g_ref[...], full_ref[...]).astype(BF)


def norm_kernel(c_in, z_in, idx_ref, aux_ref, params_ref, local_ref, inc_ref, normed_ref, other_ref, inner_ref, factor_ref, ec_ref):
    _, _, _, cum, _ = load_decay(aux_ref)
    c_ref, z_ref = c_in.ready(), z_in.ready()
    heads, length = cum.shape
    width = z_ref.shape[1]
    hmap = head_map(heads, width)
    ec_ref[...] = expand(jnp.exp(cum), hmap)
    inner_ref[...] = mm(c_ref[...], inc_ref[...])
    gain = params_ref[1:2, :]
    step = length // CHUNKS

    for n in range(CHUNKS):
        at = slice(n * step, (n + 1) * step)
        inner = local_ref[at, :] + inner_ref[at, :] * ec_ref[at, :]
        inner_ref[at, :] = inner
        z = z_ref[at, :].astype(F32)
        gated = inner * (z / (1.0 + jnp.exp(-z)))
        r = lax.rsqrt(jnp.mean(gated * gated, axis=1, keepdims=True) + 1e-05)
        factor_ref[at, :] = jnp.broadcast_to(r, (step, 128))
        normed_ref[at, :] = (gated * r * gain).astype(BF)
    block = other_ref.shape[1] // 4
    for k in range(4):
        at = (2 * k + 1 - lax.rem(idx_ref[0], 2)) * block
        other_ref[:, k * block : (k + 1) * block] = normed_ref[:, pl.ds(pl.multiple_of(at, block), block)]


def norm_back_kernel(
    c_in, z_in, x_in, aux_ref, params_ref, inner_ref, factor_ref, ng_ref,
    dy_ref, carry_ref, zg_ref, rows_ref, gains_ref, skips_ref,
    ec_ref, de_ref, hi_ref, lo_ref,
):
    _, _, _, cum, _ = load_decay(aux_ref)
    c_ref, z_ref, x_ref = c_in.ready(), z_in.ready(), x_in.ready()
    heads, length = cum.shape
    width = x_ref.shape[1]
    hmap = head_map(heads, width)
    ec_ref[...] = expand(jnp.exp(cum), hmap)
    skip, gain = params_ref[0:1, :], params_ref[1:2, :]
    step = length // CHUNKS
    gains = jnp.zeros((1, width), F32)
    skips = jnp.zeros((1, width), F32)
    for n in range(CHUNKS):
        at = slice(n * step, (n + 1) * step)
        inner = inner_ref[at, :]
        z = z_ref[at, :].astype(F32)
        sig = 1.0 / (1.0 + jnp.exp(-z))
        silu = z * sig
        r = factor_ref[at, 0:1]
        nhat = inner * silu * r
        ng = ng_ref[at, :].astype(F32)
        prod = ng * nhat
        gains = gains + jnp.sum(prod, axis=0, keepdims=True)
        m = jnp.mean(prod * gain, axis=1, keepdims=True)
        dgated = r * (ng * gain - nhat * m)
        dinner = dgated * silu
        dy = dinner.astype(BF)
        dy_ref[at, :] = dy
        de_ref[at, :] = (dinner * ec_ref[at, :]).astype(BF)
        zg_ref[at, :] = (dgated * inner * (sig + silu * (1.0 - sig))).astype(BF)
        x = x_ref[at, :].astype(F32)
        skips = skips + jnp.sum(dinner * x, axis=0, keepdims=True)
        hi_ref[at, :], lo_ref[at, :] = split(dy.astype(F32) * (inner - skip * x), 2)
    carry = mm_tn(c_ref[...], de_ref[...]).astype(BF)
    if len(carry_ref.shape) == 2:
        carry_ref[...] = carry
    else:
        store_parts(carry_ref, carry, gains)
    hb = hmap.astype(BF)
    rows_ref[...] = mm_nt(hb, hi_ref[...]) + mm_nt(hb, lo_ref[...])
    gains_ref[...] = gains
    skips_ref[...] = jnp.sum(skips * hmap, axis=1, keepdims=True)


def outer_kernel(g_in, gc_in, idx_ref, normed_ref, got_ref, keep_ref, *sends):
    g_ref, gc_ref = g_in.ready(), gc_in.ready()
    me = idx_ref[0]
    core, chip = lax.rem(me, 2), me // 2
    rows = keep_ref.shape[0]
    for k, out_ref in enumerate((keep_ref, *sends)):
        mine = pl.ds(pl.multiple_of((2 * (chip ^ k) + core) * rows, rows), rows)
        theirs = pl.ds(pl.multiple_of((chip ^ k) * rows, rows), rows)
        part = mm_tn(normed_ref[:, mine], g_ref[...]) + mm_tn(got_ref[:, theirs], gc_ref[...])
        out_ref[...] = part.astype(out_ref.dtype)


def add_kernel(keep_in, pos_ref, *refs):
    gots, outs, scratch = refs[:3], refs[3:-1], refs[-1]
    total = keep_in.ready()[...]
    for got in gots:
        total = total + got[...].astype(F32)
    scratch[...] = total
    rows = outs[0].shape[0]
    for k, out_ref in enumerate(outs):
        at = lax.rem(pos_ref[1] + k, len(outs)) * rows
        out_ref[...] = scratch[pl.ds(pl.multiple_of(at, rows), rows), :].astype(out_ref.dtype)


def add_quarter_kernel(own_in, *refs):
    gots, out_ref = refs[:-1], refs[-1]
    total = own_in.ready()[...]
    for got in gots:
        total = total + got[...].astype(F32)
    out_ref[...] = total.astype(BF)


def join_kernel(*refs):
    pos_ref, pieces, out_ref = refs[0], refs[1:-1], refs[-1]
    count, rows = len(pieces), pieces[0].shape[0]
    for k, piece in enumerate(pieces):
        at = lax.rem(pos_ref[1] + count - k, count) * rows
        out_ref[pl.ds(pl.multiple_of(at, rows), rows), :] = piece[...]


def outer_full_kernel(normed_ref, g_ref, out_ref):
    out_ref[...] = mm_tn(normed_ref[...], g_ref[...])


def back_kernel(
    dy_in, b_in, c_in, x_in, full_in, aux_ref, params_ref, inc_ref, normed_ref,
    mixed_ref, cg_ref, xg_ref, bg_ref, cols_ref, dxw_ref,
):
    _, delta, _, cum, _ = load_decay(aux_ref)
    x_ref, b_ref, c_ref = x_in.ready(), b_in.ready(), c_in.ready()
    heads, length = cum.shape
    width = x_ref.shape[1]
    hmap = head_map(heads, width)
    cum_t = cum.T
    delta_e = expand(delta, hmap)
    xd = (x_ref[...].astype(F32) * delta_e).astype(BF)
    dy = dy_in.ready()[...]
    half = length // 2
    scores = mm_nt(b_ref[...], c_ref[...])
    i = lax.broadcasted_iota(jnp.int32, (half, half), 0)
    j = lax.broadcasted_iota(jnp.int32, (half, half), 1)
    diag = j >= i
    s00 = jnp.where(diag, scores[:half, :half], 0.0)
    s01 = scores[:half, half:]
    s11 = jnp.where(diag, scores[half:, half:], 0.0)
    pair = 2 * (width // heads)
    first = lax.broadcasted_iota(jnp.int32, (half, pair), 1) < pair // 2
    whole_first = lax.broadcasted_iota(jnp.int32, (length, pair), 1) < pair // 2
    d00 = jnp.zeros((half, half), F32)
    d01 = jnp.zeros((half, half), F32)
    d11 = jnp.zeros((half, half), F32)
    none = jnp.zeros((length, pair), BF)
    for p in range(heads // 2):
        cols = slice(p * pair, (p + 1) * pair)
        xp, dp = xd[:, cols], dy[:, cols]
        stacked = jnp.concatenate([jnp.where(whole_first, xp, none), jnp.where(whole_first, none, xp)], axis=0)
        dm = mm_nt(stacked, dp)
        upper, lower = [], []
        for n, h in enumerate((2 * p, 2 * p + 1)):
            k0, k1 = cum_t[:half, h : h + 1], cum_t[half:, h : h + 1]
            q0, q1 = cum[h : h + 1, :half], cum[h : h + 1, half:]
            l00 = jnp.exp(jnp.minimum(q0 - k0, 0.0))
            l01 = jnp.exp(jnp.minimum(q1 - k0, 0.0))
            l11 = jnp.exp(jnp.minimum(q1 - k1, 0.0))
            at = n * length
            d00 = d00 + l00 * dm[at : at + half, :half]
            d01 = d01 + l01 * dm[at : at + half, half:]
            d11 = d11 + l11 * dm[at + half : at + length, half:]
            upper.append(jnp.concatenate([(l00 * s00).astype(BF), (l01 * s01).astype(BF)], axis=1))
            lower.append((l11 * s11).astype(BF))
        y0 = mm(jnp.concatenate(upper, axis=0), dp)
        y1 = mm(jnp.concatenate(lower, axis=0), dp[half:])
        dxw_ref[:half, cols] = jnp.where(first, y0[:half], y0[half:])
        dxw_ref[half:, cols] = jnp.where(first, y1[:half], y1[half:])
    d00 = jnp.where(diag, d00, 0.0).astype(BF)
    d01 = d01.astype(BF)
    d11 = jnp.where(diag, d11, 0.0).astype(BF)
    c0, c1 = c_ref[:half, :], c_ref[half:, :]
    b0, b1 = b_ref[:half, :], b_ref[half:, :]
    bg_ref[:half, :] = (mm(d00, c0) + mm(d01, c1)).astype(BF)
    bg_ref[half:, :] = mm(d11, c1).astype(BF)
    ec = expand(jnp.exp(cum), hmap)
    carried = mm_nt((dy.astype(F32) * ec).astype(BF), inc_ref[...])
    cg_ref[:half, :] = (carried[:half] + mm_tn(d00, b0).astype(BF).astype(F32)).astype(BF)
    cg_ref[half:, :] = (carried[half:] + (mm_tn(d01, b0) + mm_tn(d11, b1)).astype(BF).astype(F32)).astype(BF)
    dxw = dxw_ref[...]
    cols_ref[...] = head_sums(xd.astype(F32) * dxw, hmap)
    skip = params_ref[0:1, :]
    xg_ref[...] = delta_e * dxw + skip * dy.astype(F32)
    mixed_ref[...] = mm(normed_ref[...], full_in.ready()[...]).astype(BF)


def last_kernel(
    b_in, x_in, rows_in, cols_in, bg_in, xg_in, skips_in, aux_ref, later_ref, inc_ref, *more,
):
    more, (x_out, b_out, step_out, sums_out) = more[:-4], more[-4:]
    v, delta, ld, cum, a = load_decay(aux_ref)
    x_ref, b_ref = x_in.ready(), b_in.ready()
    heads, length = cum.shape
    width = x_ref.shape[1]
    hmap = head_map(heads, width)
    last = cum[:, -1:]
    tailing = jnp.exp(last - cum)
    tail = tailing * delta
    tail_e = expand(tail, hmap)
    x = x_ref[...].astype(F32)
    later = later_ref[...]
    dweighted = mm(b_ref[...], later)
    x_out[...] = (xg_in.ready()[...] + tail_e * dweighted).astype(BF)
    weighted = (x * tail_e).astype(BF)
    b_out[...] = (bg_in.ready()[...].astype(F32) + mm_nt(weighted, later)).astype(BF)
    dtail = head_sums(x * dweighted, hmap)
    cross = jnp.sum(later.astype(F32) * inc_ref[...].astype(F32), axis=0, keepdims=True)
    dtotal = jnp.sum(cross * hmap, axis=1, keepdims=True) * jnp.exp(last)
    cols = cols_in.ready()[...]
    dld = along_frames(rows_in.ready()[...] - cols, triangle(length, lambda i, j: i >= j))
    dld = dld + along_frames(dtail * tail, triangle(length, lambda i, j: i < j)) + dtotal
    ddelta = cols / delta + dtail * tailing + a * dld
    dstep = ddelta / (1.0 + jnp.exp(-v))
    step_out[...] = dstep
    drate = jnp.sum(dld * ld, axis=1, keepdims=True)
    dbias = jnp.sum(dstep, axis=1, keepdims=True)
    i = lax.broadcasted_iota(jnp.int32, (heads, 128), 0)
    j = lax.broadcasted_iota(jnp.int32, (heads, 128), 1)

    def lay(col, at):
        return jnp.sum(jnp.where(j == i + at, col, 0.0), axis=0, keepdims=True)

    small = lay(drate, 0) + lay(dbias, heads) + lay(skips_in.ready()[...], 2 * heads)
    sums_out[0, :, :128] = small
    if len(more) == 2:
        pos_ref, gains_ref = more
        each = gains_ref.shape[0] // TM
        for n in range(each):
            at = pl.ds(pos_ref[1] * each + n, 1)
            sums_out[0, :, (n + 1) * 128 : (n + 2) * 128] = gains_ref[at, :]
        for k in range(1, sums_out.shape[0]):
            sums_out[k] = sums_out[0]
    else:
        sums_out[0, :, 128:] = more[0][...]


def sums_kernel(all_in, rate_out, bias_out, skip_out, gain_out):
    every = all_in.ready()[...]
    heads = rate_out.shape[0]
    small = jnp.sum(every[:, 0, :128], axis=0)
    rate_out[...] = small[:heads]
    bias_out[...] = small[heads : 2 * heads]
    skip_out[...] = small[2 * heads : 3 * heads]
    share = every.shape[2] - 128
    parts = gain_out.shape[0] // share
    group = every.shape[0] // parts
    for k in range(parts):
        gain_out[k * share : (k + 1) * share] = jnp.sum(every[k * group : (k + 1) * group, 0, 128:], axis=0)


def scan_far(value, total, axis, reverse):
    count = lax.axis_size(axis)
    position = lax.axis_index(axis)
    decayed, state = total, value.astype(F32)
    step = 1
    while step < count:
        pairs = [(k, k - step) for k in range(step, count)] if reverse else [(k, k + step) for k in range(count - step)]
        inside = position + step < count if reverse else position >= step
        got_state = lax.ppermute(state.astype(BF), axis, pairs).astype(F32)
        got_total = lax.ppermute(decayed, axis, pairs)
        state = jnp.where(inside, decayed * got_state + state, state)
        decayed = jnp.where(inside, decayed * got_total, decayed)
        step *= 2
    pairs = [(k, k - 1) for k in range(1, count)] if reverse else [(k, k + 1) for k in range(count - 1)]
    return lax.ppermute(state.astype(BF), axis, pairs)


def shards(x_branch, z_gate, b_input, c_input, step_raw, rate_log, step_bias, skip_gain, norm_gain, out_weight, out_grad):
    seqs, length, width = x_branch.shape
    model = out_grad.shape[2]
    heads = rate_log.shape[0]
    state_size = b_input.shape[2]
    x, z, b, c, s, g = x_branch[0], z_gate[0], b_input[0], c_input[0], step_raw[0], out_grad[0]
    n_tm, n_tok, n_rep = lax.axis_size("tm"), lax.axis_size("tok"), lax.axis_size("rep")
    rep, tok, tm = lax.axis_index("rep"), lax.axis_index("tok"), lax.axis_index("tm")
    near = (n_tm, n_tok, n_rep) == (4, 2, 4)
    rows = out_weight.shape[0]
    full = (width, model)
    wide = (length, width)
    place = jnp.stack([tok * n_rep + rep, tm]).astype(jnp.int32)
    core = [(k, k ^ 1) for k in range(4)]
    side = [(k, k ^ 2) for k in range(4)]
    front = [(0, 1), (1, 0)]
    diagonal = [(k, k ^ 6) for k in range(8)]

    raw = (s, rate_log, step_bias, b, x, skip_gain, norm_gain)
    aux_shapes = [((5 * heads, length), F32, near_by), ((8, width), F32, near_by)]
    if near:
        part = (n_tm, state_size // n_tm)
        blocks_of = width // 128
        part_shape = (n_tm, blocks_of * part[1] + 2 * blocks_of, 128)
        aux, params, payload = call(
            payload_kernel, aux_shapes + [(part_shape, BF, away)], raw, name="state", us=3,
        )
        blocks = lax.all_to_all(payload, "tm", 0, 0, tiled=True)
        gc = lax.ppermute(g, "rep", core)
        wx = lax.ppermute(out_weight, "rep", side)
        wy = lax.ppermute(out_weight, "tok", front)
        wd = lax.ppermute(out_weight, ("tok", "rep"), diagonal)
        wc, wxc, wyc, wdc = (lax.ppermute(v, "rep", core) for v in (out_weight, wx, wy, wd))
        (local,) = call(
            inner_kernel, [(wide, F32, near_by)], (b, c, x), aux, params, name="inner", us=5, after=(payload,)
        )
        (prefixes,) = call(prefix_kernel, [(part + (width,), BF, away)], (), blocks, name="prefix", us=1, beside=(local,))
        incoming = lax.all_to_all(prefixes, "tm", 0, 0, tiled=True).reshape(state_size, width)
        pieces = (out_weight, wc, wx, wxc, wy, wyc, wd, wdc)
        weight, ng = call(
            weight_kernel, [(full, BF, away), (wide, BF, near_by)], (*pieces, g), place,
            smem=(0,), name="normed_grad", us=10, after=(prefixes,),
        )
    else:
        aux, params, state, total = call(
            payload_kernel, aux_shapes + [((state_size, width), BF, free), ((1, width), F32, free)], raw, name="state", us=3
        )
        incoming = scan_far(state, total, "tm", False)
        (local,) = call(inner_kernel, [(wide, F32, near_by)], (b, c, x), aux, params, name="inner", us=5)
        weight = lax.all_gather(out_weight, ("tok", "rep"), axis=0, tiled=True)
        (ng,) = call(grad_kernel, [(wide, BF, near_by)], (), g, weight, name="normed_grad", us=10)
    normed, other, inner, factor = call(
        norm_kernel,
        [(wide, BF, near_by), ((length, width // 2), BF, away), (wide, F32, near_by), ((length, 128), F32, near_by)],
        (c, z), place, aux, params, local, incoming, name="norm", us=4, smem=(0,), scratch=[pltpu.VMEM(wide, F32)], after=(weight,),
    )
    dy, carry, zg, row_sums, gains, skips = call(
        norm_back_kernel,
        [
            (wide, BF, away), (part_shape if near else (state_size, width), BF, away), (wide, BF, away),
            ((heads, length), F32, away), ((1, width), F32, away), ((heads, 1), F32, away),
        ],
        (c, z, x), aux, params, inner, factor, ng, name="norm_back", us=6,
        scratch=[pltpu.VMEM(wide, F32)] + [pltpu.VMEM(wide, BF)] * 3,
    )

    def back(*after):
        return call(
            back_kernel,
            [
                (wide, BF, away), ((length, state_size), BF, away), (wide, F32, away), ((length, state_size), BF, away),
                ((heads, length), F32, away),
            ],
            (dy, b, c, x, weight), aux, params, incoming, normed,
            name="back", us=14, scratch=[pltpu.VMEM(wide, F32)], after=after,
        )

    everywhere = ("tm", "tok", "rep")
    ahead = [[(i, (i + k) % n_tm) for i in range(n_tm)] for k in range(1, n_tm)]

    def last(row, far, *more):
        return call(
            last_kernel,
            [(wide, BF, away), ((length, state_size), BF, away), ((heads, length), F32, away), (row, F32, away)],
            (b, x, row_sums, col_sums, bg, xg, skips), aux, later, incoming, *more, name="last", us=6, after=far,
            smem=(3,) if near else (),
        )

    if near:
        block = (rows, model)
        theirs = lax.ppermute(other, "rep", core)
        keep, sx, sy, sd = call(
            outer_kernel, [(block, F32, away)] + [(block, BF, away)] * 3, (g, gc), place, normed, theirs,
            smem=(0,), name="outer", us=4, after=(carry,),
        )
        gx = lax.ppermute(sx, "rep", side)
        gy = lax.ppermute(sy, "tok", front)
        gd = lax.ppermute(sd, ("tok", "rep"), diagonal)
        grads = lax.all_to_all(carry, "tm", 0, 0, tiled=True)
        suffixes, gains = call(
            suffix_kernel, [(part + (width,), BF, away), ((blocks_of, 128), F32, near_by)], (), grads, blocks,
            name="suffix", us=1, after=(keep,),
        )
        later = lax.all_to_all(suffixes, "tm", 0, 0, tiled=True).reshape(state_size, width)
        mixed, c_grad, xg, bg, col_sums = back(suffixes)
        quarter = (rows // n_tm, model)
        own, *sends = call(
            add_kernel, [(quarter, F32, away)] + [(quarter, BF, away)] * (n_tm - 1), (keep,), place, gx, gy, gd,
            smem=(0,), name="add_chips", us=3, scratch=[pltpu.VMEM(block, F32)], after=(col_sums,),
        )
        gots = [lax.ppermute(v, "tm", pairs) for v, pairs in zip(sends, ahead)]
        row = (n_tm * n_tok * n_rep, 1, 128 + width // n_tm)
        x_grad, b_grad, step_grad, sums = last(row, (own,), place, gains)
        (total_quarter,) = call(
            add_quarter_kernel, [(quarter, BF, away)], (own,), *gots, name="add_blocks", us=2, after=(step_grad,)
        )
        quarters = [total_quarter] + [lax.ppermute(total_quarter, "tm", pairs) for pairs in ahead]
        (weight_grad,) = call(join_kernel, [(block, BF, away)], (), place, *quarters, smem=(0,), name="join", us=3)
        sums = lax.all_to_all(sums, everywhere, 0, 0, tiled=True)
    else:
        later = scan_far(carry, total, "tm", True)
        (outer,) = call(outer_full_kernel, [(full, F32, free)], (), normed, g, name="outer", us=4)
        share = lax.psum_scatter(outer, ("tok", "rep"), scatter_dimension=0, tiled=True)
        weight_grad = lax.psum(share, "tm").astype(BF)
        mixed, c_grad, xg, bg, col_sums = back()
        x_grad, b_grad, step_grad, sums = last((1, 1, 128 + width), (), gains)
        sums = lax.psum(sums, everywhere)
    rate_grad, bias_grad, skip_grad, gain_grad = call(
        sums_kernel, [((heads,), F32, away)] * 3 + [((width,), F32, away)], (sums,), name="sums", us=2
    )
    return (
        mixed[None], x_grad[None], zg[None], b_grad[None], c_grad[None], step_grad[None],
        rate_grad, bias_grad, skip_grad, gain_grad, weight_grad,
    )


def solution(mesh):
    tokens = P(("tok", "rep"), "tm", None)
    frames = P(("tok", "rep"), None, "tm")
    weight = P(("tok", "rep"), None)
    return jax.shard_map(
        shards,
        mesh=mesh,
        in_specs=(tokens, tokens, tokens, tokens, frames, P(), P(), P(), P(), weight, tokens),
        out_specs=(tokens, tokens, tokens, tokens, tokens, frames, P(), P(), P(), P(), weight),
        check_vma=False,
    )
```

time: 123 us -> 101 us (0.82)
  other arithmetic: 8.21 us -> 0.07 us
  local copies, waits for them, and re-layouts: 9.4 us -> 1.61 us
  waiting for transfers between devices: 24.9 us -> 21.2 us
  Pallas kernels: 40 us -> 37.9 us
    all_to_all x0 -> x4, starting transfers between devices: none -> 17.8 us  [the longest x1 6.33 us: shards(): blocks = lax.all_to_all(payload, 'tm', 0, 0, tiled=True)]
    ppermute x21 -> x13, starting transfers between devices: 21.9 us -> 9.92 us  [the longest x3 4.73 us: shards(): lax.ppermute(total_quarter, 'tm', pairs)]
    ppermute x21 -> x13, waiting for transfers between devices: 22.9 us -> 12.9 us  [the longest x3 5.98 us: shards(): lax.ppermute(total_quarter, 'tm', pairs)]
    all_to_all x0 -> x4, waiting for transfers between devices: none -> 8.24 us  [the longest x1 4.76 us: shards(): grads = lax.all_to_all(carry, 'tm', 0, 0, tiled=True)]
    all_to_all x1, starting transfers between devices: 8.24 us -> 2.56 us  [shards(): sums = lax.all_to_all(sums, everywhere, 0, 0, tiled=True)]
    convert_element_type x6 -> x0, other arithmetic: 5.39 us -> none  [chain(): send = (incoming.astype(F32) * total + value.astype(F32)).astype(BF)]
    unnamed x45 -> x18, local copies, waits for them, and re-layouts: 5.1 us -> 1.61 us
    slice x4 -> x0, local copies, waits for them, and re-layouts: 2.59 us -> none  [the longest x1 1.3 us: shards(): skip_grad = sums[width + 2 * heads:width + 3 * heads]]
  transfers between devices with their start and end apart: 27 -> 23, of which waited for: 10 -> 11; matrix products, arithmetic and copies ran while one was open for 8% -> 0% of each run, Pallas kernels for 24% -> 33%
where the time goes in v2:
time: 101 us
  starting transfers between devices  38.9 us (39%)
  Pallas kernels  37.9 us (38%)
  waiting for transfers between devices  21.2 us (21%)
  local copies, waits for them, and re-layouts  1.61 us (2%)
    pallas_call x14, Pallas kernels, call(): pl.pallas_call(body, out_shape=[where(shape, dtype) for shape, dtype, whe...  37.9 us
    all_to_all x1, starting transfers between devices, shards(): blocks = lax.all_to_all(payload, 'tm', 0, 0, tiled=True)  6.33 us
    ppermute x3, waiting for transfers between devices, shards(): lax.ppermute(total_quarter, 'tm', pairs)  5.98 us
    ppermute x3, starting transfers between devices, shards(): gots = [lax.ppermute(v, 'tm', pairs) for v, pairs in zip(sends, ahead)]  5.54 us
    all_to_all x1, waiting for transfers between devices, shards(): grads = lax.all_to_all(carry, 'tm', 0, 0, tiled=True)  4.76 us
    ppermute x3, starting transfers between devices, shards(): lax.ppermute(total_quarter, 'tm', pairs)  4.73 us
    all_to_all x1, starting transfers between devices, shards(): grads = lax.all_to_all(carry, 'tm', 0, 0, tiled=True)  4.71 us
    ppermute x1, waiting for transfers between devices, shards(): gy = lax.ppermute(sy, 'tok', front)  3.85 us
  transfers between devices with their start and end apart: 23, of which 11 were waited for; matrix products, arithmetic and copies ran while one was open for 0% of the time, Pallas kernels for 33%

profile of v2, /device:TPU:0, one launch (start us, length us, event | category | flops | bytes accessed | tf_op | source)
XLA Modules:
  0.0 100.5 jit_solution(485382426110198433)
XLA Ops:
  0.6 2.6 %state.1 = (f32[80,256]{1,0:T(8,128)S(1)}, f32[8,1024]{1,0:T(8,128)S(1)}, bf16[4,272,128]{2,1,0:T(8,128)(2,1)}) custom-call(f32[16,256]{1,0:T(8,128)} %bitcast.38, f32[16]{0:T(128)} %refs_1_.1, f32[16]{0:T(128)} %refs_2_.1, bf16[256,128]{1,0:T(8,128)(2,1)} %bitcast.34, bf16[256,1024]{1,0:T(8,128)(2,1)} %bitcast.20, f32[16]{0:T(128)} %refs_5_.1, f32[1024]{0:T(1024)} %refs_6_.1), custom_call_target="tpu_custom_call" | custom-call | bytes 11070000 | tf_op jit(solution)/shard_map/state/pallas_call | solution.py:141
  3.2 6.3 %all-to-all-start = ((bf16[4,272,128]{2,1,0:T(8,128)(2,1)}), bf16[4,272,128]{2,1,0:T(8,128)(2,1)S(1)}, u32[]{:S(2)}, u32[]{:S(2)}) async-start(bf16[4,272,128]{2,1,0:T(8,128)(2,1)} %get-tuple-element.50.refs_5_), calls=%async_computation | async-start | bytes 557056 | tf_op jit(solution)/shard_map/all_to_all | solution.py:573
  9.6 1.5 %collective-permute-start.3 = (bf16[128,1024]{1,0:T(8,128)(2,1)}, bf16[128,1024]{1,0:T(8,128)(2,1)S(1)}, u32[]{:S(2)}, u32[]{:S(2)}) collective-permute-start(bf16[128,1024]{1,0:T(8,128)(2,1)} %refs_0_.1), channel_id=1, source_target_pairs={{0,4},{4,0},{1,5},{5,1},{2,6},{6,2},{3,7},{7,3},{8,12},{12,8},{9,1... | collective-permute-start | bytes 786440 | tf_op jit(solution)/shard_map/ppermute | solution.py:576
  11.1 1.5 %collective-permute-start.1 = (bf16[128,1024]{1,0:T(8,128)(2,1)}, bf16[128,1024]{1,0:T(8,128)(2,1)S(1)}, u32[]{:S(2)}, u32[]{:S(2)}) collective-permute-start(bf16[128,1024]{1,0:T(8,128)(2,1)} %refs_0_.1), channel_id=1, source_target_pairs={{0,2},{1,3},{2,0},{3,1},{4,6},{5,7},{6,4},{7,5},{8,10},{9,11},{10,... | collective-permute-start | bytes 786440 | tf_op jit(solution)/shard_map/ppermute | solution.py:575
  12.6 0.5 collective-permute-start.5
  13.1 2.5 %inner.1.refs_1_.refs_5_ = f32[256,1024]{1,0:T(8,128)S(1)} custom-call(bf16[256,128]{1,0:T(8,128)(2,1)} %bitcast.35, bf16[256,128]{1,0:T(8,128)(2,1)} %bitcast.30, bf16[256,1024]{1,0:T(8,128)(2,1)} %bitcast.21, f32[80,256]{1,0:T(8,128)S(1)} %get-tuple-element.48.refs_3_.refs_5_.refs_7_, f32[8,1024]{1,0:T(8,128)S(1)} %get-tuple-element.49.refs_4_.refs_6_, ...), custom_call_target="tpu_custom_call" | custom-call | bytes 18450000 | tf_op jit(solution)/shard_map/inner/pallas_call | solution.py:141
  15.5 3.3 %all-to-all-done.refs_0_.refs_1_ = bf16[4,272,128]{2,1,0:T(8,128)(2,1)S(1)} async-done(((bf16[4,272,128]{2,1,0:T(8,128)(2,1)}), bf16[4,272,128]{2,1,0:T(8,128)(2,1)S(1)}, u32[]{:S(2)}, u32[]{:S(2)}) %all-to-all-start) | async-done | bytes 278560 | tf_op jit(solution)/shard_map/all_to_all | solution.py:573
  18.8 0.8 prefix.1.refs_10_
  19.6 3.4 %all-to-all-start.1 = ((bf16[4,32,1024]{2,1,0:T(8,128)(2,1)}), bf16[4,32,1024]{2,1,0:T(8,128)(2,1)S(1)}, u32[]{:S(2)}, u32[]{:S(2)}) async-start(bf16[4,32,1024]{2,1,0:T(8,128)(2,1)} %prefix.1.refs_10_), calls=%async_computation.1 | async-start | bytes 524288 | tf_op jit(solution)/shard_map/all_to_all | solution.py:583
  23.0 0.1 collective-permute-start
  23.1 0.0 collective-permute-done.3.refs_4_
  23.1 0.0 copy-start.3
  23.1 0.5 collective-permute-start.4
  23.6 0.0 collective-permute-done.1.refs_2_
  23.6 0.1 collective-permute-start.2
  23.7 0.6 collective-permute-done.5.refs_6_
  24.3 0.0 collective-permute-start.6
  24.3 0.5 collective-permute-start.7
  24.9 0.1 pad_add_fusion.refs_9_.refs_2_.refs_1_.refs_10_.refs_0_
  24.9 0.0 collective-permute-done.refs_1_
  24.9 0.2 collective-permute-done.4.refs_5_
  25.1 0.4 collective-permute-done.2.refs_3_
  25.5 0.1 copy-done.6
  25.6 0.4 collective-permute-done.6.refs_7_
  26.0 3.6 %normed_grad.1 = (bf16[1024,1024]{1,0:T(8,128)(2,1)}, bf16[256,1024]{1,0:T(8,128)(2,1)S(1)}) custom-call(bf16[128,1024]{1,0:T(8,128)(2,1)} %refs_0_.1, bf16[128,1024]{1,0:T(8,128)(2,1)} %copy-done.6, bf16[128,1024]{1,0:T(8,128)(2,1)} %copy-done.4, bf16[128,1024]{1,0:T(8,128)(2,1)} %collective-permute-done.2.refs_3_, bf16[128,1024]{1,0:T(8,128)(2,1)} %copy-done.3, ...), custom_call_target="tpu_custom_call" | custom-call | bytes 36900000 | tf_op jit(solution)/shard_map/normed_grad/pallas_call | solution.py:141
  29.7 0.2 all-to-all-done.1
  29.8 3.3 %norm.1 = (bf16[256,1024]{1,0:T(8,128)(2,1)S(1)}, bf16[256,512]{1,0:T(8,128)(2,1)}, f32[256,1024]{1,0:T(8,128)S(1)}, f32[256,128]{1,0:T(8,128)S(1)}) custom-call(bf16[256,128]{1,0:T(8,128)(2,1)} %bitcast.31, bf16[256,1024]{1,0:T(8,128)(2,1)} %bitcast.25, s32[2]{0:T(128)S(1)} %pad_add_fusion.refs_9_.refs_2_.refs_1_.refs_10_.refs_0_, ...), custom_call_target="tpu_custom_call" | custom-call | bytes 14760000 | tf_op jit(solution)/shard_map/norm/pallas_call | solution.py:141
  33.1 0.0 copy-start.8
  33.1 3.8 %norm_back.1 = (bf16[256,1024]{1,0:T(8,128)(2,1)}, bf16[4,272,128]{2,1,0:T(8,128)(2,1)}, bf16[256,1024]{1,0:T(8,128)(2,1)}, f32[16,256]{1,0:T(8,128)}, f32[1,1024]{1,0:T(1,128)}, /*index=5*/f32[16,1]{1,0:T(8,128)}) custom-call(bf16[256,128]{1,0:T(8,128)(2,1)} %bitcast.32, bf16[256,1024]{1,0:T(8,128)(2,1)} %bitcast.26, bf16[256,1024]{1,0:T(8,128)(2,1)} %bitcast.22, ...), custom_call_target="tpu_custom_call" | custom-call | bytes 22140000 | tf_op jit(solution)/shard_map/norm_back/pallas_call | solution.py:141
  37.0 4.7 %all-to-all-start.2 = ((bf16[4,272,128]{2,1,0:T(8,128)(2,1)}), bf16[4,272,128]{2,1,0:T(8,128)(2,1)S(1)}, u32[]{:S(2)}, u32[]{:S(2)}) async-start(bf16[4,272,128]{2,1,0:T(8,128)(2,1)} %get-tuple-element.57.refs_5_), calls=%async_computation.2 | async-start | bytes 557056 | tf_op jit(solution)/shard_map/all_to_all | solution.py:644
  41.7 0.0 collective-permute-start.8
  41.7 0.0 collective-permute-done.7.refs_1_
  41.7 1.5 %collective-permute-done.8.refs_4_ = bf16[256,512]{1,0:T(8,128)(2,1)S(1)} collective-permute-done((bf16[256,512]{1,0:T(8,128)(2,1)S(1)}, bf16[256,512]{1,0:T(8,128)(2,1)S(1)}, u32[]{:S(2)}, u32[]{:S(2)}) %collective-permute-start.8) | collective-permute-done | bytes 262176 | tf_op jit(solution)/shard_map/ppermute | solution.py:636
  43.2 3.3 %outer.1 = (f32[128,1024]{1,0:T(8,128)}, bf16[128,1024]{1,0:T(8,128)(2,1)}, bf16[128,1024]{1,0:T(8,128)(2,1)}, bf16[128,1024]{1,0:T(8,128)(2,1)}) custom-call(bf16[256,1024]{1,0:T(8,128)(2,1)} %bitcast.28, bf16[256,1024]{1,0:T(8,128)(2,1)} %collective-permute-done.7.refs_1_, s32[2]{0:T(128)S(1)} %pad_add_fusion.refs_9_.refs_2_.refs_1_.refs_10_.refs_0_, ...), custom_call_target="tpu_custom_call" | custom-call | bytes 14760000 | tf_op jit(solution)/shard_map/outer/pallas_call | solution.py:141
  46.5 4.8 %all-to-all-done.2.refs_0_ = bf16[4,272,128]{2,1,0:T(8,128)(2,1)S(1)} async-done(((bf16[4,272,128]{2,1,0:T(8,128)(2,1)}), bf16[4,272,128]{2,1,0:T(8,128)(2,1)S(1)}, u32[]{:S(2)}, u32[]{:S(2)}) %all-to-all-start.2) | async-done | bytes 278560 | tf_op jit(solution)/shard_map/all_to_all | solution.py:644
  51.3 0.8 suffix.1
  52.0 3.4 %all-to-all-start.3 = ((bf16[4,32,1024]{2,1,0:T(8,128)(2,1)}), bf16[4,32,1024]{2,1,0:T(8,128)(2,1)S(1)}, u32[]{:S(2)}, u32[]{:S(2)}) async-start(bf16[4,32,1024]{2,1,0:T(8,128)(2,1)} %get-tuple-element.60.refs_9_), calls=%async_computation.3 | async-start | bytes 524288 | tf_op jit(solution)/shard_map/all_to_all | solution.py:649
  55.4 1.6 %collective-permute-start.9 = (bf16[128,1024]{1,0:T(8,128)(2,1)}, bf16[128,1024]{1,0:T(8,128)(2,1)S(1)}, u32[]{:S(2)}, u32[]{:S(2)}) collective-permute-start(bf16[128,1024]{1,0:T(8,128)(2,1)} %get-tuple-element.68), channel_id=1, source_target_pairs={{0,2},{1,3},{2,0},{3,1},{4,6},{5,7},{6,4},{7,5},{8,10},{9,11},{10,... | collective-permute-start | bytes 786440 | tf_op jit(solution)/shard_map/ppermute | solution.py:641
  57.0 1.5 %collective-permute-start.10 = (bf16[128,1024]{1,0:T(8,128)(2,1)}, bf16[128,1024]{1,0:T(8,128)(2,1)S(1)}, u32[]{:S(2)}, u32[]{:S(2)}) collective-permute-start(bf16[128,1024]{1,0:T(8,128)(2,1)} %get-tuple-element.69), channel_id=1, source_target_pairs={{0,4},{4,0},{1,5},{5,1},{2,6},{6,2},{3,7},{7,3},{8,12},{12,8},{9,1... | collective-permute-start | bytes 786440 | tf_op jit(solution)/shard_map/ppermute | solution.py:642
  58.5 0.5 collective-permute-start.11
  59.0 5.9 %back.1 = (bf16[256,1024]{1,0:T(8,128)(2,1)}, bf16[256,128]{1,0:T(8,128)(2,1)}, f32[256,1024]{1,0:T(8,128)}, bf16[256,128]{1,0:T(8,128)(2,1)}, f32[16,256]{1,0:T(8,128)}) custom-call(bf16[256,1024]{1,0:T(8,128)(2,1)} %get-tuple-element.55.refs_0_, bf16[256,128]{1,0:T(8,128)(2,1)} %bitcast.36, bf16[256,128]{1,0:T(8,128)(2,1)} %bitcast.33, ...), custom_call_target="tpu_custom_call" | custom-call | bytes 51660000 | tf_op jit(solution)/shard_map/back/pallas_call | solution.py:141
  64.9 0.0 collective-permute-done.9.refs_2_
  65.0 3.9 %collective-permute-done.10.refs_3_ = bf16[128,1024]{1,0:T(8,128)(2,1)S(1)} collective-permute-done((bf16[128,1024]{1,0:T(8,128)(2,1)}, bf16[128,1024]{1,0:T(8,128)(2,1)S(1)}, u32[]{:S(2)}, u32[]{:S(2)}) %collective-permute-start.10) | collective-permute-done | bytes 262176 | tf_op jit(solution)/shard_map/ppermute | solution.py:642
  68.8 0.0 collective-permute-done.11.refs_4_
  68.8 2.5 %add_chips.1 = (f32[32,1024]{1,0:T(8,128)}, bf16[32,1024]{1,0:T(8,128)(2,1)}, bf16[32,1024]{1,0:T(8,128)(2,1)}, bf16[32,1024]{1,0:T(8,128)(2,1)}) custom-call(f32[128,1024]{1,0:T(8,128)} %get-tuple-element.59.refs_2_.refs_0_, s32[2]{0:T(128)S(1)} %pad_add_fusion.refs_9_.refs_2_.refs_1_.refs_10_.refs_0_, ...), custom_call_target="tpu_custom_call" | custom-call | bytes 11070000 | tf_op jit(solution)/shard_map/add_chips/pallas_call | solution.py:141
  71.3 1.7 %collective-permute-start.12 = (bf16[32,1024]{1,0:T(8,128)(2,1)}, bf16[32,1024]{1,0:T(8,128)(2,1)S(1)}, u32[]{:S(2)}, u32[]{:S(2)}) collective-permute-start(bf16[32,1024]{1,0:T(8,128)(2,1)} %get-tuple-element.82), channel_id=1, source_target_pairs={{0,8},{8,16},{16,24},{24,0},{1,9},{9,17},{17,25},{25,1},{2,10},{10... | collective-permute-start | bytes 196616 | tf_op jit(solution)/shard_map/ppermute | solution.py:656
  73.0 2.4 %collective-permute-start.13 = (bf16[32,1024]{1,0:T(8,128)(2,1)}, bf16[32,1024]{1,0:T(8,128)(2,1)S(1)}, u32[]{:S(2)}, u32[]{:S(2)}) collective-permute-start(bf16[32,1024]{1,0:T(8,128)(2,1)} %get-tuple-element.83), channel_id=1, source_target_pairs={{0,16},{8,24},{16,0},{24,8},{1,17},{9,25},{17,1},{25,9},{2,18},{10... | collective-permute-start | bytes 196616 | tf_op jit(solution)/shard_map/ppermute | solution.py:656
  75.4 1.5 %collective-permute-start.14 = (bf16[32,1024]{1,0:T(8,128)(2,1)}, bf16[32,1024]{1,0:T(8,128)(2,1)S(1)}, u32[]{:S(2)}, u32[]{:S(2)}) collective-permute-start(bf16[32,1024]{1,0:T(8,128)(2,1)} %get-tuple-element.84), channel_id=1, source_target_pairs={{0,24},{8,0},{16,8},{24,16},{1,25},{9,1},{17,9},{25,17},{2,26},{10... | collective-permute-start | bytes 196616 | tf_op jit(solution)/shard_map/ppermute | solution.py:656
  76.8 0.0 all-to-all-done.3
  76.8 4.6 %last.1 = (bf16[256,1024]{1,0:T(8,128)(2,1)}, bf16[256,128]{1,0:T(8,128)(2,1)}, f32[16,256]{1,0:T(8,128)}, f32[32,1,384]{2,1,0:T(1,128)}) custom-call(bf16[256,128]{1,0:T(8,128)(2,1)} %bitcast.37, bf16[256,1024]{1,0:T(8,128)(2,1)} %bitcast.24, f32[16,256]{1,0:T(8,128)} %get-tuple-element.62.refs_2_, f32[16,256]{1,0:T(8,128)} %get-tuple-element.63.refs_5_.refs_3_, ...), custom_call_target="tpu_custom_call" | custom-call | bytes 22140000 | tf_op jit(solution)/shard_map/last/pallas_call | solution.py:141
  81.4 2.6 %all-to-all-start.4 = ((f32[32,1,384]{2,1,0:T(1,128)}), f32[32,1,384]{2,1,0:T(1,128)S(1)}, u32[]{:S(2)}, u32[]{:S(2)}) async-start(f32[32,1,384]{2,1,0:T(1,128)} %get-tuple-element.77), calls=%async_computation.4 | async-start | bytes 98304 | tf_op jit(solution)/shard_map/all_to_all | solution.py:664
  84.0 0.0 collective-permute-done.12.refs_1_
  84.0 0.0 collective-permute-done.13.refs_2_
  84.0 1.6 %add_blocks.1.refs_1_ = bf16[32,1024]{1,0:T(8,128)(2,1)} custom-call(f32[32,1024]{1,0:T(8,128)} %get-tuple-element.71.refs_12_.refs_0_, bf16[32,1024]{1,0:T(8,128)(2,1)S(1)} %collective-permute-done.12.refs_1_, bf16[32,1024]{1,0:T(8,128)(2,1)S(1)} %collective-permute-done.13.refs_2_, bf16[32,1024]{1,0:T(8,128)(2,1)S(1)} %collective-permute-done.14.refs_3_, ...), custom_call_target="tpu_custom_call" | custom-call | bytes 7380000 | tf_op jit(solution)/shard_map/add_blocks/pallas_call | solution.py:141
  85.6 3.7 %collective-permute-start.17 = (bf16[32,1024]{1,0:T(8,128)(2,1)}, bf16[32,1024]{1,0:T(8,128)(2,1)S(1)}, u32[]{:S(2)}, u32[]{:S(2)}) collective-permute-start(bf16[32,1024]{1,0:T(8,128)(2,1)} %add_blocks.1.refs_1_), channel_id=1, source_target_pairs={{0,24},{8,0},{16,8},{24,16},{1,25},{9,1},{17,9},{25,17},{2,26},{10... | collective-permute-start | bytes 196616 | tf_op jit(solution)/shard_map/ppermute | solution.py:662
  89.3 1.1 %collective-permute-start.15 = (bf16[32,1024]{1,0:T(8,128)(2,1)}, bf16[32,1024]{1,0:T(8,128)(2,1)S(1)}, u32[]{:S(2)}, u32[]{:S(2)}) collective-permute-start(bf16[32,1024]{1,0:T(8,128)(2,1)} %add_blocks.1.refs_1_), channel_id=1, source_target_pairs={{0,8},{8,16},{16,24},{24,0},{1,9},{9,17},{17,25},{25,1},{2,10},{10... | collective-permute-start | bytes 196616 | tf_op jit(solution)/shard_map/ppermute | solution.py:662
  90.4 1.7 %collective-permute-done.17.refs_4_ = bf16[32,1024]{1,0:T(8,128)(2,1)S(1)} collective-permute-done((bf16[32,1024]{1,0:T(8,128)(2,1)}, bf16[32,1024]{1,0:T(8,128)(2,1)S(1)}, u32[]{:S(2)}, u32[]{:S(2)}) %collective-permute-start.17) | collective-permute-done | bytes 65568 | tf_op jit(solution)/shard_map/ppermute | solution.py:662
  92.1 4.2 %collective-permute-done.16.refs_3_ = bf16[32,1024]{1,0:T(8,128)(2,1)S(1)} collective-permute-done((bf16[32,1024]{1,0:T(8,128)(2,1)}, bf16[32,1024]{1,0:T(8,128)(2,1)S(1)}, u32[]{:S(2)}, u32[]{:S(2)}) %collective-permute-start.16) | collective-permute-done | bytes 65568 | tf_op jit(solution)/shard_map/ppermute | solution.py:662
  96.3 0.0 collective-permute-done.15.refs_2_
  96.3 0.8 copy-done
  97.2 1.3 %join.1 = bf16[128,1024]{1,0:T(8,128)(2,1)} custom-call(s32[2]{0:T(128)S(1)} %pad_add_fusion.refs_9_.refs_2_.refs_1_.refs_10_.refs_0_, bf16[32,1024]{1,0:T(8,128)(2,1)S(1)} %copy-done, bf16[32,1024]{1,0:T(8,128)(2,1)S(1)} %collective-permute-done.15.refs_2_, bf16[32,1024]{1,0:T(8,128)(2,1)S(1)} %collective-permute-done.16.refs_3_, ...), custom_call_target="tpu_custom_call" | custom-call | bytes 11070000 | tf_op jit(solution)/shard_map/join/pallas_call | solution.py:141
  98.5 0.0 all-to-all-done.4.refs_0_
  98.5 0.6 copy-done.7
  99.1 1.4 %sums.1 = (f32[16]{0:T(128)}, f32[16]{0:T(128)}, f32[16]{0:T(128)}, f32[1024]{0:T(1024)}) custom-call(f32[32,1,384]{2,1,0:T(1,128)} %copy-done.7), custom_call_target="tpu_custom_call" | custom-call | bytes 7380000 | tf_op jit(solution)/shard_map/sums/pallas_call | solution.py:141
  (15 shorter events, 0.0 us)
Async XLA Ops:
  3.2 15.6 %all-to-all-start = ((bf16[4,272,128]{2,1,0:T(8,128)(2,1)}), bf16[4,272,128]{2,1,0:T(8,128)(2,1)S(1)}, u32[]{:S(2)}, u32[]{:S(2)}) async-start(bf16[4,272,128]{2,1,0:T(8,128)(2,1)} %get-tuple-element.50.refs_5_), calls=%async_computation | async-start | bytes 557056 | tf_op jit(solution)/shard_map/all_to_all | solution.py:573
  9.6 13.5 %collective-permute-start.3 = (bf16[128,1024]{1,0:T(8,128)(2,1)}, bf16[128,1024]{1,0:T(8,128)(2,1)S(1)}, u32[]{:S(2)}, u32[]{:S(2)}) collective-permute-start(bf16[128,1024]{1,0:T(8,128)(2,1)} %refs_0_.1), channel_id=1, source_target_pairs={{0,4},{4,0},{1,5},{5,1},{2,6},{6,2},{3,7},{7,3},{8,12},{12,8},{9,1... | collective-permute-start | bytes 786440 | tf_op jit(solution)/shard_map/ppermute | solution.py:576
  11.1 12.5 %collective-permute-start.1 = (bf16[128,1024]{1,0:T(8,128)(2,1)}, bf16[128,1024]{1,0:T(8,128)(2,1)S(1)}, u32[]{:S(2)}, u32[]{:S(2)}) collective-permute-start(bf16[128,1024]{1,0:T(8,128)(2,1)} %refs_0_.1), channel_id=1, source_target_pairs={{0,2},{1,3},{2,0},{3,1},{4,6},{5,7},{6,4},{7,5},{8,10},{9,11},{10,... | collective-permute-start | bytes 786440 | tf_op jit(solution)/shard_map/ppermute | solution.py:575
  12.6 11.8 %collective-permute-start.5 = (bf16[128,1024]{1,0:T(8,128)(2,1)}, bf16[128,1024]{1,0:T(8,128)(2,1)S(1)}, u32[]{:S(2)}, u32[]{:S(2)}) collective-permute-start(bf16[128,1024]{1,0:T(8,128)(2,1)} %refs_0_.1), channel_id=1, source_target_pairs={{0,6},{1,7},{2,4},{3,5},{4,2},{5,3},{6,0},{7,1},{8,14},{9,15},{10,... | collective-permute-start | bytes 786440 | tf_op jit(solution)/shard_map/ppermute | solution.py:577
  13.0 10.0 %copy-start.2 = (bf16[128,1024]{1,0:T(8,128)(2,1)S(1)}, bf16[128,1024]{1,0:T(8,128)(2,1)}, u32[]{:S(2)}) copy-start(bf16[128,1024]{1,0:T(8,128)(2,1)} %refs_0_.1) | copy-start | bytes 786436
  13.0 11.3 %copy-start.1 = (bf16[1,256,1024]{2,1,0:T(8,128)(2,1)S(1)}, bf16[1,256,1024]{2,1,0:T(8,128)(2,1)}, u32[]{:S(2)}) copy-start(bf16[1,256,1024]{2,1,0:T(8,128)(2,1)} %param.21) | copy-start | bytes 1572868
  19.6 10.2 %all-to-all-start.1 = ((bf16[4,32,1024]{2,1,0:T(8,128)(2,1)}), bf16[4,32,1024]{2,1,0:T(8,128)(2,1)S(1)}, u32[]{:S(2)}, u32[]{:S(2)}) async-start(bf16[4,32,1024]{2,1,0:T(8,128)(2,1)} %prefix.1.refs_10_), calls=%async_computation.1 | async-start | bytes 524288 | tf_op jit(solution)/shard_map/all_to_all | solution.py:583
  23.0 1.9 %collective-permute-start = (bf16[128,1024]{1,0:T(8,128)(2,1)S(1)}, bf16[128,1024]{1,0:T(8,128)(2,1)S(1)}, u32[]{:S(2)}, u32[]{:S(2)}) collective-permute-start(bf16[128,1024]{1,0:T(8,128)(2,1)S(1)} %copy-done.2), channel_id=1, source_target_pairs={{0,1},{1,0},{2,3},{3,2},{4,5},{5,4},{6,7},{7,6},{8,9},{9,8},{10,11... | collective-permute-start | bytes 786440 | tf_op jit(solution)/shard_map/ppermute | solution.py:578
  23.1 2.9 %copy-start.3 = (bf16[128,1024]{1,0:T(8,128)(2,1)}, bf16[128,1024]{1,0:T(8,128)(2,1)S(1)}, u32[]{:S(2)}) copy-start(bf16[128,1024]{1,0:T(8,128)(2,1)S(1)} %collective-permute-done.3.refs_4_) | copy-start | bytes 786436
  23.1 2.0 %collective-permute-start.4 = (bf16[128,1024]{1,0:T(8,128)(2,1)S(1)}, bf16[128,1024]{1,0:T(8,128)(2,1)}, u32[]{:S(2)}, u32[]{:S(2)}) collective-permute-start(bf16[128,1024]{1,0:T(8,128)(2,1)S(1)} %collective-permute-done.3.refs_4_), channel_id=1, source_target_pairs={{0,1},{1,0},{2,3},{3,2},{4,5},{5,4},{6,7},{7,6},{8,9},{9,8},{10,11... | collective-permute-start | bytes 786440 | tf_op jit(solution)/shard_map/ppermute | solution.py:578
  23.6 2.4 %copy-start.4 = (bf16[128,1024]{1,0:T(8,128)(2,1)}, bf16[128,1024]{1,0:T(8,128)(2,1)S(1)}, u32[]{:S(2)}) copy-start(bf16[128,1024]{1,0:T(8,128)(2,1)S(1)} %collective-permute-done.1.refs_2_) | copy-start | bytes 786436
  23.6 1.9 %collective-permute-start.2 = (bf16[128,1024]{1,0:T(8,128)(2,1)S(1)}, bf16[128,1024]{1,0:T(8,128)(2,1)}, u32[]{:S(2)}, u32[]{:S(2)}) collective-permute-start(bf16[128,1024]{1,0:T(8,128)(2,1)S(1)} %collective-permute-done.1.refs_2_), channel_id=1, source_target_pairs={{0,1},{1,0},{2,3},{3,2},{4,5},{5,4},{6,7},{7,6},{8,9},{9,8},{10,11... | collective-permute-start | bytes 786440 | tf_op jit(solution)/shard_map/ppermute | solution.py:578
  24.3 1.2 %copy-start.5 = (bf16[128,1024]{1,0:T(8,128)(2,1)}, bf16[128,1024]{1,0:T(8,128)(2,1)S(1)}, u32[]{:S(2)}) copy-start(bf16[128,1024]{1,0:T(8,128)(2,1)S(1)} %collective-permute-done.5.refs_6_) | copy-start | bytes 786436
  24.3 1.7 %collective-permute-start.6 = (bf16[128,1024]{1,0:T(8,128)(2,1)S(1)}, bf16[128,1024]{1,0:T(8,128)(2,1)}, u32[]{:S(2)}, u32[]{:S(2)}) collective-permute-start(bf16[128,1024]{1,0:T(8,128)(2,1)S(1)} %collective-permute-done.5.refs_6_), channel_id=1, source_target_pairs={{0,1},{1,0},{2,3},{3,2},{4,5},{5,4},{6,7},{7,6},{8,9},{9,8},{10,11... | collective-permute-start | bytes 786440 | tf_op jit(solution)/shard_map/ppermute | solution.py:578
  24.3 17.3 %collective-permute-start.7 = (bf16[256,1024]{1,0:T(8,128)(2,1)S(1)}, bf16[256,1024]{1,0:T(8,128)(2,1)}, u32[]{:S(2)}, u32[]{:S(2)}) collective-permute-start(bf16[256,1024]{1,0:T(8,128)(2,1)S(1)} %bitcast.29), channel_id=1, source_target_pairs={{0,1},{1,0},{2,3},{3,2},{4,5},{5,4},{6,7},{7,6},{8,9},{9,8},{10,11... | collective-permute-start | bytes 1572872 | tf_op jit(solution)/shard_map/ppermute | solution.py:574
  24.9 0.7 copy-start.6
  33.1 8.6 %copy-start.8 = (bf16[256,512]{1,0:T(8,128)(2,1)S(1)}, bf16[256,512]{1,0:T(8,128)(2,1)}, u32[]{:S(2)}) copy-start(bf16[256,512]{1,0:T(8,128)(2,1)} %get-tuple-element.58) | copy-start | bytes 786436
  37.0 14.3 %all-to-all-start.2 = ((bf16[4,272,128]{2,1,0:T(8,128)(2,1)}), bf16[4,272,128]{2,1,0:T(8,128)(2,1)S(1)}, u32[]{:S(2)}, u32[]{:S(2)}) async-start(bf16[4,272,128]{2,1,0:T(8,128)(2,1)} %get-tuple-element.57.refs_5_), calls=%async_computation.2 | async-start | bytes 557056 | tf_op jit(solution)/shard_map/all_to_all | solution.py:644
  41.7 1.5 %collective-permute-start.8 = (bf16[256,512]{1,0:T(8,128)(2,1)S(1)}, bf16[256,512]{1,0:T(8,128)(2,1)S(1)}, u32[]{:S(2)}, u32[]{:S(2)}) collective-permute-start(bf16[256,512]{1,0:T(8,128)(2,1)S(1)} %copy-done.8), channel_id=1, source_target_pairs={{0,1},{1,0},{2,3},{3,2},{4,5},{5,4},{6,7},{7,6},{8,9},{9,8},{10,11... | collective-permute-start | bytes 786440 | tf_op jit(solution)/shard_map/ppermute | solution.py:636
  52.0 24.8 %all-to-all-start.3 = ((bf16[4,32,1024]{2,1,0:T(8,128)(2,1)}), bf16[4,32,1024]{2,1,0:T(8,128)(2,1)S(1)}, u32[]{:S(2)}, u32[]{:S(2)}) async-start(bf16[4,32,1024]{2,1,0:T(8,128)(2,1)} %get-tuple-element.60.refs_9_), calls=%async_computation.3 | async-start | bytes 524288 | tf_op jit(solution)/shard_map/all_to_all | solution.py:649
  55.4 9.5 %collective-permute-start.9 = (bf16[128,1024]{1,0:T(8,128)(2,1)}, bf16[128,1024]{1,0:T(8,128)(2,1)S(1)}, u32[]{:S(2)}, u32[]{:S(2)}) collective-permute-start(bf16[128,1024]{1,0:T(8,128)(2,1)} %get-tuple-element.68), channel_id=1, source_target_pairs={{0,2},{1,3},{2,0},{3,1},{4,6},{5,7},{6,4},{7,5},{8,10},{9,11},{10,... | collective-permute-start | bytes 786440 | tf_op jit(solution)/shard_map/ppermute | solution.py:641
  57.0 11.8 %collective-permute-start.10 = (bf16[128,1024]{1,0:T(8,128)(2,1)}, bf16[128,1024]{1,0:T(8,128)(2,1)S(1)}, u32[]{:S(2)}, u32[]{:S(2)}) collective-permute-start(bf16[128,1024]{1,0:T(8,128)(2,1)} %get-tuple-element.69), channel_id=1, source_target_pairs={{0,4},{4,0},{1,5},{5,1},{2,6},{6,2},{3,7},{7,3},{8,12},{12,8},{9,1... | collective-permute-start | bytes 786440 | tf_op jit(solution)/shard_map/ppermute | solution.py:642
  58.5 10.3 %collective-permute-start.11 = (bf16[128,1024]{1,0:T(8,128)(2,1)}, bf16[128,1024]{1,0:T(8,128)(2,1)S(1)}, u32[]{:S(2)}, u32[]{:S(2)}) collective-permute-start(bf16[128,1024]{1,0:T(8,128)(2,1)} %get-tuple-element.70), channel_id=1, source_target_pairs={{0,6},{1,7},{2,4},{3,5},{4,2},{5,3},{6,0},{7,1},{8,14},{9,15},{10,... | collective-permute-start | bytes 786440 | tf_op jit(solution)/shard_map/ppermute | solution.py:643
  71.3 12.7 %collective-permute-start.12 = (bf16[32,1024]{1,0:T(8,128)(2,1)}, bf16[32,1024]{1,0:T(8,128)(2,1)S(1)}, u32[]{:S(2)}, u32[]{:S(2)}) collective-permute-start(bf16[32,1024]{1,0:T(8,128)(2,1)} %get-tuple-element.82), channel_id=1, source_target_pairs={{0,8},{8,16},{16,24},{24,0},{1,9},{9,17},{17,25},{25,1},{2,10},{10... | collective-permute-start | bytes 196616 | tf_op jit(solution)/shard_map/ppermute | solution.py:656
  73.0 11.0 %collective-permute-start.13 = (bf16[32,1024]{1,0:T(8,128)(2,1)}, bf16[32,1024]{1,0:T(8,128)(2,1)S(1)}, u32[]{:S(2)}, u32[]{:S(2)}) collective-permute-start(bf16[32,1024]{1,0:T(8,128)(2,1)} %get-tuple-element.83), channel_id=1, source_target_pairs={{0,16},{8,24},{16,0},{24,8},{1,17},{9,25},{17,1},{25,9},{2,18},{10... | collective-permute-start | bytes 196616 | tf_op jit(solution)/shard_map/ppermute | solution.py:656
  75.4 8.7 %collective-permute-start.14 = (bf16[32,1024]{1,0:T(8,128)(2,1)}, bf16[32,1024]{1,0:T(8,128)(2,1)S(1)}, u32[]{:S(2)}, u32[]{:S(2)}) collective-permute-start(bf16[32,1024]{1,0:T(8,128)(2,1)} %get-tuple-element.84), channel_id=1, source_target_pairs={{0,24},{8,0},{16,8},{24,16},{1,25},{9,1},{17,9},{25,17},{2,26},{10... | collective-permute-start | bytes 196616 | tf_op jit(solution)/shard_map/ppermute | solution.py:656
  81.4 17.0 %all-to-all-start.4 = ((f32[32,1,384]{2,1,0:T(1,128)}), f32[32,1,384]{2,1,0:T(1,128)S(1)}, u32[]{:S(2)}, u32[]{:S(2)}) async-start(f32[32,1,384]{2,1,0:T(1,128)} %get-tuple-element.77), calls=%async_computation.4 | async-start | bytes 98304 | tf_op jit(solution)/shard_map/all_to_all | solution.py:664
  85.6 6.5 %collective-permute-start.17 = (bf16[32,1024]{1,0:T(8,128)(2,1)}, bf16[32,1024]{1,0:T(8,128)(2,1)S(1)}, u32[]{:S(2)}, u32[]{:S(2)}) collective-permute-start(bf16[32,1024]{1,0:T(8,128)(2,1)} %add_blocks.1.refs_1_), channel_id=1, source_target_pairs={{0,24},{8,0},{16,8},{24,16},{1,25},{9,1},{17,9},{25,17},{2,26},{10... | collective-permute-start | bytes 196616 | tf_op jit(solution)/shard_map/ppermute | solution.py:662
  89.3 7.0 %collective-permute-start.16 = (bf16[32,1024]{1,0:T(8,128)(2,1)}, bf16[32,1024]{1,0:T(8,128)(2,1)S(1)}, u32[]{:S(2)}, u32[]{:S(2)}) collective-permute-start(bf16[32,1024]{1,0:T(8,128)(2,1)} %add_blocks.1.refs_1_), channel_id=1, source_target_pairs={{0,16},{8,24},{16,0},{24,8},{1,17},{9,25},{17,1},{25,9},{2,18},{10... | collective-permute-start | bytes 196616 | tf_op jit(solution)/shard_map/ppermute | solution.py:662
  89.3 7.0 %collective-permute-start.15 = (bf16[32,1024]{1,0:T(8,128)(2,1)}, bf16[32,1024]{1,0:T(8,128)(2,1)S(1)}, u32[]{:S(2)}, u32[]{:S(2)}) collective-permute-start(bf16[32,1024]{1,0:T(8,128)(2,1)} %add_blocks.1.refs_1_), channel_id=1, source_target_pairs={{0,8},{8,16},{16,24},{24,0},{1,9},{9,17},{17,25},{25,1},{2,10},{10... | collective-permute-start | bytes 196616 | tf_op jit(solution)/shard_map/ppermute | solution.py:662
  96.3 0.8 copy-start
  98.5 0.6 copy-start.7

commit v3 on v2

--- a/solution.py
+++ b/solution.py
@@ -12,8 +12,6 @@
 ROWS = ((0,), (0,))
 LAST = ((1,), (1,))
 CHUNKS = 8
-HBM_BYTES_PER_US = 3.69e6
-TM = 4
 VMEM_LIMIT = 24 * 1024 * 1024
 
 
@@ -117,7 +115,7 @@
     return jax.ShapeDtypeStruct(shape, dtype)
 
 
-def call(kernel, outs, far, *args, smem=(), name=None, scratch=(), after=(), beside=(), us=3):
+def call(kernel, outs, far, *args, smem=(), name=None, scratch=(), after=(), beside=()):
     waits = len(after) + len(beside)
     specs = [pl.BlockSpec(memory_space=pl.ANY)] * len(far)
     specs += [
@@ -145,7 +143,6 @@
         out_specs=[pl.BlockSpec(memory_space=pltpu.VMEM)] * len(outs),
         scratch_shapes=list(scratch) + landing + semaphores,
         compiler_params=pltpu.CompilerParams(vmem_limit_bytes=VMEM_LIMIT),
-        cost_estimate=pl.CostEstimate(flops=0, bytes_accessed=int(us * HBM_BYTES_PER_US), transcendentals=0),
         name=name,
     )(*[pltpu.with_memory_space_constraint(v, pltpu.HBM) for v in far], *args, *[pltpu.with_memory_space_constraint(v, pltpu.HBM) for v in after], *beside)
 
@@ -212,7 +209,8 @@
                 carried = state + part_decay(all_ref, k, n, rows, blocks) * carried
 
 
-def suffix_kernel(grads_ref, all_ref, out_ref, gains_ref):
+def suffix_kernel(grads_ref, all_ref, pos_ref, *refs):
+    outs, gains_ref, out_ref = refs[:-2], refs[-2], refs[-1]
     count, rows, width = out_ref.shape
     blocks = width // 128
     for n in range(blocks):
@@ -223,6 +221,8 @@
             if k > 0:
                 grad = grads_ref[k, n * rows : (n + 1) * rows, :].astype(F32)
                 carried = grad + part_decay(all_ref, k, n, rows, blocks) * carried
+    for k, part_ref in enumerate(outs):
+        part_ref[...] = out_ref[lax.rem(pos_ref[1] + k, count)]
     gains = sum(grads_ref[k, blocks * rows :, :].astype(F32) for k in range(count))
     gains_ref[...] = gains[:blocks] + gains[blocks:]
 
@@ -350,36 +350,28 @@
     skips_ref[...] = jnp.sum(skips * hmap, axis=1, keepdims=True)
 
 
-def outer_kernel(g_in, gc_in, idx_ref, normed_ref, got_ref, keep_ref, *sends):
+def outer_kernel(g_in, gc_in, idx_ref, normed_ref, got_ref, out_ref):
     g_ref, gc_ref = g_in.ready(), gc_in.ready()
-    me = idx_ref[0]
-    core, chip = lax.rem(me, 2), me // 2
-    rows = keep_ref.shape[0]
-    for k, out_ref in enumerate((keep_ref, *sends)):
-        mine = pl.ds(pl.multiple_of((2 * (chip ^ k) + core) * rows, rows), rows)
-        theirs = pl.ds(pl.multiple_of((chip ^ k) * rows, rows), rows)
-        part = mm_tn(normed_ref[:, mine], g_ref[...]) + mm_tn(got_ref[:, theirs], gc_ref[...])
-        out_ref[...] = part.astype(out_ref.dtype)
-
-
-def add_kernel(keep_in, pos_ref, *refs):
-    gots, outs, scratch = refs[:3], refs[3:-1], refs[-1]
-    total = keep_in.ready()[...]
-    for got in gots:
-        total = total + got[...].astype(F32)
-    scratch[...] = total
-    rows = outs[0].shape[0]
-    for k, out_ref in enumerate(outs):
-        at = lax.rem(pos_ref[1] + k, len(outs)) * rows
-        out_ref[...] = scratch[pl.ds(pl.multiple_of(at, rows), rows), :].astype(out_ref.dtype)
-
-
-def add_quarter_kernel(own_in, *refs):
-    gots, out_ref = refs[:-1], refs[-1]
-    total = own_in.ready()[...]
-    for got in gots:
-        total = total + got[...].astype(F32)
-    out_ref[...] = total.astype(BF)
+    core = lax.rem(idx_ref[0], 2)
+    chips, rows = out_ref.shape[:2]
+    for k in range(chips):
+        mine = pl.ds(pl.multiple_of((2 * k + core) * rows, rows), rows)
+        part = mm_tn(normed_ref[:, mine], g_ref[...]) + mm_tn(got_ref[:, k * rows : (k + 1) * rows], gc_ref[...])
+        out_ref[k] = part.astype(BF)
+
+
+def add_kernel(all_ref, out_ref):
+    total = all_ref[0].astype(F32)
+    for k in range(1, all_ref.shape[0]):
+        total = total + all_ref[k].astype(F32)
+    total = total.astype(BF)
+    rows = out_ref.shape[1]
+    for k in range(out_ref.shape[0]):
+        out_ref[k] = total[k * rows : (k + 1) * rows]
+
+
+def mixed_kernel(full_in, normed_ref, mixed_ref):
+    mixed_ref[...] = mm(normed_ref[...], full_in.ready()[...]).astype(BF)
 
 
 def join_kernel(*refs):
@@ -395,8 +387,8 @@
 
 
 def back_kernel(
-    dy_in, b_in, c_in, x_in, full_in, aux_ref, params_ref, inc_ref, normed_ref,
-    mixed_ref, cg_ref, xg_ref, bg_ref, cols_ref, dxw_ref,
+    dy_in, b_in, c_in, x_in, aux_ref, params_ref, inc_ref,
+    cg_ref, xg_ref, bg_ref, cols_ref, dxw_ref,
 ):
     _, delta, _, cum, _ = load_decay(aux_ref)
     x_ref, b_ref, c_ref = x_in.ready(), b_in.ready(), c_in.ready()
@@ -459,13 +451,17 @@
     cols_ref[...] = head_sums(xd.astype(F32) * dxw, hmap)
     skip = params_ref[0:1, :]
     xg_ref[...] = delta_e * dxw + skip * dy.astype(F32)
-    mixed_ref[...] = mm(normed_ref[...], full_in.ready()[...]).astype(BF)
 
 
 def last_kernel(
-    b_in, x_in, rows_in, cols_in, bg_in, xg_in, skips_in, aux_ref, later_ref, inc_ref, *more,
+    gains_here, b_in, x_in, rows_in, cols_in, bg_in, xg_in, skips_in, pos_ref, aux_ref, inc_ref, *more,
 ):
-    more, (x_out, b_out, step_out, sums_out) = more[:-4], more[-4:]
+    parts, (x_out, b_out, step_out, sums_out, later_ref) = more[:-5], more[-5:]
+    gains_ref, parts = (parts[0], parts[1:]) if gains_here else (None, parts)
+    count, part = len(parts), parts[0].shape[0]
+    for k, one in enumerate(parts):
+        at = lax.rem(pos_ref[1] + count - k, count) * part
+        later_ref[pl.ds(pl.multiple_of(at, part), part), :] = one[...]
     v, delta, ld, cum, a = load_decay(aux_ref)
     x_ref, b_ref = x_in.ready(), b_in.ready()
     heads, length = cum.shape
@@ -499,17 +495,14 @@
         return jnp.sum(jnp.where(j == i + at, col, 0.0), axis=0, keepdims=True)
 
     small = lay(drate, 0) + lay(dbias, heads) + lay(skips_in.ready()[...], 2 * heads)
-    sums_out[0, :, :128] = small
-    if len(more) == 2:
-        pos_ref, gains_ref = more
-        each = gains_ref.shape[0] // TM
-        for n in range(each):
-            at = pl.ds(pos_ref[1] * each + n, 1)
-            sums_out[0, :, (n + 1) * 128 : (n + 2) * 128] = gains_ref[at, :]
-        for k in range(1, sums_out.shape[0]):
-            sums_out[k] = sums_out[0]
-    else:
-        sums_out[0, :, 128:] = more[0][...]
+    if gains_ref is None:
+        sums_out[0] = small
+        return
+    each = gains_ref.shape[0] // count
+    shares = [gains_ref[pl.ds(pos_ref[1] * each + n, 1), :] for n in range(each)]
+    row = jnp.concatenate([small] + shares, axis=1)
+    for k in range(sums_out.shape[0]):
+        sums_out[k] = row
 
 
 def sums_kernel(all_in, rate_out, bias_out, skip_out, gain_out):
@@ -568,7 +561,7 @@
         blocks_of = width // 128
         part_shape = (n_tm, blocks_of * part[1] + 2 * blocks_of, 128)
         aux, params, payload = call(
-            payload_kernel, aux_shapes + [(part_shape, BF, away)], raw, name="state", us=3,
+            payload_kernel, aux_shapes + [(part_shape, BF, away)], raw, name="state",
         )
         blocks = lax.all_to_all(payload, "tm", 0, 0, tiled=True)
         gc = lax.ppermute(g, "rep", core)
@@ -577,27 +570,27 @@
         wd = lax.ppermute(out_weight, ("tok", "rep"), diagonal)
         wc, wxc, wyc, wdc = (lax.ppermute(v, "rep", core) for v in (out_weight, wx, wy, wd))
         (local,) = call(
-            inner_kernel, [(wide, F32, near_by)], (b, c, x), aux, params, name="inner", us=5, after=(payload,)
-        )
-        (prefixes,) = call(prefix_kernel, [(part + (width,), BF, away)], (), blocks, name="prefix", us=1, beside=(local,))
+            inner_kernel, [(wide, F32, near_by)], (b, c, x), aux, params, name="inner", after=(payload,)
+        )
+        (prefixes,) = call(prefix_kernel, [(part + (width,), BF, away)], (), blocks, name="prefix", beside=(local,))
         incoming = lax.all_to_all(prefixes, "tm", 0, 0, tiled=True).reshape(state_size, width)
         pieces = (out_weight, wc, wx, wxc, wy, wyc, wd, wdc)
         weight, ng = call(
             weight_kernel, [(full, BF, away), (wide, BF, near_by)], (*pieces, g), place,
-            smem=(0,), name="normed_grad", us=10, after=(prefixes,),
+            smem=(0,), name="normed_grad", after=(prefixes,),
         )
     else:
         aux, params, state, total = call(
-            payload_kernel, aux_shapes + [((state_size, width), BF, free), ((1, width), F32, free)], raw, name="state", us=3
+            payload_kernel, aux_shapes + [((state_size, width), BF, free), ((1, width), F32, free)], raw, name="state"
         )
         incoming = scan_far(state, total, "tm", False)
-        (local,) = call(inner_kernel, [(wide, F32, near_by)], (b, c, x), aux, params, name="inner", us=5)
+        (local,) = call(inner_kernel, [(wide, F32, near_by)], (b, c, x), aux, params, name="inner")
         weight = lax.all_gather(out_weight, ("tok", "rep"), axis=0, tiled=True)
-        (ng,) = call(grad_kernel, [(wide, BF, near_by)], (), g, weight, name="normed_grad", us=10)
+        (ng,) = call(grad_kernel, [(wide, BF, near_by)], (), g, weight, name="normed_grad")
     normed, other, inner, factor = call(
         norm_kernel,
         [(wide, BF, near_by), ((length, width // 2), BF, away), (wide, F32, near_by), ((length, 128), F32, near_by)],
-        (c, z), place, aux, params, local, incoming, name="norm", us=4, smem=(0,), scratch=[pltpu.VMEM(wide, F32)], after=(weight,),
+        (c, z), place, aux, params, local, incoming, name="norm", smem=(0,), scratch=[pltpu.VMEM(wide, F32)], after=(weight,),
     )
     dy, carry, zg, row_sums, gains, skips = call(
         norm_back_kernel,
@@ -605,73 +598,73 @@
             (wide, BF, away), (part_shape if near else (state_size, width), BF, away), (wide, BF, away),
             ((heads, length), F32, away), ((1, width), F32, away), ((heads, 1), F32, away),
         ],
-        (c, z, x), aux, params, inner, factor, ng, name="norm_back", us=6,
+        (c, z, x), aux, params, inner, factor, ng, name="norm_back",
         scratch=[pltpu.VMEM(wide, F32)] + [pltpu.VMEM(wide, BF)] * 3,
     )
+
+    def mixed_of(*after):
+        return call(mixed_kernel, [(wide, BF, away)], (weight,), normed, name="mixed", after=after)[0]
 
     def back(*after):
         return call(
             back_kernel,
             [
-                (wide, BF, away), ((length, state_size), BF, away), (wide, F32, away), ((length, state_size), BF, away),
+                ((length, state_size), BF, away), (wide, F32, away), ((length, state_size), BF, away),
                 ((heads, length), F32, away),
             ],
-            (dy, b, c, x, weight), aux, params, incoming, normed,
-            name="back", us=14, scratch=[pltpu.VMEM(wide, F32)], after=after,
+            (dy, b, c, x), aux, params, incoming,
+            name="back", scratch=[pltpu.VMEM(wide, F32)], after=after,
         )
 
     everywhere = ("tm", "tok", "rep")
+
+    def last(row, parts, *more, after=()):
+        return call(
+            functools.partial(last_kernel, bool(more)),
+            [(wide, BF, away), ((length, state_size), BF, away), ((heads, length), F32, away), (row, F32, away)],
+            (b, x, row_sums, col_sums, bg, xg, skips), place, aux, incoming, *more, *parts, name="last", after=after,
+            smem=(0,), scratch=[pltpu.VMEM((state_size, width), BF)],
+        )
+
     ahead = [[(i, (i + k) % n_tm) for i in range(n_tm)] for k in range(1, n_tm)]
-
-    def last(row, far, *more):
-        return call(
-            last_kernel,
-            [(wide, BF, away), ((length, state_size), BF, away), ((heads, length), F32, away), (row, F32, away)],
-            (b, x, row_sums, col_sums, bg, xg, skips), aux, later, incoming, *more, name="last", us=6, after=far,
-            smem=(3,) if near else (),
-        )
-
     if near:
-        block = (rows, model)
         theirs = lax.ppermute(other, "rep", core)
-        keep, sx, sy, sd = call(
-            outer_kernel, [(block, F32, away)] + [(block, BF, away)] * 3, (g, gc), place, normed, theirs,
-            smem=(0,), name="outer", us=4, after=(carry,),
-        )
-        gx = lax.ppermute(sx, "rep", side)
-        gy = lax.ppermute(sy, "tok", front)
-        gd = lax.ppermute(sd, ("tok", "rep"), diagonal)
+        (products,) = call(
+            outer_kernel, [((4, rows, model), BF, away)], (g, gc), place, normed, theirs,
+            smem=(0,), name="outer", after=(carry,),
+        )
         grads = lax.all_to_all(carry, "tm", 0, 0, tiled=True)
-        suffixes, gains = call(
-            suffix_kernel, [(part + (width,), BF, away), ((blocks_of, 128), F32, near_by)], (), grads, blocks,
-            name="suffix", us=1, after=(keep,),
-        )
-        later = lax.all_to_all(suffixes, "tm", 0, 0, tiled=True).reshape(state_size, width)
-        mixed, c_grad, xg, bg, col_sums = back(suffixes)
-        quarter = (rows // n_tm, model)
-        own, *sends = call(
-            add_kernel, [(quarter, F32, away)] + [(quarter, BF, away)] * (n_tm - 1), (keep,), place, gx, gy, gd,
-            smem=(0,), name="add_chips", us=3, scratch=[pltpu.VMEM(block, F32)], after=(col_sums,),
-        )
-        gots = [lax.ppermute(v, "tm", pairs) for v, pairs in zip(sends, ahead)]
+        own, *sends, gains = call(
+            suffix_kernel, [(part[1:] + (width,), BF, away)] * n_tm + [((blocks_of, 128), F32, near_by)], (), grads, blocks, place,
+            name="suffix", smem=(2,), scratch=[pltpu.VMEM(part + (width,), BF)], after=(products,),
+        )
+        parts = [own] + [lax.ppermute(v, "tm", pairs) for v, pairs in zip(sends, ahead)]
+        (products,) = lax.optimization_barrier((products,))
+        chips = lax.all_to_all(
+            products, ("tok", "rep"), 0, 0, axis_index_groups=[[0, 2, 4, 6], [1, 3, 5, 7]], tiled=True
+        )
+        c_grad, xg, bg, col_sums = back(own)
+        mixed = mixed_of(col_sums)
+        quarters = (n_tm, rows // n_tm, model)
+        (share,) = call(add_kernel, [(quarters, BF, away)], (), chips, name="add_chips", after=(mixed,), beside=parts[1:])
+        shares = lax.all_to_all(share, "tm", 0, 0, tiled=True)
         row = (n_tm * n_tok * n_rep, 1, 128 + width // n_tm)
-        x_grad, b_grad, step_grad, sums = last(row, (own,), place, gains)
-        (total_quarter,) = call(
-            add_quarter_kernel, [(quarter, BF, away)], (own,), *gots, name="add_blocks", us=2, after=(step_grad,)
-        )
-        quarters = [total_quarter] + [lax.ppermute(total_quarter, "tm", pairs) for pairs in ahead]
-        (weight_grad,) = call(join_kernel, [(block, BF, away)], (), place, *quarters, smem=(0,), name="join", us=3)
+        x_grad, b_grad, step_grad, sums = last(row, parts, gains, after=(share,))
+        (quarter,) = call(add_kernel, [((1,) + quarters[1:], BF, away)], (), shares, name="add_blocks", after=(step_grad,))
+        pieces = [quarter[0]] + [lax.ppermute(quarter[0], "tm", pairs) for pairs in ahead]
+        (weight_grad,) = call(join_kernel, [((rows, model), BF, away)], (), place, *pieces, smem=(0,), name="join")
         sums = lax.all_to_all(sums, everywhere, 0, 0, tiled=True)
     else:
         later = scan_far(carry, total, "tm", True)
-        (outer,) = call(outer_full_kernel, [(full, F32, free)], (), normed, g, name="outer", us=4)
+        (outer,) = call(outer_full_kernel, [(full, F32, free)], (), normed, g, name="outer")
         share = lax.psum_scatter(outer, ("tok", "rep"), scatter_dimension=0, tiled=True)
         weight_grad = lax.psum(share, "tm").astype(BF)
-        mixed, c_grad, xg, bg, col_sums = back()
-        x_grad, b_grad, step_grad, sums = last((1, 1, 128 + width), (), gains)
-        sums = lax.psum(sums, everywhere)
+        mixed = mixed_of()
+        c_grad, xg, bg, col_sums = back()
+        x_grad, b_grad, step_grad, sums = last((1, 1, 128), (later,))
+        sums = lax.psum(jnp.concatenate([sums, gains[None]], axis=2), everywhere)
     rate_grad, bias_grad, skip_grad, gain_grad = call(
-        sums_kernel, [((heads,), F32, away)] * 3 + [((width,), F32, away)], (sums,), name="sums", us=2
+        sums_kernel, [((heads,), F32, away)] * 3 + [((width,), F32, away)], (sums,), name="sums"
     )
     return (
         mixed[None], x_grad[None], zg[None], b_grad[None], c_grad[None], step_grad[None],

time: 101 us -> 97.3 us (0.963)
  waiting for transfers between devices: 21.2 us -> 16.1 us
  starting transfers between devices: 38.9 us -> 40 us
    ppermute x9 -> x6, waiting for transfers between devices: 9.85 us -> 0.77 us  [the longest x3 0.76 us: shards(): lax.ppermute(quarter[0], 'tm', pairs)]
    ppermute x9 -> x6, starting transfers between devices: 13.8 us -> 7.89 us  [the longest x3 5.6 us: shards(): lax.ppermute(quarter[0], 'tm', pairs)]
    all_to_all x1 -> x2, starting transfers between devices: 3.4 us -> 8.04 us  [the longest x1 4.53 us: shards(): shares = lax.all_to_all(share, 'tm', 0, 0, tiled=True)]
    all_to_all x1 -> x2, waiting for transfers between devices: 0.01 us -> 2.76 us  [the longest x1 2.18 us: shards(): shares = lax.all_to_all(share, 'tm', 0, 0, tiled=True)]
    all_to_all x1, starting transfers between devices: 2.56 us -> 4.85 us  [shards(): sums = lax.all_to_all(sums, everywhere, 0, 0, tiled=True)]
    all_to_all x1, waiting for transfers between devices: 0.01 us -> 1.07 us  [shards(): sums = lax.all_to_all(sums, everywhere, 0, 0, tiled=True)]
    pallas_call x14 -> x15, Pallas kernels: 37.9 us -> 37.9 us  [call(): pl.pallas_call(body, out_shape=[where(shape, dtype) for shape, dtype, whe...]
  transfers between devices with their start and end apart: 23 -> 21, of which waited for: 11 -> 12; matrix products, arithmetic and copies ran while one was open for 0% -> 0% of each run, Pallas kernels for 33% -> 35%
where the time goes in v3:
time: 97.3 us; the launch traced here: 96.4 us
  starting transfers between devices  40 us (41%)
  Pallas kernels  37.9 us (39%)
  waiting for transfers between devices  16.1 us (17%)
  local copies, waits for them, and re-layouts  1.49 us (2%)
    pallas_call x15, Pallas kernels, call(): pl.pallas_call(body, out_shape=[where(shape, dtype) for shape, dtype, whe...  37.9 us
    all_to_all x1, starting transfers between devices, shards(): blocks = lax.all_to_all(payload, 'tm', 0, 0, tiled=True)  6.33 us
    ppermute x3, starting transfers between devices, shards(): lax.ppermute(quarter[0], 'tm', pairs)  5.6 us
    all_to_all x1, starting transfers between devices, shards(): sums = lax.all_to_all(sums, everywhere, 0, 0, tiled=True)  4.85 us
    all_to_all x1, starting transfers between devices, shards(): grads = lax.all_to_all(carry, 'tm', 0, 0, tiled=True)  4.82 us
    all_to_all x1, waiting for transfers between devices, shards(): grads = lax.all_to_all(carry, 'tm', 0, 0, tiled=True)  4.54 us
    all_to_all x1, starting transfers between devices, shards(): shares = lax.all_to_all(share, 'tm', 0, 0, tiled=True)  4.53 us
    all_to_all x1, starting transfers between devices, shards(): lax.all_to_all(products, ('tok', 'rep'), 0, 0, axis_index_groups=[[0, 2,...  3.52 us
  transfers between devices with their start and end apart: 21, of which 12 were waited for; matrix products, arithmetic and copies ran while one was open for 0% of the time, Pallas kernels for 35%

profile of v3, /device:TPU:0, one launch (start us, length us, event | category | flops | bytes accessed | tf_op | source)
XLA Modules:
  0.0 96.4 jit_solution(10888917522551251108)
XLA Ops:
  0.6 2.6 %state.1 = (f32[80,256]{1,0:T(8,128)S(1)}, f32[8,1024]{1,0:T(8,128)S(1)}, bf16[4,272,128]{2,1,0:T(8,128)(2,1)}) custom-call(f32[16,256]{1,0:T(8,128)} %bitcast.42, f32[16]{0:T(128)} %refs_1_.1, f32[16]{0:T(128)} %refs_2_.1, bf16[256,128]{1,0:T(8,128)(2,1)} %bitcast.38, bf16[256,1024]{1,0:T(8,128)(2,1)} %bitcast.23, f32[16]{0:T(128)} %refs_5_.1, f32[1024]{0:T(1024)} %refs_6_.1), custom_call_target="tpu_custom_call" | custom-call | tf_op jit(solution)/shard_map/state/pallas_call | solution.py:139
  3.2 6.3 %all-to-all-start = ((bf16[4,272,128]{2,1,0:T(8,128)(2,1)}), bf16[4,272,128]{2,1,0:T(8,128)(2,1)S(1)}, u32[]{:S(2)}, u32[]{:S(2)}) async-start(bf16[4,272,128]{2,1,0:T(8,128)(2,1)} %get-tuple-element.42.refs_5_), calls=%async_computation | async-start | bytes 557056 | tf_op jit(solution)/shard_map/all_to_all | solution.py:566
  9.6 1.5 %collective-permute-start.1 = (bf16[128,1024]{1,0:T(8,128)(2,1)}, bf16[128,1024]{1,0:T(8,128)(2,1)S(1)}, u32[]{:S(2)}, u32[]{:S(2)}) collective-permute-start(bf16[128,1024]{1,0:T(8,128)(2,1)} %refs_0_.1), channel_id=1, source_target_pairs={{0,2},{1,3},{2,0},{3,1},{4,6},{5,7},{6,4},{7,5},{8,10},{9,11},{10,... | collective-permute-start | bytes 786440 | tf_op jit(solution)/shard_map/ppermute | solution.py:568
  11.0 1.5 %collective-permute-start.3 = (bf16[128,1024]{1,0:T(8,128)(2,1)}, bf16[128,1024]{1,0:T(8,128)(2,1)S(1)}, u32[]{:S(2)}, u32[]{:S(2)}) collective-permute-start(bf16[128,1024]{1,0:T(8,128)(2,1)} %refs_0_.1), channel_id=1, source_target_pairs={{0,4},{4,0},{1,5},{5,1},{2,6},{6,2},{3,7},{7,3},{8,12},{12,8},{9,1... | collective-permute-start | bytes 786440 | tf_op jit(solution)/shard_map/ppermute | solution.py:569
  12.6 0.5 collective-permute-start.5
  13.1 2.5 %inner.1.refs_1_.refs_5_ = f32[256,1024]{1,0:T(8,128)S(1)} custom-call(bf16[256,128]{1,0:T(8,128)(2,1)} %bitcast.39, bf16[256,128]{1,0:T(8,128)(2,1)} %bitcast.34, bf16[256,1024]{1,0:T(8,128)(2,1)} %bitcast.24, f32[80,256]{1,0:T(8,128)S(1)} %get-tuple-element.43.refs_3_.refs_4_.refs_8_, f32[8,1024]{1,0:T(8,128)S(1)} %get-tuple-element.44.refs_4_.refs_5_, ...), custom_call_target="tpu_custom_call" | custom-call | tf_op jit(solution)/shard_map/inner/pallas_call | solution.py:139
  15.5 3.3 %all-to-all-done.refs_0_.refs_1_ = bf16[4,272,128]{2,1,0:T(8,128)(2,1)S(1)} async-done(((bf16[4,272,128]{2,1,0:T(8,128)(2,1)}), bf16[4,272,128]{2,1,0:T(8,128)(2,1)S(1)}, u32[]{:S(2)}, u32[]{:S(2)}) %all-to-all-start) | async-done | bytes 278560 | tf_op jit(solution)/shard_map/all_to_all | solution.py:566
  18.8 0.8 prefix.1.refs_10_
  19.6 3.4 %all-to-all-start.1 = ((bf16[4,32,1024]{2,1,0:T(8,128)(2,1)}), bf16[4,32,1024]{2,1,0:T(8,128)(2,1)S(1)}, u32[]{:S(2)}, u32[]{:S(2)}) async-start(bf16[4,32,1024]{2,1,0:T(8,128)(2,1)} %prefix.1.refs_10_), calls=%async_computation.1 | async-start | bytes 524288 | tf_op jit(solution)/shard_map/all_to_all | solution.py:576
  23.0 0.1 collective-permute-start
  23.1 0.0 collective-permute-done.1.refs_2_
  23.1 0.0 copy-start.4
  23.1 0.5 collective-permute-start.2
  23.6 0.8 collective-permute-done.3.refs_4_
  24.4 0.0 collective-permute-start.4
  24.4 0.0 collective-permute-done.5.refs_6_
  24.4 0.0 copy-start.6
  24.4 0.5 collective-permute-start.6
  24.9 0.1 collective-permute-start.7
  25.0 0.1 pad_add_fusion.refs_9_.refs_2_.refs_7_.refs_0_
  25.0 0.0 collective-permute-done.refs_1_
  25.0 0.1 collective-permute-done.2.refs_3_
  25.1 0.9 collective-permute-done.4.refs_5_
  26.0 0.4 collective-permute-done.6.refs_7_
  26.4 3.7 %normed_grad.1 = (bf16[1024,1024]{1,0:T(8,128)(2,1)}, bf16[256,1024]{1,0:T(8,128)(2,1)S(1)}) custom-call(bf16[128,1024]{1,0:T(8,128)(2,1)} %refs_0_.1, bf16[128,1024]{1,0:T(8,128)(2,1)} %copy-done.7, bf16[128,1024]{1,0:T(8,128)(2,1)} %copy-done.4, bf16[128,1024]{1,0:T(8,128)(2,1)} %collective-permute-done.2.refs_3_, bf16[128,1024]{1,0:T(8,128)(2,1)} %copy-done.5, ...), custom_call_target="tpu_custom_call" | custom-call | tf_op jit(solution)/shard_map/normed_grad/pallas_call | solution.py:139
  30.1 0.0 all-to-all-done.1
  30.1 3.3 %norm.1 = (bf16[256,1024]{1,0:T(8,128)(2,1)S(1)}, bf16[256,512]{1,0:T(8,128)(2,1)}, f32[256,1024]{1,0:T(8,128)S(1)}, f32[256,128]{1,0:T(8,128)S(1)}) custom-call(bf16[256,128]{1,0:T(8,128)(2,1)} %bitcast.35, bf16[256,1024]{1,0:T(8,128)(2,1)} %bitcast.28, s32[2]{0:T(128)S(1)} %pad_add_fusion.refs_9_.refs_2_.refs_7_.refs_0_, ...), custom_call_target="tpu_custom_call" | custom-call | tf_op jit(solution)/shard_map/norm/pallas_call | solution.py:139
  33.4 0.0 copy-start.9
  33.4 3.8 %norm_back.1 = (bf16[256,1024]{1,0:T(8,128)(2,1)}, bf16[4,272,128]{2,1,0:T(8,128)(2,1)}, bf16[256,1024]{1,0:T(8,128)(2,1)}, f32[16,256]{1,0:T(8,128)}, f32[1,1024]{1,0:T(1,128)}, /*index=5*/f32[16,1]{1,0:T(8,128)}) custom-call(bf16[256,128]{1,0:T(8,128)(2,1)} %bitcast.36, bf16[256,1024]{1,0:T(8,128)(2,1)} %bitcast.29, bf16[256,1024]{1,0:T(8,128)(2,1)} %bitcast.25, ...), custom_call_target="tpu_custom_call" | custom-call | tf_op jit(solution)/shard_map/norm_back/pallas_call | solution.py:139
  37.1 4.8 %all-to-all-start.2 = ((bf16[4,272,128]{2,1,0:T(8,128)(2,1)}), bf16[4,272,128]{2,1,0:T(8,128)(2,1)S(1)}, u32[]{:S(2)}, u32[]{:S(2)}) async-start(bf16[4,272,128]{2,1,0:T(8,128)(2,1)} %get-tuple-element.51.refs_5_), calls=%async_computation.2 | async-start | bytes 557056 | tf_op jit(solution)/shard_map/all_to_all | solution.py:636
  42.0 0.0 collective-permute-start.8
  42.0 0.0 collective-permute-done.7.refs_1_
  42.0 1.5 %collective-permute-done.8.refs_4_ = bf16[256,512]{1,0:T(8,128)(2,1)S(1)} collective-permute-done((bf16[256,512]{1,0:T(8,128)(2,1)S(1)}, bf16[256,512]{1,0:T(8,128)(2,1)S(1)}, u32[]{:S(2)}, u32[]{:S(2)}) %collective-permute-start.8) | collective-permute-done | bytes 262176 | tf_op jit(solution)/shard_map/ppermute | solution.py:631
  43.5 3.5 %outer.1.refs_3_ = bf16[4,128,1024]{2,1,0:T(8,128)(2,1)} custom-call(bf16[256,1024]{1,0:T(8,128)(2,1)} %bitcast.31, bf16[256,1024]{1,0:T(8,128)(2,1)} %collective-permute-done.7.refs_1_, s32[2]{0:T(128)S(1)} %pad_add_fusion.refs_9_.refs_2_.refs_7_.refs_0_, bf16[256,1024]{1,0:T(8,128)(2,1)S(1)} %get-tuple-element.46.refs_3_.refs_1_, ...), custom_call_target="tpu_custom_call" | custom-call | tf_op jit(solution)/shard_map/outer/pallas_call | solution.py:139
  47.0 4.5 %all-to-all-done.2.refs_0_ = bf16[4,272,128]{2,1,0:T(8,128)(2,1)S(1)} async-done(((bf16[4,272,128]{2,1,0:T(8,128)(2,1)}), bf16[4,272,128]{2,1,0:T(8,128)(2,1)S(1)}, u32[]{:S(2)}, u32[]{:S(2)}) %all-to-all-start.2) | async-done | bytes 278560 | tf_op jit(solution)/shard_map/all_to_all | solution.py:636
  51.5 3.5 %all-to-all-start.3 = ((bf16[4,128,1024]{2,1,0:T(8,128)(2,1)}), bf16[4,128,1024]{2,1,0:T(8,128)(2,1)S(1)}, u32[]{:S(2)}, u32[]{:S(2)}) async-start(bf16[4,128,1024]{2,1,0:T(8,128)(2,1)} %outer.1.refs_3_), calls=%async_computation.3 | async-start | bytes 2097152 | tf_op jit(solution)/shard_map/all_to_all | solution.py:643
  55.1 1.3 %suffix.1 = (bf16[32,1024]{1,0:T(8,128)(2,1)}, bf16[32,1024]{1,0:T(8,128)(2,1)}, bf16[32,1024]{1,0:T(8,128)(2,1)}, bf16[32,1024]{1,0:T(8,128)(2,1)}, f32[8,128]{1,0:T(8,128)S(1)}) custom-call(bf16[4,272,128]{2,1,0:T(8,128)(2,1)S(1)} %all-to-all-done.2.refs_0_, bf16[4,272,128]{2,1,0:T(8,128)(2,1)S(1)} %all-to-all-done.refs_0_.refs_1_, ...), custom_call_target="tpu_custom_call" | custom-call | tf_op jit(solution)/shard_map/suffix/pallas_call | solution.py:139
  56.4 0.0 collective-permute-start.10
  56.4 2.3 %collective-permute-start.11 = (bf16[32,1024]{1,0:T(8,128)(2,1)}, bf16[32,1024]{1,0:T(8,128)(2,1)S(1)}, u32[]{:S(2)}, u32[]{:S(2)}) collective-permute-start(bf16[32,1024]{1,0:T(8,128)(2,1)} %get-tuple-element.62), channel_id=1, source_target_pairs={{0,24},{8,0},{16,8},{24,16},{1,25},{9,1},{17,9},{25,17},{2,26},{10... | collective-permute-start | bytes 196616 | tf_op jit(solution)/shard_map/ppermute | solution.py:641
  58.7 0.0 collective-permute-start.9
  58.7 4.7 %back.1 = (bf16[256,128]{1,0:T(8,128)(2,1)}, f32[256,1024]{1,0:T(8,128)}, bf16[256,128]{1,0:T(8,128)(2,1)}, f32[16,256]{1,0:T(8,128)}) custom-call(bf16[256,1024]{1,0:T(8,128)(2,1)} %get-tuple-element.50.refs_0_, bf16[256,128]{1,0:T(8,128)(2,1)} %bitcast.40, bf16[256,128]{1,0:T(8,128)(2,1)} %bitcast.37, bf16[256,1024]{1,0:T(8,128)(2,1)} %bitcast.26, ...), custom_call_target="tpu_custom_call" | custom-call | tf_op jit(solution)/shard_map/back/pallas_call | solution.py:139
  63.4 0.0 copy-start
  63.4 3.1 %mixed.1.refs_1_ = bf16[256,1024]{1,0:T(8,128)(2,1)} custom-call(bf16[1024,1024]{1,0:T(8,128)(2,1)} %get-tuple-element.45.refs_7_.refs_0_, bf16[256,1024]{1,0:T(8,128)(2,1)S(1)} %get-tuple-element.46.refs_3_.refs_1_, f32[16,256]{1,0:T(8,128)} %get-tuple-element.54.refs_2_.refs_3_), custom_call_target="tpu_custom_call" | custom-call | tf_op jit(solution)/shard_map/mixed/pallas_call | solution.py:139
  66.6 0.0 collective-permute-done.10.refs_3_.refs_13_
  66.6 0.0 collective-permute-done.11.refs_4_.refs_14_
  66.6 0.0 collective-permute-done.9.refs_2_.refs_12_
  66.6 0.6 all-to-all-done.3.refs_0_
  67.2 0.8 add_chips.1.refs_15_
  68.0 4.5 %all-to-all-start.5 = ((bf16[4,32,1024]{2,1,0:T(8,128)(2,1)}), bf16[4,32,1024]{2,1,0:T(8,128)(2,1)S(1)}, u32[]{:S(2)}, u32[]{:S(2)}) async-start(bf16[4,32,1024]{2,1,0:T(8,128)(2,1)} %add_chips.1.refs_15_), calls=%async_computation.5 | async-start | bytes 524288 | tf_op jit(solution)/shard_map/all_to_all | solution.py:650
  72.5 4.6 %last.1 = (bf16[256,1024]{1,0:T(8,128)(2,1)}, bf16[256,128]{1,0:T(8,128)(2,1)}, f32[16,256]{1,0:T(8,128)}, f32[32,1,384]{2,1,0:T(1,128)}) custom-call(bf16[256,128]{1,0:T(8,128)(2,1)} %bitcast.41, bf16[256,1024]{1,0:T(8,128)(2,1)} %bitcast.27, f32[16,256]{1,0:T(8,128)} %get-tuple-element.55.refs_2_, f32[16,256]{1,0:T(8,128)} %get-tuple-element.54.refs_2_.refs_3_, ...), custom_call_target="tpu_custom_call" | custom-call | tf_op jit(solution)/shard_map/last/pallas_call | solution.py:139
  77.1 2.2 %all-to-all-done.5.refs_0_ = bf16[4,32,1024]{2,1,0:T(8,128)(2,1)S(1)} async-done(((bf16[4,32,1024]{2,1,0:T(8,128)(2,1)}), bf16[4,32,1024]{2,1,0:T(8,128)(2,1)S(1)}, u32[]{:S(2)}, u32[]{:S(2)}) %all-to-all-start.5) | async-done | bytes 262176 | tf_op jit(solution)/shard_map/all_to_all | solution.py:650
  79.3 4.8 %all-to-all-start.4 = ((f32[32,1,384]{2,1,0:T(1,128)}), f32[32,1,384]{2,1,0:T(1,128)S(1)}, u32[]{:S(2)}, u32[]{:S(2)}) async-start(f32[32,1,384]{2,1,0:T(1,128)} %get-tuple-element.68), calls=%async_computation.4 | async-start | bytes 98304 | tf_op jit(solution)/shard_map/all_to_all | solution.py:656
  84.2 0.7 add_blocks.1
  84.8 1.8 %collective-permute-start.12 = (bf16[32,1024]{1,0:T(8,128)(2,1)}, bf16[32,1024]{1,0:T(8,128)(2,1)S(1)}, u32[]{:S(2)}, u32[]{:S(2)}) collective-permute-start(bf16[32,1024]{1,0:T(8,128)(2,1)} %bitcast.19), channel_id=1, source_target_pairs={{0,8},{8,16},{16,24},{24,0},{1,9},{9,17},{17,25},{25,1},{2,10},{10... | collective-permute-start | bytes 196616 | tf_op jit(solution)/shard_map/ppermute | solution.py:654
  86.6 2.4 %collective-permute-start.13 = (bf16[32,1024]{1,0:T(8,128)(2,1)}, bf16[32,1024]{1,0:T(8,128)(2,1)S(1)}, u32[]{:S(2)}, u32[]{:S(2)}) collective-permute-start(bf16[32,1024]{1,0:T(8,128)(2,1)} %bitcast.20), channel_id=1, source_target_pairs={{0,16},{8,24},{16,0},{24,8},{1,17},{9,25},{17,1},{25,9},{2,18},{10... | collective-permute-start | bytes 196616 | tf_op jit(solution)/shard_map/ppermute | solution.py:654
  89.0 1.4 %collective-permute-start.14 = (bf16[32,1024]{1,0:T(8,128)(2,1)}, bf16[32,1024]{1,0:T(8,128)(2,1)S(1)}, u32[]{:S(2)}, u32[]{:S(2)}) collective-permute-start(bf16[32,1024]{1,0:T(8,128)(2,1)} %bitcast.21), channel_id=1, source_target_pairs={{0,24},{8,0},{16,8},{24,16},{1,25},{9,1},{17,9},{25,17},{2,26},{10... | collective-permute-start | bytes 196616 | tf_op jit(solution)/shard_map/ppermute | solution.py:654
  90.4 1.1 %all-to-all-done.4.refs_0_ = f32[32,1,384]{2,1,0:T(1,128)S(1)} async-done(((f32[32,1,384]{2,1,0:T(1,128)}), f32[32,1,384]{2,1,0:T(1,128)S(1)}, u32[]{:S(2)}, u32[]{:S(2)}) %all-to-all-start.4) | async-done | bytes 49184 | tf_op jit(solution)/shard_map/all_to_all | solution.py:656
  91.5 0.6 copy-done.8
  92.1 1.4 %sums.1 = (f32[16]{0:T(128)}, f32[16]{0:T(128)}, f32[16]{0:T(128)}, f32[1024]{0:T(1024)}) custom-call(f32[32,1,384]{2,1,0:T(1,128)} %copy-done.8), custom_call_target="tpu_custom_call" | custom-call | tf_op jit(solution)/shard_map/sums/pallas_call | solution.py:139
  93.5 0.0 collective-permute-done.12.refs_2_
  93.6 0.6 collective-permute-done.13.refs_3_
  94.1 0.2 collective-permute-done.14.refs_4_
  94.3 0.8 copy-done.1
  95.2 1.3 %join.1 = bf16[128,1024]{1,0:T(8,128)(2,1)} custom-call(s32[2]{0:T(128)S(1)} %pad_add_fusion.refs_9_.refs_2_.refs_7_.refs_0_, bf16[32,1024]{1,0:T(8,128)(2,1)S(1)} %bitcast.22, bf16[32,1024]{1,0:T(8,128)(2,1)S(1)} %collective-permute-done.12.refs_2_, bf16[32,1024]{1,0:T(8,128)(2,1)S(1)} %collective-permute-done.13.refs_3_, ...), custom_call_target="tpu_custom_call" | custom-call | tf_op jit(solution)/shard_map/join/pallas_call | solution.py:139
  (14 shorter events, 0.0 us)
Async XLA Ops:
  3.2 15.6 %all-to-all-start = ((bf16[4,272,128]{2,1,0:T(8,128)(2,1)}), bf16[4,272,128]{2,1,0:T(8,128)(2,1)S(1)}, u32[]{:S(2)}, u32[]{:S(2)}) async-start(bf16[4,272,128]{2,1,0:T(8,128)(2,1)} %get-tuple-element.42.refs_5_), calls=%async_computation | async-start | bytes 557056 | tf_op jit(solution)/shard_map/all_to_all | solution.py:566
  9.6 13.5 %collective-permute-start.1 = (bf16[128,1024]{1,0:T(8,128)(2,1)}, bf16[128,1024]{1,0:T(8,128)(2,1)S(1)}, u32[]{:S(2)}, u32[]{:S(2)}) collective-permute-start(bf16[128,1024]{1,0:T(8,128)(2,1)} %refs_0_.1), channel_id=1, source_target_pairs={{0,2},{1,3},{2,0},{3,1},{4,6},{5,7},{6,4},{7,5},{8,10},{9,11},{10,... | collective-permute-start | bytes 786440 | tf_op jit(solution)/shard_map/ppermute | solution.py:568
  11.0 13.3 %collective-permute-start.3 = (bf16[128,1024]{1,0:T(8,128)(2,1)}, bf16[128,1024]{1,0:T(8,128)(2,1)S(1)}, u32[]{:S(2)}, u32[]{:S(2)}) collective-permute-start(bf16[128,1024]{1,0:T(8,128)(2,1)} %refs_0_.1), channel_id=1, source_target_pairs={{0,4},{4,0},{1,5},{5,1},{2,6},{6,2},{3,7},{7,3},{8,12},{12,8},{9,1... | collective-permute-start | bytes 786440 | tf_op jit(solution)/shard_map/ppermute | solution.py:569
  12.6 11.8 %collective-permute-start.5 = (bf16[128,1024]{1,0:T(8,128)(2,1)}, bf16[128,1024]{1,0:T(8,128)(2,1)S(1)}, u32[]{:S(2)}, u32[]{:S(2)}) collective-permute-start(bf16[128,1024]{1,0:T(8,128)(2,1)} %refs_0_.1), channel_id=1, source_target_pairs={{0,6},{1,7},{2,4},{3,5},{4,2},{5,3},{6,0},{7,1},{8,14},{9,15},{10,... | collective-permute-start | bytes 786440 | tf_op jit(solution)/shard_map/ppermute | solution.py:570
  13.0 10.0 %copy-start.3 = (bf16[128,1024]{1,0:T(8,128)(2,1)S(1)}, bf16[128,1024]{1,0:T(8,128)(2,1)}, u32[]{:S(2)}) copy-start(bf16[128,1024]{1,0:T(8,128)(2,1)} %refs_0_.1) | copy-start | bytes 786436
  13.0 11.8 %copy-start.2 = (bf16[1,256,1024]{2,1,0:T(8,128)(2,1)S(1)}, bf16[1,256,1024]{2,1,0:T(8,128)(2,1)}, u32[]{:S(2)}) copy-start(bf16[1,256,1024]{2,1,0:T(8,128)(2,1)} %param.21) | copy-start | bytes 1572868
  19.6 10.5 %all-to-all-start.1 = ((bf16[4,32,1024]{2,1,0:T(8,128)(2,1)}), bf16[4,32,1024]{2,1,0:T(8,128)(2,1)S(1)}, u32[]{:S(2)}, u32[]{:S(2)}) async-start(bf16[4,32,1024]{2,1,0:T(8,128)(2,1)} %prefix.1.refs_10_), calls=%async_computation.1 | async-start | bytes 524288 | tf_op jit(solution)/shard_map/all_to_all | solution.py:576
  23.0 2.0 %collective-permute-start = (bf16[128,1024]{1,0:T(8,128)(2,1)S(1)}, bf16[128,1024]{1,0:T(8,128)(2,1)S(1)}, u32[]{:S(2)}, u32[]{:S(2)}) collective-permute-start(bf16[128,1024]{1,0:T(8,128)(2,1)S(1)} %copy-done.3), channel_id=1, source_target_pairs={{0,1},{1,0},{2,3},{3,2},{4,5},{5,4},{6,7},{7,6},{8,9},{9,8},{10,11... | collective-permute-start | bytes 786440 | tf_op jit(solution)/shard_map/ppermute | solution.py:571
  23.1 3.3 %copy-start.4 = (bf16[128,1024]{1,0:T(8,128)(2,1)}, bf16[128,1024]{1,0:T(8,128)(2,1)S(1)}, u32[]{:S(2)}) copy-start(bf16[128,1024]{1,0:T(8,128)(2,1)S(1)} %collective-permute-done.1.refs_2_) | copy-start | bytes 786436
  23.1 2.0 %collective-permute-start.2 = (bf16[128,1024]{1,0:T(8,128)(2,1)S(1)}, bf16[128,1024]{1,0:T(8,128)(2,1)}, u32[]{:S(2)}, u32[]{:S(2)}) collective-permute-start(bf16[128,1024]{1,0:T(8,128)(2,1)S(1)} %collective-permute-done.1.refs_2_), channel_id=1, source_target_pairs={{0,1},{1,0},{2,3},{3,2},{4,5},{5,4},{6,7},{7,6},{8,9},{9,8},{10,11... | collective-permute-start | bytes 786440 | tf_op jit(solution)/shard_map/ppermute | solution.py:571
  24.4 2.0 %copy-start.5 = (bf16[128,1024]{1,0:T(8,128)(2,1)}, bf16[128,1024]{1,0:T(8,128)(2,1)S(1)}, u32[]{:S(2)}) copy-start(bf16[128,1024]{1,0:T(8,128)(2,1)S(1)} %collective-permute-done.3.refs_4_) | copy-start | bytes 786436
  24.4 1.7 %collective-permute-start.4 = (bf16[128,1024]{1,0:T(8,128)(2,1)S(1)}, bf16[128,1024]{1,0:T(8,128)(2,1)}, u32[]{:S(2)}, u32[]{:S(2)}) collective-permute-start(bf16[128,1024]{1,0:T(8,128)(2,1)S(1)} %collective-permute-done.3.refs_4_), channel_id=1, source_target_pairs={{0,1},{1,0},{2,3},{3,2},{4,5},{5,4},{6,7},{7,6},{8,9},{9,8},{10,11... | collective-permute-start | bytes 786440 | tf_op jit(solution)/shard_map/ppermute | solution.py:571
  24.4 1.7 %copy-start.6 = (bf16[128,1024]{1,0:T(8,128)(2,1)}, bf16[128,1024]{1,0:T(8,128)(2,1)S(1)}, u32[]{:S(2)}) copy-start(bf16[128,1024]{1,0:T(8,128)(2,1)S(1)} %collective-permute-done.5.refs_6_) | copy-start | bytes 786436
  24.4 2.0 %collective-permute-start.6 = (bf16[128,1024]{1,0:T(8,128)(2,1)S(1)}, bf16[128,1024]{1,0:T(8,128)(2,1)}, u32[]{:S(2)}, u32[]{:S(2)}) collective-permute-start(bf16[128,1024]{1,0:T(8,128)(2,1)S(1)} %collective-permute-done.5.refs_6_), channel_id=1, source_target_pairs={{0,1},{1,0},{2,3},{3,2},{4,5},{5,4},{6,7},{7,6},{8,9},{9,8},{10,11... | collective-permute-start | bytes 786440 | tf_op jit(solution)/shard_map/ppermute | solution.py:571
  24.9 17.1 %collective-permute-start.7 = (bf16[256,1024]{1,0:T(8,128)(2,1)S(1)}, bf16[256,1024]{1,0:T(8,128)(2,1)}, u32[]{:S(2)}, u32[]{:S(2)}) collective-permute-start(bf16[256,1024]{1,0:T(8,128)(2,1)S(1)} %bitcast.32), channel_id=1, source_target_pairs={{0,1},{1,0},{2,3},{3,2},{4,5},{5,4},{6,7},{7,6},{8,9},{9,8},{10,11... | collective-permute-start | bytes 1572872 | tf_op jit(solution)/shard_map/ppermute | solution.py:567
  25.0 1.0 %copy-start.7 = (bf16[128,1024]{1,0:T(8,128)(2,1)}, bf16[128,1024]{1,0:T(8,128)(2,1)S(1)}, u32[]{:S(2)}) copy-start(bf16[128,1024]{1,0:T(8,128)(2,1)S(1)} %collective-permute-done.refs_1_) | copy-start | bytes 786436
  33.4 8.6 %copy-start.9 = (bf16[256,512]{1,0:T(8,128)(2,1)S(1)}, bf16[256,512]{1,0:T(8,128)(2,1)}, u32[]{:S(2)}) copy-start(bf16[256,512]{1,0:T(8,128)(2,1)} %get-tuple-element.52) | copy-start | bytes 786436
  37.1 14.4 %all-to-all-start.2 = ((bf16[4,272,128]{2,1,0:T(8,128)(2,1)}), bf16[4,272,128]{2,1,0:T(8,128)(2,1)S(1)}, u32[]{:S(2)}, u32[]{:S(2)}) async-start(bf16[4,272,128]{2,1,0:T(8,128)(2,1)} %get-tuple-element.51.refs_5_), calls=%async_computation.2 | async-start | bytes 557056 | tf_op jit(solution)/shard_map/all_to_all | solution.py:636
  42.0 1.5 %collective-permute-start.8 = (bf16[256,512]{1,0:T(8,128)(2,1)S(1)}, bf16[256,512]{1,0:T(8,128)(2,1)S(1)}, u32[]{:S(2)}, u32[]{:S(2)}) collective-permute-start(bf16[256,512]{1,0:T(8,128)(2,1)S(1)} %copy-done.9), channel_id=1, source_target_pairs={{0,1},{1,0},{2,3},{3,2},{4,5},{5,4},{6,7},{7,6},{8,9},{9,8},{10,11... | collective-permute-start | bytes 786440 | tf_op jit(solution)/shard_map/ppermute | solution.py:631
  51.5 15.6 %all-to-all-start.3 = ((bf16[4,128,1024]{2,1,0:T(8,128)(2,1)}), bf16[4,128,1024]{2,1,0:T(8,128)(2,1)S(1)}, u32[]{:S(2)}, u32[]{:S(2)}) async-start(bf16[4,128,1024]{2,1,0:T(8,128)(2,1)} %outer.1.refs_3_), calls=%async_computation.3 | async-start | bytes 2097152 | tf_op jit(solution)/shard_map/all_to_all | solution.py:643
  56.4 10.2 %collective-permute-start.10 = (bf16[32,1024]{1,0:T(8,128)(2,1)}, bf16[32,1024]{1,0:T(8,128)(2,1)S(1)}, u32[]{:S(2)}, u32[]{:S(2)}) collective-permute-start(bf16[32,1024]{1,0:T(8,128)(2,1)} %get-tuple-element.61), channel_id=1, source_target_pairs={{0,16},{8,24},{16,0},{24,8},{1,17},{9,25},{17,1},{25,9},{2,18},{10... | collective-permute-start | bytes 196616 | tf_op jit(solution)/shard_map/ppermute | solution.py:641
  56.4 10.2 %collective-permute-start.11 = (bf16[32,1024]{1,0:T(8,128)(2,1)}, bf16[32,1024]{1,0:T(8,128)(2,1)S(1)}, u32[]{:S(2)}, u32[]{:S(2)}) collective-permute-start(bf16[32,1024]{1,0:T(8,128)(2,1)} %get-tuple-element.62), channel_id=1, source_target_pairs={{0,24},{8,0},{16,8},{24,16},{1,25},{9,1},{17,9},{25,17},{2,26},{10... | collective-permute-start | bytes 196616 | tf_op jit(solution)/shard_map/ppermute | solution.py:641
  58.7 7.9 %collective-permute-start.9 = (bf16[32,1024]{1,0:T(8,128)(2,1)}, bf16[32,1024]{1,0:T(8,128)(2,1)S(1)}, u32[]{:S(2)}, u32[]{:S(2)}) collective-permute-start(bf16[32,1024]{1,0:T(8,128)(2,1)} %get-tuple-element.60), channel_id=1, source_target_pairs={{0,8},{8,16},{16,24},{24,0},{1,9},{9,17},{17,25},{25,1},{2,10},{10... | collective-permute-start | bytes 196616 | tf_op jit(solution)/shard_map/ppermute | solution.py:641
  63.4 9.1 %copy-start = (bf16[32,1024]{1,0:T(8,128)(2,1)S(1)}, bf16[32,1024]{1,0:T(8,128)(2,1)}, u32[]{:S(2)}) copy-start(bf16[32,1024]{1,0:T(8,128)(2,1)} %get-tuple-element.53.refs_7_.refs_11_) | copy-start | bytes 196612
  68.0 11.3 %all-to-all-start.5 = ((bf16[4,32,1024]{2,1,0:T(8,128)(2,1)}), bf16[4,32,1024]{2,1,0:T(8,128)(2,1)S(1)}, u32[]{:S(2)}, u32[]{:S(2)}) async-start(bf16[4,32,1024]{2,1,0:T(8,128)(2,1)} %add_chips.1.refs_15_), calls=%async_computation.5 | async-start | bytes 524288 | tf_op jit(solution)/shard_map/all_to_all | solution.py:650
  79.3 12.2 %all-to-all-start.4 = ((f32[32,1,384]{2,1,0:T(1,128)}), f32[32,1,384]{2,1,0:T(1,128)S(1)}, u32[]{:S(2)}, u32[]{:S(2)}) async-start(f32[32,1,384]{2,1,0:T(1,128)} %get-tuple-element.68), calls=%async_computation.4 | async-start | bytes 98304 | tf_op jit(solution)/shard_map/all_to_all | solution.py:656
  84.8 8.7 %collective-permute-start.12 = (bf16[32,1024]{1,0:T(8,128)(2,1)}, bf16[32,1024]{1,0:T(8,128)(2,1)S(1)}, u32[]{:S(2)}, u32[]{:S(2)}) collective-permute-start(bf16[32,1024]{1,0:T(8,128)(2,1)} %bitcast.19), channel_id=1, source_target_pairs={{0,8},{8,16},{16,24},{24,0},{1,9},{9,17},{17,25},{25,1},{2,10},{10... | collective-permute-start | bytes 196616 | tf_op jit(solution)/shard_map/ppermute | solution.py:654
  86.6 7.5 %collective-permute-start.13 = (bf16[32,1024]{1,0:T(8,128)(2,1)}, bf16[32,1024]{1,0:T(8,128)(2,1)S(1)}, u32[]{:S(2)}, u32[]{:S(2)}) collective-permute-start(bf16[32,1024]{1,0:T(8,128)(2,1)} %bitcast.20), channel_id=1, source_target_pairs={{0,16},{8,24},{16,0},{24,8},{1,17},{9,25},{17,1},{25,9},{2,18},{10... | collective-permute-start | bytes 196616 | tf_op jit(solution)/shard_map/ppermute | solution.py:654
  89.0 5.3 %collective-permute-start.14 = (bf16[32,1024]{1,0:T(8,128)(2,1)}, bf16[32,1024]{1,0:T(8,128)(2,1)S(1)}, u32[]{:S(2)}, u32[]{:S(2)}) collective-permute-start(bf16[32,1024]{1,0:T(8,128)(2,1)} %bitcast.21), channel_id=1, source_target_pairs={{0,24},{8,0},{16,8},{24,16},{1,25},{9,1},{17,9},{25,17},{2,26},{10... | collective-permute-start | bytes 196616 | tf_op jit(solution)/shard_map/ppermute | solution.py:654
  91.5 0.6 copy-start.8
  94.3 0.8 copy-start.1

commit v4 on v3

--- a/solution.py
+++ b/solution.py
@@ -115,11 +115,17 @@
     return jax.ShapeDtypeStruct(shape, dtype)
 
 
-def call(kernel, outs, far, *args, smem=(), name=None, scratch=(), after=(), beside=()):
+def call(kernel, outs, far, *args, name=None, scratch=(), after=(), beside=(), aliases=None, far_operands=(), held=0, loose=False):
     waits = len(after) + len(beside)
+
+    def fix(v):
+        return v if loose else pltpu.with_memory_space_constraint(v, pltpu.HBM)
+
+    far_operands = (*far_operands, *range(len(args) - held, len(args)))
+    args = args[: len(args) - held] + tuple(fix(v) for v in args[len(args) - held :])
     specs = [pl.BlockSpec(memory_space=pl.ANY)] * len(far)
     specs += [
-        pl.BlockSpec(memory_space=pltpu.SMEM if k in smem else pltpu.VMEM) for k in range(len(args))
+        pl.BlockSpec(memory_space=pl.ANY if k in far_operands else pltpu.VMEM) for k in range(len(args))
     ]
     specs += [pl.BlockSpec(memory_space=pl.ANY)] * waits
     first, used = len(far), len(far) + len(args)
@@ -140,11 +146,14 @@
         body,
         out_shape=[where(shape, dtype) for shape, dtype, where in outs],
         in_specs=specs,
-        out_specs=[pl.BlockSpec(memory_space=pltpu.VMEM)] * len(outs),
+        out_specs=[
+            pl.BlockSpec(memory_space=pl.ANY if k in (aliases or {}).values() else pltpu.VMEM) for k in range(len(outs))
+        ],
         scratch_shapes=list(scratch) + landing + semaphores,
+        input_output_aliases=aliases or {},
         compiler_params=pltpu.CompilerParams(vmem_limit_bytes=VMEM_LIMIT),
         name=name,
-    )(*[pltpu.with_memory_space_constraint(v, pltpu.HBM) for v in far], *args, *[pltpu.with_memory_space_constraint(v, pltpu.HBM) for v in after], *beside)
+    )(*[fix(v) for v in far], *args, *[pltpu.with_memory_space_constraint(v, pltpu.HBM) for v in after], *beside)
 
 
 def store_decay(aux_ref, rows_ref, v, delta, a, ld, cum, skip, gain):
@@ -171,7 +180,7 @@
         out_ref[k, blocks * rows :, :] = tail
 
 
-def payload_kernel(s_in, rate_in, bias_in, b_in, x_in, skip_in, gain_in, aux_ref, rows_ref, *outs):
+def payload_kernel(s_in, rate_in, bias_in, b_in, x_in, skip_in, gain_in, w_in, aux_ref, rows_ref, w_ref, *outs):
     v, delta, a, ld, cum = decay(s_in.ready(), rate_in.ready(), bias_in.ready())
     x_ref, b_ref = x_in.ready(), b_in.ready()
     width = x_ref.shape[1]
@@ -183,22 +192,32 @@
     weighted = (x_ref[...].astype(F32) * tail).astype(BF)
     state = mm_tn(b_ref[...], weighted).astype(BF)
     total = expand_row(jnp.exp(last), hmap)
+    w_ref[...] = w_in.ready()[...]
     if len(outs) == 2:
         outs[0][...] = state
         outs[1][...] = total
         return
-    (out_ref,) = outs
+    outs, out_ref = outs[:-1], outs[-1]
     store_parts(out_ref, state, total)
-
-
-def part_decay(all_ref, k, n, rows, blocks):
-    pair = all_ref[k, blocks * rows :, :].astype(F32)
-    return pair[n : n + 1] + pair[blocks + n : blocks + n + 1]
-
-
-def prefix_kernel(all_ref, out_ref):
+    for k, part_ref in enumerate(outs):
+        part_ref[...] = out_ref[turn(k, len(outs))]
+
+
+def turn(k, count):
+    return lax.rem(lax.axis_index("tm") + k + count, count)
+
+
+def prefix_kernel(*refs):
+    gots, (out_ref, decays_ref, all_ref) = refs[:-3], refs[-3:]
     count, rows, width = out_ref.shape
+    for k, got in enumerate(gots):
+        all_ref[turn(-k, count)] = got[...]
     blocks = width // 128
+    decays = []
+    for k in range(count):
+        pair = all_ref[k, blocks * rows :, :].astype(F32)
+        decays.append(pair[:blocks] + pair[blocks:])
+        decays_ref[k * blocks : (k + 1) * blocks, :] = decays[k]
     for n in range(blocks):
         cols = slice(n * 128, (n + 1) * 128)
         carried = jnp.zeros((rows, 128), F32)
@@ -206,24 +225,34 @@
             out_ref[k, :, cols] = carried.astype(BF)
             if k + 1 < count:
                 state = all_ref[k, n * rows : (n + 1) * rows, :].astype(F32)
-                carried = state + part_decay(all_ref, k, n, rows, blocks) * carried
-
-
-def suffix_kernel(grads_ref, all_ref, pos_ref, *refs):
-    outs, gains_ref, out_ref = refs[:-2], refs[-2], refs[-1]
-    count, rows, width = out_ref.shape
+                carried = state + decays[k][n : n + 1] * carried
+
+
+def gather_rows(parts, out_ref):
+    count, rows = len(parts), parts[0].shape[0]
+    for k, one in enumerate(parts):
+        out_ref[pl.ds(pl.multiple_of(turn(-k, count) * rows, rows), rows), :] = one[...]
+
+
+def suffix_kernel(decays_ref, *refs):
+    count = (len(refs) - 3) // 2
+    gots, outs, (gains_ref, out_ref, all_ref) = refs[:count], refs[count:-3], refs[-3:]
+    _, rows, width = out_ref.shape
     blocks = width // 128
+    for k, got in enumerate(gots):
+        all_ref[turn(-k, count)] = got[...]
+    decays = decays_ref[...]
     for n in range(blocks):
         cols = slice(n * 128, (n + 1) * 128)
         carried = jnp.zeros((rows, 128), F32)
         for k in reversed(range(count)):
             out_ref[k, :, cols] = carried.astype(BF)
             if k > 0:
-                grad = grads_ref[k, n * rows : (n + 1) * rows, :].astype(F32)
-                carried = grad + part_decay(all_ref, k, n, rows, blocks) * carried
+                grad = all_ref[k, n * rows : (n + 1) * rows, :].astype(F32)
+                carried = grad + decays[k * blocks + n : k * blocks + n + 1] * carried
     for k, part_ref in enumerate(outs):
-        part_ref[...] = out_ref[lax.rem(pos_ref[1] + k, count)]
-    gains = sum(grads_ref[k, blocks * rows :, :].astype(F32) for k in range(count))
+        part_ref[...] = out_ref[turn(k, count)]
+    gains = sum(all_ref[k, blocks * rows :, :].astype(F32) for k in range(count))
     gains_ref[...] = gains[:blocks] + gains[blocks:]
 
 
@@ -264,68 +293,55 @@
         inner_ref[half:, cols] = jnp.where(first, y1[:half], y1[half:]) + skip[:, cols] * x[half:, cols]
 
 
-def weight_kernel(*refs):
-    pieces, g_in, idx_ref, full_ref, ng_ref = [v.ready() for v in refs[:8]], *refs[8:]
-    me = idx_ref[0]
-    rows = pieces[0].shape[0]
-    for k, piece in enumerate(pieces):
-        full_ref[pl.ds(pl.multiple_of((me ^ k) * rows, rows), rows), :] = piece[...]
-    ng_ref[...] = mm_nt(g_in.ready()[...], full_ref[...]).astype(BF)
-
-
-def grad_kernel(g_ref, full_ref, ng_ref):
-    ng_ref[...] = mm_nt(g_ref[...], full_ref[...]).astype(BF)
-
-
-def norm_kernel(c_in, z_in, idx_ref, aux_ref, params_ref, local_ref, inc_ref, normed_ref, other_ref, inner_ref, factor_ref, ec_ref):
-    _, _, _, cum, _ = load_decay(aux_ref)
-    c_ref, z_ref = c_in.ready(), z_in.ready()
-    heads, length = cum.shape
-    width = z_ref.shape[1]
-    hmap = head_map(heads, width)
-    ec_ref[...] = expand(jnp.exp(cum), hmap)
-    inner_ref[...] = mm(c_ref[...], inc_ref[...])
-    gain = params_ref[1:2, :]
-    step = length // CHUNKS
-
-    for n in range(CHUNKS):
-        at = slice(n * step, (n + 1) * step)
-        inner = local_ref[at, :] + inner_ref[at, :] * ec_ref[at, :]
-        inner_ref[at, :] = inner
-        z = z_ref[at, :].astype(F32)
-        gated = inner * (z / (1.0 + jnp.exp(-z)))
-        r = lax.rsqrt(jnp.mean(gated * gated, axis=1, keepdims=True) + 1e-05)
-        factor_ref[at, :] = jnp.broadcast_to(r, (step, 128))
-        normed_ref[at, :] = (gated * r * gain).astype(BF)
-    block = other_ref.shape[1] // 4
-    for k in range(4):
-        at = (2 * k + 1 - lax.rem(idx_ref[0], 2)) * block
-        other_ref[:, k * block : (k + 1) * block] = normed_ref[:, pl.ds(pl.multiple_of(at, block), block)]
-
-
-def norm_back_kernel(
-    c_in, z_in, x_in, aux_ref, params_ref, inner_ref, factor_ref, ng_ref,
-    dy_ref, carry_ref, zg_ref, rows_ref, gains_ref, skips_ref,
-    ec_ref, de_ref, hi_ref, lo_ref,
+def unit():
+    return lax.axis_index("tok") * lax.axis_size("rep") + lax.axis_index("rep")
+
+
+def weight_pieces(refs, full_ref, semaphore):
+    copies = []
+    for k, piece in enumerate(refs):
+        rows = piece.shape[0]
+        at = pl.ds(pl.multiple_of((unit() ^ k) * rows, rows), rows) if len(refs) > 1 else pl.ds(0, rows)
+        copies.append(Coming(piece, full_ref.at[at, :], semaphore.at[k]))
+    return copies
+
+
+def weight_kernel(g_in, *refs):
+    pieces, (ng_ref, full_ref, semaphore) = refs[:-3], refs[-3:]
+    copies = weight_pieces(pieces, full_ref, semaphore)
+    g = g_in.ready()[...]
+    for one in copies:
+        one.ready()
+    ng_ref[...] = mm_nt(g, full_ref[...]).astype(BF)
+
+
+def norm_kernel(
+    c_in, z_in, x_in, aux_ref, params_ref, local_ref, ng_ref, inc_ref,
+    normed_ref, other_ref, dy_ref, zg_ref, rows_ref, sums_ref, *refs,
 ):
+    carries, (all_ref, inner_ref, ec_ref, de_ref, hi_ref, lo_ref) = refs[:-6], refs[-6:]
     _, _, _, cum, _ = load_decay(aux_ref)
     c_ref, z_ref, x_ref = c_in.ready(), z_in.ready(), x_in.ready()
     heads, length = cum.shape
     width = x_ref.shape[1]
     hmap = head_map(heads, width)
     ec_ref[...] = expand(jnp.exp(cum), hmap)
+    inner_ref[...] = mm(c_ref[...], inc_ref[...])
     skip, gain = params_ref[0:1, :], params_ref[1:2, :]
     step = length // CHUNKS
     gains = jnp.zeros((1, width), F32)
     skips = jnp.zeros((1, width), F32)
     for n in range(CHUNKS):
         at = slice(n * step, (n + 1) * step)
-        inner = inner_ref[at, :]
+        ec = ec_ref[at, :]
+        inner = local_ref[at, :] + inner_ref[at, :] * ec
         z = z_ref[at, :].astype(F32)
         sig = 1.0 / (1.0 + jnp.exp(-z))
         silu = z * sig
-        r = factor_ref[at, 0:1]
-        nhat = inner * silu * r
+        gated = inner * silu
+        r = lax.rsqrt(jnp.mean(gated * gated, axis=1, keepdims=True) + 1e-05)
+        nhat = gated * r
+        normed_ref[at, :] = (nhat * gain).astype(BF)
         ng = ng_ref[at, :].astype(F32)
         prod = ng * nhat
         gains = gains + jnp.sum(prod, axis=0, keepdims=True)
@@ -334,25 +350,31 @@
         dinner = dgated * silu
         dy = dinner.astype(BF)
         dy_ref[at, :] = dy
-        de_ref[at, :] = (dinner * ec_ref[at, :]).astype(BF)
+        de_ref[at, :] = (dinner * ec).astype(BF)
         zg_ref[at, :] = (dgated * inner * (sig + silu * (1.0 - sig))).astype(BF)
         x = x_ref[at, :].astype(F32)
         skips = skips + jnp.sum(dinner * x, axis=0, keepdims=True)
         hi_ref[at, :], lo_ref[at, :] = split(dy.astype(F32) * (inner - skip * x), 2)
     carry = mm_tn(c_ref[...], de_ref[...]).astype(BF)
-    if len(carry_ref.shape) == 2:
-        carry_ref[...] = carry
+    if len(carries) == 1:
+        carries[0][...] = carry
     else:
-        store_parts(carry_ref, carry, gains)
+        store_parts(all_ref, carry, gains)
+        for k, part_ref in enumerate(carries):
+            part_ref[...] = all_ref[turn(k, len(carries))]
     hb = hmap.astype(BF)
     rows_ref[...] = mm_nt(hb, hi_ref[...]) + mm_nt(hb, lo_ref[...])
-    gains_ref[...] = gains
-    skips_ref[...] = jnp.sum(skips * hmap, axis=1, keepdims=True)
-
-
-def outer_kernel(g_in, gc_in, idx_ref, normed_ref, got_ref, out_ref):
+    sums_ref[0:1, :] = gains
+    sums_ref[1:2, :] = skips
+    block = other_ref.shape[1] // 4
+    for k in range(4):
+        at = (2 * k + 1 - lax.rem(lax.axis_index("rep"), 2)) * block
+        other_ref[:, k * block : (k + 1) * block] = normed_ref[:, pl.ds(pl.multiple_of(at, block), block)]
+
+
+def outer_kernel(g_in, gc_in, normed_ref, got_ref, out_ref):
     g_ref, gc_ref = g_in.ready(), gc_in.ready()
-    core = lax.rem(idx_ref[0], 2)
+    core = lax.rem(lax.axis_index("rep"), 2)
     chips, rows = out_ref.shape[:2]
     for k in range(chips):
         mine = pl.ds(pl.multiple_of((2 * k + core) * rows, rows), rows)
@@ -360,26 +382,32 @@
         out_ref[k] = part.astype(BF)
 
 
-def add_kernel(all_ref, out_ref):
+def share_kernel(all_ref, *refs):
+    outs, total_ref = refs[:-1], refs[-1]
     total = all_ref[0].astype(F32)
     for k in range(1, all_ref.shape[0]):
         total = total + all_ref[k].astype(F32)
-    total = total.astype(BF)
-    rows = out_ref.shape[1]
-    for k in range(out_ref.shape[0]):
-        out_ref[k] = total[k * rows : (k + 1) * rows]
-
-
-def mixed_kernel(full_in, normed_ref, mixed_ref):
-    mixed_ref[...] = mm(normed_ref[...], full_in.ready()[...]).astype(BF)
-
-
-def join_kernel(*refs):
-    pos_ref, pieces, out_ref = refs[0], refs[1:-1], refs[-1]
-    count, rows = len(pieces), pieces[0].shape[0]
-    for k, piece in enumerate(pieces):
-        at = lax.rem(pos_ref[1] + count - k, count) * rows
-        out_ref[pl.ds(pl.multiple_of(at, rows), rows), :] = piece[...]
+    total_ref[...] = total
+    rows = outs[0].shape[0]
+    for k, out_ref in enumerate(outs):
+        part = total_ref[pl.ds(pl.multiple_of(turn(max(k - 1, 0), len(outs) - 1) * rows, rows), rows), :]
+        out_ref[...] = part.astype(out_ref.dtype)
+
+
+def add_kernel(*refs):
+    own_ref, gots, out_ref = refs[0], refs[1:-1], refs[-1]
+    total = own_ref[...]
+    for got in gots:
+        total = total + got[...].astype(F32)
+    out_ref[...] = total.astype(BF)
+
+
+def mixed_kernel(weight_in, normed_ref, mixed_ref):
+    mixed_ref[...] = mm(normed_ref[...], weight_in.ready()[...]).astype(BF)
+
+
+def join_kernel(own_in, *refs):
+    gather_rows((own_in.ready(),) + refs[:-1], refs[-1])
 
 
 def outer_full_kernel(normed_ref, g_ref, out_ref):
@@ -392,13 +420,14 @@
 ):
     _, delta, _, cum, _ = load_decay(aux_ref)
     x_ref, b_ref, c_ref = x_in.ready(), b_in.ready(), c_in.ready()
+    dy_ref = dy_in.ready()
     heads, length = cum.shape
     width = x_ref.shape[1]
     hmap = head_map(heads, width)
     cum_t = cum.T
     delta_e = expand(delta, hmap)
     xd = (x_ref[...].astype(F32) * delta_e).astype(BF)
-    dy = dy_in.ready()[...]
+    dy = dy_ref[...]
     half = length // 2
     scores = mm_nt(b_ref[...], c_ref[...])
     i = lax.broadcasted_iota(jnp.int32, (half, half), 0)
@@ -454,14 +483,15 @@
 
 
 def last_kernel(
-    gains_here, b_in, x_in, rows_in, cols_in, bg_in, xg_in, skips_in, pos_ref, aux_ref, inc_ref, *more,
+    gains_here, b_in, x_in, rows_in, cols_in, bg_in, xg_in, sums_in, aux_ref, inc_ref, *more,
 ):
     parts, (x_out, b_out, step_out, sums_out, later_ref) = more[:-5], more[-5:]
     gains_ref, parts = (parts[0], parts[1:]) if gains_here else (None, parts)
-    count, part = len(parts), parts[0].shape[0]
-    for k, one in enumerate(parts):
-        at = lax.rem(pos_ref[1] + count - k, count) * part
-        later_ref[pl.ds(pl.multiple_of(at, part), part), :] = one[...]
+    count = len(parts)
+    if count > 1:
+        gather_rows(parts, later_ref)
+    else:
+        later_ref[...] = parts[0][...]
     v, delta, ld, cum, a = load_decay(aux_ref)
     x_ref, b_ref = x_in.ready(), b_in.ready()
     heads, length = cum.shape
@@ -494,12 +524,12 @@
     def lay(col, at):
         return jnp.sum(jnp.where(j == i + at, col, 0.0), axis=0, keepdims=True)
 
-    small = lay(drate, 0) + lay(dbias, heads) + lay(skips_in.ready()[...], 2 * heads)
+    small = lay(drate, 0) + lay(dbias, heads) + lay(jnp.sum(sums_in.ready()[1:2, :] * hmap, axis=1, keepdims=True), 2 * heads)
     if gains_ref is None:
         sums_out[0] = small
         return
     each = gains_ref.shape[0] // count
-    shares = [gains_ref[pl.ds(pos_ref[1] * each + n, 1), :] for n in range(each)]
+    shares = [gains_ref[pl.ds(lax.axis_index("tm") * each + n, 1), :] for n in range(each)]
     row = jnp.concatenate([small] + shares, axis=1)
     for k in range(sums_out.shape[0]):
         sums_out[k] = row
@@ -543,63 +573,64 @@
     state_size = b_input.shape[2]
     x, z, b, c, s, g = x_branch[0], z_gate[0], b_input[0], c_input[0], step_raw[0], out_grad[0]
     n_tm, n_tok, n_rep = lax.axis_size("tm"), lax.axis_size("tok"), lax.axis_size("rep")
-    rep, tok, tm = lax.axis_index("rep"), lax.axis_index("tok"), lax.axis_index("tm")
     near = (n_tm, n_tok, n_rep) == (4, 2, 4)
     rows = out_weight.shape[0]
     full = (width, model)
     wide = (length, width)
-    place = jnp.stack([tok * n_rep + rep, tm]).astype(jnp.int32)
     core = [(k, k ^ 1) for k in range(4)]
     side = [(k, k ^ 2) for k in range(4)]
     front = [(0, 1), (1, 0)]
     diagonal = [(k, k ^ 6) for k in range(8)]
-
-    raw = (s, rate_log, step_bias, b, x, skip_gain, norm_gain)
-    aux_shapes = [((5 * heads, length), F32, near_by), ((8, width), F32, near_by)]
+    ahead = [[(i, (i + k) % n_tm) for i in range(n_tm)] for k in range(1, n_tm)]
+
+    raw = (s, rate_log, step_bias, b, x, skip_gain, norm_gain, out_weight)
+    aux_shapes = [((5 * heads, length), F32, near_by), ((8, width), F32, near_by), (out_weight.shape, BF, away)]
     if near:
         part = (n_tm, state_size // n_tm)
+        row_part = (part[1], width)
         blocks_of = width // 128
         part_shape = (n_tm, blocks_of * part[1] + 2 * blocks_of, 128)
-        aux, params, payload = call(
-            payload_kernel, aux_shapes + [(part_shape, BF, away)], raw, name="state",
-        )
-        blocks = lax.all_to_all(payload, "tm", 0, 0, tiled=True)
+        aux, params, out_weight, *payload = call(
+            payload_kernel, aux_shapes + [(part_shape[1:], BF, away)] * n_tm, raw, name="state",
+            scratch=[pltpu.VMEM(part_shape, BF)],
+        )
+        blocks = [payload[0]] + [lax.ppermute(v, "tm", pairs) for v, pairs in zip(payload[1:], ahead)]
         gc = lax.ppermute(g, "rep", core)
         wx = lax.ppermute(out_weight, "rep", side)
         wy = lax.ppermute(out_weight, "tok", front)
         wd = lax.ppermute(out_weight, ("tok", "rep"), diagonal)
         wc, wxc, wyc, wdc = (lax.ppermute(v, "rep", core) for v in (out_weight, wx, wy, wd))
         (local,) = call(
-            inner_kernel, [(wide, F32, near_by)], (b, c, x), aux, params, name="inner", after=(payload,)
-        )
-        (prefixes,) = call(prefix_kernel, [(part + (width,), BF, away)], (), blocks, name="prefix", beside=(local,))
+            inner_kernel, [(wide, F32, near_by)], (b, c, x), aux, params, name="inner", after=(payload[0],)
+        )
+        prefixes, decays = call(
+            prefix_kernel, [(part + (width,), BF, away), ((n_tm * blocks_of, 128), F32, near_by)], (), *blocks,
+            name="prefix", beside=(local,), scratch=[pltpu.VMEM(part_shape, BF)],
+        )
         incoming = lax.all_to_all(prefixes, "tm", 0, 0, tiled=True).reshape(state_size, width)
         pieces = (out_weight, wc, wx, wxc, wy, wyc, wd, wdc)
-        weight, ng = call(
-            weight_kernel, [(full, BF, away), (wide, BF, near_by)], (*pieces, g), place,
-            smem=(0,), name="normed_grad", after=(prefixes,),
-        )
+        after = (prefixes,)
     else:
-        aux, params, state, total = call(
+        aux, params, out_weight, state, total = call(
             payload_kernel, aux_shapes + [((state_size, width), BF, free), ((1, width), F32, free)], raw, name="state"
         )
         incoming = scan_far(state, total, "tm", False)
         (local,) = call(inner_kernel, [(wide, F32, near_by)], (b, c, x), aux, params, name="inner")
-        weight = lax.all_gather(out_weight, ("tok", "rep"), axis=0, tiled=True)
-        (ng,) = call(grad_kernel, [(wide, BF, near_by)], (), g, weight, name="normed_grad")
-    normed, other, inner, factor = call(
+        pieces = (lax.all_gather(out_weight, ("tok", "rep"), axis=0, tiled=True),)
+        after = ()
+    ng, weight = call(
+        weight_kernel, [(wide, BF, near_by), (full, BF, away)], (g,), *pieces, name="normed_grad", after=after, held=len(pieces), loose=True,
+        scratch=[pltpu.SemaphoreType.DMA((len(pieces),))],
+    )
+    normed, other, dy, zg, row_sums, gains, *carry = call(
         norm_kernel,
-        [(wide, BF, near_by), ((length, width // 2), BF, away), (wide, F32, near_by), ((length, 128), F32, near_by)],
-        (c, z), place, aux, params, local, incoming, name="norm", smem=(0,), scratch=[pltpu.VMEM(wide, F32)], after=(weight,),
-    )
-    dy, carry, zg, row_sums, gains, skips = call(
-        norm_back_kernel,
         [
-            (wide, BF, away), (part_shape if near else (state_size, width), BF, away), (wide, BF, away),
-            ((heads, length), F32, away), ((1, width), F32, away), ((heads, 1), F32, away),
-        ],
-        (c, z, x), aux, params, inner, factor, ng, name="norm_back",
-        scratch=[pltpu.VMEM(wide, F32)] + [pltpu.VMEM(wide, BF)] * 3,
+            (wide, BF, near_by), ((length, width // 2), BF, away), (wide, BF, away),
+            (wide, BF, away), ((heads, length), F32, away), ((8, width), F32, away),
+        ]
+        + ([(part_shape[1:], BF, away)] * n_tm if near else [((state_size, width), BF, away)]),
+        (c, z, x), aux, params, local, ng, incoming, name="norm",
+        scratch=[pltpu.VMEM(part_shape if near else (8, 128), BF)] + [pltpu.VMEM(wide, F32)] * 2 + [pltpu.VMEM(wide, BF)] * 3,
     )
 
     def mixed_of(*after):
@@ -612,8 +643,7 @@
                 ((length, state_size), BF, away), (wide, F32, away), ((length, state_size), BF, away),
                 ((heads, length), F32, away),
             ],
-            (dy, b, c, x), aux, params, incoming,
-            name="back", scratch=[pltpu.VMEM(wide, F32)], after=after,
+            (dy, b, c, x), aux, params, incoming, name="back", after=after, scratch=[pltpu.VMEM(wide, F32)],
         )
 
     everywhere = ("tm", "tok", "rep")
@@ -622,49 +652,49 @@
         return call(
             functools.partial(last_kernel, bool(more)),
             [(wide, BF, away), ((length, state_size), BF, away), ((heads, length), F32, away), (row, F32, away)],
-            (b, x, row_sums, col_sums, bg, xg, skips), place, aux, incoming, *more, *parts, name="last", after=after,
-            smem=(0,), scratch=[pltpu.VMEM((state_size, width), BF)],
-        )
-
-    ahead = [[(i, (i + k) % n_tm) for i in range(n_tm)] for k in range(1, n_tm)]
+            (b, x, row_sums, col_sums, bg, xg, gains), aux, incoming, *more, *parts, name="last", after=after,
+            scratch=[pltpu.VMEM((state_size, width), BF)],
+        )
+
     if near:
         theirs = lax.ppermute(other, "rep", core)
         (products,) = call(
-            outer_kernel, [((4, rows, model), BF, away)], (g, gc), place, normed, theirs,
-            smem=(0,), name="outer", after=(carry,),
-        )
-        grads = lax.all_to_all(carry, "tm", 0, 0, tiled=True)
-        own, *sends, gains = call(
-            suffix_kernel, [(part[1:] + (width,), BF, away)] * n_tm + [((blocks_of, 128), F32, near_by)], (), grads, blocks, place,
-            name="suffix", smem=(2,), scratch=[pltpu.VMEM(part + (width,), BF)], after=(products,),
+            outer_kernel, [((4, rows, model), BF, away)], (g, gc), normed, theirs, name="outer", after=(carry[0],)
+        )
+        grads = [carry[0]] + [lax.ppermute(v, "tm", pairs) for v, pairs in zip(carry[1:], ahead)]
+        mixed = mixed_of(products)
+        own, *sends, gains_tm = call(
+            suffix_kernel, [(row_part, BF, away)] * n_tm + [((blocks_of, 128), F32, near_by)], (),
+            decays, *grads, name="suffix", scratch=[pltpu.VMEM(part + (width,), BF), pltpu.VMEM(part_shape, BF)], after=(mixed,),
         )
         parts = [own] + [lax.ppermute(v, "tm", pairs) for v, pairs in zip(sends, ahead)]
-        (products,) = lax.optimization_barrier((products,))
         chips = lax.all_to_all(
             products, ("tok", "rep"), 0, 0, axis_index_groups=[[0, 2, 4, 6], [1, 3, 5, 7]], tiled=True
         )
         c_grad, xg, bg, col_sums = back(own)
-        mixed = mixed_of(col_sums)
-        quarters = (n_tm, rows // n_tm, model)
-        (share,) = call(add_kernel, [(quarters, BF, away)], (), chips, name="add_chips", after=(mixed,), beside=parts[1:])
-        shares = lax.all_to_all(share, "tm", 0, 0, tiled=True)
+        quarter = (rows // n_tm, model)
+        own, token, *sends = call(
+            share_kernel, [(quarter, F32, near_by), (quarter, BF, away)] + [(quarter, BF, away)] * (n_tm - 1), (), chips, name="add_chips",
+            after=(col_sums,), beside=parts[1:], scratch=[pltpu.VMEM((rows, model), F32)],
+        )
+        shares = [lax.ppermute(v, "tm", pairs) for v, pairs in zip(sends, ahead)]
         row = (n_tm * n_tok * n_rep, 1, 128 + width // n_tm)
-        x_grad, b_grad, step_grad, sums = last(row, parts, gains, after=(share,))
-        (quarter,) = call(add_kernel, [((1,) + quarters[1:], BF, away)], (), shares, name="add_blocks", after=(step_grad,))
-        pieces = [quarter[0]] + [lax.ppermute(quarter[0], "tm", pairs) for pairs in ahead]
-        (weight_grad,) = call(join_kernel, [((rows, model), BF, away)], (), place, *pieces, smem=(0,), name="join")
+        x_grad, b_grad, step_grad, sums = last(row, parts, gains_tm, after=(token,))
+        (quarter,) = call(add_kernel, [(quarter, BF, away)], (), own, *shares, name="add_blocks", after=(step_grad,))
+        pieces = [lax.ppermute(quarter, "tm", pairs) for pairs in ahead]
+        (weight_grad,) = call(join_kernel, [((rows, model), BF, away)], (quarter,), *pieces, name="join")
         sums = lax.all_to_all(sums, everywhere, 0, 0, tiled=True)
     else:
-        later = scan_far(carry, total, "tm", True)
+        later = scan_far(carry[0], total, "tm", True)
         (outer,) = call(outer_full_kernel, [(full, F32, free)], (), normed, g, name="outer")
         share = lax.psum_scatter(outer, ("tok", "rep"), scatter_dimension=0, tiled=True)
         weight_grad = lax.psum(share, "tm").astype(BF)
         mixed = mixed_of()
         c_grad, xg, bg, col_sums = back()
         x_grad, b_grad, step_grad, sums = last((1, 1, 128), (later,))
-        sums = lax.psum(jnp.concatenate([sums, gains[None]], axis=2), everywhere)
+        sums = lax.psum(jnp.concatenate([sums, gains[None, :1]], axis=2), everywhere)
     rate_grad, bias_grad, skip_grad, gain_grad = call(
-        sums_kernel, [((heads,), F32, away)] * 3 + [((width,), F32, away)], (sums,), name="sums"
+        sums_kernel, [((heads,), F32, away)] * 3 + [((width,), F32, away)], (sums,), name="sums", loose=True
     )
     return (
         mixed[None], x_grad[None], zg[None], b_grad[None], c_grad[None], step_grad[None],

time: 97.3 us -> 87.3 us (0.90)
  Pallas kernels: 37.9 us -> 31.4 us
  waiting for transfers between devices: 16.1 us -> 11.6 us
  starting transfers between devices: 40 us -> 42 us
    all_to_all x3 -> x0, starting transfers between devices: 15.7 us -> none  [the longest x1 6.33 us: shards(): blocks = lax.all_to_all(payload, 'tm', 0, 0, tiled=True)]
    ppermute x3 -> x9, starting transfers between devices: 2.29 us -> 15.3 us  [shards(): lax.ppermute(v, 'tm', pairs)]
    all_to_all x3 -> x0, waiting for transfers between devices: 10 us -> none  [the longest x1 4.54 us: shards(): grads = lax.all_to_all(carry, 'tm', 0, 0, tiled=True)]
    pallas_call x15 -> x14, Pallas kernels: 37.9 us -> 31.4 us  [call(): pl.pallas_call(body, out_shape=[where(shape, dtype) for shape, dtype, whe...]
    ppermute x3 -> x6, starting transfers between devices: 5.6 us -> 10 us  [the longest x3 5.6 us: shards(): pieces = [lax.ppermute(quarter, 'tm', pairs) for pairs in ahead]]
    ppermute x3 -> x9, waiting for transfers between devices: 0.01 us -> 2.66 us  [shards(): lax.ppermute(v, 'tm', pairs)]
    all_to_all x1, waiting for transfers between devices: 0.01 us -> 2.09 us  [shards(): lax.all_to_all(prefixes, 'tm', 0, 0, tiled=True).reshape(state_size, width)]
    ppermute x3 -> x6, waiting for transfers between devices: 0.76 us -> 2.14 us  [the longest x3 2.13 us: shards(): pieces = [lax.ppermute(quarter, 'tm', pairs) for pairs in ahead]]
  transfers between devices with their start and end apart: 21 -> 27, of which waited for: 12 -> 11; matrix products, arithmetic and copies ran while one was open for 0% -> 0% of each run, Pallas kernels for 35% -> 27%
where the time goes in v4:
time: 87.3 us; the launch traced here: 86.8 us
  starting transfers between devices  42 us (48%)
  Pallas kernels  31.4 us (36%)
  waiting for transfers between devices  11.6 us (13%)
  local copies, waits for them, and re-layouts  0.91 us (1%)
  between operations  0.88 us (1%)
    pallas_call x14, Pallas kernels, call(): pl.pallas_call(body, out_shape=[where(shape, dtype) for shape, dtype, whe...  31.4 us
    ppermute x9, starting transfers between devices, shards(): lax.ppermute(v, 'tm', pairs)  15.3 us
    ppermute x3, starting transfers between devices, shards(): pieces = [lax.ppermute(quarter, 'tm', pairs) for pairs in ahead]  5.6 us
    all_to_all x1, starting transfers between devices, shards(): lax.all_to_all(prefixes, 'tm', 0, 0, tiled=True).reshape(state_size, width)  4.41 us
    ppermute x3, starting transfers between devices, shards(): shares = [lax.ppermute(v, 'tm', pairs) for v, pairs in zip(sends, ahead)]  4.41 us
    all_to_all x1, starting transfers between devices, shards(): sums = lax.all_to_all(sums, everywhere, 0, 0, tiled=True)  3.96 us
    all_to_all x1, starting transfers between devices, shards(): lax.all_to_all(products, ('tok', 'rep'), 0, 0, axis_index_groups=[[0, 2,...  3.73 us
    ppermute x9, waiting for transfers between devices, shards(): lax.ppermute(v, 'tm', pairs)  2.66 us
  transfers between devices with their start and end apart: 27, of which 11 were waited for; matrix products, arithmetic and copies ran while one was open for 0% of the time, Pallas kernels for 27%

profile of v4, /device:TPU:0, one launch (start us, length us, event | category | flops | bytes accessed | tf_op | source)
XLA Modules:
  0.0 86.8 jit_solution(13312433450693366471)
XLA Ops:
  0.6 2.7 %state.1 = (f32[80,256]{1,0:T(8,128)S(1)}, f32[8,1024]{1,0:T(8,128)S(1)}, bf16[128,1024]{1,0:T(8,128)(2,1)}, bf16[272,128]{1,0:T(8,128)(2,1)}, bf16[272,128]{1,0...) custom-call(f32[16,256]{1,0:T(8,128)} %bitcast.33, f32[16]{0:T(128)} %refs_1_.1, f32[16]{0:T(128)} %refs_2_.1, ...), custom_call_target="tpu_custom_call" | custom-call | tf_op jit(solution)/shard_map/state/pallas_call | solution.py:145
  3.3 0.0 copy-start.4
  3.4 0.0 copy-start
  3.4 3.1 %collective-permute-start.7 = (bf16[272,128]{1,0:T(8,128)(2,1)}, bf16[272,128]{1,0:T(8,128)(2,1)S(1)}, u32[]{:S(2)}, u32[]{:S(2)}) collective-permute-start(bf16[272,128]{1,0:T(8,128)(2,1)} %get-tuple-element.56), channel_id=1, source_target_pairs={{0,8},{8,16},{16,24},{24,0},{1,9},{9,17},{17,25},{25,1},{2,10},{10... | collective-permute-start | bytes 208904 | tf_op jit(solution)/shard_map/ppermute | solution.py:597
  6.5 1.5 %collective-permute-start.1 = (bf16[128,1024]{1,0:T(8,128)(2,1)}, bf16[128,1024]{1,0:T(8,128)(2,1)S(1)}, u32[]{:S(2)}, u32[]{:S(2)}) collective-permute-start(bf16[128,1024]{1,0:T(8,128)(2,1)} %get-tuple-element.54.refs_1_), channel_id=1, source_target_pairs={{0,2},{1,3},{2,0},{3,1},{4,6},{5,7},{6,4},{7,5},{8,10},{9,11},{10,... | collective-permute-start | bytes 786440 | tf_op jit(solution)/shard_map/ppermute | solution.py:599
  7.9 1.5 %collective-permute-start.3 = (bf16[128,1024]{1,0:T(8,128)(2,1)}, bf16[128,1024]{1,0:T(8,128)(2,1)S(1)}, u32[]{:S(2)}, u32[]{:S(2)}) collective-permute-start(bf16[128,1024]{1,0:T(8,128)(2,1)} %get-tuple-element.54.refs_1_), channel_id=1, source_target_pairs={{0,4},{4,0},{1,5},{5,1},{2,6},{6,2},{3,7},{7,3},{8,12},{12,8},{9,1... | collective-permute-start | bytes 786440 | tf_op jit(solution)/shard_map/ppermute | solution.py:600
  9.5 0.5 collective-permute-start.5
  9.9 2.6 %collective-permute-start.8 = (bf16[272,128]{1,0:T(8,128)(2,1)}, bf16[272,128]{1,0:T(8,128)(2,1)S(1)}, u32[]{:S(2)}, u32[]{:S(2)}) collective-permute-start(bf16[272,128]{1,0:T(8,128)(2,1)} %get-tuple-element.57), channel_id=1, source_target_pairs={{0,16},{8,24},{16,0},{24,8},{1,17},{9,25},{17,1},{25,9},{2,18},{10... | collective-permute-start | bytes 208904 | tf_op jit(solution)/shard_map/ppermute | solution.py:597
  12.5 0.0 collective-permute-done.7.refs_1_
  12.5 1.3 %collective-permute-start.9 = (bf16[272,128]{1,0:T(8,128)(2,1)}, bf16[272,128]{1,0:T(8,128)(2,1)S(1)}, u32[]{:S(2)}, u32[]{:S(2)}) collective-permute-start(bf16[272,128]{1,0:T(8,128)(2,1)} %get-tuple-element.58), channel_id=1, source_target_pairs={{0,24},{8,0},{16,8},{24,16},{1,25},{9,1},{17,9},{25,17},{2,26},{10... | collective-permute-start | bytes 208904 | tf_op jit(solution)/shard_map/ppermute | solution.py:597
  13.9 2.4 %inner.1.refs_4_.refs_5_ = f32[256,1024]{1,0:T(8,128)S(1)} custom-call(bf16[256,128]{1,0:T(8,128)(2,1)} %bitcast.26, bf16[256,128]{1,0:T(8,128)(2,1)} %bitcast.29, bf16[256,1024]{1,0:T(8,128)(2,1)} %bitcast.20, f32[80,256]{1,0:T(8,128)S(1)} %get-tuple-element.59.refs_3_.refs_4_.refs_7_, f32[8,1024]{1,0:T(8,128)S(1)} %get-tuple-element.60.refs_4_.refs_5_, ...), custom_call_target="tpu_custom_call" | custom-call | tf_op jit(solution)/shard_map/inner/pallas_call | solution.py:145
  16.3 0.0 collective-permute-done.8.refs_2_
  16.3 0.7 collective-permute-done.9.refs_3_
  17.1 0.9 %copy-done.2 = bf16[272,128]{1,0:T(8,128)(2,1)S(1)} copy-done((bf16[272,128]{1,0:T(8,128)(2,1)S(1)}, bf16[272,128]{1,0:T(8,128)(2,1)}, u32[]{:S(2)}) %copy-start.2) | copy-done | bytes 69656
  17.9 0.8 prefix.1
  18.7 4.4 %all-to-all-start = ((bf16[4,32,1024]{2,1,0:T(8,128)(2,1)}), bf16[4,32,1024]{2,1,0:T(8,128)(2,1)S(1)}, u32[]{:S(2)}, u32[]{:S(2)}) async-start(bf16[4,32,1024]{2,1,0:T(8,128)(2,1)} %get-tuple-element.61.refs_9_), calls=%async_computation | async-start | bytes 524288 | tf_op jit(solution)/shard_map/all_to_all | solution.py:610
  23.2 0.0 collective-permute-start
  23.2 0.0 collective-permute-done.1.refs_3_
  23.2 0.5 collective-permute-start.2
  23.7 0.0 collective-permute-done.3.refs_5_
  23.7 0.1 collective-permute-start.4
  23.7 0.0 collective-permute-done.5.refs_7_
  23.8 0.4 collective-permute-start.6
  24.2 0.1 collective-permute-start.10
  24.3 0.4 collective-permute-done.refs_2_
  24.7 0.4 collective-permute-done.2.refs_4_
  25.1 0.4 collective-permute-done.4.refs_6_
  25.4 0.7 collective-permute-done.6.refs_8_
  26.2 1.6 %normed_grad.1 = (bf16[256,1024]{1,0:T(8,128)(2,1)S(1)}, bf16[1024,1024]{1,0:T(8,128)(2,1)}) custom-call(bf16[256,1024]{1,0:T(8,128)(2,1)S(1)} %bitcast.18, bf16[128,1024]{1,0:T(8,128)(2,1)S(1)} %copy-done.4, bf16[128,1024]{1,0:T(8,128)(2,1)S(1)} %collective-permute-done.refs_2_, bf16[128,1024]{1,0:T(8,128)(2,1)S(1)} %collective-permute-done.1.refs_3_, ...), custom_call_target="tpu_custom_call" | custom-call | tf_op jit(solution)/shard_map/normed_grad/pallas_call | solution.py:145
  27.8 2.1 %all-to-all-done = bf16[4,32,1024]{2,1,0:T(8,128)(2,1)S(1)} async-done(((bf16[4,32,1024]{2,1,0:T(8,128)(2,1)}), bf16[4,32,1024]{2,1,0:T(8,128)(2,1)S(1)}, u32[]{:S(2)}, u32[]{:S(2)}) %all-to-all-start) | async-done | bytes 262176 | tf_op jit(solution)/shard_map/all_to_all | solution.py:610
  29.9 4.4 %norm.1 = (bf16[256,1024]{1,0:T(8,128)(2,1)S(1)}, bf16[256,512]{1,0:T(8,128)(2,1)}, bf16[256,1024]{1,0:T(8,128)(2,1)}, bf16[256,1024]{1,0:T(8,128)(2,1)}, f32[16...) custom-call(bf16[256,128]{1,0:T(8,128)(2,1)} %bitcast.30, ...), custom_call_target="tpu_custom_call" | custom-call | tf_op jit(solution)/shard_map/norm/pallas_call | solution.py:145
  34.3 0.1 collective-permute-start.11
  34.4 1.7 %collective-permute-done.11.refs_3_ = bf16[256,512]{1,0:T(8,128)(2,1)S(1)} collective-permute-done((bf16[256,512]{1,0:T(8,128)(2,1)}, bf16[256,512]{1,0:T(8,128)(2,1)S(1)}, u32[]{:S(2)}, u32[]{:S(2)}) %collective-permute-start.11) | collective-permute-done | bytes 262176 | tf_op jit(solution)/shard_map/ppermute | solution.py:660
  36.2 3.0 %outer.1.refs_2_ = bf16[4,128,1024]{2,1,0:T(8,128)(2,1)} custom-call(bf16[256,1024]{1,0:T(8,128)(2,1)} %bitcast.16, bf16[256,1024]{1,0:T(8,128)(2,1)} %collective-permute-done.10.refs_1_, bf16[256,1024]{1,0:T(8,128)(2,1)S(1)} %get-tuple-element.64.refs_2_.refs_1_, bf16[256,512]{1,0:T(8,128)(2,1)S(1)} %collective-permute-done.11.refs_3_, ...), custom_call_target="tpu_custom_call" | custom-call | tf_op jit(solution)/shard_map/outer/pallas_call | solution.py:145
  39.2 3.7 %all-to-all-start.1 = ((bf16[4,128,1024]{2,1,0:T(8,128)(2,1)}), bf16[4,128,1024]{2,1,0:T(8,128)(2,1)S(1)}, u32[]{:S(2)}, u32[]{:S(2)}) async-start(bf16[4,128,1024]{2,1,0:T(8,128)(2,1)} %outer.1.refs_2_), calls=%async_computation.1 | async-start | bytes 2097152 | tf_op jit(solution)/shard_map/all_to_all | solution.py:671
  42.9 1.5 %collective-permute-start.12 = (bf16[272,128]{1,0:T(8,128)(2,1)S(1)}, bf16[272,128]{1,0:T(8,128)(2,1)S(1)}, u32[]{:S(2)}, u32[]{:S(2)}) collective-permute-start(bf16[272,128]{1,0:T(8,128)(2,1)S(1)} %copy-done.7), channel_id=1, source_target_pairs={{0,8},{8,16},{16,24},{24,0},{1,9},{9,17},{17,25},{25,1},{2,10},{10... | collective-permute-start | bytes 208904 | tf_op jit(solution)/shard_map/ppermute | solution.py:664
  44.4 1.3 %collective-permute-start.13 = (bf16[272,128]{1,0:T(8,128)(2,1)S(1)}, bf16[272,128]{1,0:T(8,128)(2,1)S(1)}, u32[]{:S(2)}, u32[]{:S(2)}) collective-permute-start(bf16[272,128]{1,0:T(8,128)(2,1)S(1)} %copy-done.6), channel_id=1, source_target_pairs={{0,16},{8,24},{16,0},{24,8},{1,17},{9,25},{17,1},{25,9},{2,18},{10... | collective-permute-start | bytes 208904 | tf_op jit(solution)/shard_map/ppermute | solution.py:664
  45.6 1.2 %collective-permute-start.14 = (bf16[272,128]{1,0:T(8,128)(2,1)S(1)}, bf16[272,128]{1,0:T(8,128)(2,1)S(1)}, u32[]{:S(2)}, u32[]{:S(2)}) collective-permute-start(bf16[272,128]{1,0:T(8,128)(2,1)S(1)} %copy-done.5), channel_id=1, source_target_pairs={{0,24},{8,0},{16,8},{24,16},{1,25},{9,1},{17,9},{25,17},{2,26},{10... | collective-permute-start | bytes 208904 | tf_op jit(solution)/shard_map/ppermute | solution.py:664
  46.8 3.1 %mixed.1.refs_5_ = bf16[256,1024]{1,0:T(8,128)(2,1)} custom-call(bf16[1024,1024]{1,0:T(8,128)(2,1)} %get-tuple-element.62.refs_0_, bf16[256,1024]{1,0:T(8,128)(2,1)S(1)} %get-tuple-element.64.refs_2_.refs_1_, bf16[4,128,1024]{2,1,0:T(8,128)(2,1)} %outer.1.refs_2_), custom_call_target="tpu_custom_call" | custom-call | tf_op jit(solution)/shard_map/mixed/pallas_call | solution.py:145
  50.0 1.9 %collective-permute-done.13.refs_3_ = bf16[272,128]{1,0:T(8,128)(2,1)S(1)} collective-permute-done((bf16[272,128]{1,0:T(8,128)(2,1)S(1)}, bf16[272,128]{1,0:T(8,128)(2,1)S(1)}, u32[]{:S(2)}, u32[]{:S(2)}) %collective-permute-start.13) | collective-permute-done | bytes 69664 | tf_op jit(solution)/shard_map/ppermute | solution.py:664
  51.9 0.8 suffix.1
  52.7 2.0 %collective-permute-start.15 = (bf16[32,1024]{1,0:T(8,128)(2,1)}, bf16[32,1024]{1,0:T(8,128)(2,1)S(1)}, u32[]{:S(2)}, u32[]{:S(2)}) collective-permute-start(bf16[32,1024]{1,0:T(8,128)(2,1)} %get-tuple-element.79), channel_id=1, source_target_pairs={{0,8},{8,16},{16,24},{24,0},{1,9},{9,17},{17,25},{25,1},{2,10},{10... | collective-permute-start | bytes 196616 | tf_op jit(solution)/shard_map/ppermute | solution.py:670
  54.7 1.1 %collective-permute-start.16 = (bf16[32,1024]{1,0:T(8,128)(2,1)}, bf16[32,1024]{1,0:T(8,128)(2,1)S(1)}, u32[]{:S(2)}, u32[]{:S(2)}) collective-permute-start(bf16[32,1024]{1,0:T(8,128)(2,1)} %get-tuple-element.80), channel_id=1, source_target_pairs={{0,16},{8,24},{16,0},{24,8},{1,17},{9,25},{17,1},{25,9},{2,18},{10... | collective-permute-start | bytes 196616 | tf_op jit(solution)/shard_map/ppermute | solution.py:670
  55.7 1.3 %collective-permute-start.17 = (bf16[32,1024]{1,0:T(8,128)(2,1)}, bf16[32,1024]{1,0:T(8,128)(2,1)S(1)}, u32[]{:S(2)}, u32[]{:S(2)}) collective-permute-start(bf16[32,1024]{1,0:T(8,128)(2,1)} %get-tuple-element.81), channel_id=1, source_target_pairs={{0,24},{8,0},{16,8},{24,16},{1,25},{9,1},{17,9},{25,17},{2,26},{10... | collective-permute-start | bytes 196616 | tf_op jit(solution)/shard_map/ppermute | solution.py:670
  57.1 4.6 %back.1 = (bf16[256,128]{1,0:T(8,128)(2,1)}, f32[256,1024]{1,0:T(8,128)}, bf16[256,128]{1,0:T(8,128)(2,1)}, f32[16,256]{1,0:T(8,128)}) custom-call(bf16[256,1024]{1,0:T(8,128)(2,1)} %get-tuple-element.68.refs_0_, bf16[256,128]{1,0:T(8,128)(2,1)} %bitcast.27, bf16[256,128]{1,0:T(8,128)(2,1)} %bitcast.31, bf16[256,1024]{1,0:T(8,128)(2,1)} %bitcast.22, ...), custom_call_target="tpu_custom_call" | custom-call | tf_op jit(solution)/shard_map/back/pallas_call | solution.py:145
  61.7 0.0 collective-permute-done.15.refs_2_.refs_11_
  61.7 0.0 collective-permute-done.16.refs_3_.refs_12_
  61.7 0.9 %add_chips.1 = (f32[32,1024]{1,0:T(8,128)S(1)}, bf16[32,1024]{1,0:T(8,128)(2,1)}, bf16[32,1024]{1,0:T(8,128)(2,1)}, bf16[32,1024]{1,0:T(8,128)(2,1)}, bf16[32,1024]{1,0:T(8,128)(2,1)}) custom-call(bf16[4,128,1024]{2,1,0:T(8,128)(2,1)S(1)} %all-to-all-done.1.refs_0_, f32[16,256]{1,0:T(8,128)} %get-tuple-element.74.refs_1_.refs_3_, ...), custom_call_target="tpu_custom_call" | custom-call | tf_op jit(solution)/shard_map/add_chips/pallas_call | solution.py:145
  62.6 1.7 %collective-permute-start.18 = (bf16[32,1024]{1,0:T(8,128)(2,1)}, bf16[32,1024]{1,0:T(8,128)(2,1)S(1)}, u32[]{:S(2)}, u32[]{:S(2)}) collective-permute-start(bf16[32,1024]{1,0:T(8,128)(2,1)} %get-tuple-element.94), channel_id=1, source_target_pairs={{0,8},{8,16},{16,24},{24,0},{1,9},{9,17},{17,25},{25,1},{2,10},{10... | collective-permute-start | bytes 196616 | tf_op jit(solution)/shard_map/ppermute | solution.py:680
  64.3 1.2 %collective-permute-start.19 = (bf16[32,1024]{1,0:T(8,128)(2,1)}, bf16[32,1024]{1,0:T(8,128)(2,1)S(1)}, u32[]{:S(2)}, u32[]{:S(2)}) collective-permute-start(bf16[32,1024]{1,0:T(8,128)(2,1)} %get-tuple-element.95), channel_id=1, source_target_pairs={{0,16},{8,24},{16,0},{24,8},{1,17},{9,25},{17,1},{25,9},{2,18},{10... | collective-permute-start | bytes 196616 | tf_op jit(solution)/shard_map/ppermute | solution.py:680
  65.6 1.5 %collective-permute-start.20 = (bf16[32,1024]{1,0:T(8,128)(2,1)}, bf16[32,1024]{1,0:T(8,128)(2,1)S(1)}, u32[]{:S(2)}, u32[]{:S(2)}) collective-permute-start(bf16[32,1024]{1,0:T(8,128)(2,1)} %get-tuple-element.96), channel_id=1, source_target_pairs={{0,24},{8,0},{16,8},{24,16},{1,25},{9,1},{17,9},{25,17},{2,26},{10... | collective-permute-start | bytes 196616 | tf_op jit(solution)/shard_map/ppermute | solution.py:680
  67.0 4.0 %last.1 = (bf16[256,1024]{1,0:T(8,128)(2,1)}, bf16[256,128]{1,0:T(8,128)(2,1)}, f32[16,256]{1,0:T(8,128)}, f32[32,1,384]{2,1,0:T(1,128)}) custom-call(bf16[256,128]{1,0:T(8,128)(2,1)} %bitcast.28, bf16[256,1024]{1,0:T(8,128)(2,1)} %bitcast.23, f32[16,256]{1,0:T(8,128)} %get-tuple-element.67.refs_2_, f32[16,256]{1,0:T(8,128)} %get-tuple-element.74.refs_1_.refs_3_, ...), custom_call_target="tpu_custom_call" | custom-call | tf_op jit(solution)/shard_map/last/pallas_call | solution.py:145
  71.1 4.0 %all-to-all-start.2 = ((f32[32,1,384]{2,1,0:T(1,128)}), f32[32,1,384]{2,1,0:T(1,128)S(1)}, u32[]{:S(2)}, u32[]{:S(2)}) async-start(f32[32,1,384]{2,1,0:T(1,128)} %get-tuple-element.88), calls=%async_computation.2 | async-start | bytes 98304 | tf_op jit(solution)/shard_map/all_to_all | solution.py:686
  75.0 0.0 collective-permute-done.18.refs_1_
  75.0 0.0 collective-permute-done.19.refs_2_
  75.1 0.7 add_blocks.1.refs_0_
  75.7 1.8 %collective-permute-start.21 = (bf16[32,1024]{1,0:T(8,128)(2,1)}, bf16[32,1024]{1,0:T(8,128)(2,1)S(1)}, u32[]{:S(2)}, u32[]{:S(2)}) collective-permute-start(bf16[32,1024]{1,0:T(8,128)(2,1)} %add_blocks.1.refs_0_), channel_id=1, source_target_pairs={{0,8},{8,16},{16,24},{24,0},{1,9},{9,17},{17,25},{25,1},{2,10},{10... | collective-permute-start | bytes 196616 | tf_op jit(solution)/shard_map/ppermute | solution.py:684
  77.5 2.4 %collective-permute-start.22 = (bf16[32,1024]{1,0:T(8,128)(2,1)}, bf16[32,1024]{1,0:T(8,128)(2,1)S(1)}, u32[]{:S(2)}, u32[]{:S(2)}) collective-permute-start(bf16[32,1024]{1,0:T(8,128)(2,1)} %add_blocks.1.refs_0_), channel_id=1, source_target_pairs={{0,16},{8,24},{16,0},{24,8},{1,17},{9,25},{17,1},{25,9},{2,18},{10... | collective-permute-start | bytes 196616 | tf_op jit(solution)/shard_map/ppermute | solution.py:684
  79.9 1.4 %collective-permute-start.23 = (bf16[32,1024]{1,0:T(8,128)(2,1)}, bf16[32,1024]{1,0:T(8,128)(2,1)S(1)}, u32[]{:S(2)}, u32[]{:S(2)}) collective-permute-start(bf16[32,1024]{1,0:T(8,128)(2,1)} %add_blocks.1.refs_0_), channel_id=1, source_target_pairs={{0,24},{8,0},{16,8},{24,16},{1,25},{9,1},{17,9},{25,17},{2,26},{10... | collective-permute-start | bytes 196616 | tf_op jit(solution)/shard_map/ppermute | solution.py:684
  81.3 1.0 %all-to-all-done.2.refs_0_ = f32[32,1,384]{2,1,0:T(1,128)S(1)} async-done(((f32[32,1,384]{2,1,0:T(1,128)}), f32[32,1,384]{2,1,0:T(1,128)S(1)}, u32[]{:S(2)}, u32[]{:S(2)}) %all-to-all-start.2) | async-done | bytes 49184 | tf_op jit(solution)/shard_map/all_to_all | solution.py:686
  82.4 0.7 sums.1
  83.1 1.9 %collective-permute-done.22.refs_2_ = bf16[32,1024]{1,0:T(8,128)(2,1)S(1)} collective-permute-done((bf16[32,1024]{1,0:T(8,128)(2,1)}, bf16[32,1024]{1,0:T(8,128)(2,1)S(1)}, u32[]{:S(2)}, u32[]{:S(2)}) %collective-permute-start.22) | collective-permute-done | bytes 65568 | tf_op jit(solution)/shard_map/ppermute | solution.py:684
  85.0 0.2 collective-permute-done.23.refs_3_
  85.2 1.6 %join.1 = bf16[128,1024]{1,0:T(8,128)(2,1)} custom-call(bf16[32,1024]{1,0:T(8,128)(2,1)} %add_blocks.1.refs_0_, bf16[32,1024]{1,0:T(8,128)(2,1)S(1)} %collective-permute-done.21.refs_1_, bf16[32,1024]{1,0:T(8,128)(2,1)S(1)} %collective-permute-done.22.refs_2_, bf16[32,1024]{1,0:T(8,128)(2,1)S(1)} %collective-permute-done.23.refs_3_), custom_call_target="tpu_custom_call" | custom-call | tf_op jit(solution)/shard_map/join/pallas_call | solution.py:145
  (20 shorter events, 0.0 us)
Async XLA Ops:
  3.3 19.8 %copy-start.4 = (bf16[128,1024]{1,0:T(8,128)(2,1)S(1)}, bf16[128,1024]{1,0:T(8,128)(2,1)}, u32[]{:S(2)}) copy-start(bf16[128,1024]{1,0:T(8,128)(2,1)} %get-tuple-element.54.refs_1_) | copy-start | bytes 786436
  3.4 20.8 %copy-start = (bf16[1,256,1024]{2,1,0:T(8,128)(2,1)S(1)}, bf16[1,256,1024]{2,1,0:T(8,128)(2,1)}, u32[]{:S(2)}) copy-start(bf16[1,256,1024]{2,1,0:T(8,128)(2,1)} %param.21) | copy-start | bytes 1572868
  3.4 9.2 %collective-permute-start.7 = (bf16[272,128]{1,0:T(8,128)(2,1)}, bf16[272,128]{1,0:T(8,128)(2,1)S(1)}, u32[]{:S(2)}, u32[]{:S(2)}) collective-permute-start(bf16[272,128]{1,0:T(8,128)(2,1)} %get-tuple-element.56), channel_id=1, source_target_pairs={{0,8},{8,16},{16,24},{24,0},{1,9},{9,17},{17,25},{25,1},{2,10},{10... | collective-permute-start | bytes 208904 | tf_op jit(solution)/shard_map/ppermute | solution.py:597
  6.5 16.7 %collective-permute-start.1 = (bf16[128,1024]{1,0:T(8,128)(2,1)}, bf16[128,1024]{1,0:T(8,128)(2,1)S(1)}, u32[]{:S(2)}, u32[]{:S(2)}) collective-permute-start(bf16[128,1024]{1,0:T(8,128)(2,1)} %get-tuple-element.54.refs_1_), channel_id=1, source_target_pairs={{0,2},{1,3},{2,0},{3,1},{4,6},{5,7},{6,4},{7,5},{8,10},{9,11},{10,... | collective-permute-start | bytes 786440 | tf_op jit(solution)/shard_map/ppermute | solution.py:599
  7.9 15.7 %collective-permute-start.3 = (bf16[128,1024]{1,0:T(8,128)(2,1)}, bf16[128,1024]{1,0:T(8,128)(2,1)S(1)}, u32[]{:S(2)}, u32[]{:S(2)}) collective-permute-start(bf16[128,1024]{1,0:T(8,128)(2,1)} %get-tuple-element.54.refs_1_), channel_id=1, source_target_pairs={{0,4},{4,0},{1,5},{5,1},{2,6},{6,2},{3,7},{7,3},{8,12},{12,8},{9,1... | collective-permute-start | bytes 786440 | tf_op jit(solution)/shard_map/ppermute | solution.py:600
  9.5 14.3 %collective-permute-start.5 = (bf16[128,1024]{1,0:T(8,128)(2,1)}, bf16[128,1024]{1,0:T(8,128)(2,1)S(1)}, u32[]{:S(2)}, u32[]{:S(2)}) collective-permute-start(bf16[128,1024]{1,0:T(8,128)(2,1)} %get-tuple-element.54.refs_1_), channel_id=1, source_target_pairs={{0,6},{1,7},{2,4},{3,5},{4,2},{5,3},{6,0},{7,1},{8,14},{9,15},{10,... | collective-permute-start | bytes 786440 | tf_op jit(solution)/shard_map/ppermute | solution.py:601
  9.9 6.4 %collective-permute-start.8 = (bf16[272,128]{1,0:T(8,128)(2,1)}, bf16[272,128]{1,0:T(8,128)(2,1)S(1)}, u32[]{:S(2)}, u32[]{:S(2)}) collective-permute-start(bf16[272,128]{1,0:T(8,128)(2,1)} %get-tuple-element.57), channel_id=1, source_target_pairs={{0,16},{8,24},{16,0},{24,8},{1,17},{9,25},{17,1},{25,9},{2,18},{10... | collective-permute-start | bytes 208904 | tf_op jit(solution)/shard_map/ppermute | solution.py:597
  12.5 4.5 %collective-permute-start.9 = (bf16[272,128]{1,0:T(8,128)(2,1)}, bf16[272,128]{1,0:T(8,128)(2,1)S(1)}, u32[]{:S(2)}, u32[]{:S(2)}) collective-permute-start(bf16[272,128]{1,0:T(8,128)(2,1)} %get-tuple-element.58), channel_id=1, source_target_pairs={{0,24},{8,0},{16,8},{24,16},{1,25},{9,1},{17,9},{25,17},{2,26},{10... | collective-permute-start | bytes 208904 | tf_op jit(solution)/shard_map/ppermute | solution.py:597
  17.1 0.9 %copy-start.2 = (bf16[272,128]{1,0:T(8,128)(2,1)S(1)}, bf16[272,128]{1,0:T(8,128)(2,1)}, u32[]{:S(2)}) copy-start(bf16[272,128]{1,0:T(8,128)(2,1)} %get-tuple-element.55.refs_5_.refs_0_) | copy-start | bytes 208900
  18.7 11.2 %all-to-all-start = ((bf16[4,32,1024]{2,1,0:T(8,128)(2,1)}), bf16[4,32,1024]{2,1,0:T(8,128)(2,1)S(1)}, u32[]{:S(2)}, u32[]{:S(2)}) async-start(bf16[4,32,1024]{2,1,0:T(8,128)(2,1)} %get-tuple-element.61.refs_9_), calls=%async_computation | async-start | bytes 524288 | tf_op jit(solution)/shard_map/all_to_all | solution.py:610
  23.2 1.5 %collective-permute-start = (bf16[128,1024]{1,0:T(8,128)(2,1)S(1)}, bf16[128,1024]{1,0:T(8,128)(2,1)S(1)}, u32[]{:S(2)}, u32[]{:S(2)}) collective-permute-start(bf16[128,1024]{1,0:T(8,128)(2,1)S(1)} %copy-done.4), channel_id=1, source_target_pairs={{0,1},{1,0},{2,3},{3,2},{4,5},{5,4},{6,7},{7,6},{8,9},{9,8},{10,11... | collective-permute-start | bytes 786440 | tf_op jit(solution)/shard_map/ppermute | solution.py:602
  23.2 1.9 %collective-permute-start.2 = (bf16[128,1024]{1,0:T(8,128)(2,1)S(1)}, bf16[128,1024]{1,0:T(8,128)(2,1)S(1)}, u32[]{:S(2)}, u32[]{:S(2)}) collective-permute-start(bf16[128,1024]{1,0:T(8,128)(2,1)S(1)} %collective-permute-done.1.refs_3_), channel_id=1, source_target_pairs={{0,1},{1,0},{2,3},{3,2},{4,5},{5,4},{6,7},{7,6},{8,9},{9,8},{10,11... | collective-permute-start | bytes 786440 | tf_op jit(solution)/shard_map/ppermute | solution.py:602
  23.7 1.8 %collective-permute-start.4 = (bf16[128,1024]{1,0:T(8,128)(2,1)S(1)}, bf16[128,1024]{1,0:T(8,128)(2,1)S(1)}, u32[]{:S(2)}, u32[]{:S(2)}) collective-permute-start(bf16[128,1024]{1,0:T(8,128)(2,1)S(1)} %collective-permute-done.3.refs_5_), channel_id=1, source_target_pairs={{0,1},{1,0},{2,3},{3,2},{4,5},{5,4},{6,7},{7,6},{8,9},{9,8},{10,11... | collective-permute-start | bytes 786440 | tf_op jit(solution)/shard_map/ppermute | solution.py:602
  23.8 2.4 %collective-permute-start.6 = (bf16[128,1024]{1,0:T(8,128)(2,1)S(1)}, bf16[128,1024]{1,0:T(8,128)(2,1)S(1)}, u32[]{:S(2)}, u32[]{:S(2)}) collective-permute-start(bf16[128,1024]{1,0:T(8,128)(2,1)S(1)} %collective-permute-done.5.refs_7_), channel_id=1, source_target_pairs={{0,1},{1,0},{2,3},{3,2},{4,5},{5,4},{6,7},{7,6},{8,9},{9,8},{10,11... | collective-permute-start | bytes 786440 | tf_op jit(solution)/shard_map/ppermute | solution.py:602
  24.2 10.2 %collective-permute-start.10 = (bf16[256,1024]{1,0:T(8,128)(2,1)S(1)}, bf16[256,1024]{1,0:T(8,128)(2,1)}, u32[]{:S(2)}, u32[]{:S(2)}) collective-permute-start(bf16[256,1024]{1,0:T(8,128)(2,1)S(1)} %bitcast.17), channel_id=1, source_target_pairs={{0,1},{1,0},{2,3},{3,2},{4,5},{5,4},{6,7},{7,6},{8,9},{9,8},{10,11... | collective-permute-start | bytes 1572872 | tf_op jit(solution)/shard_map/ppermute | solution.py:598
  34.3 1.8 %collective-permute-start.11 = (bf16[256,512]{1,0:T(8,128)(2,1)}, bf16[256,512]{1,0:T(8,128)(2,1)S(1)}, u32[]{:S(2)}, u32[]{:S(2)}) collective-permute-start(bf16[256,512]{1,0:T(8,128)(2,1)} %get-tuple-element.65), channel_id=1, source_target_pairs={{0,1},{1,0},{2,3},{3,2},{4,5},{5,4},{6,7},{7,6},{8,9},{9,8},{10,11... | collective-permute-start | bytes 786440 | tf_op jit(solution)/shard_map/ppermute | solution.py:660
  36.2 6.8 %copy-start.7 = (bf16[272,128]{1,0:T(8,128)(2,1)S(1)}, bf16[272,128]{1,0:T(8,128)(2,1)}, u32[]{:S(2)}) copy-start(bf16[272,128]{1,0:T(8,128)(2,1)} %get-tuple-element.70) | copy-start | bytes 208900
  36.2 8.2 %copy-start.6 = (bf16[272,128]{1,0:T(8,128)(2,1)S(1)}, bf16[272,128]{1,0:T(8,128)(2,1)}, u32[]{:S(2)}) copy-start(bf16[272,128]{1,0:T(8,128)(2,1)} %get-tuple-element.71) | copy-start | bytes 208900
  36.2 9.5 %copy-start.5 = (bf16[272,128]{1,0:T(8,128)(2,1)S(1)}, bf16[272,128]{1,0:T(8,128)(2,1)}, u32[]{:S(2)}) copy-start(bf16[272,128]{1,0:T(8,128)(2,1)} %get-tuple-element.72) | copy-start | bytes 208900
  39.2 22.5 %all-to-all-start.1 = ((bf16[4,128,1024]{2,1,0:T(8,128)(2,1)}), bf16[4,128,1024]{2,1,0:T(8,128)(2,1)S(1)}, u32[]{:S(2)}, u32[]{:S(2)}) async-start(bf16[4,128,1024]{2,1,0:T(8,128)(2,1)} %outer.1.refs_2_), calls=%async_computation.1 | async-start | bytes 2097152 | tf_op jit(solution)/shard_map/all_to_all | solution.py:671
  42.9 7.1 %collective-permute-start.12 = (bf16[272,128]{1,0:T(8,128)(2,1)S(1)}, bf16[272,128]{1,0:T(8,128)(2,1)S(1)}, u32[]{:S(2)}, u32[]{:S(2)}) collective-permute-start(bf16[272,128]{1,0:T(8,128)(2,1)S(1)} %copy-done.7), channel_id=1, source_target_pairs={{0,8},{8,16},{16,24},{24,0},{1,9},{9,17},{17,25},{25,1},{2,10},{10... | collective-permute-start | bytes 208904 | tf_op jit(solution)/shard_map/ppermute | solution.py:664
  44.4 7.5 %collective-permute-start.13 = (bf16[272,128]{1,0:T(8,128)(2,1)S(1)}, bf16[272,128]{1,0:T(8,128)(2,1)S(1)}, u32[]{:S(2)}, u32[]{:S(2)}) collective-permute-start(bf16[272,128]{1,0:T(8,128)(2,1)S(1)} %copy-done.6), channel_id=1, source_target_pairs={{0,16},{8,24},{16,0},{24,8},{1,17},{9,25},{17,1},{25,9},{2,18},{10... | collective-permute-start | bytes 208904 | tf_op jit(solution)/shard_map/ppermute | solution.py:664
  45.6 6.2 %collective-permute-start.14 = (bf16[272,128]{1,0:T(8,128)(2,1)S(1)}, bf16[272,128]{1,0:T(8,128)(2,1)S(1)}, u32[]{:S(2)}, u32[]{:S(2)}) collective-permute-start(bf16[272,128]{1,0:T(8,128)(2,1)S(1)} %copy-done.5), channel_id=1, source_target_pairs={{0,24},{8,0},{16,8},{24,16},{1,25},{9,1},{17,9},{25,17},{2,26},{10... | collective-permute-start | bytes 208904 | tf_op jit(solution)/shard_map/ppermute | solution.py:664
  46.8 5.1 %copy-start.1 = (bf16[272,128]{1,0:T(8,128)(2,1)S(1)}, bf16[272,128]{1,0:T(8,128)(2,1)}, u32[]{:S(2)}) copy-start(bf16[272,128]{1,0:T(8,128)(2,1)} %get-tuple-element.66.refs_4_.refs_1_) | copy-start | bytes 208900
  52.7 14.3 %copy-start.3 = (bf16[32,1024]{1,0:T(8,128)(2,1)S(1)}, bf16[32,1024]{1,0:T(8,128)(2,1)}, u32[]{:S(2)}) copy-start(bf16[32,1024]{1,0:T(8,128)(2,1)} %get-tuple-element.73.refs_7_.refs_10_) | copy-start | bytes 196612
  52.7 9.0 %collective-permute-start.15 = (bf16[32,1024]{1,0:T(8,128)(2,1)}, bf16[32,1024]{1,0:T(8,128)(2,1)S(1)}, u32[]{:S(2)}, u32[]{:S(2)}) collective-permute-start(bf16[32,1024]{1,0:T(8,128)(2,1)} %get-tuple-element.79), channel_id=1, source_target_pairs={{0,8},{8,16},{16,24},{24,0},{1,9},{9,17},{17,25},{25,1},{2,10},{10... | collective-permute-start | bytes 196616 | tf_op jit(solution)/shard_map/ppermute | solution.py:670
  54.7 7.0 %collective-permute-start.16 = (bf16[32,1024]{1,0:T(8,128)(2,1)}, bf16[32,1024]{1,0:T(8,128)(2,1)S(1)}, u32[]{:S(2)}, u32[]{:S(2)}) collective-permute-start(bf16[32,1024]{1,0:T(8,128)(2,1)} %get-tuple-element.80), channel_id=1, source_target_pairs={{0,16},{8,24},{16,0},{24,8},{1,17},{9,25},{17,1},{25,9},{2,18},{10... | collective-permute-start | bytes 196616 | tf_op jit(solution)/shard_map/ppermute | solution.py:670
  55.7 6.0 %collective-permute-start.17 = (bf16[32,1024]{1,0:T(8,128)(2,1)}, bf16[32,1024]{1,0:T(8,128)(2,1)S(1)}, u32[]{:S(2)}, u32[]{:S(2)}) collective-permute-start(bf16[32,1024]{1,0:T(8,128)(2,1)} %get-tuple-element.81), channel_id=1, source_target_pairs={{0,24},{8,0},{16,8},{24,16},{1,25},{9,1},{17,9},{25,17},{2,26},{10... | collective-permute-start | bytes 196616 | tf_op jit(solution)/shard_map/ppermute | solution.py:670
  62.6 12.4 %collective-permute-start.18 = (bf16[32,1024]{1,0:T(8,128)(2,1)}, bf16[32,1024]{1,0:T(8,128)(2,1)S(1)}, u32[]{:S(2)}, u32[]{:S(2)}) collective-permute-start(bf16[32,1024]{1,0:T(8,128)(2,1)} %get-tuple-element.94), channel_id=1, source_target_pairs={{0,8},{8,16},{16,24},{24,0},{1,9},{9,17},{17,25},{25,1},{2,10},{10... | collective-permute-start | bytes 196616 | tf_op jit(solution)/shard_map/ppermute | solution.py:680
  64.3 10.7 %collective-permute-start.19 = (bf16[32,1024]{1,0:T(8,128)(2,1)}, bf16[32,1024]{1,0:T(8,128)(2,1)S(1)}, u32[]{:S(2)}, u32[]{:S(2)}) collective-permute-start(bf16[32,1024]{1,0:T(8,128)(2,1)} %get-tuple-element.95), channel_id=1, source_target_pairs={{0,16},{8,24},{16,0},{24,8},{1,17},{9,25},{17,1},{25,9},{2,18},{10... | collective-permute-start | bytes 196616 | tf_op jit(solution)/shard_map/ppermute | solution.py:680
  65.6 9.5 %collective-permute-start.20 = (bf16[32,1024]{1,0:T(8,128)(2,1)}, bf16[32,1024]{1,0:T(8,128)(2,1)S(1)}, u32[]{:S(2)}, u32[]{:S(2)}) collective-permute-start(bf16[32,1024]{1,0:T(8,128)(2,1)} %get-tuple-element.96), channel_id=1, source_target_pairs={{0,24},{8,0},{16,8},{24,16},{1,25},{9,1},{17,9},{25,17},{2,26},{10... | collective-permute-start | bytes 196616 | tf_op jit(solution)/shard_map/ppermute | solution.py:680
  71.1 11.3 %all-to-all-start.2 = ((f32[32,1,384]{2,1,0:T(1,128)}), f32[32,1,384]{2,1,0:T(1,128)S(1)}, u32[]{:S(2)}, u32[]{:S(2)}) async-start(f32[32,1,384]{2,1,0:T(1,128)} %get-tuple-element.88), calls=%async_computation.2 | async-start | bytes 98304 | tf_op jit(solution)/shard_map/all_to_all | solution.py:686
  75.7 7.3 %collective-permute-start.21 = (bf16[32,1024]{1,0:T(8,128)(2,1)}, bf16[32,1024]{1,0:T(8,128)(2,1)S(1)}, u32[]{:S(2)}, u32[]{:S(2)}) collective-permute-start(bf16[32,1024]{1,0:T(8,128)(2,1)} %add_blocks.1.refs_0_), channel_id=1, source_target_pairs={{0,8},{8,16},{16,24},{24,0},{1,9},{9,17},{17,25},{25,1},{2,10},{10... | collective-permute-start | bytes 196616 | tf_op jit(solution)/shard_map/ppermute | solution.py:684
  77.5 7.5 %collective-permute-start.22 = (bf16[32,1024]{1,0:T(8,128)(2,1)}, bf16[32,1024]{1,0:T(8,128)(2,1)S(1)}, u32[]{:S(2)}, u32[]{:S(2)}) collective-permute-start(bf16[32,1024]{1,0:T(8,128)(2,1)} %add_blocks.1.refs_0_), channel_id=1, source_target_pairs={{0,16},{8,24},{16,0},{24,8},{1,17},{9,25},{17,1},{25,9},{2,18},{10... | collective-permute-start | bytes 196616 | tf_op jit(solution)/shard_map/ppermute | solution.py:684
  79.9 5.3 %collective-permute-start.23 = (bf16[32,1024]{1,0:T(8,128)(2,1)}, bf16[32,1024]{1,0:T(8,128)(2,1)S(1)}, u32[]{:S(2)}, u32[]{:S(2)}) collective-permute-start(bf16[32,1024]{1,0:T(8,128)(2,1)} %add_blocks.1.refs_0_), channel_id=1, source_target_pairs={{0,24},{8,0},{16,8},{24,16},{1,25},{9,1},{17,9},{25,17},{2,26},{10... | collective-permute-start | bytes 196616 | tf_op jit(solution)/shard_map/ppermute | solution.py:684

commit v5 on v4

--- a/solution.py
+++ b/solution.py
@@ -117,6 +117,8 @@
 
 def call(kernel, outs, far, *args, name=None, scratch=(), after=(), beside=(), aliases=None, far_operands=(), held=0, loose=False):
     waits = len(after) + len(beside)
+    anywhere = [isinstance(v, list) for v in far]
+    far = [v[0] if isinstance(v, list) else v for v in far]
 
     def fix(v):
         return v if loose else pltpu.with_memory_space_constraint(v, pltpu.HBM)
@@ -153,7 +155,7 @@
         input_output_aliases=aliases or {},
         compiler_params=pltpu.CompilerParams(vmem_limit_bytes=VMEM_LIMIT),
         name=name,
-    )(*[fix(v) for v in far], *args, *[pltpu.with_memory_space_constraint(v, pltpu.HBM) for v in after], *beside)
+    )(*[v if any_place else fix(v) for v, any_place in zip(far, anywhere)], *args, *[pltpu.with_memory_space_constraint(v, pltpu.HBM) for v in after], *beside)
 
 
 def store_decay(aux_ref, rows_ref, v, delta, a, ld, cum, skip, gain):
@@ -234,9 +236,10 @@
         out_ref[pl.ds(pl.multiple_of(turn(-k, count) * rows, rows), rows), :] = one[...]
 
 
-def suffix_kernel(decays_ref, *refs):
-    count = (len(refs) - 3) // 2
-    gots, outs, (gains_ref, out_ref, all_ref) = refs[:count], refs[count:-3], refs[-3:]
+def suffix_kernel(decays_ref, products_ref, *refs):
+    count = (len(refs) - 4) // 2
+    gots, outs, (passed_ref, gains_ref, out_ref, all_ref) = refs[:count], refs[count:-4], refs[-4:]
+    del products_ref, passed_ref
     _, rows, width = out_ref.shape
     blocks = width // 128
     for k, got in enumerate(gots):
@@ -321,12 +324,13 @@
 ):
     carries, (all_ref, inner_ref, ec_ref, de_ref, hi_ref, lo_ref) = refs[:-6], refs[-6:]
     _, _, _, cum, _ = load_decay(aux_ref)
-    c_ref, z_ref, x_ref = c_in.ready(), z_in.ready(), x_in.ready()
     heads, length = cum.shape
-    width = x_ref.shape[1]
+    width = params_ref.shape[1]
     hmap = head_map(heads, width)
     ec_ref[...] = expand(jnp.exp(cum), hmap)
+    c_ref = c_in.ready()
     inner_ref[...] = mm(c_ref[...], inc_ref[...])
+    z_ref, x_ref = z_in.ready(), x_in.ready()
     skip, gain = params_ref[0:1, :], params_ref[1:2, :]
     step = length // CHUNKS
     gains = jnp.zeros((1, width), F32)
@@ -390,7 +394,7 @@
     total_ref[...] = total
     rows = outs[0].shape[0]
     for k, out_ref in enumerate(outs):
-        part = total_ref[pl.ds(pl.multiple_of(turn(max(k - 1, 0), len(outs) - 1) * rows, rows), rows), :]
+        part = total_ref[pl.ds(pl.multiple_of(turn(k, len(outs)) * rows, rows), rows), :]
         out_ref[...] = part.astype(out_ref.dtype)
 
 
@@ -406,8 +410,8 @@
     mixed_ref[...] = mm(normed_ref[...], weight_in.ready()[...]).astype(BF)
 
 
-def join_kernel(own_in, *refs):
-    gather_rows((own_in.ready(),) + refs[:-1], refs[-1])
+def join_kernel(*refs):
+    gather_rows(refs[:-1], refs[-1])
 
 
 def outer_full_kernel(normed_ref, g_ref, out_ref):
@@ -493,17 +497,17 @@
     else:
         later_ref[...] = parts[0][...]
     v, delta, ld, cum, a = load_decay(aux_ref)
-    x_ref, b_ref = x_in.ready(), b_in.ready()
     heads, length = cum.shape
-    width = x_ref.shape[1]
+    width = xg_in.target.shape[1]
     hmap = head_map(heads, width)
     last = cum[:, -1:]
     tailing = jnp.exp(last - cum)
     tail = tailing * delta
     tail_e = expand(tail, hmap)
-    x = x_ref[...].astype(F32)
+    b_ref = b_in.ready()
     later = later_ref[...]
     dweighted = mm(b_ref[...], later)
+    x = x_in.ready()[...].astype(F32)
     x_out[...] = (xg_in.ready()[...] + tail_e * dweighted).astype(BF)
     weighted = (x * tail_e).astype(BF)
     b_out[...] = (bg_in.ready()[...].astype(F32) + mm_nt(weighted, later)).astype(BF)
@@ -591,7 +595,7 @@
         blocks_of = width // 128
         part_shape = (n_tm, blocks_of * part[1] + 2 * blocks_of, 128)
         aux, params, out_weight, *payload = call(
-            payload_kernel, aux_shapes + [(part_shape[1:], BF, away)] * n_tm, raw, name="state",
+            payload_kernel, aux_shapes + [(part_shape[1:], BF, free)] * n_tm, raw, name="state",
             scratch=[pltpu.VMEM(part_shape, BF)],
         )
         blocks = [payload[0]] + [lax.ppermute(v, "tm", pairs) for v, pairs in zip(payload[1:], ahead)]
@@ -600,16 +604,16 @@
         wy = lax.ppermute(out_weight, "tok", front)
         wd = lax.ppermute(out_weight, ("tok", "rep"), diagonal)
         wc, wxc, wyc, wdc = (lax.ppermute(v, "rep", core) for v in (out_weight, wx, wy, wd))
+        prefixes, decays = call(
+            prefix_kernel, [(part + (width,), BF, free), ((n_tm * blocks_of, 128), F32, near_by)], (), *blocks,
+            name="prefix", scratch=[pltpu.VMEM(part_shape, BF)],
+        )
+        incoming = lax.all_to_all(prefixes, "tm", 0, 0, tiled=True).reshape(state_size, width)
         (local,) = call(
-            inner_kernel, [(wide, F32, near_by)], (b, c, x), aux, params, name="inner", after=(payload[0],)
-        )
-        prefixes, decays = call(
-            prefix_kernel, [(part + (width,), BF, away), ((n_tm * blocks_of, 128), F32, near_by)], (), *blocks,
-            name="prefix", beside=(local,), scratch=[pltpu.VMEM(part_shape, BF)],
-        )
-        incoming = lax.all_to_all(prefixes, "tm", 0, 0, tiled=True).reshape(state_size, width)
+            inner_kernel, [(wide, F32, near_by)], (b, c, x), aux, params, name="inner", beside=(prefixes,)
+        )
         pieces = (out_weight, wc, wx, wxc, wy, wyc, wd, wdc)
-        after = (prefixes,)
+        after = ()
     else:
         aux, params, out_weight, state, total = call(
             payload_kernel, aux_shapes + [((state_size, width), BF, free), ((1, width), F32, free)], raw, name="state"
@@ -619,16 +623,16 @@
         pieces = (lax.all_gather(out_weight, ("tok", "rep"), axis=0, tiled=True),)
         after = ()
     ng, weight = call(
-        weight_kernel, [(wide, BF, near_by), (full, BF, away)], (g,), *pieces, name="normed_grad", after=after, held=len(pieces), loose=True,
+        weight_kernel, [(wide, BF, near_by), (full, BF, away)], (g,), *pieces, name="normed_grad", after=after, beside=(local,), held=len(pieces), loose=True,
         scratch=[pltpu.SemaphoreType.DMA((len(pieces),))],
     )
     normed, other, dy, zg, row_sums, gains, *carry = call(
         norm_kernel,
         [
-            (wide, BF, near_by), ((length, width // 2), BF, away), (wide, BF, away),
-            (wide, BF, away), ((heads, length), F32, away), ((8, width), F32, away),
+            (wide, BF, near_by), ((length, width // 2), BF, free), (wide, BF, free),
+            (wide, BF, away), ((heads, length), F32, free), ((8, width), F32, free),
         ]
-        + ([(part_shape[1:], BF, away)] * n_tm if near else [((state_size, width), BF, away)]),
+        + ([(part_shape[1:], BF, free)] * n_tm if near else [((state_size, width), BF, away)]),
         (c, z, x), aux, params, local, ng, incoming, name="norm",
         scratch=[pltpu.VMEM(part_shape if near else (8, 128), BF)] + [pltpu.VMEM(wide, F32)] * 2 + [pltpu.VMEM(wide, BF)] * 3,
     )
@@ -640,10 +644,10 @@
         return call(
             back_kernel,
             [
-                ((length, state_size), BF, away), (wide, F32, away), ((length, state_size), BF, away),
-                ((heads, length), F32, away),
+                ((length, state_size), BF, away), (wide, F32, free), ((length, state_size), BF, free),
+                ((heads, length), F32, free),
             ],
-            (dy, b, c, x), aux, params, incoming, name="back", after=after, scratch=[pltpu.VMEM(wide, F32)],
+            ([dy], b, c, x), aux, params, incoming, name="back", beside=after, scratch=[pltpu.VMEM(wide, F32)],
         )
 
     everywhere = ("tm", "tok", "rep")
@@ -652,37 +656,37 @@
         return call(
             functools.partial(last_kernel, bool(more)),
             [(wide, BF, away), ((length, state_size), BF, away), ((heads, length), F32, away), (row, F32, away)],
-            (b, x, row_sums, col_sums, bg, xg, gains), aux, incoming, *more, *parts, name="last", after=after,
+            (b, x, [row_sums], [col_sums], [bg], [xg], [gains]), aux, incoming, *more, *parts, name="last", after=after,
             scratch=[pltpu.VMEM((state_size, width), BF)],
         )
 
     if near:
         theirs = lax.ppermute(other, "rep", core)
         (products,) = call(
-            outer_kernel, [((4, rows, model), BF, away)], (g, gc), normed, theirs, name="outer", after=(carry[0],)
+            outer_kernel, [((4, rows, model), BF, away)], (g, gc), normed, theirs, name="outer", beside=(carry[0],)
         )
         grads = [carry[0]] + [lax.ppermute(v, "tm", pairs) for v, pairs in zip(carry[1:], ahead)]
         mixed = mixed_of(products)
-        own, *sends, gains_tm = call(
-            suffix_kernel, [(row_part, BF, away)] * n_tm + [((blocks_of, 128), F32, near_by)], (),
-            decays, *grads, name="suffix", scratch=[pltpu.VMEM(part + (width,), BF), pltpu.VMEM(part_shape, BF)], after=(mixed,),
+        own, *sends, products, gains_tm = call(
+            suffix_kernel, [(row_part, BF, free)] * n_tm + [(products.shape, BF, away), ((blocks_of, 128), F32, near_by)], (),
+            decays, products, *grads, name="suffix", far_operands=(1,), aliases={1: n_tm}, scratch=[pltpu.VMEM(part + (width,), BF), pltpu.VMEM(part_shape, BF)], after=(mixed,),
         )
         parts = [own] + [lax.ppermute(v, "tm", pairs) for v, pairs in zip(sends, ahead)]
         chips = lax.all_to_all(
             products, ("tok", "rep"), 0, 0, axis_index_groups=[[0, 2, 4, 6], [1, 3, 5, 7]], tiled=True
         )
         c_grad, xg, bg, col_sums = back(own)
+        row = (n_tm * n_tok * n_rep, 1, 128 + width // n_tm)
+        x_grad, b_grad, step_grad, sums = last(row, parts, gains_tm)
         quarter = (rows // n_tm, model)
-        own, token, *sends = call(
-            share_kernel, [(quarter, F32, near_by), (quarter, BF, away)] + [(quarter, BF, away)] * (n_tm - 1), (), chips, name="add_chips",
-            after=(col_sums,), beside=parts[1:], scratch=[pltpu.VMEM((rows, model), F32)],
+        own, *sends = call(
+            share_kernel, [(quarter, F32, near_by)] + [(quarter, BF, free)] * (n_tm - 1), (), chips, name="add_chips",
+            after=(step_grad,), scratch=[pltpu.VMEM((rows, model), F32)],
         )
         shares = [lax.ppermute(v, "tm", pairs) for v, pairs in zip(sends, ahead)]
-        row = (n_tm * n_tok * n_rep, 1, 128 + width // n_tm)
-        x_grad, b_grad, step_grad, sums = last(row, parts, gains_tm, after=(token,))
-        (quarter,) = call(add_kernel, [(quarter, BF, away)], (), own, *shares, name="add_blocks", after=(step_grad,))
+        (quarter,) = call(add_kernel, [(quarter, BF, free)], (), own, *shares, name="add_blocks")
         pieces = [lax.ppermute(quarter, "tm", pairs) for pairs in ahead]
-        (weight_grad,) = call(join_kernel, [((rows, model), BF, away)], (quarter,), *pieces, name="join")
+        (weight_grad,) = call(join_kernel, [((rows, model), BF, away)], (), quarter, *pieces, name="join")
         sums = lax.all_to_all(sums, everywhere, 0, 0, tiled=True)
     else:
         later = scan_far(carry[0], total, "tm", True)

time: 87.3 us -> 79.2 us (0.907)
  Pallas kernels: 31.4 us -> 26.9 us
  starting transfers between devices: 42 us -> 40.4 us
  waiting for transfers between devices: 11.6 us -> 10.5 us
  local copies, waits for them, and re-layouts: 0.91 us -> 0.01 us
    pallas_call x14, Pallas kernels: 31.4 us -> 26.9 us  [call(): pl.pallas_call(body, out_shape=[where(shape, dtype) for shape, dtype, whe...]
    ppermute x4, waiting for transfers between devices: 1.92 us -> 0.01 us  [shards(): lax.ppermute(v, 'rep', core)]
    ppermute x1, waiting for transfers between devices: 1.72 us -> 0.01 us  [shards(): theirs = lax.ppermute(other, 'rep', core)]
    all_to_all x1, waiting for transfers between devices: 0.01 us -> 1.42 us  [shards(): lax.all_to_all(products, ('tok', 'rep'), 0, 0, axis_index_groups=[[0, 2,...]
    all_to_all x1, starting transfers between devices: 3.96 us -> 2.78 us  [shards(): sums = lax.all_to_all(sums, everywhere, 0, 0, tiled=True)]
    ppermute x3, waiting for transfers between devices: 0.01 us -> 1.13 us  [shards(): shares = [lax.ppermute(v, 'tm', pairs) for v, pairs in zip(sends, ahead)]]
    ppermute x3, starting transfers between devices: 5.6 us -> 4.55 us  [shards(): pieces = [lax.ppermute(quarter, 'tm', pairs) for pairs in ahead]]
    unnamed x16 -> x4, local copies, waits for them, and re-layouts: 0.91 us -> 0.01 us
  transfers between devices with their start and end apart: 27 -> 27, of which waited for: 11 -> 8; matrix products, arithmetic and copies ran while one was open for 0% -> 0% of each run, Pallas kernels for 27% -> 29%
where the time goes in v5:
time: 79.2 us; the launch traced here: 78.7 us
  starting transfers between devices  40.4 us (51%)
  Pallas kernels  26.9 us (34%)
  waiting for transfers between devices  10.5 us (13%)
  between operations  0.9 us (1%)
    pallas_call x14, Pallas kernels, call(): pl.pallas_call(body, out_shape=[where(shape, dtype) for shape, dtype, whe...  26.9 us
    ppermute x9, starting transfers between devices, shards(): lax.ppermute(v, 'tm', pairs)  15.8 us
    ppermute x3, starting transfers between devices, shards(): pieces = [lax.ppermute(quarter, 'tm', pairs) for pairs in ahead]  4.55 us
    ppermute x3, starting transfers between devices, shards(): shares = [lax.ppermute(v, 'tm', pairs) for v, pairs in zip(sends, ahead)]  4.43 us
    all_to_all x1, starting transfers between devices, shards(): lax.all_to_all(prefixes, 'tm', 0, 0, tiled=True).reshape(state_size, width)  4.41 us
    all_to_all x1, starting transfers between devices, shards(): lax.all_to_all(products, ('tok', 'rep'), 0, 0, axis_index_groups=[[0, 2,...  3.75 us
    ppermute x9, waiting for transfers between devices, shards(): lax.ppermute(v, 'tm', pairs)  2.98 us
    all_to_all x1, starting transfers between devices, shards(): sums = lax.all_to_all(sums, everywhere, 0, 0, tiled=True)  2.78 us
  transfers between devices with their start and end apart: 27, of which 8 were waited for; matrix products, arithmetic and copies ran while one was open for 0% of the time, Pallas kernels for 29%

profile of v5, /device:TPU:0, one launch (start us, length us, event | category | flops | bytes accessed | tf_op | source)
XLA Modules:
  0.0 78.7 jit_solution(10042902050251564648)
XLA Ops:
  0.6 0.0 copy-start
  0.7 2.7 %state.1 = (f32[80,256]{1,0:T(8,128)S(1)}, f32[8,1024]{1,0:T(8,128)S(1)}, bf16[128,1024]{1,0:T(8,128)(2,1)}, bf16[272,128]{1,0:T(8,128)(2,1)S(1)}, bf16[272,128]...) custom-call(f32[16,256]{1,0:T(8,128)} %bitcast.34, f32[16]{0:T(128)} %refs_1_.1, ...), custom_call_target="tpu_custom_call" | custom-call | tf_op jit(solution)/shard_map/state/pallas_call | solution.py:147
  3.4 0.0 copy-start.1
  3.4 3.1 %collective-permute-start.7 = (bf16[272,128]{1,0:T(8,128)(2,1)S(1)}, bf16[272,128]{1,0:T(8,128)(2,1)S(1)}, u32[]{:S(2)}, u32[]{:S(2)}) collective-permute-start(bf16[272,128]{1,0:T(8,128)(2,1)S(1)} %get-tuple-element.58), channel_id=1, source_target_pairs={{0,8},{8,16},{16,24},{24,0},{1,9},{9,17},{17,25},{25,1},{2,10},{10... | collective-permute-start | bytes 208904 | tf_op jit(solution)/shard_map/ppermute | solution.py:601
  6.4 1.5 %collective-permute-start.1 = (bf16[128,1024]{1,0:T(8,128)(2,1)}, bf16[128,1024]{1,0:T(8,128)(2,1)S(1)}, u32[]{:S(2)}, u32[]{:S(2)}) collective-permute-start(bf16[128,1024]{1,0:T(8,128)(2,1)} %get-tuple-element.54.refs_1_), channel_id=1, source_target_pairs={{0,2},{1,3},{2,0},{3,1},{4,6},{5,7},{6,4},{7,5},{8,10},{9,11},{10,... | collective-permute-start | bytes 786440 | tf_op jit(solution)/shard_map/ppermute | solution.py:603
  7.9 1.5 %collective-permute-start.3 = (bf16[128,1024]{1,0:T(8,128)(2,1)}, bf16[128,1024]{1,0:T(8,128)(2,1)S(1)}, u32[]{:S(2)}, u32[]{:S(2)}) collective-permute-start(bf16[128,1024]{1,0:T(8,128)(2,1)} %get-tuple-element.54.refs_1_), channel_id=1, source_target_pairs={{0,4},{4,0},{1,5},{5,1},{2,6},{6,2},{3,7},{7,3},{8,12},{12,8},{9,1... | collective-permute-start | bytes 786440 | tf_op jit(solution)/shard_map/ppermute | solution.py:604
  9.5 0.5 collective-permute-start.5
  9.9 2.6 %collective-permute-start.8 = (bf16[272,128]{1,0:T(8,128)(2,1)S(1)}, bf16[272,128]{1,0:T(8,128)(2,1)S(1)}, u32[]{:S(2)}, u32[]{:S(2)}) collective-permute-start(bf16[272,128]{1,0:T(8,128)(2,1)S(1)} %get-tuple-element.59), channel_id=1, source_target_pairs={{0,16},{8,24},{16,0},{24,8},{1,17},{9,25},{17,1},{25,9},{2,18},{10... | collective-permute-start | bytes 208904 | tf_op jit(solution)/shard_map/ppermute | solution.py:601
  12.5 0.0 collective-permute-done.7.refs_1_
  12.5 1.3 %collective-permute-start.9 = (bf16[272,128]{1,0:T(8,128)(2,1)S(1)}, bf16[272,128]{1,0:T(8,128)(2,1)S(1)}, u32[]{:S(2)}, u32[]{:S(2)}) collective-permute-start(bf16[272,128]{1,0:T(8,128)(2,1)S(1)} %get-tuple-element.60), channel_id=1, source_target_pairs={{0,24},{8,0},{16,8},{24,16},{1,25},{9,1},{17,9},{25,17},{2,26},{10... | collective-permute-start | bytes 208904 | tf_op jit(solution)/shard_map/ppermute | solution.py:601
  13.9 1.5 %collective-permute-done.8.refs_2_ = bf16[272,128]{1,0:T(8,128)(2,1)S(1)} collective-permute-done((bf16[272,128]{1,0:T(8,128)(2,1)S(1)}, bf16[272,128]{1,0:T(8,128)(2,1)S(1)}, u32[]{:S(2)}, u32[]{:S(2)}) %collective-permute-start.8) | collective-permute-done | bytes 69664 | tf_op jit(solution)/shard_map/ppermute | solution.py:601
  15.4 1.4 %collective-permute-done.9.refs_3_ = bf16[272,128]{1,0:T(8,128)(2,1)S(1)} collective-permute-done((bf16[272,128]{1,0:T(8,128)(2,1)S(1)}, bf16[272,128]{1,0:T(8,128)(2,1)S(1)}, u32[]{:S(2)}, u32[]{:S(2)}) %collective-permute-start.9) | collective-permute-done | bytes 69664 | tf_op jit(solution)/shard_map/ppermute | solution.py:601
  16.8 0.8 %prefix.1 = (bf16[4,32,1024]{2,1,0:T(8,128)(2,1)}, f32[32,128]{1,0:T(8,128)S(1)}) custom-call(bf16[272,128]{1,0:T(8,128)(2,1)S(1)} %get-tuple-element.57.refs_0_, bf16[272,128]{1,0:T(8,128)(2,1)S(1)} %collective-permute-done.7.refs_1_, bf16[272,128]{1,0:T(8,128)(2,1)S(1)} %collective-permute-done.8.refs_2_, bf16[272,128]{1,0:T(8,128)(2,1)S(1)} %collective-permute-done.9.refs_3_), custom_call_target="tpu_custom_call" | custom-call | tf_op jit(solution)/shard_map/prefix/pallas_call | solution.py:147
  17.6 4.4 %all-to-all-start = ((bf16[4,32,1024]{2,1,0:T(8,128)(2,1)}), bf16[4,32,1024]{2,1,0:T(8,128)(2,1)S(1)}, u32[]{:S(2)}, u32[]{:S(2)}) async-start(bf16[4,32,1024]{2,1,0:T(8,128)(2,1)} %get-tuple-element.61.refs_5_), calls=%async_computation | async-start | bytes 524288 | tf_op jit(solution)/shard_map/all_to_all | solution.py:611
  22.0 0.0 collective-permute-start
  22.1 0.0 collective-permute-done.1.refs_3_
  22.1 0.5 collective-permute-start.2
  22.6 0.0 collective-permute-done.3.refs_5_
  22.6 0.1 collective-permute-start.4
  22.6 0.0 collective-permute-done.5.refs_7_
  22.6 0.4 collective-permute-start.6
  23.1 0.1 collective-permute-start.10
  23.2 2.4 %inner.1.refs_9_.refs_5_ = f32[256,1024]{1,0:T(8,128)S(1)} custom-call(bf16[256,128]{1,0:T(8,128)(2,1)} %bitcast.26, bf16[256,128]{1,0:T(8,128)(2,1)} %bitcast.29, bf16[256,1024]{1,0:T(8,128)(2,1)} %bitcast.20, f32[80,256]{1,0:T(8,128)S(1)} %get-tuple-element.55.refs_3_.refs_4_.refs_7_, f32[8,1024]{1,0:T(8,128)S(1)} %get-tuple-element.56.refs_4_.refs_5_, ...), custom_call_target="tpu_custom_call" | custom-call | tf_op jit(solution)/shard_map/inner/pallas_call | solution.py:147
  25.6 0.0 collective-permute-done.refs_2_
  25.6 0.0 collective-permute-done.2.refs_4_
  25.6 0.0 collective-permute-done.4.refs_6_
  25.6 0.0 collective-permute-done.6.refs_8_
  25.6 1.7 %normed_grad.1 = (bf16[256,1024]{1,0:T(8,128)(2,1)S(1)}, bf16[1024,1024]{1,0:T(8,128)(2,1)}) custom-call(bf16[256,1024]{1,0:T(8,128)(2,1)S(1)} %bitcast.18, bf16[128,1024]{1,0:T(8,128)(2,1)S(1)} %copy-done.1, bf16[128,1024]{1,0:T(8,128)(2,1)S(1)} %collective-permute-done.refs_2_, bf16[128,1024]{1,0:T(8,128)(2,1)S(1)} %collective-permute-done.1.refs_3_, ...), custom_call_target="tpu_custom_call" | custom-call | tf_op jit(solution)/shard_map/normed_grad/pallas_call | solution.py:147
  27.3 1.5 %all-to-all-done = bf16[4,32,1024]{2,1,0:T(8,128)(2,1)S(1)} async-done(((bf16[4,32,1024]{2,1,0:T(8,128)(2,1)}), bf16[4,32,1024]{2,1,0:T(8,128)(2,1)S(1)}, u32[]{:S(2)}, u32[]{:S(2)}) %all-to-all-start) | async-done | bytes 262176 | tf_op jit(solution)/shard_map/all_to_all | solution.py:611
  28.8 3.8 %norm.1 = (bf16[256,1024]{1,0:T(8,128)(2,1)S(1)}, bf16[256,512]{1,0:T(8,128)(2,1)S(1)}, bf16[256,1024]{1,0:T(8,128)(2,1)S(1)}, bf16[256,1024]{1,0:T(8,128)(2,1)}...) custom-call(bf16[256,128]{1,0:T(8,128)(2,1)} %bitcast.30, ...), custom_call_target="tpu_custom_call" | custom-call | tf_op jit(solution)/shard_map/norm/pallas_call | solution.py:147
  32.7 0.1 collective-permute-start.11
  32.8 1.5 %collective-permute-start.12 = (bf16[272,128]{1,0:T(8,128)(2,1)S(1)}, bf16[272,128]{1,0:T(8,128)(2,1)S(1)}, u32[]{:S(2)}, u32[]{:S(2)}) collective-permute-start(bf16[272,128]{1,0:T(8,128)(2,1)S(1)} %get-tuple-element.70), channel_id=1, source_target_pairs={{0,8},{8,16},{16,24},{24,0},{1,9},{9,17},{17,25},{25,1},{2,10},{10... | collective-permute-start | bytes 208904 | tf_op jit(solution)/shard_map/ppermute | solution.py:668
  34.3 1.8 %collective-permute-start.13 = (bf16[272,128]{1,0:T(8,128)(2,1)S(1)}, bf16[272,128]{1,0:T(8,128)(2,1)S(1)}, u32[]{:S(2)}, u32[]{:S(2)}) collective-permute-start(bf16[272,128]{1,0:T(8,128)(2,1)S(1)} %get-tuple-element.71), channel_id=1, source_target_pairs={{0,16},{8,24},{16,0},{24,8},{1,17},{9,25},{17,1},{25,9},{2,18},{10... | collective-permute-start | bytes 208904 | tf_op jit(solution)/shard_map/ppermute | solution.py:668
  36.1 1.5 %collective-permute-start.14 = (bf16[272,128]{1,0:T(8,128)(2,1)S(1)}, bf16[272,128]{1,0:T(8,128)(2,1)S(1)}, u32[]{:S(2)}, u32[]{:S(2)}) collective-permute-start(bf16[272,128]{1,0:T(8,128)(2,1)S(1)} %get-tuple-element.72), channel_id=1, source_target_pairs={{0,24},{8,0},{16,8},{24,16},{1,25},{9,1},{17,9},{25,17},{2,26},{10... | collective-permute-start | bytes 208904 | tf_op jit(solution)/shard_map/ppermute | solution.py:668
  37.6 0.0 collective-permute-done.10.refs_1_
  37.6 2.9 %outer.1.refs_2_.refs_1_ = bf16[4,128,1024]{2,1,0:T(8,128)(2,1)} custom-call(bf16[256,1024]{1,0:T(8,128)(2,1)} %bitcast.17, bf16[256,1024]{1,0:T(8,128)(2,1)} %collective-permute-done.10.refs_1_, bf16[256,1024]{1,0:T(8,128)(2,1)S(1)} %get-tuple-element.64.refs_2_.refs_1_, bf16[256,512]{1,0:T(8,128)(2,1)S(1)} %collective-permute-done.11.refs_3_, ...), custom_call_target="tpu_custom_call" | custom-call | tf_op jit(solution)/shard_map/outer/pallas_call | solution.py:147
  40.5 3.1 %mixed.1.refs_6_ = bf16[256,1024]{1,0:T(8,128)(2,1)} custom-call(bf16[1024,1024]{1,0:T(8,128)(2,1)} %get-tuple-element.62.refs_0_, bf16[256,1024]{1,0:T(8,128)(2,1)S(1)} %get-tuple-element.64.refs_2_.refs_1_, bf16[4,128,1024]{2,1,0:T(8,128)(2,1)} %outer.1.refs_2_.refs_1_), custom_call_target="tpu_custom_call" | custom-call | tf_op jit(solution)/shard_map/mixed/pallas_call | solution.py:147
  43.6 0.0 collective-permute-done.12.refs_3_
  43.7 0.1 suffix.1
  43.8 3.8 %all-to-all-start.2 = ((bf16[4,128,1024]{2,1,0:T(8,128)(2,1)}), bf16[4,128,1024]{2,1,0:T(8,128)(2,1)S(1)}, u32[]{:S(2)}, u32[]{:S(2)}) async-start(bf16[4,128,1024]{2,1,0:T(8,128)(2,1)} %get-tuple-element.92), calls=%async_computation.2 | async-start | bytes 2097152 | tf_op jit(solution)/shard_map/all_to_all | solution.py:675
  47.6 0.6 collective-permute-start.15
  48.1 1.1 %collective-permute-start.16 = (bf16[32,1024]{1,0:T(8,128)(2,1)S(1)}, bf16[32,1024]{1,0:T(8,128)(2,1)S(1)}, u32[]{:S(2)}, u32[]{:S(2)}) collective-permute-start(bf16[32,1024]{1,0:T(8,128)(2,1)S(1)} %get-tuple-element.80), channel_id=1, source_target_pairs={{0,16},{8,24},{16,0},{24,8},{1,17},{9,25},{17,1},{25,9},{2,18},{10... | collective-permute-start | bytes 196616 | tf_op jit(solution)/shard_map/ppermute | solution.py:674
  49.2 2.4 %collective-permute-start.17 = (bf16[32,1024]{1,0:T(8,128)(2,1)S(1)}, bf16[32,1024]{1,0:T(8,128)(2,1)S(1)}, u32[]{:S(2)}, u32[]{:S(2)}) collective-permute-start(bf16[32,1024]{1,0:T(8,128)(2,1)S(1)} %get-tuple-element.81), channel_id=1, source_target_pairs={{0,24},{8,0},{16,8},{24,16},{1,25},{9,1},{17,9},{25,17},{2,26},{10... | collective-permute-start | bytes 196616 | tf_op jit(solution)/shard_map/ppermute | solution.py:674
  51.6 4.1 %back.1 = (bf16[256,128]{1,0:T(8,128)(2,1)}, f32[256,1024]{1,0:T(8,128)S(1)}, bf16[256,128]{1,0:T(8,128)(2,1)S(1)}, f32[16,256]{1,0:T(8,128)S(1)}) custom-call(bf16[256,1024]{1,0:T(8,128)(2,1)S(1)} %get-tuple-element.68.refs_0_, bf16[256,128]{1,0:T(8,128)(2,1)} %bitcast.27, bf16[256,128]{1,0:T(8,128)(2,1)} %bitcast.31, bf16[256,1024]{1,0:T(8,128)(2,1)} %bitcast.22, ...), custom_call_target="tpu_custom_call" | custom-call | tf_op jit(solution)/shard_map/back/pallas_call | solution.py:147
  55.7 0.0 collective-permute-done.16.refs_12_
  55.7 0.0 collective-permute-done.17.refs_13_
  55.7 3.5 %last.1 = (bf16[256,1024]{1,0:T(8,128)(2,1)}, bf16[256,128]{1,0:T(8,128)(2,1)}, f32[16,256]{1,0:T(8,128)}, f32[32,1,384]{2,1,0:T(1,128)}) custom-call(bf16[256,128]{1,0:T(8,128)(2,1)} %bitcast.28, bf16[256,1024]{1,0:T(8,128)(2,1)} %bitcast.23, f32[16,256]{1,0:T(8,128)S(1)} %get-tuple-element.67.refs_2_, f32[16,256]{1,0:T(8,128)S(1)} %get-tuple-element.74.refs_3_, ...), custom_call_target="tpu_custom_call" | custom-call | tf_op jit(solution)/shard_map/last/pallas_call | solution.py:147
  59.2 1.4 %all-to-all-done.2.refs_0_ = bf16[4,128,1024]{2,1,0:T(8,128)(2,1)S(1)} async-done(((bf16[4,128,1024]{2,1,0:T(8,128)(2,1)}), bf16[4,128,1024]{2,1,0:T(8,128)(2,1)S(1)}, u32[]{:S(2)}, u32[]{:S(2)}) %all-to-all-start.2) | async-done | bytes 1048608 | tf_op jit(solution)/shard_map/all_to_all | solution.py:675
  60.6 0.2 add_chips.1
  60.9 1.3 %collective-permute-start.18 = (bf16[32,1024]{1,0:T(8,128)(2,1)S(1)}, bf16[32,1024]{1,0:T(8,128)(2,1)S(1)}, u32[]{:S(2)}, u32[]{:S(2)}) collective-permute-start(bf16[32,1024]{1,0:T(8,128)(2,1)S(1)} %get-tuple-element.94), channel_id=1, source_target_pairs={{0,8},{8,16},{16,24},{24,0},{1,9},{9,17},{17,25},{25,1},{2,10},{10... | collective-permute-start | bytes 196616 | tf_op jit(solution)/shard_map/ppermute | solution.py:686
  62.2 0.9 %collective-permute-start.19 = (bf16[32,1024]{1,0:T(8,128)(2,1)S(1)}, bf16[32,1024]{1,0:T(8,128)(2,1)S(1)}, u32[]{:S(2)}, u32[]{:S(2)}) collective-permute-start(bf16[32,1024]{1,0:T(8,128)(2,1)S(1)} %get-tuple-element.95), channel_id=1, source_target_pairs={{0,16},{8,24},{16,0},{24,8},{1,17},{9,25},{17,1},{25,9},{2,18},{10... | collective-permute-start | bytes 196616 | tf_op jit(solution)/shard_map/ppermute | solution.py:686
  63.1 2.2 %collective-permute-start.20 = (bf16[32,1024]{1,0:T(8,128)(2,1)S(1)}, bf16[32,1024]{1,0:T(8,128)(2,1)S(1)}, u32[]{:S(2)}, u32[]{:S(2)}) collective-permute-start(bf16[32,1024]{1,0:T(8,128)(2,1)S(1)} %get-tuple-element.96), channel_id=1, source_target_pairs={{0,24},{8,0},{16,8},{24,16},{1,25},{9,1},{17,9},{25,17},{2,26},{10... | collective-permute-start | bytes 196616 | tf_op jit(solution)/shard_map/ppermute | solution.py:686
  65.3 2.8 %all-to-all-start.1 = ((f32[32,1,384]{2,1,0:T(1,128)}), f32[32,1,384]{2,1,0:T(1,128)S(1)}, u32[]{:S(2)}, u32[]{:S(2)}) async-start(f32[32,1,384]{2,1,0:T(1,128)} %get-tuple-element.87), calls=%async_computation.1 | async-start | bytes 98304 | tf_op jit(solution)/shard_map/all_to_all | solution.py:690
  68.1 0.0 collective-permute-done.18.refs_1_
  68.1 1.1 %collective-permute-done.19.refs_2_ = bf16[32,1024]{1,0:T(8,128)(2,1)S(1)} collective-permute-done((bf16[32,1024]{1,0:T(8,128)(2,1)S(1)}, bf16[32,1024]{1,0:T(8,128)(2,1)S(1)}, u32[]{:S(2)}, u32[]{:S(2)}) %collective-permute-start.19) | collective-permute-done | bytes 65568 | tf_op jit(solution)/shard_map/ppermute | solution.py:686
  69.2 0.0 collective-permute-done.20.refs_3_
  69.3 1.3 %collective-permute-start.21 = (bf16[32,1024]{1,0:T(8,128)(2,1)S(1)}, bf16[32,1024]{1,0:T(8,128)(2,1)S(1)}, u32[]{:S(2)}, u32[]{:S(2)}) collective-permute-start(bf16[32,1024]{1,0:T(8,128)(2,1)S(1)} %add_blocks.1.refs_0_), channel_id=1, source_target_pairs={{0,8},{8,16},{16,24},{24,0},{1,9},{9,17},{17,25},{25,1},{2,10},{10... | collective-permute-start | bytes 196616 | tf_op jit(solution)/shard_map/ppermute | solution.py:688
  70.6 1.8 %collective-permute-start.22 = (bf16[32,1024]{1,0:T(8,128)(2,1)S(1)}, bf16[32,1024]{1,0:T(8,128)(2,1)S(1)}, u32[]{:S(2)}, u32[]{:S(2)}) collective-permute-start(bf16[32,1024]{1,0:T(8,128)(2,1)S(1)} %add_blocks.1.refs_0_), channel_id=1, source_target_pairs={{0,16},{8,24},{16,0},{24,8},{1,17},{9,25},{17,1},{25,9},{2,18},{10... | collective-permute-start | bytes 196616 | tf_op jit(solution)/shard_map/ppermute | solution.py:688
  72.4 1.4 %collective-permute-start.23 = (bf16[32,1024]{1,0:T(8,128)(2,1)S(1)}, bf16[32,1024]{1,0:T(8,128)(2,1)S(1)}, u32[]{:S(2)}, u32[]{:S(2)}) collective-permute-start(bf16[32,1024]{1,0:T(8,128)(2,1)S(1)} %add_blocks.1.refs_0_), channel_id=1, source_target_pairs={{0,24},{8,0},{16,8},{24,16},{1,25},{9,1},{17,9},{25,17},{2,26},{10... | collective-permute-start | bytes 196616 | tf_op jit(solution)/shard_map/ppermute | solution.py:688
  73.8 1.8 %all-to-all-done.1.refs_0_ = f32[32,1,384]{2,1,0:T(1,128)S(1)} async-done(((f32[32,1,384]{2,1,0:T(1,128)}), f32[32,1,384]{2,1,0:T(1,128)S(1)}, u32[]{:S(2)}, u32[]{:S(2)}) %all-to-all-start.1) | async-done | bytes 49184 | tf_op jit(solution)/shard_map/all_to_all | solution.py:690
  75.6 0.7 sums.1
  76.3 1.5 %collective-permute-done.22.refs_2_ = bf16[32,1024]{1,0:T(8,128)(2,1)S(1)} collective-permute-done((bf16[32,1024]{1,0:T(8,128)(2,1)S(1)}, bf16[32,1024]{1,0:T(8,128)(2,1)S(1)}, u32[]{:S(2)}, u32[]{:S(2)}) %collective-permute-start.22) | collective-permute-done | bytes 65568 | tf_op jit(solution)/shard_map/ppermute | solution.py:688
  77.8 0.2 collective-permute-done.23.refs_3_
  78.0 0.7 join.1
  (8 shorter events, 0.0 us)
Async XLA Ops:
  0.6 25.0 %copy-start = (bf16[1,256,1024]{2,1,0:T(8,128)(2,1)S(1)}, bf16[1,256,1024]{2,1,0:T(8,128)(2,1)}, u32[]{:S(2)}) copy-start(bf16[1,256,1024]{2,1,0:T(8,128)(2,1)} %param.21) | copy-start | bytes 1572868
  3.4 22.3 %copy-start.1 = (bf16[128,1024]{1,0:T(8,128)(2,1)S(1)}, bf16[128,1024]{1,0:T(8,128)(2,1)}, u32[]{:S(2)}) copy-start(bf16[128,1024]{1,0:T(8,128)(2,1)} %get-tuple-element.54.refs_1_) | copy-start | bytes 786436
  3.4 9.2 %collective-permute-start.7 = (bf16[272,128]{1,0:T(8,128)(2,1)S(1)}, bf16[272,128]{1,0:T(8,128)(2,1)S(1)}, u32[]{:S(2)}, u32[]{:S(2)}) collective-permute-start(bf16[272,128]{1,0:T(8,128)(2,1)S(1)} %get-tuple-element.58), channel_id=1, source_target_pairs={{0,8},{8,16},{16,24},{24,0},{1,9},{9,17},{17,25},{25,1},{2,10},{10... | collective-permute-start | bytes 208904 | tf_op jit(solution)/shard_map/ppermute | solution.py:601
  6.4 15.6 %collective-permute-start.1 = (bf16[128,1024]{1,0:T(8,128)(2,1)}, bf16[128,1024]{1,0:T(8,128)(2,1)S(1)}, u32[]{:S(2)}, u32[]{:S(2)}) collective-permute-start(bf16[128,1024]{1,0:T(8,128)(2,1)} %get-tuple-element.54.refs_1_), channel_id=1, source_target_pairs={{0,2},{1,3},{2,0},{3,1},{4,6},{5,7},{6,4},{7,5},{8,10},{9,11},{10,... | collective-permute-start | bytes 786440 | tf_op jit(solution)/shard_map/ppermute | solution.py:603
  7.9 14.6 %collective-permute-start.3 = (bf16[128,1024]{1,0:T(8,128)(2,1)}, bf16[128,1024]{1,0:T(8,128)(2,1)S(1)}, u32[]{:S(2)}, u32[]{:S(2)}) collective-permute-start(bf16[128,1024]{1,0:T(8,128)(2,1)} %get-tuple-element.54.refs_1_), channel_id=1, source_target_pairs={{0,4},{4,0},{1,5},{5,1},{2,6},{6,2},{3,7},{7,3},{8,12},{12,8},{9,1... | collective-permute-start | bytes 786440 | tf_op jit(solution)/shard_map/ppermute | solution.py:604
  9.5 13.2 %collective-permute-start.5 = (bf16[128,1024]{1,0:T(8,128)(2,1)}, bf16[128,1024]{1,0:T(8,128)(2,1)S(1)}, u32[]{:S(2)}, u32[]{:S(2)}) collective-permute-start(bf16[128,1024]{1,0:T(8,128)(2,1)} %get-tuple-element.54.refs_1_), channel_id=1, source_target_pairs={{0,6},{1,7},{2,4},{3,5},{4,2},{5,3},{6,0},{7,1},{8,14},{9,15},{10,... | collective-permute-start | bytes 786440 | tf_op jit(solution)/shard_map/ppermute | solution.py:605
  9.9 5.5 %collective-permute-start.8 = (bf16[272,128]{1,0:T(8,128)(2,1)S(1)}, bf16[272,128]{1,0:T(8,128)(2,1)S(1)}, u32[]{:S(2)}, u32[]{:S(2)}) collective-permute-start(bf16[272,128]{1,0:T(8,128)(2,1)S(1)} %get-tuple-element.59), channel_id=1, source_target_pairs={{0,16},{8,24},{16,0},{24,8},{1,17},{9,25},{17,1},{25,9},{2,18},{10... | collective-permute-start | bytes 208904 | tf_op jit(solution)/shard_map/ppermute | solution.py:601
  12.5 4.3 %collective-permute-start.9 = (bf16[272,128]{1,0:T(8,128)(2,1)S(1)}, bf16[272,128]{1,0:T(8,128)(2,1)S(1)}, u32[]{:S(2)}, u32[]{:S(2)}) collective-permute-start(bf16[272,128]{1,0:T(8,128)(2,1)S(1)} %get-tuple-element.60), channel_id=1, source_target_pairs={{0,24},{8,0},{16,8},{24,16},{1,25},{9,1},{17,9},{25,17},{2,26},{10... | collective-permute-start | bytes 208904 | tf_op jit(solution)/shard_map/ppermute | solution.py:601
  17.6 11.2 %all-to-all-start = ((bf16[4,32,1024]{2,1,0:T(8,128)(2,1)}), bf16[4,32,1024]{2,1,0:T(8,128)(2,1)S(1)}, u32[]{:S(2)}, u32[]{:S(2)}) async-start(bf16[4,32,1024]{2,1,0:T(8,128)(2,1)} %get-tuple-element.61.refs_5_), calls=%async_computation | async-start | bytes 524288 | tf_op jit(solution)/shard_map/all_to_all | solution.py:611
  22.0 3.5 %collective-permute-start = (bf16[128,1024]{1,0:T(8,128)(2,1)}, bf16[128,1024]{1,0:T(8,128)(2,1)S(1)}, u32[]{:S(2)}, u32[]{:S(2)}) collective-permute-start(bf16[128,1024]{1,0:T(8,128)(2,1)} %get-tuple-element.54.refs_1_), channel_id=1, source_target_pairs={{0,1},{1,0},{2,3},{3,2},{4,5},{5,4},{6,7},{7,6},{8,9},{9,8},{10,11... | collective-permute-start | bytes 786440 | tf_op jit(solution)/shard_map/ppermute | solution.py:606
  22.1 3.5 %collective-permute-start.2 = (bf16[128,1024]{1,0:T(8,128)(2,1)S(1)}, bf16[128,1024]{1,0:T(8,128)(2,1)S(1)}, u32[]{:S(2)}, u32[]{:S(2)}) collective-permute-start(bf16[128,1024]{1,0:T(8,128)(2,1)S(1)} %collective-permute-done.1.refs_3_), channel_id=1, source_target_pairs={{0,1},{1,0},{2,3},{3,2},{4,5},{5,4},{6,7},{7,6},{8,9},{9,8},{10,11... | collective-permute-start | bytes 786440 | tf_op jit(solution)/shard_map/ppermute | solution.py:606
  22.6 3.0 %collective-permute-start.4 = (bf16[128,1024]{1,0:T(8,128)(2,1)S(1)}, bf16[128,1024]{1,0:T(8,128)(2,1)S(1)}, u32[]{:S(2)}, u32[]{:S(2)}) collective-permute-start(bf16[128,1024]{1,0:T(8,128)(2,1)S(1)} %collective-permute-done.3.refs_5_), channel_id=1, source_target_pairs={{0,1},{1,0},{2,3},{3,2},{4,5},{5,4},{6,7},{7,6},{8,9},{9,8},{10,11... | collective-permute-start | bytes 786440 | tf_op jit(solution)/shard_map/ppermute | solution.py:606
  22.6 3.0 %collective-permute-start.6 = (bf16[128,1024]{1,0:T(8,128)(2,1)S(1)}, bf16[128,1024]{1,0:T(8,128)(2,1)S(1)}, u32[]{:S(2)}, u32[]{:S(2)}) collective-permute-start(bf16[128,1024]{1,0:T(8,128)(2,1)S(1)} %collective-permute-done.5.refs_7_), channel_id=1, source_target_pairs={{0,1},{1,0},{2,3},{3,2},{4,5},{5,4},{6,7},{7,6},{8,9},{9,8},{10,11... | collective-permute-start | bytes 786440 | tf_op jit(solution)/shard_map/ppermute | solution.py:606
  23.1 14.5 %collective-permute-start.10 = (bf16[256,1024]{1,0:T(8,128)(2,1)}, bf16[256,1024]{1,0:T(8,128)(2,1)}, u32[]{:S(2)}, u32[]{:S(2)}) collective-permute-start(bf16[256,1024]{1,0:T(8,128)(2,1)} %bitcast.16), channel_id=1, source_target_pairs={{0,1},{1,0},{2,3},{3,2},{4,5},{5,4},{6,7},{7,6},{8,9},{9,8},{10,11... | collective-permute-start | bytes 1572872 | tf_op jit(solution)/shard_map/ppermute | solution.py:602
  32.7 4.9 %collective-permute-start.11 = (bf16[256,512]{1,0:T(8,128)(2,1)S(1)}, bf16[256,512]{1,0:T(8,128)(2,1)S(1)}, u32[]{:S(2)}, u32[]{:S(2)}) collective-permute-start(bf16[256,512]{1,0:T(8,128)(2,1)S(1)} %get-tuple-element.65), channel_id=1, source_target_pairs={{0,1},{1,0},{2,3},{3,2},{4,5},{5,4},{6,7},{7,6},{8,9},{9,8},{10,11... | collective-permute-start | bytes 786440 | tf_op jit(solution)/shard_map/ppermute | solution.py:664
  32.8 10.9 %collective-permute-start.12 = (bf16[272,128]{1,0:T(8,128)(2,1)S(1)}, bf16[272,128]{1,0:T(8,128)(2,1)S(1)}, u32[]{:S(2)}, u32[]{:S(2)}) collective-permute-start(bf16[272,128]{1,0:T(8,128)(2,1)S(1)} %get-tuple-element.70), channel_id=1, source_target_pairs={{0,8},{8,16},{16,24},{24,0},{1,9},{9,17},{17,25},{25,1},{2,10},{10... | collective-permute-start | bytes 208904 | tf_op jit(solution)/shard_map/ppermute | solution.py:668
  34.3 9.4 %collective-permute-start.13 = (bf16[272,128]{1,0:T(8,128)(2,1)S(1)}, bf16[272,128]{1,0:T(8,128)(2,1)S(1)}, u32[]{:S(2)}, u32[]{:S(2)}) collective-permute-start(bf16[272,128]{1,0:T(8,128)(2,1)S(1)} %get-tuple-element.71), channel_id=1, source_target_pairs={{0,16},{8,24},{16,0},{24,8},{1,17},{9,25},{17,1},{25,9},{2,18},{10... | collective-permute-start | bytes 208904 | tf_op jit(solution)/shard_map/ppermute | solution.py:668
  36.1 7.6 %collective-permute-start.14 = (bf16[272,128]{1,0:T(8,128)(2,1)S(1)}, bf16[272,128]{1,0:T(8,128)(2,1)S(1)}, u32[]{:S(2)}, u32[]{:S(2)}) collective-permute-start(bf16[272,128]{1,0:T(8,128)(2,1)S(1)} %get-tuple-element.72), channel_id=1, source_target_pairs={{0,24},{8,0},{16,8},{24,16},{1,25},{9,1},{17,9},{25,17},{2,26},{10... | collective-permute-start | bytes 208904 | tf_op jit(solution)/shard_map/ppermute | solution.py:668
  43.8 16.8 %all-to-all-start.2 = ((bf16[4,128,1024]{2,1,0:T(8,128)(2,1)}), bf16[4,128,1024]{2,1,0:T(8,128)(2,1)S(1)}, u32[]{:S(2)}, u32[]{:S(2)}) async-start(bf16[4,128,1024]{2,1,0:T(8,128)(2,1)} %get-tuple-element.92), calls=%async_computation.2 | async-start | bytes 2097152 | tf_op jit(solution)/shard_map/all_to_all | solution.py:675
  47.6 8.1 %collective-permute-start.15 = (bf16[32,1024]{1,0:T(8,128)(2,1)S(1)}, bf16[32,1024]{1,0:T(8,128)(2,1)S(1)}, u32[]{:S(2)}, u32[]{:S(2)}) collective-permute-start(bf16[32,1024]{1,0:T(8,128)(2,1)S(1)} %get-tuple-element.79), channel_id=1, source_target_pairs={{0,8},{8,16},{16,24},{24,0},{1,9},{9,17},{17,25},{25,1},{2,10},{10... | collective-permute-start | bytes 196616 | tf_op jit(solution)/shard_map/ppermute | solution.py:674
  48.1 7.5 %collective-permute-start.16 = (bf16[32,1024]{1,0:T(8,128)(2,1)S(1)}, bf16[32,1024]{1,0:T(8,128)(2,1)S(1)}, u32[]{:S(2)}, u32[]{:S(2)}) collective-permute-start(bf16[32,1024]{1,0:T(8,128)(2,1)S(1)} %get-tuple-element.80), channel_id=1, source_target_pairs={{0,16},{8,24},{16,0},{24,8},{1,17},{9,25},{17,1},{25,9},{2,18},{10... | collective-permute-start | bytes 196616 | tf_op jit(solution)/shard_map/ppermute | solution.py:674
  49.2 6.5 %collective-permute-start.17 = (bf16[32,1024]{1,0:T(8,128)(2,1)S(1)}, bf16[32,1024]{1,0:T(8,128)(2,1)S(1)}, u32[]{:S(2)}, u32[]{:S(2)}) collective-permute-start(bf16[32,1024]{1,0:T(8,128)(2,1)S(1)} %get-tuple-element.81), channel_id=1, source_target_pairs={{0,24},{8,0},{16,8},{24,16},{1,25},{9,1},{17,9},{25,17},{2,26},{10... | collective-permute-start | bytes 196616 | tf_op jit(solution)/shard_map/ppermute | solution.py:674
  60.9 7.2 %collective-permute-start.18 = (bf16[32,1024]{1,0:T(8,128)(2,1)S(1)}, bf16[32,1024]{1,0:T(8,128)(2,1)S(1)}, u32[]{:S(2)}, u32[]{:S(2)}) collective-permute-start(bf16[32,1024]{1,0:T(8,128)(2,1)S(1)} %get-tuple-element.94), channel_id=1, source_target_pairs={{0,8},{8,16},{16,24},{24,0},{1,9},{9,17},{17,25},{25,1},{2,10},{10... | collective-permute-start | bytes 196616 | tf_op jit(solution)/shard_map/ppermute | solution.py:686
  62.2 7.0 %collective-permute-start.19 = (bf16[32,1024]{1,0:T(8,128)(2,1)S(1)}, bf16[32,1024]{1,0:T(8,128)(2,1)S(1)}, u32[]{:S(2)}, u32[]{:S(2)}) collective-permute-start(bf16[32,1024]{1,0:T(8,128)(2,1)S(1)} %get-tuple-element.95), channel_id=1, source_target_pairs={{0,16},{8,24},{16,0},{24,8},{1,17},{9,25},{17,1},{25,9},{2,18},{10... | collective-permute-start | bytes 196616 | tf_op jit(solution)/shard_map/ppermute | solution.py:686
  63.1 6.1 %collective-permute-start.20 = (bf16[32,1024]{1,0:T(8,128)(2,1)S(1)}, bf16[32,1024]{1,0:T(8,128)(2,1)S(1)}, u32[]{:S(2)}, u32[]{:S(2)}) collective-permute-start(bf16[32,1024]{1,0:T(8,128)(2,1)S(1)} %get-tuple-element.96), channel_id=1, source_target_pairs={{0,24},{8,0},{16,8},{24,16},{1,25},{9,1},{17,9},{25,17},{2,26},{10... | collective-permute-start | bytes 196616 | tf_op jit(solution)/shard_map/ppermute | solution.py:686
  65.3 10.3 %all-to-all-start.1 = ((f32[32,1,384]{2,1,0:T(1,128)}), f32[32,1,384]{2,1,0:T(1,128)S(1)}, u32[]{:S(2)}, u32[]{:S(2)}) async-start(f32[32,1,384]{2,1,0:T(1,128)} %get-tuple-element.87), calls=%async_computation.1 | async-start | bytes 98304 | tf_op jit(solution)/shard_map/all_to_all | solution.py:690
  69.3 7.0 %collective-permute-start.21 = (bf16[32,1024]{1,0:T(8,128)(2,1)S(1)}, bf16[32,1024]{1,0:T(8,128)(2,1)S(1)}, u32[]{:S(2)}, u32[]{:S(2)}) collective-permute-start(bf16[32,1024]{1,0:T(8,128)(2,1)S(1)} %add_blocks.1.refs_0_), channel_id=1, source_target_pairs={{0,8},{8,16},{16,24},{24,0},{1,9},{9,17},{17,25},{25,1},{2,10},{10... | collective-permute-start | bytes 196616 | tf_op jit(solution)/shard_map/ppermute | solution.py:688
  70.6 7.2 %collective-permute-start.22 = (bf16[32,1024]{1,0:T(8,128)(2,1)S(1)}, bf16[32,1024]{1,0:T(8,128)(2,1)S(1)}, u32[]{:S(2)}, u32[]{:S(2)}) collective-permute-start(bf16[32,1024]{1,0:T(8,128)(2,1)S(1)} %add_blocks.1.refs_0_), channel_id=1, source_target_pairs={{0,16},{8,24},{16,0},{24,8},{1,17},{9,25},{17,1},{25,9},{2,18},{10... | collective-permute-start | bytes 196616 | tf_op jit(solution)/shard_map/ppermute | solution.py:688
  72.4 5.6 %collective-permute-start.23 = (bf16[32,1024]{1,0:T(8,128)(2,1)S(1)}, bf16[32,1024]{1,0:T(8,128)(2,1)S(1)}, u32[]{:S(2)}, u32[]{:S(2)}) collective-permute-start(bf16[32,1024]{1,0:T(8,128)(2,1)S(1)} %add_blocks.1.refs_0_), channel_id=1, source_target_pairs={{0,24},{8,0},{16,8},{24,16},{1,25},{9,1},{17,9},{25,17},{2,26},{10... | collective-permute-start | bytes 196616 | tf_op jit(solution)/shard_map/ppermute | solution.py:688

commit v6 on v5

--- a/solution.py
+++ b/solution.py
@@ -12,7 +12,7 @@
 ROWS = ((0,), (0,))
 LAST = ((1,), (1,))
 CHUNKS = 8
-VMEM_LIMIT = 24 * 1024 * 1024
+VMEM_LIMIT = 16 * 1024 * 1024
 
 
 def mm(a, b):
@@ -588,7 +588,7 @@
     ahead = [[(i, (i + k) % n_tm) for i in range(n_tm)] for k in range(1, n_tm)]
 
     raw = (s, rate_log, step_bias, b, x, skip_gain, norm_gain, out_weight)
-    aux_shapes = [((5 * heads, length), F32, near_by), ((8, width), F32, near_by), (out_weight.shape, BF, away)]
+    aux_shapes = [((5 * heads, length), F32, near_by), ((8, width), F32, near_by), (out_weight.shape, BF, free)]
     if near:
         part = (n_tm, state_size // n_tm)
         row_part = (part[1], width)
@@ -638,7 +638,7 @@
     )
 
     def mixed_of(*after):
-        return call(mixed_kernel, [(wide, BF, away)], (weight,), normed, name="mixed", after=after)[0]
+        return call(mixed_kernel, [(wide, BF, away)], (weight,), normed, name="mixed", beside=after)[0]
 
     def back(*after):
         return call(
@@ -663,12 +663,12 @@
     if near:
         theirs = lax.ppermute(other, "rep", core)
         (products,) = call(
-            outer_kernel, [((4, rows, model), BF, away)], (g, gc), normed, theirs, name="outer", beside=(carry[0],)
+            outer_kernel, [((4, rows, model), BF, free)], (g, gc), normed, theirs, name="outer", beside=(carry[0],)
         )
         grads = [carry[0]] + [lax.ppermute(v, "tm", pairs) for v, pairs in zip(carry[1:], ahead)]
         mixed = mixed_of(products)
         own, *sends, products, gains_tm = call(
-            suffix_kernel, [(row_part, BF, free)] * n_tm + [(products.shape, BF, away), ((blocks_of, 128), F32, near_by)], (),
+            suffix_kernel, [(row_part, BF, free)] * n_tm + [(products.shape, BF, free), ((blocks_of, 128), F32, near_by)], (),
             decays, products, *grads, name="suffix", far_operands=(1,), aliases={1: n_tm}, scratch=[pltpu.VMEM(part + (width,), BF), pltpu.VMEM(part_shape, BF)], after=(mixed,),
         )
         parts = [own] + [lax.ppermute(v, "tm", pairs) for v, pairs in zip(sends, ahead)]

time: 79.2 us -> 78.4 us (0.990)
  transfers between devices with their start and end apart: 27 -> 27, of which waited for: 8 -> 8; matrix products, arithmetic and copies ran while one was open for 0% -> 0% of each run, Pallas kernels for 29% -> 30%
where the time goes in v6:
time: 78.4 us; the launch traced here: 78 us
  starting transfers between devices  40.4 us (52%)
  Pallas kernels  26.2 us (33%)
  waiting for transfers between devices  10.5 us (13%)
  between operations  0.88 us (1%)
    pallas_call x14, Pallas kernels, call(): pl.pallas_call(body, out_shape=[where(shape, dtype) for shape, dtype, whe...  26.2 us
    ppermute x9, starting transfers between devices, shards(): lax.ppermute(v, 'tm', pairs)  15.8 us
    ppermute x3, starting transfers between devices, shards(): pieces = [lax.ppermute(quarter, 'tm', pairs) for pairs in ahead]  4.55 us
    ppermute x3, starting transfers between devices, shards(): shares = [lax.ppermute(v, 'tm', pairs) for v, pairs in zip(sends, ahead)]  4.45 us
    all_to_all x1, starting transfers between devices, shards(): lax.all_to_all(prefixes, 'tm', 0, 0, tiled=True).reshape(state_size, width)  4.41 us
    all_to_all x1, starting transfers between devices, shards(): lax.all_to_all(products, ('tok', 'rep'), 0, 0, axis_index_groups=[[0, 2,...  3.75 us
    ppermute x9, waiting for transfers between devices, shards(): lax.ppermute(v, 'tm', pairs)  2.98 us
    all_to_all x1, starting transfers between devices, shards(): sums = lax.all_to_all(sums, everywhere, 0, 0, tiled=True)  2.76 us
  transfers between devices with their start and end apart: 27, of which 8 were waited for; matrix products, arithmetic and copies ran while one was open for 0% of the time, Pallas kernels for 30%

profile of v6, /device:TPU:0, one launch (start us, length us, event | category | flops | bytes accessed | tf_op | source)
XLA Modules:
  0.0 78.0 jit_solution(8397909089715125556)
XLA Ops:
  0.6 0.0 copy-start
  0.7 2.0 %state.1 = (f32[80,256]{1,0:T(8,128)S(1)}, f32[8,1024]{1,0:T(8,128)S(1)}, bf16[128,1024]{1,0:T(8,128)(2,1)S(1)}, bf16[272,128]{1,0:T(8,128)(2,1)S(1)}, bf16[272,...) custom-call(f32[16,256]{1,0:T(8,128)} %bitcast.34, f32[16]{0:T(128)} %refs_1_.1, ...), custom_call_target="tpu_custom_call" | custom-call | tf_op jit(solution)/shard_map/state/pallas_call | solution.py:147
  2.7 3.1 %collective-permute-start.7 = (bf16[272,128]{1,0:T(8,128)(2,1)S(1)}, bf16[272,128]{1,0:T(8,128)(2,1)S(1)}, u32[]{:S(2)}, u32[]{:S(2)}) collective-permute-start(bf16[272,128]{1,0:T(8,128)(2,1)S(1)} %get-tuple-element.58), channel_id=1, source_target_pairs={{0,8},{8,16},{16,24},{24,0},{1,9},{9,17},{17,25},{25,1},{2,10},{10... | collective-permute-start | bytes 208904 | tf_op jit(solution)/shard_map/ppermute | solution.py:601
  5.7 1.5 %collective-permute-start.1 = (bf16[128,1024]{1,0:T(8,128)(2,1)S(1)}, bf16[128,1024]{1,0:T(8,128)(2,1)S(1)}, u32[]{:S(2)}, u32[]{:S(2)}) collective-permute-start(bf16[128,1024]{1,0:T(8,128)(2,1)S(1)} %get-tuple-element.54.refs_1_), channel_id=1, source_target_pairs={{0,2},{1,3},{2,0},{3,1},{4,6},{5,7},{6,4},{7,5},{8,10},{9,11},{10,... | collective-permute-start | bytes 786440 | tf_op jit(solution)/shard_map/ppermute | solution.py:603
  7.2 1.5 %collective-permute-start.3 = (bf16[128,1024]{1,0:T(8,128)(2,1)S(1)}, bf16[128,1024]{1,0:T(8,128)(2,1)S(1)}, u32[]{:S(2)}, u32[]{:S(2)}) collective-permute-start(bf16[128,1024]{1,0:T(8,128)(2,1)S(1)} %get-tuple-element.54.refs_1_), channel_id=1, source_target_pairs={{0,4},{4,0},{1,5},{5,1},{2,6},{6,2},{3,7},{7,3},{8,12},{12,8},{9,1... | collective-permute-start | bytes 786440 | tf_op jit(solution)/shard_map/ppermute | solution.py:604
  8.7 0.5 collective-permute-start.5
  9.2 2.6 %collective-permute-start.8 = (bf16[272,128]{1,0:T(8,128)(2,1)S(1)}, bf16[272,128]{1,0:T(8,128)(2,1)S(1)}, u32[]{:S(2)}, u32[]{:S(2)}) collective-permute-start(bf16[272,128]{1,0:T(8,128)(2,1)S(1)} %get-tuple-element.59), channel_id=1, source_target_pairs={{0,16},{8,24},{16,0},{24,8},{1,17},{9,25},{17,1},{25,9},{2,18},{10... | collective-permute-start | bytes 208904 | tf_op jit(solution)/shard_map/ppermute | solution.py:601
  11.8 0.0 collective-permute-done.7.refs_1_
  11.8 1.3 %collective-permute-start.9 = (bf16[272,128]{1,0:T(8,128)(2,1)S(1)}, bf16[272,128]{1,0:T(8,128)(2,1)S(1)}, u32[]{:S(2)}, u32[]{:S(2)}) collective-permute-start(bf16[272,128]{1,0:T(8,128)(2,1)S(1)} %get-tuple-element.60), channel_id=1, source_target_pairs={{0,24},{8,0},{16,8},{24,16},{1,25},{9,1},{17,9},{25,17},{2,26},{10... | collective-permute-start | bytes 208904 | tf_op jit(solution)/shard_map/ppermute | solution.py:601
  13.2 1.5 %collective-permute-done.8.refs_2_ = bf16[272,128]{1,0:T(8,128)(2,1)S(1)} collective-permute-done((bf16[272,128]{1,0:T(8,128)(2,1)S(1)}, bf16[272,128]{1,0:T(8,128)(2,1)S(1)}, u32[]{:S(2)}, u32[]{:S(2)}) %collective-permute-start.8) | collective-permute-done | bytes 69664 | tf_op jit(solution)/shard_map/ppermute | solution.py:601
  14.7 1.4 %collective-permute-done.9.refs_3_ = bf16[272,128]{1,0:T(8,128)(2,1)S(1)} collective-permute-done((bf16[272,128]{1,0:T(8,128)(2,1)S(1)}, bf16[272,128]{1,0:T(8,128)(2,1)S(1)}, u32[]{:S(2)}, u32[]{:S(2)}) %collective-permute-start.9) | collective-permute-done | bytes 69664 | tf_op jit(solution)/shard_map/ppermute | solution.py:601
  16.1 0.8 %prefix.1 = (bf16[4,32,1024]{2,1,0:T(8,128)(2,1)}, f32[32,128]{1,0:T(8,128)S(1)}) custom-call(bf16[272,128]{1,0:T(8,128)(2,1)S(1)} %get-tuple-element.57.refs_0_, bf16[272,128]{1,0:T(8,128)(2,1)S(1)} %collective-permute-done.7.refs_1_, bf16[272,128]{1,0:T(8,128)(2,1)S(1)} %collective-permute-done.8.refs_2_, bf16[272,128]{1,0:T(8,128)(2,1)S(1)} %collective-permute-done.9.refs_3_), custom_call_target="tpu_custom_call" | custom-call | tf_op jit(solution)/shard_map/prefix/pallas_call | solution.py:147
  16.9 4.4 %all-to-all-start = ((bf16[4,32,1024]{2,1,0:T(8,128)(2,1)}), bf16[4,32,1024]{2,1,0:T(8,128)(2,1)S(1)}, u32[]{:S(2)}, u32[]{:S(2)}) async-start(bf16[4,32,1024]{2,1,0:T(8,128)(2,1)} %get-tuple-element.61.refs_5_), calls=%async_computation | async-start | bytes 524288 | tf_op jit(solution)/shard_map/all_to_all | solution.py:611
  21.3 0.0 collective-permute-start
  21.3 0.0 collective-permute-done.1.refs_3_
  21.3 0.5 collective-permute-start.2
  21.8 0.0 collective-permute-done.3.refs_5_
  21.9 0.1 collective-permute-start.4
  21.9 0.0 collective-permute-done.5.refs_7_
  21.9 0.4 collective-permute-start.6
  22.4 0.1 collective-permute-start.10
  22.4 2.4 %inner.1.refs_9_.refs_5_ = f32[256,1024]{1,0:T(8,128)S(1)} custom-call(bf16[256,128]{1,0:T(8,128)(2,1)} %bitcast.26, bf16[256,128]{1,0:T(8,128)(2,1)} %bitcast.29, bf16[256,1024]{1,0:T(8,128)(2,1)} %bitcast.20, f32[80,256]{1,0:T(8,128)S(1)} %get-tuple-element.55.refs_3_.refs_4_.refs_7_, f32[8,1024]{1,0:T(8,128)S(1)} %get-tuple-element.56.refs_4_.refs_5_, ...), custom_call_target="tpu_custom_call" | custom-call | tf_op jit(solution)/shard_map/inner/pallas_call | solution.py:147
  24.8 0.0 collective-permute-done.refs_2_
  24.9 0.0 collective-permute-done.2.refs_4_
  24.9 0.0 collective-permute-done.4.refs_6_
  24.9 1.7 %normed_grad.1 = (bf16[256,1024]{1,0:T(8,128)(2,1)S(1)}, bf16[1024,1024]{1,0:T(8,128)(2,1)}) custom-call(bf16[256,1024]{1,0:T(8,128)(2,1)S(1)} %bitcast.18, bf16[128,1024]{1,0:T(8,128)(2,1)S(1)} %get-tuple-element.54.refs_1_, bf16[128,1024]{1,0:T(8,128)(2,1)S(1)} %collective-permute-done.refs_2_, bf16[128,1024]{1,0:T(8,128)(2,1)S(1)} %collective-permute-done.1.refs_3_, ...), custom_call_target="tpu_custom_call" | custom-call | tf_op jit(solution)/shard_map/normed_grad/pallas_call | solution.py:147
  26.6 1.5 %all-to-all-done = bf16[4,32,1024]{2,1,0:T(8,128)(2,1)S(1)} async-done(((bf16[4,32,1024]{2,1,0:T(8,128)(2,1)}), bf16[4,32,1024]{2,1,0:T(8,128)(2,1)S(1)}, u32[]{:S(2)}, u32[]{:S(2)}) %all-to-all-start) | async-done | bytes 262176 | tf_op jit(solution)/shard_map/all_to_all | solution.py:611
  28.1 3.8 %norm.1 = (bf16[256,1024]{1,0:T(8,128)(2,1)S(1)}, bf16[256,512]{1,0:T(8,128)(2,1)S(1)}, bf16[256,1024]{1,0:T(8,128)(2,1)S(1)}, bf16[256,1024]{1,0:T(8,128)(2,1)}...) custom-call(bf16[256,128]{1,0:T(8,128)(2,1)} %bitcast.30, ...), custom_call_target="tpu_custom_call" | custom-call | tf_op jit(solution)/shard_map/norm/pallas_call | solution.py:147
  32.0 0.1 collective-permute-start.11
  32.0 1.5 %collective-permute-start.12 = (bf16[272,128]{1,0:T(8,128)(2,1)S(1)}, bf16[272,128]{1,0:T(8,128)(2,1)S(1)}, u32[]{:S(2)}, u32[]{:S(2)}) collective-permute-start(bf16[272,128]{1,0:T(8,128)(2,1)S(1)} %get-tuple-element.70), channel_id=1, source_target_pairs={{0,8},{8,16},{16,24},{24,0},{1,9},{9,17},{17,25},{25,1},{2,10},{10... | collective-permute-start | bytes 208904 | tf_op jit(solution)/shard_map/ppermute | solution.py:668
  33.6 1.8 %collective-permute-start.13 = (bf16[272,128]{1,0:T(8,128)(2,1)S(1)}, bf16[272,128]{1,0:T(8,128)(2,1)S(1)}, u32[]{:S(2)}, u32[]{:S(2)}) collective-permute-start(bf16[272,128]{1,0:T(8,128)(2,1)S(1)} %get-tuple-element.71), channel_id=1, source_target_pairs={{0,16},{8,24},{16,0},{24,8},{1,17},{9,25},{17,1},{25,9},{2,18},{10... | collective-permute-start | bytes 208904 | tf_op jit(solution)/shard_map/ppermute | solution.py:668
  35.4 1.5 %collective-permute-start.14 = (bf16[272,128]{1,0:T(8,128)(2,1)S(1)}, bf16[272,128]{1,0:T(8,128)(2,1)S(1)}, u32[]{:S(2)}, u32[]{:S(2)}) collective-permute-start(bf16[272,128]{1,0:T(8,128)(2,1)S(1)} %get-tuple-element.72), channel_id=1, source_target_pairs={{0,24},{8,0},{16,8},{24,16},{1,25},{9,1},{17,9},{25,17},{2,26},{10... | collective-permute-start | bytes 208904 | tf_op jit(solution)/shard_map/ppermute | solution.py:668
  36.8 0.0 collective-permute-done.10.refs_1_
  36.8 0.0 collective-permute-done.11.refs_3_
  36.8 3.0 %outer.1.refs_2_.refs_1_ = bf16[4,128,1024]{2,1,0:T(8,128)(2,1)} custom-call(bf16[256,1024]{1,0:T(8,128)(2,1)} %bitcast.17, bf16[256,1024]{1,0:T(8,128)(2,1)} %collective-permute-done.10.refs_1_, bf16[256,1024]{1,0:T(8,128)(2,1)S(1)} %get-tuple-element.64.refs_2_.refs_1_, bf16[256,512]{1,0:T(8,128)(2,1)S(1)} %collective-permute-done.11.refs_3_, ...), custom_call_target="tpu_custom_call" | custom-call | tf_op jit(solution)/shard_map/outer/pallas_call | solution.py:147
  39.8 3.1 %mixed.1.refs_6_ = bf16[256,1024]{1,0:T(8,128)(2,1)} custom-call(bf16[1024,1024]{1,0:T(8,128)(2,1)} %get-tuple-element.62.refs_0_, bf16[256,1024]{1,0:T(8,128)(2,1)S(1)} %get-tuple-element.64.refs_2_.refs_1_, bf16[4,128,1024]{2,1,0:T(8,128)(2,1)} %outer.1.refs_2_.refs_1_), custom_call_target="tpu_custom_call" | custom-call | tf_op jit(solution)/shard_map/mixed/pallas_call | solution.py:147
  42.9 0.0 collective-permute-done.13.refs_4_
  42.9 0.0 collective-permute-done.14.refs_5_
  43.0 0.1 suffix.1
  43.1 3.8 %all-to-all-start.2 = ((bf16[4,128,1024]{2,1,0:T(8,128)(2,1)}), bf16[4,128,1024]{2,1,0:T(8,128)(2,1)S(1)}, u32[]{:S(2)}, u32[]{:S(2)}) async-start(bf16[4,128,1024]{2,1,0:T(8,128)(2,1)} %get-tuple-element.92), calls=%async_computation.2 | async-start | bytes 2097152 | tf_op jit(solution)/shard_map/all_to_all | solution.py:675
  46.8 0.6 collective-permute-start.15
  47.4 1.1 %collective-permute-start.16 = (bf16[32,1024]{1,0:T(8,128)(2,1)S(1)}, bf16[32,1024]{1,0:T(8,128)(2,1)S(1)}, u32[]{:S(2)}, u32[]{:S(2)}) collective-permute-start(bf16[32,1024]{1,0:T(8,128)(2,1)S(1)} %get-tuple-element.80), channel_id=1, source_target_pairs={{0,16},{8,24},{16,0},{24,8},{1,17},{9,25},{17,1},{25,9},{2,18},{10... | collective-permute-start | bytes 196616 | tf_op jit(solution)/shard_map/ppermute | solution.py:674
  48.5 2.4 %collective-permute-start.17 = (bf16[32,1024]{1,0:T(8,128)(2,1)S(1)}, bf16[32,1024]{1,0:T(8,128)(2,1)S(1)}, u32[]{:S(2)}, u32[]{:S(2)}) collective-permute-start(bf16[32,1024]{1,0:T(8,128)(2,1)S(1)} %get-tuple-element.81), channel_id=1, source_target_pairs={{0,24},{8,0},{16,8},{24,16},{1,25},{9,1},{17,9},{25,17},{2,26},{10... | collective-permute-start | bytes 196616 | tf_op jit(solution)/shard_map/ppermute | solution.py:674
  50.9 4.1 %back.1 = (bf16[256,128]{1,0:T(8,128)(2,1)}, f32[256,1024]{1,0:T(8,128)S(1)}, bf16[256,128]{1,0:T(8,128)(2,1)S(1)}, f32[16,256]{1,0:T(8,128)S(1)}) custom-call(bf16[256,1024]{1,0:T(8,128)(2,1)S(1)} %get-tuple-element.68.refs_0_, bf16[256,128]{1,0:T(8,128)(2,1)} %bitcast.27, bf16[256,128]{1,0:T(8,128)(2,1)} %bitcast.31, bf16[256,1024]{1,0:T(8,128)(2,1)} %bitcast.22, ...), custom_call_target="tpu_custom_call" | custom-call | tf_op jit(solution)/shard_map/back/pallas_call | solution.py:147
  54.9 0.0 collective-permute-done.15.refs_11_
  55.0 0.0 collective-permute-done.17.refs_13_
  55.0 3.5 %last.1 = (bf16[256,1024]{1,0:T(8,128)(2,1)}, bf16[256,128]{1,0:T(8,128)(2,1)}, f32[16,256]{1,0:T(8,128)}, f32[32,1,384]{2,1,0:T(1,128)}) custom-call(bf16[256,128]{1,0:T(8,128)(2,1)} %bitcast.28, bf16[256,1024]{1,0:T(8,128)(2,1)} %bitcast.23, f32[16,256]{1,0:T(8,128)S(1)} %get-tuple-element.67.refs_2_, f32[16,256]{1,0:T(8,128)S(1)} %get-tuple-element.74.refs_3_, ...), custom_call_target="tpu_custom_call" | custom-call | tf_op jit(solution)/shard_map/last/pallas_call | solution.py:147
  58.5 1.4 %all-to-all-done.2.refs_0_ = bf16[4,128,1024]{2,1,0:T(8,128)(2,1)S(1)} async-done(((bf16[4,128,1024]{2,1,0:T(8,128)(2,1)}), bf16[4,128,1024]{2,1,0:T(8,128)(2,1)S(1)}, u32[]{:S(2)}, u32[]{:S(2)}) %all-to-all-start.2) | async-done | bytes 1048608 | tf_op jit(solution)/shard_map/all_to_all | solution.py:675
  59.9 0.2 add_chips.1
  60.2 1.3 %collective-permute-start.18 = (bf16[32,1024]{1,0:T(8,128)(2,1)S(1)}, bf16[32,1024]{1,0:T(8,128)(2,1)S(1)}, u32[]{:S(2)}, u32[]{:S(2)}) collective-permute-start(bf16[32,1024]{1,0:T(8,128)(2,1)S(1)} %get-tuple-element.94), channel_id=1, source_target_pairs={{0,8},{8,16},{16,24},{24,0},{1,9},{9,17},{17,25},{25,1},{2,10},{10... | collective-permute-start | bytes 196616 | tf_op jit(solution)/shard_map/ppermute | solution.py:686
  61.5 0.9 %collective-permute-start.19 = (bf16[32,1024]{1,0:T(8,128)(2,1)S(1)}, bf16[32,1024]{1,0:T(8,128)(2,1)S(1)}, u32[]{:S(2)}, u32[]{:S(2)}) collective-permute-start(bf16[32,1024]{1,0:T(8,128)(2,1)S(1)} %get-tuple-element.95), channel_id=1, source_target_pairs={{0,16},{8,24},{16,0},{24,8},{1,17},{9,25},{17,1},{25,9},{2,18},{10... | collective-permute-start | bytes 196616 | tf_op jit(solution)/shard_map/ppermute | solution.py:686
  62.4 2.2 %collective-permute-start.20 = (bf16[32,1024]{1,0:T(8,128)(2,1)S(1)}, bf16[32,1024]{1,0:T(8,128)(2,1)S(1)}, u32[]{:S(2)}, u32[]{:S(2)}) collective-permute-start(bf16[32,1024]{1,0:T(8,128)(2,1)S(1)} %get-tuple-element.96), channel_id=1, source_target_pairs={{0,24},{8,0},{16,8},{24,16},{1,25},{9,1},{17,9},{25,17},{2,26},{10... | collective-permute-start | bytes 196616 | tf_op jit(solution)/shard_map/ppermute | solution.py:686
  64.6 2.8 %all-to-all-start.1 = ((f32[32,1,384]{2,1,0:T(1,128)}), f32[32,1,384]{2,1,0:T(1,128)S(1)}, u32[]{:S(2)}, u32[]{:S(2)}) async-start(f32[32,1,384]{2,1,0:T(1,128)} %get-tuple-element.87), calls=%async_computation.1 | async-start | bytes 98304 | tf_op jit(solution)/shard_map/all_to_all | solution.py:690
  67.4 1.1 %collective-permute-done.19.refs_2_ = bf16[32,1024]{1,0:T(8,128)(2,1)S(1)} collective-permute-done((bf16[32,1024]{1,0:T(8,128)(2,1)S(1)}, bf16[32,1024]{1,0:T(8,128)(2,1)S(1)}, u32[]{:S(2)}, u32[]{:S(2)}) %collective-permute-start.19) | collective-permute-done | bytes 65568 | tf_op jit(solution)/shard_map/ppermute | solution.py:686
  68.5 0.0 collective-permute-done.20.refs_3_
  68.6 1.3 %collective-permute-start.21 = (bf16[32,1024]{1,0:T(8,128)(2,1)S(1)}, bf16[32,1024]{1,0:T(8,128)(2,1)S(1)}, u32[]{:S(2)}, u32[]{:S(2)}) collective-permute-start(bf16[32,1024]{1,0:T(8,128)(2,1)S(1)} %add_blocks.1.refs_0_), channel_id=1, source_target_pairs={{0,8},{8,16},{16,24},{24,0},{1,9},{9,17},{17,25},{25,1},{2,10},{10... | collective-permute-start | bytes 196616 | tf_op jit(solution)/shard_map/ppermute | solution.py:688
  69.9 1.8 %collective-permute-start.22 = (bf16[32,1024]{1,0:T(8,128)(2,1)S(1)}, bf16[32,1024]{1,0:T(8,128)(2,1)S(1)}, u32[]{:S(2)}, u32[]{:S(2)}) collective-permute-start(bf16[32,1024]{1,0:T(8,128)(2,1)S(1)} %add_blocks.1.refs_0_), channel_id=1, source_target_pairs={{0,16},{8,24},{16,0},{24,8},{1,17},{9,25},{17,1},{25,9},{2,18},{10... | collective-permute-start | bytes 196616 | tf_op jit(solution)/shard_map/ppermute | solution.py:688
  71.7 1.4 %collective-permute-start.23 = (bf16[32,1024]{1,0:T(8,128)(2,1)S(1)}, bf16[32,1024]{1,0:T(8,128)(2,1)S(1)}, u32[]{:S(2)}, u32[]{:S(2)}) collective-permute-start(bf16[32,1024]{1,0:T(8,128)(2,1)S(1)} %add_blocks.1.refs_0_), channel_id=1, source_target_pairs={{0,24},{8,0},{16,8},{24,16},{1,25},{9,1},{17,9},{25,17},{2,26},{10... | collective-permute-start | bytes 196616 | tf_op jit(solution)/shard_map/ppermute | solution.py:688
  73.1 1.8 %all-to-all-done.1.refs_0_ = f32[32,1,384]{2,1,0:T(1,128)S(1)} async-done(((f32[32,1,384]{2,1,0:T(1,128)}), f32[32,1,384]{2,1,0:T(1,128)S(1)}, u32[]{:S(2)}, u32[]{:S(2)}) %all-to-all-start.1) | async-done | bytes 49184 | tf_op jit(solution)/shard_map/all_to_all | solution.py:690
  74.9 0.7 sums.1
  75.6 0.0 collective-permute-done.21.refs_1_
  75.6 1.5 %collective-permute-done.22.refs_2_ = bf16[32,1024]{1,0:T(8,128)(2,1)S(1)} collective-permute-done((bf16[32,1024]{1,0:T(8,128)(2,1)S(1)}, bf16[32,1024]{1,0:T(8,128)(2,1)S(1)}, u32[]{:S(2)}, u32[]{:S(2)}) %collective-permute-start.22) | collective-permute-done | bytes 65568 | tf_op jit(solution)/shard_map/ppermute | solution.py:688
  77.1 0.2 collective-permute-done.23.refs_3_
  77.3 0.7 join.1
  (6 shorter events, 0.0 us)
Async XLA Ops:
  0.6 24.2 %copy-start = (bf16[1,256,1024]{2,1,0:T(8,128)(2,1)S(1)}, bf16[1,256,1024]{2,1,0:T(8,128)(2,1)}, u32[]{:S(2)}) copy-start(bf16[1,256,1024]{2,1,0:T(8,128)(2,1)} %param.21) | copy-start | bytes 1572868
  2.7 9.2 %collective-permute-start.7 = (bf16[272,128]{1,0:T(8,128)(2,1)S(1)}, bf16[272,128]{1,0:T(8,128)(2,1)S(1)}, u32[]{:S(2)}, u32[]{:S(2)}) collective-permute-start(bf16[272,128]{1,0:T(8,128)(2,1)S(1)} %get-tuple-element.58), channel_id=1, source_target_pairs={{0,8},{8,16},{16,24},{24,0},{1,9},{9,17},{17,25},{25,1},{2,10},{10... | collective-permute-start | bytes 208904 | tf_op jit(solution)/shard_map/ppermute | solution.py:601
  5.7 15.6 %collective-permute-start.1 = (bf16[128,1024]{1,0:T(8,128)(2,1)S(1)}, bf16[128,1024]{1,0:T(8,128)(2,1)S(1)}, u32[]{:S(2)}, u32[]{:S(2)}) collective-permute-start(bf16[128,1024]{1,0:T(8,128)(2,1)S(1)} %get-tuple-element.54.refs_1_), channel_id=1, source_target_pairs={{0,2},{1,3},{2,0},{3,1},{4,6},{5,7},{6,4},{7,5},{8,10},{9,11},{10,... | collective-permute-start | bytes 786440 | tf_op jit(solution)/shard_map/ppermute | solution.py:603
  7.2 14.6 %collective-permute-start.3 = (bf16[128,1024]{1,0:T(8,128)(2,1)S(1)}, bf16[128,1024]{1,0:T(8,128)(2,1)S(1)}, u32[]{:S(2)}, u32[]{:S(2)}) collective-permute-start(bf16[128,1024]{1,0:T(8,128)(2,1)S(1)} %get-tuple-element.54.refs_1_), channel_id=1, source_target_pairs={{0,4},{4,0},{1,5},{5,1},{2,6},{6,2},{3,7},{7,3},{8,12},{12,8},{9,1... | collective-permute-start | bytes 786440 | tf_op jit(solution)/shard_map/ppermute | solution.py:604
  8.7 13.2 %collective-permute-start.5 = (bf16[128,1024]{1,0:T(8,128)(2,1)S(1)}, bf16[128,1024]{1,0:T(8,128)(2,1)S(1)}, u32[]{:S(2)}, u32[]{:S(2)}) collective-permute-start(bf16[128,1024]{1,0:T(8,128)(2,1)S(1)} %get-tuple-element.54.refs_1_), channel_id=1, source_target_pairs={{0,6},{1,7},{2,4},{3,5},{4,2},{5,3},{6,0},{7,1},{8,14},{9,15},{10,... | collective-permute-start | bytes 786440 | tf_op jit(solution)/shard_map/ppermute | solution.py:605
  9.2 5.5 %collective-permute-start.8 = (bf16[272,128]{1,0:T(8,128)(2,1)S(1)}, bf16[272,128]{1,0:T(8,128)(2,1)S(1)}, u32[]{:S(2)}, u32[]{:S(2)}) collective-permute-start(bf16[272,128]{1,0:T(8,128)(2,1)S(1)} %get-tuple-element.59), channel_id=1, source_target_pairs={{0,16},{8,24},{16,0},{24,8},{1,17},{9,25},{17,1},{25,9},{2,18},{10... | collective-permute-start | bytes 208904 | tf_op jit(solution)/shard_map/ppermute | solution.py:601
  11.8 4.3 %collective-permute-start.9 = (bf16[272,128]{1,0:T(8,128)(2,1)S(1)}, bf16[272,128]{1,0:T(8,128)(2,1)S(1)}, u32[]{:S(2)}, u32[]{:S(2)}) collective-permute-start(bf16[272,128]{1,0:T(8,128)(2,1)S(1)} %get-tuple-element.60), channel_id=1, source_target_pairs={{0,24},{8,0},{16,8},{24,16},{1,25},{9,1},{17,9},{25,17},{2,26},{10... | collective-permute-start | bytes 208904 | tf_op jit(solution)/shard_map/ppermute | solution.py:601
  16.9 11.2 %all-to-all-start = ((bf16[4,32,1024]{2,1,0:T(8,128)(2,1)}), bf16[4,32,1024]{2,1,0:T(8,128)(2,1)S(1)}, u32[]{:S(2)}, u32[]{:S(2)}) async-start(bf16[4,32,1024]{2,1,0:T(8,128)(2,1)} %get-tuple-element.61.refs_5_), calls=%async_computation | async-start | bytes 524288 | tf_op jit(solution)/shard_map/all_to_all | solution.py:611
  21.3 3.5 %collective-permute-start = (bf16[128,1024]{1,0:T(8,128)(2,1)S(1)}, bf16[128,1024]{1,0:T(8,128)(2,1)S(1)}, u32[]{:S(2)}, u32[]{:S(2)}) collective-permute-start(bf16[128,1024]{1,0:T(8,128)(2,1)S(1)} %get-tuple-element.54.refs_1_), channel_id=1, source_target_pairs={{0,1},{1,0},{2,3},{3,2},{4,5},{5,4},{6,7},{7,6},{8,9},{9,8},{10,11... | collective-permute-start | bytes 786440 | tf_op jit(solution)/shard_map/ppermute | solution.py:606
  21.3 3.5 %collective-permute-start.2 = (bf16[128,1024]{1,0:T(8,128)(2,1)S(1)}, bf16[128,1024]{1,0:T(8,128)(2,1)S(1)}, u32[]{:S(2)}, u32[]{:S(2)}) collective-permute-start(bf16[128,1024]{1,0:T(8,128)(2,1)S(1)} %collective-permute-done.1.refs_3_), channel_id=1, source_target_pairs={{0,1},{1,0},{2,3},{3,2},{4,5},{5,4},{6,7},{7,6},{8,9},{9,8},{10,11... | collective-permute-start | bytes 786440 | tf_op jit(solution)/shard_map/ppermute | solution.py:606
  21.9 3.0 %collective-permute-start.4 = (bf16[128,1024]{1,0:T(8,128)(2,1)S(1)}, bf16[128,1024]{1,0:T(8,128)(2,1)S(1)}, u32[]{:S(2)}, u32[]{:S(2)}) collective-permute-start(bf16[128,1024]{1,0:T(8,128)(2,1)S(1)} %collective-permute-done.3.refs_5_), channel_id=1, source_target_pairs={{0,1},{1,0},{2,3},{3,2},{4,5},{5,4},{6,7},{7,6},{8,9},{9,8},{10,11... | collective-permute-start | bytes 786440 | tf_op jit(solution)/shard_map/ppermute | solution.py:606
  21.9 3.0 %collective-permute-start.6 = (bf16[128,1024]{1,0:T(8,128)(2,1)S(1)}, bf16[128,1024]{1,0:T(8,128)(2,1)S(1)}, u32[]{:S(2)}, u32[]{:S(2)}) collective-permute-start(bf16[128,1024]{1,0:T(8,128)(2,1)S(1)} %collective-permute-done.5.refs_7_), channel_id=1, source_target_pairs={{0,1},{1,0},{2,3},{3,2},{4,5},{5,4},{6,7},{7,6},{8,9},{9,8},{10,11... | collective-permute-start | bytes 786440 | tf_op jit(solution)/shard_map/ppermute | solution.py:606
  22.4 14.5 %collective-permute-start.10 = (bf16[256,1024]{1,0:T(8,128)(2,1)}, bf16[256,1024]{1,0:T(8,128)(2,1)}, u32[]{:S(2)}, u32[]{:S(2)}) collective-permute-start(bf16[256,1024]{1,0:T(8,128)(2,1)} %bitcast.16), channel_id=1, source_target_pairs={{0,1},{1,0},{2,3},{3,2},{4,5},{5,4},{6,7},{7,6},{8,9},{9,8},{10,11... | collective-permute-start | bytes 1572872 | tf_op jit(solution)/shard_map/ppermute | solution.py:602
  32.0 4.9 %collective-permute-start.11 = (bf16[256,512]{1,0:T(8,128)(2,1)S(1)}, bf16[256,512]{1,0:T(8,128)(2,1)S(1)}, u32[]{:S(2)}, u32[]{:S(2)}) collective-permute-start(bf16[256,512]{1,0:T(8,128)(2,1)S(1)} %get-tuple-element.65), channel_id=1, source_target_pairs={{0,1},{1,0},{2,3},{3,2},{4,5},{5,4},{6,7},{7,6},{8,9},{9,8},{10,11... | collective-permute-start | bytes 786440 | tf_op jit(solution)/shard_map/ppermute | solution.py:664
  32.0 10.9 %collective-permute-start.12 = (bf16[272,128]{1,0:T(8,128)(2,1)S(1)}, bf16[272,128]{1,0:T(8,128)(2,1)S(1)}, u32[]{:S(2)}, u32[]{:S(2)}) collective-permute-start(bf16[272,128]{1,0:T(8,128)(2,1)S(1)} %get-tuple-element.70), channel_id=1, source_target_pairs={{0,8},{8,16},{16,24},{24,0},{1,9},{9,17},{17,25},{25,1},{2,10},{10... | collective-permute-start | bytes 208904 | tf_op jit(solution)/shard_map/ppermute | solution.py:668
  33.6 9.4 %collective-permute-start.13 = (bf16[272,128]{1,0:T(8,128)(2,1)S(1)}, bf16[272,128]{1,0:T(8,128)(2,1)S(1)}, u32[]{:S(2)}, u32[]{:S(2)}) collective-permute-start(bf16[272,128]{1,0:T(8,128)(2,1)S(1)} %get-tuple-element.71), channel_id=1, source_target_pairs={{0,16},{8,24},{16,0},{24,8},{1,17},{9,25},{17,1},{25,9},{2,18},{10... | collective-permute-start | bytes 208904 | tf_op jit(solution)/shard_map/ppermute | solution.py:668
  35.4 7.6 %collective-permute-start.14 = (bf16[272,128]{1,0:T(8,128)(2,1)S(1)}, bf16[272,128]{1,0:T(8,128)(2,1)S(1)}, u32[]{:S(2)}, u32[]{:S(2)}) collective-permute-start(bf16[272,128]{1,0:T(8,128)(2,1)S(1)} %get-tuple-element.72), channel_id=1, source_target_pairs={{0,24},{8,0},{16,8},{24,16},{1,25},{9,1},{17,9},{25,17},{2,26},{10... | collective-permute-start | bytes 208904 | tf_op jit(solution)/shard_map/ppermute | solution.py:668
  43.1 16.8 %all-to-all-start.2 = ((bf16[4,128,1024]{2,1,0:T(8,128)(2,1)}), bf16[4,128,1024]{2,1,0:T(8,128)(2,1)S(1)}, u32[]{:S(2)}, u32[]{:S(2)}) async-start(bf16[4,128,1024]{2,1,0:T(8,128)(2,1)} %get-tuple-element.92), calls=%async_computation.2 | async-start | bytes 2097152 | tf_op jit(solution)/shard_map/all_to_all | solution.py:675
  46.8 8.1 %collective-permute-start.15 = (bf16[32,1024]{1,0:T(8,128)(2,1)S(1)}, bf16[32,1024]{1,0:T(8,128)(2,1)S(1)}, u32[]{:S(2)}, u32[]{:S(2)}) collective-permute-start(bf16[32,1024]{1,0:T(8,128)(2,1)S(1)} %get-tuple-element.79), channel_id=1, source_target_pairs={{0,8},{8,16},{16,24},{24,0},{1,9},{9,17},{17,25},{25,1},{2,10},{10... | collective-permute-start | bytes 196616 | tf_op jit(solution)/shard_map/ppermute | solution.py:674
  47.4 7.5 %collective-permute-start.16 = (bf16[32,1024]{1,0:T(8,128)(2,1)S(1)}, bf16[32,1024]{1,0:T(8,128)(2,1)S(1)}, u32[]{:S(2)}, u32[]{:S(2)}) collective-permute-start(bf16[32,1024]{1,0:T(8,128)(2,1)S(1)} %get-tuple-element.80), channel_id=1, source_target_pairs={{0,16},{8,24},{16,0},{24,8},{1,17},{9,25},{17,1},{25,9},{2,18},{10... | collective-permute-start | bytes 196616 | tf_op jit(solution)/shard_map/ppermute | solution.py:674
  48.5 6.5 %collective-permute-start.17 = (bf16[32,1024]{1,0:T(8,128)(2,1)S(1)}, bf16[32,1024]{1,0:T(8,128)(2,1)S(1)}, u32[]{:S(2)}, u32[]{:S(2)}) collective-permute-start(bf16[32,1024]{1,0:T(8,128)(2,1)S(1)} %get-tuple-element.81), channel_id=1, source_target_pairs={{0,24},{8,0},{16,8},{24,16},{1,25},{9,1},{17,9},{25,17},{2,26},{10... | collective-permute-start | bytes 196616 | tf_op jit(solution)/shard_map/ppermute | solution.py:674
  60.2 7.2 %collective-permute-start.18 = (bf16[32,1024]{1,0:T(8,128)(2,1)S(1)}, bf16[32,1024]{1,0:T(8,128)(2,1)S(1)}, u32[]{:S(2)}, u32[]{:S(2)}) collective-permute-start(bf16[32,1024]{1,0:T(8,128)(2,1)S(1)} %get-tuple-element.94), channel_id=1, source_target_pairs={{0,8},{8,16},{16,24},{24,0},{1,9},{9,17},{17,25},{25,1},{2,10},{10... | collective-permute-start | bytes 196616 | tf_op jit(solution)/shard_map/ppermute | solution.py:686
  61.5 7.0 %collective-permute-start.19 = (bf16[32,1024]{1,0:T(8,128)(2,1)S(1)}, bf16[32,1024]{1,0:T(8,128)(2,1)S(1)}, u32[]{:S(2)}, u32[]{:S(2)}) collective-permute-start(bf16[32,1024]{1,0:T(8,128)(2,1)S(1)} %get-tuple-element.95), channel_id=1, source_target_pairs={{0,16},{8,24},{16,0},{24,8},{1,17},{9,25},{17,1},{25,9},{2,18},{10... | collective-permute-start | bytes 196616 | tf_op jit(solution)/shard_map/ppermute | solution.py:686
  62.4 6.1 %collective-permute-start.20 = (bf16[32,1024]{1,0:T(8,128)(2,1)S(1)}, bf16[32,1024]{1,0:T(8,128)(2,1)S(1)}, u32[]{:S(2)}, u32[]{:S(2)}) collective-permute-start(bf16[32,1024]{1,0:T(8,128)(2,1)S(1)} %get-tuple-element.96), channel_id=1, source_target_pairs={{0,24},{8,0},{16,8},{24,16},{1,25},{9,1},{17,9},{25,17},{2,26},{10... | collective-permute-start | bytes 196616 | tf_op jit(solution)/shard_map/ppermute | solution.py:686
  64.6 10.3 %all-to-all-start.1 = ((f32[32,1,384]{2,1,0:T(1,128)}), f32[32,1,384]{2,1,0:T(1,128)S(1)}, u32[]{:S(2)}, u32[]{:S(2)}) async-start(f32[32,1,384]{2,1,0:T(1,128)} %get-tuple-element.87), calls=%async_computation.1 | async-start | bytes 98304 | tf_op jit(solution)/shard_map/all_to_all | solution.py:690
  68.6 7.0 %collective-permute-start.21 = (bf16[32,1024]{1,0:T(8,128)(2,1)S(1)}, bf16[32,1024]{1,0:T(8,128)(2,1)S(1)}, u32[]{:S(2)}, u32[]{:S(2)}) collective-permute-start(bf16[32,1024]{1,0:T(8,128)(2,1)S(1)} %add_blocks.1.refs_0_), channel_id=1, source_target_pairs={{0,8},{8,16},{16,24},{24,0},{1,9},{9,17},{17,25},{25,1},{2,10},{10... | collective-permute-start | bytes 196616 | tf_op jit(solution)/shard_map/ppermute | solution.py:688
  69.9 7.2 %collective-permute-start.22 = (bf16[32,1024]{1,0:T(8,128)(2,1)S(1)}, bf16[32,1024]{1,0:T(8,128)(2,1)S(1)}, u32[]{:S(2)}, u32[]{:S(2)}) collective-permute-start(bf16[32,1024]{1,0:T(8,128)(2,1)S(1)} %add_blocks.1.refs_0_), channel_id=1, source_target_pairs={{0,16},{8,24},{16,0},{24,8},{1,17},{9,25},{17,1},{25,9},{2,18},{10... | collective-permute-start | bytes 196616 | tf_op jit(solution)/shard_map/ppermute | solution.py:688
  71.7 5.6 %collective-permute-start.23 = (bf16[32,1024]{1,0:T(8,128)(2,1)S(1)}, bf16[32,1024]{1,0:T(8,128)(2,1)S(1)}, u32[]{:S(2)}, u32[]{:S(2)}) collective-permute-start(bf16[32,1024]{1,0:T(8,128)(2,1)S(1)} %add_blocks.1.refs_0_), channel_id=1, source_target_pairs={{0,24},{8,0},{16,8},{24,16},{1,25},{9,1},{17,9},{25,17},{2,26},{10... | collective-permute-start | bytes 196616 | tf_op jit(solution)/shard_map/ppermute | solution.py:688
